TPU v7x, 32 devices: a whole 2x2x4 slice. The times are simulated.
32 devices in a mesh: dp: 16 (over z, y, x), tensor: 2 (over core).
Axes of the slice: x: 2, y: 2, z: 4, core: 2. Of those that a mesh axis runs over, the one named last changes fastest.
Arguments:
- tokens: bfloat16 [4096, 2048], P(('dp', 'tensor')), may hold values from -6 to 6
- w_query: bfloat16 [2048, 2048], P('dp', 'tensor'), may hold values from -0.125 to 0.125
- key_weight: bfloat16 [2048, 1024], P('dp', 'tensor'), may hold values from -0.125 to 0.125
- value_weight: bfloat16 [2048, 1024], P('dp', 'tensor'), may hold values from -0.125 to 0.125
- w_out: bfloat16 [2048, 2048], P('tensor', 'dp'), may hold values from -0.375 to 0.375
- gain_attn: bfloat16 [2048], P('dp'), may hold values from 0.25 to 1.75
- w_gate: bfloat16 [2048, 8192], P('dp', 'tensor'), may hold values from -0.125 to 0.125
- w_up: bfloat16 [2048, 8192], P('dp', 'tensor'), may hold values from -0.125 to 0.125
- w_down: bfloat16 [8192, 2048], P('tensor', 'dp'), may hold values from -0.09375 to 0.09375
- gain_mlp: bfloat16 [2048], P('dp'), may hold values from 0.25 to 1.75
- cotangent: bfloat16 [4096, 2048], P(('dp', 'tensor')), may hold values from -6 to 6
- lengths: int32 [16], replicated, may hold values from 160 to 256, as said below
- seq_of_group: int32 [16], P('dp'), may hold values from 0 to 15, each once
Outputs:
- output: bfloat16 [4096, 2048], P(('dp', 'tensor'))
- grad_tokens: float32 [4096, 2048], P(('dp', 'tensor'))
- grad_w_query: float32 [2048, 2048], P('dp', 'tensor')
- grad_w_key: float32 [2048, 1024], P('dp', 'tensor')
- grad_w_value: float32 [2048, 1024], P('dp', 'tensor')
- grad_w_out: float32 [2048, 2048], P('tensor', 'dp')
- grad_gain_attn: float32 [2048], P('dp')
- grad_w_gate: float32 [2048, 8192], P('dp', 'tensor')
- grad_w_up: float32 [2048, 8192], P('dp', 'tensor')
- grad_w_down: float32 [8192, 2048], P('tensor', 'dp')
- grad_gain_mlp: float32 [2048], P('dp')
Inputs may be any that keep to these rules, and one draw needn't show every extreme that they name: `lengths`: every length lies in 160 to 256; both ends are reached in every draw. `seq_of_group`: A permutation of 0 to 15.
All inputs are finite; a program needn't handle non-finite values.
Results may differ from a plain program's by a relative error of at most 0.015.
Values may be sent and summed in bfloat16 or wider, within the bound.
A program may use at most 320 MiB of HBM per device.

v0:
```python
import math

import jax
import jax.numpy as jnp
from jax import lax
from jax.sharding import PartitionSpec as P

HEAD_SIZE = 256


EPS = 1e-06
THETA = 1000042.0


def rope_tables(count, head_dim):
    half = head_dim // 2
    index = jnp.arange(half, dtype=jnp.float32)
    freqs = jnp.exp(index * (-2.0 * math.log(THETA) / head_dim))
    angles = jnp.arange(count, dtype=jnp.float32)[:, None] * freqs[None, :]
    return (jnp.cos(angles)[:, None, :], jnp.sin(angles)[:, None, :])


def apply_rotary(values, cosine_table, rotary_sine_table):
    half = values.shape[-1] // 2
    first = values[..., :half]
    second = values[..., half:]
    return jnp.concatenate(
        [
            first * cosine_table - second * rotary_sine_table,
            second * cosine_table + first * rotary_sine_table,
        ],
        -1,
    )


def rotate_back(grads, cosine_table, rotary_sine_table):
    half = grads.shape[-1] // 2
    first = grads[..., :half]
    second = grads[..., half:]
    return jnp.concatenate(
        [
            first * cosine_table + second * rotary_sine_table,
            second * cosine_table - first * rotary_sine_table,
        ],
        -1,
    )


def dot_nt(left, right):
    return lax.dot_general(
        left, right, (((1,), (1,)), ((), ())), preferred_element_type=jnp.float32
    )


def dot_tn(left, right):
    return lax.dot_general(
        left, right, (((0,), (0,)), ((), ())), preferred_element_type=jnp.float32
    )


def gather_rows(values):
    return lax.all_gather(values, "tensor", axis=0, tiled=True)


def sum_rows(values):
    return lax.psum_scatter(values, "tensor", scatter_dimension=0, tiled=True)


def norm_back(inputs, factor, gain, upstream):
    scaled = upstream * gain
    grad_in = factor * scaled - inputs * factor**3 * jnp.mean(scaled * inputs, -1, keepdims=True)
    return (grad_in, jnp.sum(upstream * inputs * factor, 0))


def shards(
    tokens,
    w_query,
    key_weight,
    value_weight,
    w_out,
    gain_attn,
    w_gate,
    w_up,
    w_down,
    gain_mlp,
    cotangent,
    lengths,
    seq_of_group,
):
    local_rows = tokens.shape[0]
    full_rows = local_rows * lax.axis_size("tensor")
    q_heads = w_query.shape[1] // HEAD_SIZE
    kv_heads = key_weight.shape[1] // HEAD_SIZE
    group_size = q_heads // kv_heads
    score_scale = HEAD_SIZE ** (-0.5)
    chosen = jnp.sum(
        jnp.where(jnp.arange(lengths.shape[0], dtype=jnp.int32) == seq_of_group[0], lengths, 0)
    )
    positions = lax.axis_index("tensor") * local_rows + jnp.arange(local_rows, dtype=jnp.int32)
    valid_rows = (positions < chosen).astype(jnp.float32)[:, None]
    row_ids = jnp.arange(full_rows, dtype=jnp.int32)
    key_allowed = (row_ids[None, :] <= row_ids[:, None]) & (row_ids[None, :] < chosen)
    cosine_table, rotary_sine_table = rope_tables(full_rows, HEAD_SIZE)
    inputs = tokens.astype(jnp.float32)
    query_full, key_full, value_full, out_full, attn_gain = (
        lax.all_gather(w_query, "dp", axis=0, tiled=True),
        lax.all_gather(key_weight, "dp", axis=0, tiled=True),
        lax.all_gather(value_weight, "dp", axis=0, tiled=True),
        lax.all_gather(w_out, "dp", axis=1, tiled=True),
        lax.all_gather(gain_attn, "dp", axis=0, tiled=True),
    )
    attn_factor = lax.rsqrt(jnp.mean(inputs * inputs, -1, keepdims=True) + EPS)
    attention_normed_input = gather_rows(
        (inputs * attn_factor * attn_gain.astype(jnp.float32)).astype(jnp.bfloat16)
    )
    query_rows = apply_rotary(
        jnp.dot(attention_normed_input, query_full, preferred_element_type=jnp.float32).reshape(
            full_rows, q_heads, HEAD_SIZE
        ),
        cosine_table,
        rotary_sine_table,
    ).astype(jnp.bfloat16)
    key_row_block = apply_rotary(
        jnp.dot(attention_normed_input, key_full, preferred_element_type=jnp.float32).reshape(
            full_rows, kv_heads, HEAD_SIZE
        ),
        cosine_table,
        rotary_sine_table,
    ).astype(jnp.bfloat16)
    value_row_block = (
        jnp.dot(attention_normed_input, value_full, preferred_element_type=jnp.float32)
        .astype(jnp.bfloat16)
        .reshape(full_rows, kv_heads, HEAD_SIZE)
    )
    grouped_query_rows = query_rows.reshape(full_rows, kv_heads, group_size, HEAD_SIZE)

    def masked_scores():
        scores = (
            jnp.einsum(
                "skgd,tkd->kgst",
                grouped_query_rows,
                key_row_block,
                preferred_element_type=jnp.float32,
            )
            * score_scale
        )
        return jnp.where(key_allowed, scores, -1e30)

    scores = masked_scores()
    row_max = jnp.max(scores, -1, keepdims=True)
    row_exp = jnp.exp(scores - row_max)
    row_total = jnp.sum(row_exp, -1, keepdims=True)
    log_total = row_max + jnp.log(row_total)
    probs_low = (row_exp / row_total).astype(jnp.bfloat16)
    attended = (
        jnp.einsum("kgst,tkd->skgd", probs_low, value_row_block, preferred_element_type=jnp.float32)
        .reshape(full_rows, q_heads * HEAD_SIZE)
        .astype(jnp.bfloat16)
    )
    middle = inputs + sum_rows(jnp.dot(attended, out_full, preferred_element_type=jnp.float32))
    gate_full, up_full, down_full, mlp_gain = (
        lax.all_gather(w_gate, "dp", axis=0, tiled=True),
        lax.all_gather(w_up, "dp", axis=0, tiled=True),
        lax.all_gather(w_down, "dp", axis=1, tiled=True),
        lax.all_gather(gain_mlp, "dp", axis=0, tiled=True),
    )
    mlp_factor = lax.rsqrt(jnp.mean(middle * middle, -1, keepdims=True) + EPS)
    normed_mlp = gather_rows(
        (middle * mlp_factor * mlp_gain.astype(jnp.float32)).astype(jnp.bfloat16)
    )
    gate_lin = jnp.dot(normed_mlp, gate_full, preferred_element_type=jnp.float32)
    up_lin = jnp.dot(normed_mlp, up_full, preferred_element_type=jnp.float32)
    sigmoid_gate = jax.nn.sigmoid(gate_lin)
    silu_gate = gate_lin * sigmoid_gate
    hidden = (silu_gate * up_lin).astype(jnp.bfloat16)
    outputs = middle + sum_rows(jnp.dot(hidden, down_full, preferred_element_type=jnp.float32))
    gate_full, up_full, down_full, mlp_gain = (
        lax.all_gather(w_gate, "dp", axis=0, tiled=True),
        lax.all_gather(w_up, "dp", axis=0, tiled=True),
        lax.all_gather(w_down, "dp", axis=1, tiled=True),
        lax.all_gather(gain_mlp, "dp", axis=0, tiled=True),
    )
    grad_out = cotangent.astype(jnp.float32) * valid_rows
    grad_mlp = gather_rows(grad_out.astype(jnp.bfloat16))
    grad_down = dot_tn(hidden, grad_mlp)
    grad_hidden = dot_nt(grad_mlp, down_full)
    grad_gate_low = (
        grad_hidden * up_lin * sigmoid_gate * (1.0 + gate_lin * (1.0 - sigmoid_gate))
    ).astype(jnp.bfloat16)
    grad_up_low = (grad_hidden * silu_gate).astype(jnp.bfloat16)
    grad_norm_mlp = sum_rows(dot_nt(grad_gate_low, gate_full) + dot_nt(grad_up_low, up_full))
    grad_gate_w = dot_tn(normed_mlp, grad_gate_low)
    grad_up_w = dot_tn(normed_mlp, grad_up_low)
    grad_mid_norm, gain_mlp_part = norm_back(
        middle, mlp_factor, mlp_gain.astype(jnp.float32), grad_norm_mlp
    )
    grad_middle = grad_out + grad_mid_norm
    grad_gate_w, grad_up_w, grad_down, gain_mlp_sum = (
        lax.psum_scatter(grad_gate_w, "dp", scatter_dimension=0, tiled=True),
        lax.psum_scatter(grad_up_w, "dp", scatter_dimension=0, tiled=True),
        lax.psum_scatter(grad_down, "dp", scatter_dimension=1, tiled=True),
        lax.psum_scatter(gain_mlp_part, "dp", scatter_dimension=0, tiled=True),
    )
    query_full, key_full, value_full, out_full, attn_gain = (
        lax.all_gather(w_query, "dp", axis=0, tiled=True),
        lax.all_gather(key_weight, "dp", axis=0, tiled=True),
        lax.all_gather(value_weight, "dp", axis=0, tiled=True),
        lax.all_gather(w_out, "dp", axis=1, tiled=True),
        lax.all_gather(gain_attn, "dp", axis=0, tiled=True),
    )
    grad_attn = gather_rows(grad_middle.astype(jnp.bfloat16))
    grad_out_w = dot_tn(attended, grad_attn)
    grad_attended = dot_nt(grad_attn, out_full).astype(jnp.bfloat16)
    grad_groups = grad_attended.reshape(full_rows, kv_heads, group_size, HEAD_SIZE)
    probs = jnp.exp(masked_scores() - log_total)
    grad_probs = jnp.einsum(
        "skgd,tkd->kgst", grad_groups, value_row_block, preferred_element_type=jnp.float32
    )
    grad_scores = (probs * (grad_probs - jnp.sum(probs * grad_probs, -1, keepdims=True))).astype(
        jnp.bfloat16
    )
    grad_queries = (
        jnp.einsum("kgst,tkd->skgd", grad_scores, key_row_block, preferred_element_type=jnp.float32)
        * score_scale
    )
    grad_keys = (
        jnp.einsum(
            "kgst,skgd->tkd", grad_scores, grouped_query_rows, preferred_element_type=jnp.float32
        )
        * score_scale
    )
    grad_values = jnp.einsum(
        "kgst,skgd->tkd",
        probs.astype(jnp.bfloat16),
        grad_groups,
        preferred_element_type=jnp.float32,
    )
    query_low = (
        rotate_back(
            grad_queries.reshape(full_rows, q_heads, HEAD_SIZE), cosine_table, rotary_sine_table
        )
        .reshape(full_rows, q_heads * HEAD_SIZE)
        .astype(jnp.bfloat16)
    )
    key_low = (
        rotate_back(grad_keys, cosine_table, rotary_sine_table)
        .reshape(full_rows, kv_heads * HEAD_SIZE)
        .astype(jnp.bfloat16)
    )
    value_low = grad_values.reshape(full_rows, kv_heads * HEAD_SIZE).astype(jnp.bfloat16)
    grad_norm_attn = sum_rows(
        dot_nt(query_low, query_full) + dot_nt(key_low, key_full) + dot_nt(value_low, value_full)
    )
    grad_query_w = dot_tn(attention_normed_input, query_low)
    grad_key_w = dot_tn(attention_normed_input, key_low)
    grad_value_w = dot_tn(attention_normed_input, value_low)
    grad_in_norm, gain_attn_part = norm_back(
        inputs, attn_factor, attn_gain.astype(jnp.float32), grad_norm_attn
    )
    grad_inputs = grad_middle + grad_in_norm
    grad_query_w, grad_key_w, grad_value_w, grad_out_w, gain_attn_sum = (
        lax.psum_scatter(grad_query_w, "dp", scatter_dimension=0, tiled=True),
        lax.psum_scatter(grad_key_w, "dp", scatter_dimension=0, tiled=True),
        lax.psum_scatter(grad_value_w, "dp", scatter_dimension=0, tiled=True),
        lax.psum_scatter(grad_out_w, "dp", scatter_dimension=1, tiled=True),
        lax.psum_scatter(gain_attn_part, "dp", scatter_dimension=0, tiled=True),
    )
    gain_attn_sum, gain_mlp_sum = lax.psum((gain_attn_sum, gain_mlp_sum), "tensor")
    return (
        outputs.astype(jnp.bfloat16),
        grad_inputs,
        grad_query_w,
        grad_key_w,
        grad_value_w,
        grad_out_w,
        gain_attn_sum,
        grad_gate_w,
        grad_up_w,
        grad_down,
        gain_mlp_sum,
    )


def solution(mesh):
    in_specs = (
        P(("dp", "tensor"), None),
        P("dp", "tensor"),
        P("dp", "tensor"),
        P("dp", "tensor"),
        P("tensor", "dp"),
        P("dp"),
        P("dp", "tensor"),
        P("dp", "tensor"),
        P("tensor", "dp"),
        P("dp"),
        P(("dp", "tensor"), None),
        P(),
        P("dp"),
    )
    out_specs = (
        P(("dp", "tensor"), None),
        P(("dp", "tensor"), None),
        P("dp", "tensor"),
        P("dp", "tensor"),
        P("dp", "tensor"),
        P("tensor", "dp"),
        P("dp"),
        P("dp", "tensor"),
        P("dp", "tensor"),
        P("tensor", "dp"),
        P("dp"),
    )
    return jax.shard_map(shards, mesh=mesh, in_specs=in_specs, out_specs=out_specs, check_vma=False)
```

profile of v0, /device:TPU:8, one launch (start us, length us, event | category | flops | bytes accessed | tf_op | source)
XLA Modules:
  0.0 3800.2 jit_solution(193314446953888339)
XLA Ops:
  7.2 1.2 fusion.6
  9.1 34.5 all-gather
  43.6 2.0 fusion.8
  49.0 1.3 fusion.25
  50.9 0.7 fusion.20
  52.2 5.1 all-gather.14.cloned.1.call-done
  57.2 64.5 %all-gather.16.cloned.1.call-done = bf16[2048,512]{1,0:T(8,128)(2,1)} async-done(((bf16[128,512]{1,0:T(8,128)(2,1)}), bf16[2048,512]{1,0:T(8,128)(2,1)}) %all-gather.16.cloned.1.call-update) | async-done | bytes 2097168 | tf_op jit(solution)/shard_map/all_gather | solution.py:108
  121.7 2.6 convolution_convert_fusion.2
  124.3 0.8 reshape.149
  125.1 58.8 %all-gather.18.cloned.1.call-done = bf16[2048,512]{1,0:T(8,128)(2,1)} async-done(((bf16[128,512]{1,0:T(8,128)(2,1)}), bf16[2048,512]{1,0:T(8,128)(2,1)}) %all-gather.18.cloned.1.call-update) | async-done | bytes 2097168 | tf_op jit(solution)/shard_map/all_gather | solution.py:107
  183.9 2.3 fusion.33
  186.7 0.7 subtract_convert_fusion.3
  187.5 73.8 %all-gather.20.cloned.1.call-done = bf16[2048,1024]{1,0:T(8,128)(2,1)} async-done(((bf16[128,1024]{1,0:T(8,128)(2,1)}), bf16[2048,1024]{1,0:T(8,128)(2,1)}) %all-gather.20.cloned.1.call-update) | async-done | bytes 4194320 | tf_op jit(solution)/shard_map/all_gather | solution.py:106
  261.2 3.4 fusion.34
  265.6 1.4 fusion.32
  268.2 81.6 %all-gather.22.cloned.1.call-done = bf16[1024,2048]{1,0:T(8,128)(2,1)} async-done(((bf16[1024,128]{1,0:T(8,128)(2,1)}), bf16[1024,2048]{1,0:T(8,128)(2,1)}) %all-gather.22.cloned.1.call-update) | async-done | bytes 4194320 | tf_op jit(solution)/shard_map/all_gather | solution.py:109
  349.8 4.8 fusion.35
  354.6 33.2 all-gather.1
  387.8 1.6 multiply_reduce_fusion.3
  390.5 0.9 multiply_convert_fusion.4
  394.2 2.0 fusion.15
  397.5 5.7 all-gather.24.cloned.1.call-done
  403.1 193.9 %all-gather.28.cloned.1.call-done = bf16[2048,4096]{1,0:T(8,128)(2,1)} async-done(((bf16[128,4096]{1,0:T(8,128)(2,1)}), bf16[2048,4096]{1,0:T(8,128)(2,1)}) %all-gather.28.cloned.1.call-update) | async-done | bytes 16777232 | tf_op jit(solution)/shard_map/all_gather | solution.py:163
  597.0 12.6 fusion.37
  609.6 180.4 %all-gather.26.cloned.1.call-done = bf16[2048,4096]{1,0:T(8,128)(2,1)} async-done(((bf16[128,4096]{1,0:T(8,128)(2,1)}), bf16[2048,4096]{1,0:T(8,128)(2,1)}) %all-gather.26.cloned.1.call-update) | async-done | bytes 16777232 | tf_op jit(solution)/shard_map/all_gather | solution.py:162
  790.0 12.6 fusion.36
  802.6 250.6 %all-gather.30.cloned.1.call-done = bf16[4096,2048]{1,0:T(8,128)(2,1)} async-done(((bf16[4096,128]{1,0:T(8,128)(2,1)}), bf16[4096,2048]{1,0:T(8,128)(2,1)}) %all-gather.30.cloned.1.call-update) | async-done | bytes 16777232 | tf_op jit(solution)/shard_map/all_gather | solution.py:164
  1053.2 13.5 multiply_convert_fusion
  1066.6 12.3 fusion.39
  1078.9 12.9 convolution_add_fusion.2
  1092.1 12.4 fusion.38
  1104.6 1.5 multiply_reduce_fusion
  1106.6 8.5 reduce-scatter.14.cloned.1.call-done
  1115.1 3.5 fusion.29
  1119.4 9.6 all-gather.34.cloned.1.call-done
  1129.1 4.6 convolution_convert_fusion.1
  1133.6 1.2 copy.99
  1136.9 0.9 fusion.30
  1137.8 1.3 copy.98
  1139.9 3.6 fusion.40
  1143.6 0.8 convolution_add_fusion.1
  1144.3 0.8 copy-done.5
  1145.1 2.2 convolution_add_fusion
  1147.4 2.8 fusion.43
  1150.5 2.7 fusion.42
  1153.3 4.6 fusion.41
  1158.0 1.2 copy-done.10
  1159.3 4.5 fusion.44
  1163.9 1.1 copy-done.2
  1165.7 13.3 fusion.46
  1179.1 1.5 copy-done.7
  1180.6 13.3 fusion.45
  1194.1 1.5 copy-done.4
  1195.9 13.4 fusion.47
  1211.2 1.5 fusion.14
  1212.7 71.9 %all-reduce.2 = (f32[2048]{0:T(1024)S(1)}, f32[2048]{0:T(1024)S(1)}) all-reduce(f32[2048]{0:T(1024)S(1)} %get-tuple-element.13, f32[2048]{0:T(1024)S(1)} %get-tuple-element.11), channel_id=10, replica_groups=mesh['dp'=16,'tensor'=2] {'dp'}, use_global_device_ids=true, to_apply=%region_17.18.clone | all-reduce | flops 4096 | bytes 32768
  1284.8 3.0 all-reduce.3
  1287.8 2.7 fusion.11
  1290.4 64.2 %reduce-scatter.22.cloned.1.call-done = f32[128,512]{1,0:T(8,128)} async-done(((f32[2048,512]{1,0:T(8,128)}), f32[128,512]{1,0:T(8,128)}) %reduce-scatter.22.cloned.1.call-update) | async-done | bytes 262160 | tf_op jit(solution)/shard_map/reduce_scatter | solution.py:263
  1354.6 182.2 %reduce-scatter.20.cloned.1.call-done = f32[128,1024]{1,0:T(8,128)} async-done(((f32[2048,1024]{1,0:T(8,128)}), f32[128,1024]{1,0:T(8,128)}) %reduce-scatter.20.cloned.1.call-update) | async-done | bytes 524304 | tf_op jit(solution)/shard_map/reduce_scatter | solution.py:262
  1536.8 183.1 %reduce-scatter.26.cloned.1.call-done = f32[1024,128]{1,0:T(8,128)} async-done(((f32[1024,2048]{1,0:T(8,128)}), f32[1024,128]{1,0:T(8,128)}) %reduce-scatter.26.cloned.1.call-update) | async-done | bytes 524304 | tf_op jit(solution)/shard_map/reduce_scatter | solution.py:265
  1720.0 688.9 %reduce-scatter.30.cloned.1.call-done = f32[128,4096]{1,0:T(8,128)} async-done(((f32[2048,4096]{1,0:T(8,128)}), f32[128,4096]{1,0:T(8,128)}) %reduce-scatter.30.cloned.1.call-update) | async-done | bytes 2097168 | tf_op jit(solution)/shard_map/reduce_scatter | solution.py:200
  2408.9 692.0 %reduce-scatter.28.cloned.1.call-done = f32[128,4096]{1,0:T(8,128)} async-done(((f32[2048,4096]{1,0:T(8,128)}), f32[128,4096]{1,0:T(8,128)}) %reduce-scatter.28.cloned.1.call-update) | async-done | bytes 2097168 | tf_op jit(solution)/shard_map/reduce_scatter | solution.py:199
  3100.9 692.0 %reduce-scatter.32.cloned.1.call-done = f32[4096,128]{1,0:T(8,128)} async-done(((f32[4096,2048]{1,0:T(8,128)}), f32[4096,128]{1,0:T(8,128)}) %reduce-scatter.32.cloned.1.call-update) | async-done | bytes 2097168 | tf_op jit(solution)/shard_map/reduce_scatter | solution.py:201
  (140 shorter events, 19.6 us)
Async XLA Ops:
  7.2 50.1 %all-gather.14.cloned.1.call-start = ((), (), s32[]{:S(2)}) async-start(), calls=%async_computation.11 | async-start | bytes 1572864 | tf_op jit(solution)/shard_map/all_gather | solution.py:62
  9.1 43.1 %copy-start.24 = (f32[128]{0:T(128)}, f32[128]{0:T(128)S(1)}, u32[]{:S(2)}) copy-start(f32[128]{0:T(128)S(1)} %get-tuple-element.40) | copy-start | bytes 1540
  43.6 8.6 copy-start.20
  45.6 76.1 %all-gather.16.cloned.1.call-start = ((), (), s32[]{:S(2)}) async-start(), calls=%async_computation.12 | async-start | bytes 2228224 | tf_op jit(solution)/shard_map/all_gather | solution.py:108
  46.4 137.5 %all-gather.18.cloned.1.call-start = ((), (), s32[]{:S(2)}) async-start(), calls=%async_computation.13 | async-start | bytes 2228224 | tf_op jit(solution)/shard_map/all_gather | solution.py:107
  47.1 214.1 %all-gather.20.cloned.1.call-start = ((), (), s32[]{:S(2)}) async-start(), calls=%async_computation.14 | async-start | bytes 4456448 | tf_op jit(solution)/shard_map/all_gather | solution.py:106
  47.7 302.1 %all-gather.22.cloned.1.call-start = ((), (), s32[]{:S(2)}) async-start(), calls=%async_computation.15 | async-start | bytes 4456448 | tf_op jit(solution)/shard_map/all_gather | solution.py:109
  48.3 339.6 %reduce-scatter.12.cloned.1.call-start = ((), (), s32[]{:S(2)}) async-start(), calls=%async_computation.16 | async-start | bytes 3145728 | tf_op jit(solution)/shard_map/reduce_scatter | solution.py:66
  57.2 126.6 %copy-start = (bf16[256,2048]{1,0:T(8,128)(2,1)S(1)}, bf16[256,2048]{1,0:T(8,128)(2,1)}, u32[]{:S(2)}) copy-start(bf16[256,2048]{1,0:T(8,128)(2,1)} %all-gather.14.cloned.1.call-done) | copy-start | bytes 3145732
  265.2 2.6 copy-start.11
  265.5 2.6 copy-start.16
  265.6 1.6 copy-start.18
  267.0 0.6 copy-start.22
  267.2 0.6 copy-start.23
  268.2 86.4 %copy-start.13 = (bf16[2,256,2,256]{3,1,2,0:T(8,128)(2,1)}, bf16[2,256,2,256]{3,1,2,0:T(8,128)(2,1)S(1)}, u32[]{:S(2)}) copy-start(bf16[2,256,2,256]{3,1,2,0:T(8,128)(2,1)S(1)} %convolution_convert_fusion) | copy-start | bytes 1572868
  349.8 4.9 copy-start.29
  354.6 48.5 %all-gather.24.cloned.1.call-start = ((), (), s32[]{:S(2)}) async-start(), calls=%async_computation.17 | async-start | bytes 1572864 | tf_op jit(solution)/shard_map/all_gather | solution.py:62
  389.9 0.6 copy-start.26
  391.5 205.5 %all-gather.28.cloned.1.call-start = ((), (), s32[]{:S(2)}) async-start(), calls=%async_computation.19 | async-start | bytes 17825792 | tf_op jit(solution)/shard_map/all_gather | solution.py:163
  392.2 397.7 %all-gather.26.cloned.1.call-start = ((), (), s32[]{:S(2)}) async-start(), calls=%async_computation.18 | async-start | bytes 17825792 | tf_op jit(solution)/shard_map/all_gather | solution.py:162
  393.0 409.6 %all-gather.32.cloned.1.call-start = ((), (), s32[]{:S(2)}) async-start(), calls=%async_computation.22 | async-start | bytes 1572864 | tf_op jit(solution)/shard_map/all_gather | solution.py:62
  393.7 0.5 copy-start.27
  396.2 657.0 %all-gather.30.cloned.1.call-start = ((), (), s32[]{:S(2)}) async-start(), calls=%async_computation.20 | async-start | bytes 17825792 | tf_op jit(solution)/shard_map/all_gather | solution.py:164
  396.9 707.7 %reduce-scatter.16.cloned.1.call-start = ((), (), s32[]{:S(2)}) async-start(), calls=%async_computation.23 | async-start | bytes 3145728 | tf_op jit(solution)/shard_map/reduce_scatter | solution.py:66
  1091.8 23.3 reduce-scatter.14.cloned.1.call-start
  1104.5 24.5 all-gather.34.cloned.1.call-start
  1118.7 92.5 %reduce-scatter.18.cloned.1.call-start = ((), (), s32[]{:S(2)}) async-start(), calls=%async_computation.25 | async-start | bytes 3145728 | tf_op jit(solution)/shard_map/reduce_scatter | solution.py:66
  1119.4 15.8 copy-start.12
  1134.9 1.0 copy-start.17
  1134.9 1.0 copy-start.19
  1134.9 1.3 copy-start.15
  1139.8 3.7 copy-start.6
  1143.6 1.6 copy-start.5
  1147.3 143.1 %reduce-scatter.24.cloned.1.call-start = ((), (), s32[]{:S(2)}) async-start(), calls=%async_computation.28 | async-start | bytes 4456448 | tf_op jit(solution)/shard_map/reduce_scatter | solution.py:264
  1150.2 204.4 %reduce-scatter.22.cloned.1.call-start = ((), (), s32[]{:S(2)}) async-start(), calls=%async_computation.27 | async-start | bytes 4456448 | tf_op jit(solution)/shard_map/reduce_scatter | solution.py:263
  1153.3 383.6 %reduce-scatter.20.cloned.1.call-start = ((), (), s32[]{:S(2)}) async-start(), calls=%async_computation.26 | async-start | bytes 8912896 | tf_op jit(solution)/shard_map/reduce_scatter | solution.py:262
  1157.9 1.2 copy-start.10
  1157.9 1.4 copy-start.14
  1157.9 562.0 %reduce-scatter.26.cloned.1.call-start = ((), (), s32[]{:S(2)}) async-start(), calls=%async_computation.29 | async-start | bytes 8912896 | tf_op jit(solution)/shard_map/reduce_scatter | solution.py:265
  1163.8 1.2 copy-start.2
  1163.8 1.9 copy-start.8
  1163.8 1245.1 %reduce-scatter.30.cloned.1.call-start = ((), (), s32[]{:S(2)}) async-start(), calls=%async_computation.31 | async-start | bytes 35651584 | tf_op jit(solution)/shard_map/reduce_scatter | solution.py:200
  1179.0 1.6 copy-start.7
  1179.1 1921.8 %reduce-scatter.28.cloned.1.call-start = ((), (), s32[]{:S(2)}) async-start(), calls=%async_computation.30 | async-start | bytes 35651584 | tf_op jit(solution)/shard_map/reduce_scatter | solution.py:199
  1194.0 1.6 copy-start.4
  1194.0 1.9 copy-start.9
  1194.0 2598.9 %reduce-scatter.32.cloned.1.call-start = ((), (), s32[]{:S(2)}) async-start(), calls=%async_computation.32 | async-start | bytes 35651584 | tf_op jit(solution)/shard_map/reduce_scatter | solution.py:201
  1209.2 0.7 copy-start.30
  1209.2 1.9 copy-start.1
  1209.2 1.9 copy-start.21
  1209.2 1.9 copy-start.25
  1209.3 78.5 %copy-start.3 = (f32[128,2048]{1,0:T(8,128)S(1)}, f32[128,2048]{1,0:T(8,128)}, u32[]{:S(2)}) copy-start(f32[128,2048]{1,0:T(8,128)} %get-tuple-element.20) | copy-start | bytes 3145732
  1209.3 78.5 %copy-start.28 = (f32[128]{0:T(128)S(1)}, f32[128]{0:T(128)}, u32[]{:S(2)}) copy-start(f32[128]{0:T(128)} %get-tuple-element.39) | copy-start | bytes 1540
Sparse Core Ops, SparseCore 0:
  45.7 11.4 all-gather.13
  60.0 61.6 all-gather.15
  124.5 59.3 all-gather.17
  186.5 74.6 all-gather.19
  263.8 85.9 all-gather.21
  354.7 9.8 reduce-scatter.11
  391.6 11.4 all-gather.23
  406.3 190.6 all-gather.27
  600.1 189.7 all-gather.25
  792.0 9.3 all-gather.31
  804.5 248.6 all-gather.29
  1091.9 9.9 reduce-scatter.15
  1104.6 10.4 reduce-scatter.13
  1118.8 10.1 all-gather.33
  1147.4 10.7 reduce-scatter.17
  1161.0 96.8 reduce-scatter.23
  1260.6 93.9 reduce-scatter.21
  1357.3 179.4 reduce-scatter.19
  1539.7 180.2 reduce-scatter.25
  1722.7 686.0 reduce-scatter.29
  2411.8 689.0 reduce-scatter.27
  3103.8 689.0 reduce-scatter.31
where the time goes:
time: 3810 us; the launch traced here: 3800 us
  waiting for transfers between devices  3440 us (90%)
  matrix products  158 us (4%)
  blocking collectives  143 us (4%)
    reduce_scatter x1, waiting for transfers between devices, shards(): lax.psum_scatter(grad_gate_w, 'dp', scatter_dimension=0, tiled=True)  692 us
    reduce_scatter x1, waiting for transfers between devices, shards(): lax.psum_scatter(grad_down, 'dp', scatter_dimension=1, tiled=True)  692 us
    reduce_scatter x1, waiting for transfers between devices, shards(): lax.psum_scatter(grad_up_w, 'dp', scatter_dimension=0, tiled=True)  689 us
    all_gather x1, waiting for transfers between devices, shards(): lax.all_gather(w_down, 'dp', axis=1, tiled=True)  251 us
    all_gather x1, waiting for transfers between devices, shards(): lax.all_gather(w_up, 'dp', axis=0, tiled=True)  194 us
    reduce_scatter x1, waiting for transfers between devices, shards(): lax.psum_scatter(grad_out_w, 'dp', scatter_dimension=1, tiled=True)  183 us
    reduce_scatter x1, waiting for transfers between devices, shards(): lax.psum_scatter(grad_query_w, 'dp', scatter_dimension=0, tiled=True)  182 us
    all_gather x1, waiting for transfers between devices, shards(): lax.all_gather(w_gate, 'dp', axis=0, tiled=True)  180 us
  transfers between devices with their start and end apart: 22, of which 17 were waited for; matrix products, arithmetic and copies ran while one was open for 3% of the time, Pallas kernels for 0%

commit v1 on v0

v1 whole, which is shorter than its diff:
```python
import functools
import math

import jax
import jax.numpy as jnp
from jax import lax
from jax.experimental import pallas as pl
from jax.experimental.pallas import tpu as pltpu
from jax.sharding import PartitionSpec as P

HEAD_SIZE = 256
EPS = 1e-06
THETA = 1000042.0
LINE = 4
MESH = pl.DeviceIdType.MESH
BF16 = jnp.bfloat16
F32 = jnp.float32
MB = 1024 * 1024


def rope_tables(count, head_dim):
    half = head_dim // 2
    index = jnp.arange(half, dtype=jnp.float32)
    freqs = jnp.exp(index * (-2.0 * math.log(THETA) / head_dim))
    angles = jnp.arange(count, dtype=jnp.float32)[:, None] * freqs[None, :]
    return (jnp.cos(angles)[:, None, :], jnp.sin(angles)[:, None, :])


def apply_rotary(values, cosine_table, rotary_sine_table):
    half = values.shape[-1] // 2
    first = values[..., :half]
    second = values[..., half:]
    return jnp.concatenate(
        [
            first * cosine_table - second * rotary_sine_table,
            second * cosine_table + first * rotary_sine_table,
        ],
        -1,
    )


def rotate_back(grads, cosine_table, rotary_sine_table):
    return apply_rotary(grads, cosine_table, -rotary_sine_table)


def dot_nn(left, right):
    return jnp.dot(left, right, preferred_element_type=F32)


def dot_nt(left, right):
    return lax.dot_general(left, right, (((1,), (1,)), ((), ())), preferred_element_type=F32)


def dot_tn(left, right):
    return lax.dot_general(left, right, (((0,), (0,)), ((), ())), preferred_element_type=F32)


def gather_rows(values):
    return lax.all_gather(values, "tensor", axis=0, tiled=True)


def sum_rows(values):
    return lax.psum_scatter(values, "tensor", scatter_dimension=0, tiled=True)


def norm_back(inputs, factor, gain, upstream):
    scaled = upstream * gain
    grad_in = factor * scaled - inputs * factor**3 * jnp.mean(scaled * inputs, -1, keepdims=True)
    return (grad_in, jnp.sum(upstream * inputs * factor, 0))


class Place:
    def __init__(self, plane):
        self.d = lax.axis_index("dp")
        self.t = lax.axis_index("tensor")
        self.plane = plane
        self.z = lax.div(self.d, plane)
        self.p = lax.rem(self.d, plane)
        if plane == 4:
            x = lax.rem(self.p, 2)
            y = lax.div(self.p, 2)
            self.px = 2 * y + 1 - x
            self.py = 2 * (1 - y) + x
            self.pd = 2 * (1 - y) + 1 - x

    def at(self, z, p):
        return (z * self.plane + p, self.t)

    def sibling(self):
        return (self.d, 1 - self.t)


def remote(src, dst, send, recv, device):
    return pltpu.make_async_remote_copy(
        src_ref=src, dst_ref=dst, send_sem=send, recv_sem=recv, device_id=device, device_id_type=MESH
    )


def arrival(ref, sem):
    pltpu.make_async_copy(ref, ref, sem).wait()


def greet_all(me, count):
    barrier = pltpu.get_barrier_semaphore()
    for step in range(1, count):
        pl.semaphore_signal(
            barrier, inc=1, device_id=(lax.rem(me.d + step, count), me.t), device_id_type=MESH
        )
    pl.semaphore_signal(barrier, inc=1, device_id=me.sibling(), device_id_type=MESH)
    pl.semaphore_wait(barrier, count)


def greet_line(me):
    barrier = pltpu.get_barrier_semaphore()
    for step in range(1, LINE):
        pl.semaphore_signal(
            barrier, inc=1, device_id=me.at(lax.rem(me.z + step, LINE), me.p), device_id_type=MESH
        )
    pl.semaphore_signal(barrier, inc=1, device_id=me.sibling(), device_id_type=MESH)
    pl.semaphore_wait(barrier, LINE)


def reach(me, way, k):
    return (me.z >= k, me.z - k) if way == 0 else (me.z + k < LINE, me.z + k)


class Chain:
    def __init__(self, me, first, held, send, recv):
        self.me, self.first, self.held, self.send, self.recv = me, first, held, send, recv

    def copy(self, way, k):
        me = self.me
        _, origin = reach(me, way, k)
        target = me.z + 1 if way == 0 else me.z - 1
        src = self.first if k == 0 else self.held(origin)
        return remote(
            src, self.held(origin), self.send.at[way, k], self.recv.at[way, k + 1], me.at(target, me.p)
        )

    def goes(self, way, k):
        have, _ = reach(self.me, way, k)
        ahead, _ = reach(self.me, 1 - way, 1)
        return jnp.logical_and(have, ahead)

    def start(self, way, k):
        if k < LINE - 1:

            @pl.when(self.goes(way, k))
            def _():
                self.copy(way, k).start()

    def wait_block(self, way, k):
        _, origin = reach(self.me, way, k)
        arrival(self.held(origin), self.recv.at[way, k])

    def finish(self):
        for way in range(2):
            for k in range(LINE - 1):

                @pl.when(self.goes(way, k))
                def _():
                    self.copy(way, k).wait_send()


class PlaneGather:
    def __init__(self, me, job, held, rows, send, recv):
        self.me, self.job, self.held, self.send, self.recv = me, job, held, send, recv
        self.half = rows // 2

    def piece(self, z, p, half):
        return self.held.at[z * self.me.plane + p, pl.ds(half * self.half, self.half)]

    def copy(self, z, kind, first=None):
        me = self.me
        if me.plane != 4:
            ref = first if first is not None else self.held.at[z * me.plane + me.p]
            target = lax.rem(me.p + kind + 1, me.plane)
            dst = self.held.at[z * me.plane + me.p]
        else:
            owner = (me.p, me.p, me.p, me.p, me.px, me.py)[kind]
            half = (0, 1, 1, 0, 0, 1)[kind]
            target = (me.px, me.px, me.py, me.py, me.py, me.px)[kind]
            dst = self.piece(z, owner, half)
            ref = dst if first is None else first.at[pl.ds(half * self.half, self.half)]
        return remote(
            ref, dst, self.send.at[self.job, z, kind], self.recv.at[self.job, z, kind], me.at(me.z, target)
        )

    def start(self, z, first=None):
        kinds = (0, 2, 1, 3) if self.me.plane == 4 else range(self.me.plane - 1)
        for kind in kinds:
            self.copy(z, kind, first).start()

    def forward(self, z):
        if self.me.plane == 4:
            self.copy(z, 0).wait_recv()
            self.copy(z, 4).start()
            self.copy(z, 2).wait_recv()
            self.copy(z, 5).start()

    def finish(self):
        kinds = 6 if self.me.plane == 4 else self.me.plane - 1
        for z in range(LINE):
            for kind in range(kinds):
                copy = self.copy(z, kind)
                if self.me.plane != 4 or kind not in (0, 2):
                    copy.wait_recv()
                copy.wait_send()


def gather_kernel(
    count, a_ref, w_ref, gain_ref, tok_ref, dm_ref, a_all, w_all, gain_all, tok_all, dm_all,
    chain_send, chain_recv, part_send, part_recv, plane_send, plane_recv, gain_send, gain_recv,
    pair_send, pair_recv, local_sem,
):
    plane = count // LINE
    me = Place(plane)
    rows = a_ref.shape[0]
    local = [
        pltpu.make_async_copy(a_ref, a_all.at[me.d], local_sem.at[0]),
        pltpu.make_async_copy(w_ref.at[me.z], w_all.at[me.d], local_sem.at[1]),
        pltpu.make_async_copy(gain_ref, gain_all.at[me.d], local_sem.at[2]),
        pltpu.make_async_copy(tok_ref, tok_all.at[me.t], local_sem.at[3]),
        pltpu.make_async_copy(dm_ref, dm_all.at[me.z, me.t], local_sem.at[4]),
    ]
    for copy in local:
        copy.start()
    greet_all(me, count)

    attn = Chain(me, a_ref, lambda z: a_all.at[z * plane + me.p], chain_send.at[0], chain_recv.at[0])
    dms = Chain(me, dm_ref, lambda z: dm_all.at[z, me.t], chain_send.at[1], chain_recv.at[1])
    planes = (
        PlaneGather(me, 0, a_all, rows, plane_send, plane_recv),
        PlaneGather(me, 1, w_all, rows, plane_send, plane_recv),
    )

    def part(way, k):
        _, target = reach(me, 1 - way, k)
        return remote(
            w_ref.at[target], w_all.at[me.d], part_send.at[way, k], part_recv.at[way, k],
            me.at(target, me.p),
        )

    def pair(z, first=None):
        src = dm_all.at[z, me.t] if first is None else first
        return remote(src, dm_all.at[z, me.t], pair_send.at[z], pair_recv.at[z], me.sibling())

    for way in range(2):
        attn.start(way, 0)
    planes[0].start(me.z, a_ref)
    for k in range(1, LINE):
        for way in range(2):

            @pl.when(reach(me, 1 - way, k)[0])
            def _():
                part(way, k).start()

    def give_gain(step):
        target = lax.rem(me.d + step, count)
        return remote(
            gain_ref, gain_all.at[me.d], gain_send.at[step], gain_recv.at[step], (target, me.t)
        )

    for step in range(1, count):
        give_gain(step).start()
    tokens = remote(tok_ref, tok_all.at[me.t], pair_send.at[LINE], pair_recv.at[LINE], me.sibling())
    tokens.start()
    planes[1].start(me.z, w_ref.at[me.z])
    for way in range(2):
        dms.start(way, 0)
    pair(me.z, dm_ref).start()

    for k in range(1, LINE + 1):
        if k < LINE:
            for way in range(2):
                have, z = reach(me, way, k)

                @pl.when(have)
                def _():
                    attn.wait_block(way, k)
                    attn.start(way, k)
                    planes[0].start(z)
                    arrival(w_all.at[z * plane + me.p], part_recv.at[way, k])
                    planes[1].start(z)
                    dms.wait_block(way, k)
                    dms.start(way, k)
                    pair(z).start()

        if k == 1:
            planes[0].forward(me.z)
            planes[1].forward(me.z)
        else:
            for way in range(2):
                have, z = reach(me, way, k - 1)

                @pl.when(have)
                def _():
                    planes[0].forward(z)
                    planes[1].forward(z)

    attn.finish()
    dms.finish()
    for k in range(1, LINE):
        for way in range(2):

            @pl.when(reach(me, 1 - way, k)[0])
            def _():
                part(way, k).wait_send()

    for step in range(1, count):
        give_gain(step).wait()
    tokens.wait()
    for z in range(LINE):
        pair(z).wait()
    for job in planes:
        job.finish()
    for copy in local:
        copy.wait()


ANY = pl.BlockSpec(memory_space=pl.ANY)
DMA = pltpu.SemaphoreType.DMA


def gather_all(count, attn, mlp, gains, tokens, dm):
    rows, width = attn.shape
    kinds = max(6, count // LINE - 1)
    return pl.pallas_call(
        functools.partial(gather_kernel, count),
        name="gather_all",
        out_shape=(
            jax.ShapeDtypeStruct((count, rows, width), BF16),
            jax.ShapeDtypeStruct((count, rows, width), BF16),
            jax.ShapeDtypeStruct((count,) + gains.shape, gains.dtype),
            jax.ShapeDtypeStruct((2,) + tokens.shape, BF16),
            jax.ShapeDtypeStruct((LINE, 2) + dm.shape, BF16),
        ),
        in_specs=[ANY] * 5,
        out_specs=(ANY,) * 5,
        scratch_shapes=[
            DMA((2, 2, LINE)), DMA((2, 2, LINE)), DMA((2, LINE)), DMA((2, LINE)),
            DMA((2, LINE, kinds)), DMA((2, LINE, kinds)), DMA((count,)), DMA((count,)),
            DMA((LINE + 1,)), DMA((LINE + 1,)), DMA((5,)),
        ],
        compiler_params=pltpu.CompilerParams(collective_id=0, has_side_effects=True),
    )(attn, mlp, gains, tokens, dm)


def line_gather_kernel(plane, h_ref, h_all, chain_send, chain_recv, pair_send, pair_recv, local_sem):
    me = Place(plane)
    local = pltpu.make_async_copy(h_ref, h_all.at[me.z, me.t], local_sem)
    local.start()
    greet_line(me)
    chain = Chain(me, h_ref, lambda z: h_all.at[z, me.t], chain_send, chain_recv)

    def pair(z, first=None):
        src = h_all.at[z, me.t] if first is None else first
        return remote(src, h_all.at[z, me.t], pair_send.at[z], pair_recv.at[z], me.sibling())

    for way in range(2):
        chain.start(way, 0)
    pair(me.z, h_ref).start()
    for k in range(1, LINE):
        for way in range(2):
            have, z = reach(me, way, k)

            @pl.when(have)
            def _():
                chain.wait_block(way, k)
                chain.start(way, k)
                pair(z).start()

    chain.finish()
    for z in range(LINE):
        pair(z).wait()
    local.wait()


def line_gather(count, values):
    return pl.pallas_call(
        functools.partial(line_gather_kernel, count // LINE),
        name="line_gather",
        out_shape=jax.ShapeDtypeStruct((LINE, 2) + values.shape, values.dtype),
        in_specs=[ANY],
        out_specs=ANY,
        scratch_shapes=[DMA((2, LINE)), DMA((2, LINE)), DMA((LINE,)), DMA((LINE,)), DMA],
        compiler_params=pltpu.CompilerParams(collective_id=1, has_side_effects=True),
    )(values)


def line_sum_kernel(
    plane, part_ref, total_ref, own, from_pair, from_line, pair_send, pair_recv, line_send, line_recv, local_sem
):
    me = Place(plane)
    jobs = part_ref.shape[0]

    def load(job, z):
        return pltpu.make_async_copy(part_ref.at[job, z, me.t], own.at[job, z], local_sem.at[job, z])

    def pair(job, z):
        return remote(
            part_ref.at[job, z, 1 - me.t], from_pair.at[job, z], pair_send.at[job, z],
            pair_recv.at[job, z], me.sibling(),
        )

    def pass_on(job, way, k):
        _, target = reach(me, 1 - way, k)
        ahead = me.z + 1 if way == 0 else me.z - 1
        return remote(
            own.at[job, target], from_line.at[job, way, k - 1], line_send.at[job, way, k],
            line_recv.at[job, way, k - 1], me.at(ahead, me.p),
        )

    for job in range(jobs):
        for z in range(LINE):
            load(job, z).start()
    greet_line(me)
    order = [(way, k) for k in range(LINE - 1, 0, -1) for way in range(2)]
    for job in range(jobs):
        for way, k in order:
            have, z = reach(me, 1 - way, k)

            @pl.when(have)
            def _():
                pair(job, z).start()

        pair(job, me.z).start()
    for job in range(jobs):
        for way, k in order:
            have, z = reach(me, 1 - way, k)

            @pl.when(have)
            def _():
                load(job, z).wait()
                pair(job, z).wait_recv()
                both = own[job, z].astype(F32) + from_pair[job, z].astype(F32)
                own[job, z] = both.astype(BF16)
                behind, _ = reach(me, way, 1)

                @pl.when(behind)
                def _():
                    arrival(from_line.at[job, way, k], line_recv.at[job, way, k])
                    own[job, z] = (both + from_line[job, way, k].astype(F32)).astype(BF16)

                pass_on(job, way, k).start()

        load(job, me.z).wait()
        pair(job, me.z).wait_recv()
        total_ref[job] = own[job, me.z].astype(F32) + from_pair[job, me.z].astype(F32)
        for way in range(2):
            behind, _ = reach(me, way, 1)

            @pl.when(behind)
            def _():
                arrival(from_line.at[job, way, 0], line_recv.at[job, way, 0])
                total_ref[job] += from_line[job, way, 0].astype(F32)

    for job in range(jobs):
        for way, k in order:
            have, z = reach(me, 1 - way, k)

            @pl.when(have)
            def _():
                pass_on(job, way, k).wait_send()

        for z in range(LINE):
            pair(job, z).wait_send()


def line_sum(count, parts):
    jobs, _, _, rows, width = parts.shape
    return pl.pallas_call(
        functools.partial(line_sum_kernel, count // LINE),
        name="line_sum",
        out_shape=jax.ShapeDtypeStruct((jobs, rows, width), F32),
        in_specs=[ANY],
        out_specs=pl.BlockSpec(memory_space=pltpu.VMEM),
        scratch_shapes=[
            pltpu.VMEM((jobs, LINE, rows, width), BF16),
            pltpu.VMEM((jobs, LINE, rows, width), BF16),
            pltpu.VMEM((jobs, 2, LINE, rows, width), BF16),
            DMA((jobs, LINE)), DMA((jobs, LINE)),
            DMA((jobs, 2, LINE + 1)), DMA((jobs, 2, LINE + 1)),
            DMA((jobs, LINE)),
        ],
        compiler_params=pltpu.CompilerParams(
            collective_id=2, has_side_effects=True, vmem_limit_bytes=40 * MB
        ),
    )(parts)


def add_rows(target, terms, rows, start=0):
    step = 16

    @pl.loop(0, rows // step)
    def _(i):
        at = pl.ds(pl.multiple_of(start + i * step, step), step)
        total = terms[0][at].astype(F32)
        for term in terms[1:]:
            total += term[at].astype(F32)
        target[at] = total.astype(target.dtype)


def grad_sum_kernel(
    count, ga_ref, gw_ref, gain_ref, a_out, w_out, gain_out, own, other, first, second, from_line,
    gain_in, gain_pair, first_send, first_recv, second_send, second_recv, line_send, line_recv,
    part_send, part_recv, gain_send, gain_recv, load_sem, other_sem, local_sem,
):
    plane = count // LINE
    me = Place(plane)
    rows = a_out.shape[0]
    half = rows // 2
    grads = (ga_ref, gw_ref)
    halves = (pl.ds(0, half), pl.ds(half, half))
    square = plane == 4
    if square:
        near = (me.px, me.py)
        far = (me.py, me.px)

    def load(job, z):
        return pltpu.make_async_copy(grads[job].at[z * plane + me.p], own.at[job, z], load_sem.at[job, z])

    def load_other(job, z, i):
        return pltpu.make_async_copy(
            grads[job].at[z * plane + far[i], halves[i]], other.at[job, z, halves[i]],
            other_sem.at[job, z, i],
        )

    def give(job, z, i, which):
        if not square:
            return remote(
                grads[job].at[z * plane + lax.rem(me.p + which + 1, plane)], first.at[job, z, which],
                first_send.at[job, z, which], first_recv.at[job, z, which],
                me.at(me.z, lax.rem(me.p + which + 1, plane)),
            )
        block = (near[i], me.pd)[which]
        return remote(
            grads[job].at[z * plane + block, halves[i]], first.at[job, z, which, halves[i]],
            first_send.at[job, z, 2 * i + which], first_recv.at[job, z, 2 * i + which],
            me.at(me.z, near[i]),
        )

    def give_both(job, z, i):
        return remote(
            other.at[job, z, halves[i]], second.at[job, z, halves[i]], second_send.at[job, z, i],
            second_recv.at[job, z, i], me.at(me.z, far[i]),
        )

    def gives(job, z):
        if square:
            return [give(job, z, i, which) for which in (1, 0) for i in range(2)]
        return [give(job, z, 0, which) for which in range(plane - 1)]

    def begin(job, z):
        for copy in gives(job, z):
            copy.start()

    def middle(job, z):
        if not square:
            return
        for i in range(2):
            arrival(first.at[job, z, 1, halves[i]], first_recv.at[job, z, 2 * i + 1])
            load_other(job, z, i).wait()
            add_rows(other.at[job, z], (other.at[job, z], first.at[job, z, 1]), half, i * half)
            give_both(job, z, i).start()

    def end(job, z):
        load(job, z).wait()
        if square:
            for i in range(2):
                arrival(first.at[job, z, 0, halves[i]], first_recv.at[job, z, 2 * i])
                arrival(second.at[job, z, halves[i]], second_recv.at[job, z, i])
            terms = (first.at[job, z, 0], second.at[job, z])
        else:
            for which in range(plane - 1):
                arrival(first.at[job, z, which], first_recv.at[job, z, which])
            terms = tuple(first.at[job, z, which] for which in range(plane - 1))
        add_rows(own.at[job, z], (own.at[job, z],) + terms, rows)

    def pass_on(way, k):
        _, target = reach(me, 1 - way, k)
        ahead = me.z + 1 if way == 0 else me.z - 1
        return remote(
            own.at[0, target], from_line.at[way, k - 1], line_send.at[way, k], line_recv.at[way, k - 1],
            me.at(ahead, me.p),
        )

    def part(way, k):
        _, target = reach(me, 1 - way, k)
        return remote(
            own.at[1, target], w_out.at[me.z], part_send.at[way, k], part_recv.at[way, k],
            me.at(target, me.p),
        )

    def line(way, k, z):
        behind, _ = reach(me, way, 1)

        @pl.when(behind)
        def _():
            arrival(from_line.at[way, k], line_recv.at[way, k])
            add_rows(own.at[0, z], (own.at[0, z], from_line.at[way, k]), rows)

        pass_on(way, k).start()

    for job in range(2):
        for z in range(LINE):
            load(job, z).start()
            if square:
                for i in range(2):
                    load_other(job, z, i).start()
    greet_all(me, count)

    def give_gain(step):
        target = lax.rem(me.d + step, count)
        return remote(
            gain_ref.at[target], gain_in.at[step], gain_send.at[step], gain_recv.at[step], (target, me.t)
        )

    order = [(way, k) for k in range(LINE - 1, 0, -1) for way in range(2)] + [(0, 0)]
    events = [(job, way, k) for job in range(2) for way, k in order]

    def on(event, act):
        job, way, k = event
        have, z = reach(me, 1 - way, k)
        if k == 0:
            act(job, me.z)
        else:

            @pl.when(have)
            def _():
                act(job, z)

    lead, lag, line_lag = 4, 2, 6
    last = len(events)
    for i in range(-lead, last + line_lag):
        if 0 <= i + lead < last:
            on(events[i + lead], begin)
        if i + lead == last:
            for step in range(1, count):
                give_gain(step).start()
        if 0 <= i < last:
            on(events[i], middle)
        if 0 <= i - lag < last:
            job, way, k = events[i - lag]
            on(events[i - lag], end)
            if job == 1 and k > 0:
                on(events[i - lag], lambda job, z: part(way, k).start())
        if 0 <= i - line_lag < last:
            job, way, k = events[i - line_lag]
            if job == 0 and k > 0:
                on(events[i - line_lag], lambda job, z: line(way, k, z))

    keep = pltpu.make_async_copy(own.at[1, me.z], w_out.at[me.z], local_sem)
    keep.start()
    add_rows(a_out, (own.at[0, me.z],), rows)
    for way in range(2):

        @pl.when(reach(me, way, 1)[0])
        def _():
            arrival(from_line.at[way, 0], line_recv.at[way, 0])
            add_rows(a_out, (a_out, from_line.at[way, 0]), rows)

    total = gain_ref[me.d]
    for step in range(1, count):
        give_gain(step).wait()
        total += gain_in[step]
    gain_pair[0] = total
    swap = remote(gain_pair.at[0], gain_pair.at[1], gain_send.at[0], gain_recv.at[0], me.sibling())
    swap.start()
    swap.wait()
    gain_out[...] = gain_pair[0] + gain_pair[1]

    for way, k in order[:-1]:

        @pl.when(reach(me, 1 - way, k)[0])
        def _():
            pass_on(way, k).wait_send()
            part(way, k).wait_send()

        @pl.when(reach(me, way, k)[0])
        def _():
            arrival(w_out.at[me.z], part_recv.at[way, k])

    for job in range(2):
        for z in range(LINE):
            for copy in gives(job, z):
                copy.wait_send()
            if square:
                for i in range(2):
                    give_both(job, z, i).wait_send()
    keep.wait()


def grad_sum(count, ga, gw, gains):
    _, rows, width = ga.shape
    plane = count // LINE
    square = plane == 4
    slots = 2 if square else plane - 1
    block = (2, LINE, rows, width)
    small = (2, LINE, rows, width) if square else (1, 1, 16, 128)
    vmem = pl.BlockSpec(memory_space=pltpu.VMEM)
    return pl.pallas_call(
        functools.partial(grad_sum_kernel, count),
        name="grad_sum",
        out_shape=(
            jax.ShapeDtypeStruct((rows, width), F32),
            jax.ShapeDtypeStruct((LINE, rows, width), BF16),
            jax.ShapeDtypeStruct(gains.shape[1:], F32),
        ),
        in_specs=[ANY, ANY, vmem],
        out_specs=(vmem, ANY, vmem),
        scratch_shapes=[
            pltpu.VMEM(block, BF16),
            pltpu.VMEM(small, BF16),
            pltpu.VMEM((2, LINE, slots, rows, width), BF16),
            pltpu.VMEM(small, BF16),
            pltpu.VMEM((2, LINE, rows, width), BF16),
            pltpu.VMEM(gains.shape, F32),
            pltpu.VMEM((2,) + gains.shape[1:], F32),
            DMA((2, LINE, max(4, slots))), DMA((2, LINE, max(4, slots))),
            DMA((2, LINE, 2)), DMA((2, LINE, 2)),
            DMA((2, LINE)), DMA((2, LINE)), DMA((2, LINE)), DMA((2, LINE)),
            DMA((count,)), DMA((count,)),
            DMA((2, LINE)), DMA((2, LINE, 2)), DMA,
        ],
        compiler_params=pltpu.CompilerParams(
            collective_id=3, has_side_effects=True, vmem_limit_bytes=56 * MB
        ),
    )(ga, gw, gains)


def shards(
    tokens, w_query, key_weight, value_weight, w_out, gain_attn, w_gate, w_up, w_down, gain_mlp,
    cotangent, lengths, seq_of_group,
):
    count = lax.axis_size("dp")
    local_rows = tokens.shape[0]
    full_rows = local_rows * lax.axis_size("tensor")
    rows = w_query.shape[0]
    model = rows * count
    q_width = w_query.shape[1]
    kv_width = key_weight.shape[1]
    q_heads = q_width // HEAD_SIZE
    kv_heads = kv_width // HEAD_SIZE
    group_size = q_heads // kv_heads
    units = w_gate.shape[1] // LINE
    score_scale = HEAD_SIZE ** (-0.5)
    chosen = jnp.sum(
        jnp.where(jnp.arange(lengths.shape[0], dtype=jnp.int32) == seq_of_group[0], lengths, 0)
    )
    positions = lax.axis_index("tensor") * local_rows + jnp.arange(local_rows, dtype=jnp.int32)
    valid_rows = (positions < chosen).astype(F32)[:, None]
    row_ids = jnp.arange(full_rows, dtype=jnp.int32)
    key_allowed = (row_ids[None, :] <= row_ids[:, None]) & (row_ids[None, :] < chosen)
    cosine_table, rotary_sine_table = rope_tables(full_rows, HEAD_SIZE)
    inputs = tokens.astype(F32)
    grad_out = cotangent.astype(F32) * valid_rows

    attn_pack = jnp.concatenate([w_query, key_weight, value_weight, w_out.T], axis=1)
    down_t = w_down.T
    mlp_pack = jnp.stack(
        [
            jnp.concatenate([m[:, z * units : (z + 1) * units] for m in (w_gate, w_up, down_t)], axis=1)
            for z in range(LINE)
        ]
    )
    lanes = -rows % 128
    gains = jnp.pad(jnp.stack([gain_attn, gain_mlp]), ((0, 14), (0, lanes)))
    attn_all, mlp_all, gains_all, tokens_all, dm_all = gather_all(
        count, attn_pack, mlp_pack, gains, tokens, grad_out.astype(BF16)
    )
    attn_gain, mlp_gain = (gains_all[:, i, :rows].reshape(model).astype(F32) for i in range(2))
    attn_all = attn_all.reshape(model, -1)
    mlp_all = mlp_all.reshape(model, -1)
    qkv_full = attn_all[:, : q_width + 2 * kv_width]
    out_t = attn_all[:, q_width + 2 * kv_width :]
    gate_up, down_full = mlp_all[:, : 2 * units], mlp_all[:, 2 * units :]
    dm_all = dm_all.reshape(-1, model)

    both = tokens_all.reshape(full_rows, model).astype(F32)
    both_factor = lax.rsqrt(jnp.mean(both * both, -1, keepdims=True) + EPS)
    normed_attn = (both * both_factor * attn_gain).astype(BF16)
    attn_factor = lax.rsqrt(jnp.mean(inputs * inputs, -1, keepdims=True) + EPS)
    qkv = dot_nn(normed_attn, qkv_full)
    query_rows = apply_rotary(
        qkv[:, :q_width].reshape(full_rows, q_heads, HEAD_SIZE), cosine_table, rotary_sine_table
    ).astype(BF16)
    key_rows = apply_rotary(
        qkv[:, q_width : q_width + kv_width].reshape(full_rows, kv_heads, HEAD_SIZE),
        cosine_table,
        rotary_sine_table,
    ).astype(BF16)
    value_rows = qkv[:, q_width + kv_width :].astype(BF16).reshape(full_rows, kv_heads, HEAD_SIZE)
    grouped = query_rows.reshape(full_rows, kv_heads, group_size, HEAD_SIZE)
    scores = (
        jnp.einsum("skgd,tkd->kgst", grouped, key_rows, preferred_element_type=F32) * score_scale
    )
    scores = jnp.where(key_allowed, scores, -1e30)
    row_exp = jnp.exp(scores - jnp.max(scores, -1, keepdims=True))
    probs = row_exp / jnp.sum(row_exp, -1, keepdims=True)
    probs_low = probs.astype(BF16)
    attended = (
        jnp.einsum("kgst,tkd->skgd", probs_low, value_rows, preferred_element_type=F32)
        .reshape(full_rows, q_width)
        .astype(BF16)
    )
    middle = inputs + sum_rows(dot_nt(attended, out_t))
    mlp_factor = lax.rsqrt(jnp.mean(middle * middle, -1, keepdims=True) + EPS)
    normed_mlp = (middle * mlp_factor * mlp_gain).astype(BF16)

    normed_all = line_gather(count, normed_mlp).reshape(-1, model)
    gate_up_lin = dot_nn(normed_all, gate_up)
    gate_lin, up_lin = gate_up_lin[:, :units], gate_up_lin[:, units:]
    sigmoid_gate = jax.nn.sigmoid(gate_lin)
    silu_gate = gate_lin * sigmoid_gate
    hidden = (silu_gate * up_lin).astype(BF16)
    grad_hidden = dot_nn(dm_all, down_full)
    grad_gate = (
        grad_hidden * up_lin * sigmoid_gate * (1.0 + gate_lin * (1.0 - sigmoid_gate))
    ).astype(BF16)
    grad_up = (grad_hidden * silu_gate).astype(BF16)
    grad_gate_up = jnp.concatenate([grad_gate, grad_up], axis=1)
    parts = jnp.stack([dot_nt(grad_gate_up, gate_up), dot_nt(hidden, down_full)]).astype(BF16)
    grad_norm_mlp, mlp_out = line_sum(
        count, parts.reshape(2, LINE, 2, local_rows, model)
    )
    outputs = middle + mlp_out
    grad_mlp_w = jnp.concatenate(
        [dot_tn(normed_all, grad_gate_up), dot_tn(dm_all, hidden)], axis=1
    ).astype(BF16)

    grad_mid_norm, gain_mlp_part = norm_back(middle, mlp_factor, mlp_gain, grad_norm_mlp)
    grad_middle = grad_out + grad_mid_norm
    grad_attn = gather_rows(grad_middle.astype(BF16))
    grad_out_t = dot_tn(grad_attn, attended)
    grad_groups = (
        dot_nn(grad_attn, out_t).astype(BF16).reshape(full_rows, kv_heads, group_size, HEAD_SIZE)
    )
    grad_probs = jnp.einsum("skgd,tkd->kgst", grad_groups, value_rows, preferred_element_type=F32)
    grad_scores = (probs * (grad_probs - jnp.sum(probs * grad_probs, -1, keepdims=True))).astype(BF16)
    grad_queries = (
        jnp.einsum("kgst,tkd->skgd", grad_scores, key_rows, preferred_element_type=F32) * score_scale
    )
    grad_keys = (
        jnp.einsum("kgst,skgd->tkd", grad_scores, grouped, preferred_element_type=F32) * score_scale
    )
    grad_values = jnp.einsum("kgst,skgd->tkd", probs_low, grad_groups, preferred_element_type=F32)
    grad_qkv = jnp.concatenate(
        [
            rotate_back(
                grad_queries.reshape(full_rows, q_heads, HEAD_SIZE), cosine_table, rotary_sine_table
            ).reshape(full_rows, q_width),
            rotate_back(grad_keys, cosine_table, rotary_sine_table).reshape(full_rows, kv_width),
            grad_values.reshape(full_rows, kv_width),
        ],
        axis=1,
    ).astype(BF16)
    grad_norm_attn = sum_rows(dot_nt(grad_qkv, qkv_full))
    grad_attn_w = jnp.concatenate([dot_tn(normed_attn, grad_qkv), grad_out_t], axis=1).astype(BF16)
    grad_in_norm, gain_attn_part = norm_back(inputs, attn_factor, attn_gain, grad_norm_attn)
    grad_inputs = grad_middle + grad_in_norm

    gain_parts = jnp.stack([gain_attn_part, gain_mlp_part]).reshape(2, count, rows)
    gain_parts = jnp.pad(gain_parts.transpose(1, 0, 2), ((0, 0), (0, 6), (0, lanes)))
    attn_sum, mlp_sum, gain_sum = grad_sum(
        count,
        grad_attn_w.reshape(count, rows, -1),
        grad_mlp_w.reshape(count, rows, -1),
        gain_parts,
    )
    mlp_sum = mlp_sum.astype(F32)
    grad_gate_w, grad_up_w, grad_down_t = (
        jnp.concatenate([mlp_sum[z, :, i * units : (i + 1) * units] for z in range(LINE)], axis=1)
        for i in range(3)
    )
    return (
        outputs.astype(BF16),
        grad_inputs,
        attn_sum[:, :q_width],
        attn_sum[:, q_width : q_width + kv_width],
        attn_sum[:, q_width + kv_width : q_width + 2 * kv_width],
        attn_sum[:, q_width + 2 * kv_width :].T,
        gain_sum[0, :rows],
        grad_gate_w,
        grad_up_w,
        grad_down_t.T,
        gain_sum[1, :rows],
    )


def solution(mesh):
    both = P(("dp", "tensor"), None)
    row = P("dp", "tensor")
    column = P("tensor", "dp")
    in_specs = (
        both, row, row, row, column, P("dp"), row, row, column, P("dp"), both, P(), P("dp"),
    )
    out_specs = (both, both, row, row, row, column, P("dp"), row, row, column, P("dp"))
    return jax.shard_map(shards, mesh=mesh, in_specs=in_specs, out_specs=out_specs, check_vma=False)
```

time: 3810 us -> 841 us (0.22)
  waiting for transfers between devices: 3440 us -> 27 us
  Pallas kernels: 0 us -> 592 us
  blocking collectives: 143 us -> 0 us
  matrix products: 158 us -> 101 us
    reduce_scatter x7 -> x0, waiting for transfers between devices: 2500 us -> none  [the longest x1 692 us: shards(): lax.psum_scatter(grad_gate_w, 'dp', scatter_dimension=0, tiled=True)]
    all_gather x7 -> x0, waiting for transfers between devices: 903 us -> none  [the longest x1 251 us: shards(): lax.all_gather(w_down, 'dp', axis=1, tiled=True)]
    pallas_call x0 -> x4, Pallas kernels: none -> 592 us  [the longest x1 248 us: grad_sum(): pl.pallas_call(functools.partial(grad_sum_kernel, count), name='grad_sum'...]
    unnamed x1 -> x0, blocking collectives: 71.9 us -> none
    all_gather x2 -> x0, blocking collectives: 67.6 us -> none  [the longest x1 34.5 us: shards(): lax.all_gather(gain_attn, 'dp', axis=0, tiled=True)]
  transfers between devices with their start and end apart: 22 -> 3, of which waited for: 17 -> 2; matrix products, arithmetic and copies ran while one was open for 3% -> 7% of each run, Pallas kernels for 0% -> 0%
where the time goes in v1:
time: 841 us; the launch traced here: 832 us
  Pallas kernels  592 us (70%)
  matrix products  101 us (12%)
  other arithmetic  53.7 us (6%)
  local copies, waits for them, and re-layouts  41.9 us (5%)
  waiting for transfers between devices  27 us (3%)
  between operations  15.6 us (2%)
    pallas_call x1, Pallas kernels, grad_sum(): pl.pallas_call(functools.partial(grad_sum_kernel, count), name='grad_sum'...  248 us
    pallas_call x1, Pallas kernels, gather_all(): pl.pallas_call(functools.partial(gather_kernel, count), name='gather_all'...  224 us
    pallas_call x1, Pallas kernels, line_sum(): pl.pallas_call(functools.partial(line_sum_kernel, count // LINE), name='l...  80.9 us
    pallas_call x1, Pallas kernels, line_gather(): pl.pallas_call(functools.partial(line_gather_kernel, count // LINE), name...  39.9 us
    dot_general x4, matrix products, dot_nn(): return jnp.dot(left, right, preferred_element_type=F32)  33.7 us
    dot_general x4, matrix products, dot_nt(): lax.dot_general(left, right, (((1,), (1,)), ((), ())), preferred_element_...  33.1 us
    dot_general x4, matrix products, dot_tn(): lax.dot_general(left, right, (((0,), (0,)), ((), ())), preferred_element_...  26.4 us
    reduce_scatter x2, waiting for transfers between devices, sum_rows(): return lax.psum_scatter(values, 'tensor', scatter_dimension=0, tiled=True)  24.9 us
  transfers between devices with their start and end apart: 3, of which 2 were waited for; matrix products, arithmetic and copies ran while one was open for 7% of the time, Pallas kernels for 0%

profile of v1, /device:TPU:8, one launch (start us, length us, event | category | flops | bytes accessed | tf_op | source)
XLA Modules:
  0.0 832.0 jit_solution(605303476293481501)
XLA Ops:
  7.3 1.6 copy.56
  8.9 0.9 fusion.75
  9.8 0.9 fusion.73
  10.7 0.8 fusion.74
  12.1 1.1 copy.55
  14.5 0.9 fusion.45.dm_ref
  16.1 1.4 maximum_bitcast_fusion.1
  17.6 1.9 pad_maximum_fusion.4.w_ref
  19.5 0.9 pad_maximum_fusion.10.a_ref
  20.4 223.9 %gather_all.1 = (bf16[16,128,3072]{2,1,0:T(8,128)(2,1)}, bf16[16,128,3072]{2,1,0:T(8,128)(2,1)}, bf16[16,16,128]{2,1,0:T(8,128)(2,1)}, bf16[2,128,2048]{2,1,0:T(8,128)(2,1)}, bf16[4,2,128,2048]{3,2,1,0:T(8,128)(2,1)}) custom-call(bf16[128,3072]{1,0:T(8,128)(2,1)} %pad_maximum_fusion.10.a_ref, bf16[4,128,3072]{2,1,0:T(8,128)(2,1)} %pad_maximum_fusion.4.w_ref, ...), custom_call_target="tpu_custom_call" | custom-call | tf_op jit(solution)/shard_map/gather_all/pallas_call | solution.py:328
  244.3 0.8 slice_convert_fusion.1
  245.2 1.5 multiply_reduce_fusion
  246.7 1.5 fusion.23
  248.3 5.7 fusion.7
  254.1 1.2 iota_compare_fusion.2
  255.3 0.7 slice.284
  256.4 1.0 fusion.76
  258.9 1.0 reshape.232
  260.0 1.2 subtract_convert_fusion.3
  261.2 1.5 fusion.77
  262.7 0.8 convolution_convert_fusion.5
  263.5 5.0 fusion.19
  268.8 24.9 %reduce-scatter.3.cloned.1.call-done = f32[128,2048]{1,0:T(8,128)} async-done(((f32[256,2048]{1,0:T(8,128)}), f32[128,2048]{1,0:T(8,128)}) %reduce-scatter.3.cloned.1.call-update) | async-done | bytes 1048592 | tf_op jit(solution)/shard_map/reduce_scatter | solution.py:63
  293.8 1.5 multiply_reduce_fusion.3
  295.3 1.0 multiply_convert_fusion.4.h_ref
  296.3 39.9 %line_gather.1 = bf16[4,2,128,2048]{3,2,1,0:T(8,128)(2,1)} custom-call(bf16[128,2048]{1,0:T(8,128)(2,1)} %multiply_convert_fusion.4.h_ref), custom_call_target="tpu_custom_call" | custom-call | tf_op jit(solution)/shard_map/line_gather/pallas_call | solution.py:380
  336.1 13.3 %fusion.3 = f32[1024,2048]{0,1:T(8,128)S(1)} fusion(bf16[1024,2048]{1,0:T(8,128)(2,1)} %bitcast.191, bf16[2048,3072]{1,0:T(8,128)(2,1)} %bitcast.239), kind=kOutput, calls=%fused_computation.6 | convolution fusion | flops 8589934592 | bytes 20971520 | tf_op jit(solution)/shard_map/dot_general | solution.py:47
  349.4 10.2 %multiply_convert_fusion.2 = (bf16[1024,1024]{0,1:T(8,128)(2,1)}, bf16[1024,1024]{0,1:T(8,128)(2,1)}, bf16[1024,1024]{0,1:T(8,128)(2,1)S(1)}) fusion(f32[1024,2048]{0,1:T(8,128)S(1)} %fusion.3, bf16[1024,2048]{1,0:T(8,128)(2,1)S(1)} %bitcast.196, bf16[2048,3072]{1,0:T(8,128)(2,1)} %bitcast.240), kind=kOutput, calls=%fused_computation.18 | convolution fusion | flops 4310695936 | bytes 23068672 | tf_op jit(solution)/shard_map/dot_general | solution.py:47
  359.6 7.8 convolution_convert_fusion.2
  367.4 13.1 %fusion.11 = bf16[1024,2048]{1,0:T(8,128)(2,1)} fusion(bf16[2048,3072]{1,0:T(8,128)(2,1)} %bitcast.242, bf16[1024,1024]{0,1:T(8,128)(2,1)S(1)} %copy-done.41, bf16[1024,1024]{0,1:T(8,128)(2,1)S(1)} %copy-done.40), kind=kOutput, calls=%fused_computation.21 | convolution fusion | flops 8600420352 | bytes 16777216 | tf_op jit(solution)/shard_map/dot_general | solution.py:51
  380.6 6.2 pad_maximum_fusion.2.part_ref
  386.7 3.4 copy-done
  390.1 80.9 %line_sum.1 = f32[2,128,2048]{2,1,0:T(8,128)S(1)} custom-call(bf16[2,4,2,128,2048]{4,3,2,1,0:T(8,128)(2,1)S(1)} %copy-done), custom_call_target="tpu_custom_call" | custom-call | tf_op jit(solution)/shard_map/line_sum/pallas_call | solution.py:472
  471.4 1.8 fusion.70
  473.2 6.6 copy.84
  480.3 2.0 all-gather.2.cloned.1.call-done
  482.4 4.6 fusion.28
  487.0 1.3 copy.118
  488.3 1.5 multiply_reduce_fusion.1
  490.4 1.1 fusion.32
  491.5 2.6 fusion.33
  495.3 1.1 subtract_convert_fusion.2
  496.7 1.1 copy.78
  497.8 7.1 fusion.5
  504.9 9.4 %convolution_convert_fusion.3 = bf16[16,128,1024]{2,1,0:T(8,128)(2,1)} fusion(bf16[16,128,1024]{2,1,0:T(8,128)(2,1)} %bitcast.197, bf16[1024,1024]{0,1:T(8,128)(2,1)} %copy-done.39), kind=kOutput, calls=%fused_computation.31 | convolution fusion | flops 4297064448 | bytes 10485760 | tf_op jit(solution)/shard_map/dot_general | solution.py:55
  514.3 6.5 copy.82
  520.9 12.3 %convolution_convert_fusion = bf16[16,128,2048]{2,1,0:T(8,128)(2,1)S(1)} fusion(bf16[16,128,1024]{2,1,0:T(8,128)(2,1)} %bitcast.198, bf16[1024,1024]{0,1:T(8,128)(2,1)} %get-tuple-element.58, bf16[1024,1024]{0,1:T(8,128)(2,1)} %get-tuple-element.57), kind=kOutput, calls=%fused_computation.12 | convolution fusion | flops 8602517504 | bytes 16777216 | tf_op jit(solution)/shard_map/dot_general | solution.py:55
  533.3 9.3 %pad_maximum_fusion.1.gw_ref = bf16[16,128,3072]{2,1,0:T(8,128)(2,1)} fusion(bf16[16,128,1024]{2,1,0:T(8,128)(2,1)S(1)} %copy-done.6, bf16[16,128,2048]{2,1,0:T(8,128)(2,1)S(1)} %convolution_convert_fusion), kind=kLoop, calls=%fused_computation.2 | loop fusion | flops 25165824 | bytes 25165824 | tf_op jit(solution)/shard_map/concatenate | solution.py:828
  542.5 1.5 copy.110
  544.0 2.3 convolution_convert_fusion.4
  546.3 2.3 convolution_convert_fusion.1
  548.7 9.0 %pad_maximum_fusion.ga_ref = bf16[16,128,3072]{2,1,0:T(8,128)(2,1)} fusion(bf16[16,128,1024]{2,1,0:T(8,128)(2,1)S(1)} %convolution_convert_fusion.4, bf16[16,128,2048]{2,1,0:T(8,128)(2,1)S(1)} %convolution_convert_fusion.1), kind=kLoop, calls=%fused_computation.1 | loop fusion | flops 25165824 | bytes 25165824 | tf_op jit(solution)/shard_map/concatenate | solution.py:859
  557.8 1.5 fusion.40
  559.9 247.6 %grad_sum.1 = (f32[128,3072]{1,0:T(8,128)}, bf16[4,128,3072]{2,1,0:T(8,128)(2,1)}, f32[8,128]{1,0:T(8,128)}) custom-call(bf16[16,128,3072]{2,1,0:T(8,128)(2,1)} %pad_maximum_fusion.ga_ref, bf16[16,128,3072]{2,1,0:T(8,128)(2,1)} %pad_maximum_fusion.1.gw_ref, f32[16,8,128]{2,1,0:T(8,128)} %pad.9.gain_ref), custom_call_target="tpu_custom_call" | custom-call | tf_op jit(solution)/shard_map/grad_sum/pallas_call | solution.py:702
  807.6 2.3 slice_bitcast_fusion.12
  809.8 1.9 fusion.71
  811.7 0.8 convert_element_type.128
  812.5 2.1 slice_bitcast_fusion.3
  814.8 1.8 copy.87
  816.6 1.0 copy.86
  817.6 1.3 slice_bitcast_fusion.13
  818.9 3.2 pad_maximum_fusion.8
  822.1 1.5 pad_maximum_fusion.7
  823.5 1.5 fusion.37
  (125 shorter events, 8.2 us)
Async XLA Ops:
  7.2 2.6 copy-start.14
  7.2 286.6 %reduce-scatter.3.cloned.1.call-start = ((), (), s32[]{:S(2)}) async-start(), calls=%async_computation.2 | async-start | bytes 3145728 | tf_op jit(solution)/shard_map/reduce_scatter | solution.py:63
  7.3 6.0 copy-start.38
  7.3 7.3 copy-start.12
  8.9 1.8 copy-start.15
  8.9 6.6 copy-start.36
  8.9 6.6 copy-start.37
  10.7 6.8 copy-start.17
  17.5 2.0 copy-start.29
  17.5 2.0 copy-start.32
  17.5 2.0 copy-start.33
  245.2 3.1 copy-start.30
  257.9 0.9 copy-start.35
  258.7 4.8 copy-start.24
  258.8 4.7 copy-start.26
  258.9 4.6 copy-start.34
  259.9 3.5 copy-start.28
  261.2 2.3 copy-start.18
  261.2 2.3 copy-start.20
  263.5 5.1 copy-start.23
  263.5 30.2 %copy-start.1 = (bf16[128,2048]{1,0:T(8,128)(2,1)S(1)}, bf16[128,2048]{1,0:T(8,128)(2,1)}, u32[]{:S(2)}) copy-start(bf16[128,2048]{1,0:T(8,128)(2,1)} %tok_ref.1) | copy-start | bytes 1572868
  268.6 213.8 %all-gather.2.cloned.1.call-start = ((), (), s32[]{:S(2)}) async-start(), calls=%async_computation.3 | async-start | bytes 1572864 | tf_op jit(solution)/shard_map/all_gather | solution.py:59
  336.1 13.3 %copy-start.4 = (bf16[4,2,128,2048]{3,2,1,0:T(8,128)(2,1)S(1)}, bf16[4,2,128,2048]{3,2,1,0:T(8,128)(2,1)}, u32[]{:S(2)}) copy-start(bf16[4,2,128,2048]{3,2,1,0:T(8,128)(2,1)} %get-tuple-element.22) | copy-start | bytes 12582916
  359.6 7.8 copy-start.39
  359.6 7.9 copy-start.40
  359.6 7.9 copy-start.41
  386.7 3.4 copy-start
  390.1 81.2 %copy-start.13 = (bf16[128,2048]{1,0:T(8,128)(2,1)S(1)}, bf16[128,2048]{1,0:T(8,128)(2,1)}, u32[]{:S(2)}) copy-start(bf16[128,2048]{1,0:T(8,128)(2,1)} %param.23) | copy-start | bytes 1572868
  473.2 84.6 %reduce-scatter.5.cloned.1.call-start = ((), (), s32[]{:S(2)}) async-start(), calls=%async_computation.4 | async-start | bytes 3145728 | tf_op jit(solution)/shard_map/reduce_scatter | solution.py:63
  480.3 7.9 copy-start.16
  486.9 3.0 copy-start.19
  487.0 3.0 copy-start.21
  488.2 1.5 copy-start.22
  488.3 2.1 copy-start.25
  488.3 2.1 copy-start.27
  520.9 12.4 %copy-start.6 = (bf16[16,128,1024]{2,1,0:T(8,128)(2,1)S(1)}, bf16[16,128,1024]{2,1,0:T(8,128)(2,1)}, u32[]{:S(2)}) copy-start(bf16[16,128,1024]{2,1,0:T(8,128)(2,1)} %convolution_convert_fusion.3) | copy-start | bytes 12582916
  548.7 9.1 %copy-start.2 = (bf16[128,2048]{1,0:T(8,128)(2,1)S(1)}, bf16[128,2048]{1,0:T(8,128)(2,1)}, u32[]{:S(2)}) copy-start(bf16[128,2048]{1,0:T(8,128)(2,1)} %tok_ref.1) | copy-start | bytes 1572868
  548.7 9.1 %copy-start.31 = (f32[16,1,128]{2,1,0:T(1,128)S(1)}, f32[16,1,128]{2,1,0:T(1,128)}, u32[]{:S(2)}) copy-start(f32[16,1,128]{2,1,0:T(1,128)} %copy-done.30) | copy-start | bytes 24580
  807.6 4.1 copy-start.7
  816.6 5.5 copy-start.8
  816.6 5.5 copy-start.9
  816.6 5.5 copy-start.10
  816.6 5.5 copy-start.11
  818.9 4.7 copy-start.3
  818.9 4.7 copy-start.5
Sparse Core Ops, SparseCore 0:
  268.7 25.0 reduce-scatter.2
  473.3 9.0 all-gather.1
  505.1 10.7 reduce-scatter.4

commit v2 on v1

v2 whole, which is shorter than its diff:
```python
import functools
import math

import jax
import jax.numpy as jnp
from jax import lax
from jax.experimental import pallas as pl
from jax.experimental.pallas import tpu as pltpu
from jax.sharding import PartitionSpec as P

HEAD_SIZE = 256
EPS = 1e-06
THETA = 1000042.0
LINE = 4
MESH = pl.DeviceIdType.MESH
BF16 = jnp.bfloat16
F32 = jnp.float32
MB = 1024 * 1024


def rope_tables(count, head_dim):
    half = head_dim // 2
    index = jnp.arange(half, dtype=jnp.float32)
    freqs = jnp.exp(index * (-2.0 * math.log(THETA) / head_dim))
    angles = jnp.arange(count, dtype=jnp.float32)[:, None] * freqs[None, :]
    return (jnp.cos(angles)[:, None, :], jnp.sin(angles)[:, None, :])


def dot_tn(left, right):
    return lax.dot_general(left, right, (((0,), (0,)), ((), ())), preferred_element_type=F32)


class Place:
    def __init__(self, plane):
        self.d = lax.axis_index("dp")
        self.t = lax.axis_index("tensor")
        self.plane = plane
        self.z = lax.div(self.d, plane)
        self.p = lax.rem(self.d, plane)
        if plane == 4:
            x = lax.rem(self.p, 2)
            y = lax.div(self.p, 2)
            self.px = 2 * y + 1 - x
            self.py = 2 * (1 - y) + x
            self.pd = 2 * (1 - y) + 1 - x

    def at(self, z, p):
        return (z * self.plane + p, self.t)

    def sibling(self):
        return (self.d, 1 - self.t)


def remote(src, dst, send, recv, device):
    return pltpu.make_async_remote_copy(
        src_ref=src, dst_ref=dst, send_sem=send, recv_sem=recv, device_id=device, device_id_type=MESH
    )


def arrival(ref, sem):
    pltpu.make_async_copy(ref, ref, sem).wait()


def greet_all(me, count):
    barrier = pltpu.get_barrier_semaphore()
    for step in range(1, count):
        pl.semaphore_signal(
            barrier, inc=1, device_id=(lax.rem(me.d + step, count), me.t), device_id_type=MESH
        )
    pl.semaphore_signal(barrier, inc=1, device_id=me.sibling(), device_id_type=MESH)
    pl.semaphore_wait(barrier, count)


def greet_line(me):
    barrier = pltpu.get_barrier_semaphore()
    for step in range(1, LINE):
        pl.semaphore_signal(
            barrier, inc=1, device_id=me.at(lax.rem(me.z + step, LINE), me.p), device_id_type=MESH
        )
    pl.semaphore_signal(barrier, inc=1, device_id=me.sibling(), device_id_type=MESH)
    pl.semaphore_wait(barrier, LINE)


def reach(me, way, k):
    return (me.z >= k, me.z - k) if way == 0 else (me.z + k < LINE, me.z + k)


class Chain:
    def __init__(self, me, first, held, send, recv):
        self.me, self.first, self.held, self.send, self.recv = me, first, held, send, recv

    def copy(self, way, k):
        me = self.me
        _, origin = reach(me, way, k)
        target = me.z + 1 if way == 0 else me.z - 1
        src = self.first if k == 0 else self.held(origin)
        return remote(
            src, self.held(origin), self.send.at[way, k], self.recv.at[way, k + 1], me.at(target, me.p)
        )

    def goes(self, way, k):
        have, _ = reach(self.me, way, k)
        ahead, _ = reach(self.me, 1 - way, 1)
        return jnp.logical_and(have, ahead)

    def start(self, way, k):
        if k < LINE - 1:

            @pl.when(self.goes(way, k))
            def _():
                self.copy(way, k).start()

    def wait_block(self, way, k):
        _, origin = reach(self.me, way, k)
        arrival(self.held(origin), self.recv.at[way, k])

    def finish(self):
        for way in range(2):
            for k in range(LINE - 1):

                @pl.when(self.goes(way, k))
                def _():
                    self.copy(way, k).wait_send()


class PlaneGather:
    def __init__(self, me, job, held, rows, send, recv, late=None):
        self.me, self.job, self.held, self.send, self.recv = me, job, held, send, recv
        self.late = late
        self.half = rows // 2

    def piece(self, z, p, half):
        return self.held.at[z * self.me.plane + p, pl.ds(half * self.half, self.half)]

    def copy(self, z, kind, first=None):
        me = self.me
        if me.plane != 4:
            ref = first if first is not None else self.held.at[z * me.plane + me.p]
            target = lax.rem(me.p + kind + 1, me.plane)
            dst = self.held.at[z * me.plane + me.p]
        else:
            owner = (me.p, me.p, me.p, me.p, me.px, me.py)[kind]
            half = (0, 1, 1, 0, 0, 1)[kind]
            target = (me.px, me.px, me.py, me.py, me.py, me.px)[kind]
            dst = self.piece(z, owner, half)
            ref = dst if first is None else first.at[pl.ds(half * self.half, self.half)]
        return remote(
            ref, dst, self.send.at[self.job, z, kind], self.recv.at[self.job, z, kind], me.at(me.z, target)
        )

    def unless_late(self, z, act):
        if self.late is None:
            act()
        else:
            pl.when(z != self.late)(act)

    def start(self, z, first=None):
        kinds = (0, 2, 1, 3) if self.me.plane == 4 else range(self.me.plane - 1)

        def act():
            for kind in kinds:
                self.copy(z, kind, first).start()

        self.unless_late(z, act)

    def forward(self, z):
        def act():
            self.copy(z, 0).wait_recv()
            self.copy(z, 4).start()
            self.copy(z, 2).wait_recv()
            self.copy(z, 5).start()

        if self.me.plane == 4:
            self.unless_late(z, act)

    def finish(self, zs=range(LINE)):
        kinds = 6 if self.me.plane == 4 else self.me.plane - 1
        for z in zs:
            if z == self.late:
                continue
            for kind in range(kinds):
                copy = self.copy(z, kind)
                if self.me.plane != 4 or kind not in (0, 2):
                    copy.wait_recv()
                copy.wait_send()


def gather_kernel(
    count, a_ref, w_ref, gain_ref, tok_ref, dm_ref, a_all, w_all, w_last, gain_all, tok_all, dm_all,
    chain_send, chain_recv, part_send, part_recv, plane_send, plane_recv, gain_send, gain_recv,
    pair_send, pair_recv, local_sem,
):
    plane = count // LINE
    me = Place(plane)
    rows = a_ref.shape[0]
    late = LINE - 1
    own_w = [
        pltpu.make_async_copy(w_ref.at[me.z], w_all.at[me.d], local_sem.at[1]),
        pltpu.make_async_copy(w_ref.at[me.z], w_last, local_sem.at[1]),
    ]
    for ref, here in zip(own_w, (me.z != late, me.z == late)):

        @pl.when(here)
        def _():
            ref.start()

    local = [
        pltpu.make_async_copy(a_ref, a_all.at[me.d], local_sem.at[0]),
        pltpu.make_async_copy(gain_ref, gain_all.at[me.d], local_sem.at[2]),
        pltpu.make_async_copy(tok_ref, tok_all.at[me.t], local_sem.at[3]),
        pltpu.make_async_copy(dm_ref, dm_all.at[me.z, me.t], local_sem.at[4]),
    ]
    for copy in local:
        copy.start()
    greet_all(me, count)

    attn = Chain(me, a_ref, lambda z: a_all.at[z * plane + me.p], chain_send.at[0], chain_recv.at[0])
    dms = Chain(me, dm_ref, lambda z: dm_all.at[z, me.t], chain_send.at[1], chain_recv.at[1])
    planes = (
        PlaneGather(me, 0, a_all, rows, plane_send, plane_recv),
        PlaneGather(me, 1, w_all, rows, plane_send, plane_recv, late),
    )

    def part(way, k, last):
        _, target = reach(me, 1 - way, k)
        dst = w_last if last else w_all.at[me.d]
        return remote(
            w_ref.at[target], dst, part_send.at[way, k], part_recv.at[way, k], me.at(target, me.p)
        )

    def pair(z, first=None):
        src = dm_all.at[z, me.t] if first is None else first
        return remote(src, dm_all.at[z, me.t], pair_send.at[z], pair_recv.at[z], me.sibling())

    for way in range(2):
        attn.start(way, 0)
    planes[0].start(me.z, a_ref)
    for k in range(1, LINE):
        for way in range(2):

            for last in range(2):

                @pl.when(jnp.logical_and(reach(me, 1 - way, k)[0], (me.z == late) == bool(last)))
                def _():
                    part(way, k, last).start()

    def give_gain(step):
        target = lax.rem(me.d + step, count)
        return remote(
            gain_ref, gain_all.at[me.d], gain_send.at[step], gain_recv.at[step], (target, me.t)
        )

    for step in range(1, count):
        give_gain(step).start()
    tokens = remote(tok_ref, tok_all.at[me.t], pair_send.at[LINE], pair_recv.at[LINE], me.sibling())
    tokens.start()
    planes[1].start(me.z, w_ref.at[me.z])
    for way in range(2):
        dms.start(way, 0)
    pair(me.z, dm_ref).start()

    for k in range(1, LINE + 1):
        if k < LINE:
            for way in range(2):
                have, z = reach(me, way, k)

                @pl.when(have)
                def _():
                    attn.wait_block(way, k)
                    attn.start(way, k)
                    planes[0].start(z)
                    arrival(w_last, part_recv.at[way, k])
                    planes[1].start(z)
                    dms.wait_block(way, k)
                    dms.start(way, k)
                    pair(z).start()

        if k == 1:
            planes[0].forward(me.z)
            planes[1].forward(me.z)
        else:
            for way in range(2):
                have, z = reach(me, way, k - 1)

                @pl.when(have)
                def _():
                    planes[0].forward(z)
                    planes[1].forward(z)

    attn.finish()
    dms.finish()
    for k in range(1, LINE):
        for way in range(2):

            @pl.when(reach(me, 1 - way, k)[0])
            def _():
                part(way, k, 1).wait_send()

    for step in range(1, count):
        give_gain(step).wait()
    tokens.wait()
    for z in range(LINE):
        pair(z).wait()
    for job in planes:
        job.finish()
    for copy in local:
        copy.wait()
    own_w[1].wait()


ANY = pl.BlockSpec(memory_space=pl.ANY)
DMA = pltpu.SemaphoreType.DMA


def gather_all(count, attn, mlp, gains, tokens, dm):
    rows, width = attn.shape
    kinds = max(6, count // LINE - 1)
    return pl.pallas_call(
        functools.partial(gather_kernel, count),
        name="gather_all",
        out_shape=(
            jax.ShapeDtypeStruct((count, rows, width), BF16),
            jax.ShapeDtypeStruct((count - count // LINE, rows, width), BF16),
            jax.ShapeDtypeStruct((rows, width), BF16),
            jax.ShapeDtypeStruct((count,) + gains.shape, gains.dtype),
            jax.ShapeDtypeStruct((2,) + tokens.shape, BF16),
            jax.ShapeDtypeStruct((LINE, 2) + dm.shape, BF16),
        ),
        in_specs=[ANY] * 5,
        out_specs=(ANY,) * 6,
        scratch_shapes=[
            DMA((2, 2, LINE)), DMA((2, 2, LINE)), DMA((2, LINE)), DMA((2, LINE)),
            DMA((2, LINE, kinds)), DMA((2, LINE, kinds)), DMA((count,)), DMA((count,)),
            DMA((LINE + 1,)), DMA((LINE + 1,)), DMA((5,)),
        ],
        compiler_params=pltpu.CompilerParams(collective_id=0, has_side_effects=True),
    )(attn, mlp, gains, tokens, dm)


def dot_cols(left, right):
    return lax.dot_general(left, right, (((1,), (1,)), ((), ())), preferred_element_type=F32)


def feed_forward_kernel(
    plane, h_ref, dm_ref, w_ref, w_late, total_ref, out_ref, grad_ref, rows_in, weights, inner, part,
    from_pair, from_line, chain_send, chain_recv, pass_send, pass_recv, pair_send, pair_recv,
    line_send, line_recv, load_sem, dm_sem, grad_sem, out_sem,
):
    me = Place(plane)
    rows, model = h_ref.shape
    units = inner.shape[1]
    wide = 2 * rows
    tokens = LINE * wide
    most, block, _ = w_ref.shape
    tile = 512

    def slot(z, t):
        return rows_in.at[pl.ds(pl.multiple_of((z * 2 + t) * rows, rows), rows)]

    loads = [
        pltpu.make_async_copy(w_ref, weights.at[pl.ds(0, most)], load_sem.at[0]),
        pltpu.make_async_copy(w_late, weights.at[pl.ds(most, plane)], load_sem.at[2]),
    ]
    for load in loads:
        load.start()
    load_dm = pltpu.make_async_copy(dm_ref, rows_in.at[pl.ds(tokens, tokens)], dm_sem)
    load_dm.start()
    keep = pltpu.make_async_copy(h_ref, slot(me.z, me.t), load_sem.at[1])
    keep.start()
    greet_line(me)
    chain = Chain(me, h_ref, lambda z: slot(z, me.t), chain_send, chain_recv)

    def share(z, first=None):
        src = slot(z, me.t) if first is None else first
        return remote(src, slot(z, me.t), pass_send.at[z], pass_recv.at[z], me.sibling())

    for way in range(2):
        chain.start(way, 0)
    share(me.z, h_ref).start()

    def w_rows(n, width, column):
        return weights[pl.ds(n * (width // block), width // block), :, pl.ds(column, units)].reshape(
            width, units
        )

    def compute(z):
        at = pl.ds(pl.multiple_of(z * wide, wide), wide)
        dm_at = pl.ds(pl.multiple_of(tokens + z * wide, wide), wide)

        @pl.loop(0, units // tile)
        def _(c):
            def column(job):
                return weights[:, :, pl.ds(pl.multiple_of(job * units + c * tile, tile), tile)].reshape(
                    model, tile
                )

            h = rows_in[at, :]
            gate = jnp.dot(h, column(0), preferred_element_type=F32)
            up = jnp.dot(h, column(1), preferred_element_type=F32)
            grad_hidden = jnp.dot(rows_in[dm_at, :], column(2), preferred_element_type=F32)
            sigmoid = jax.nn.sigmoid(gate)
            silu = gate * sigmoid
            here = pl.ds(pl.multiple_of(c * tile, tile), tile)
            inner[at, here] = (silu * up).astype(BF16)
            inner[pl.ds(pl.multiple_of(tokens + z * wide, wide), wide), here] = (
                grad_hidden * up * sigmoid * (1.0 + gate * (1.0 - sigmoid))
            ).astype(BF16)
            inner[pl.ds(pl.multiple_of(2 * tokens + z * wide, wide), wide), here] = (
                grad_hidden * silu
            ).astype(BF16)

        @pl.loop(0, model // tile)
        def _(n):
            here = pl.ds(pl.multiple_of(n * tile, tile), tile)
            grad = dot_cols(inner[pl.ds(pl.multiple_of(tokens + z * wide, wide), wide)], w_rows(n, tile, 0))
            grad += dot_cols(
                inner[pl.ds(pl.multiple_of(2 * tokens + z * wide, wide), wide)], w_rows(n, tile, units)
            )
            part[0, z, :, :, here] = grad.astype(BF16).reshape(2, rows, tile)
            out = dot_cols(inner[at, :], w_rows(n, tile, 2 * units))
            part[1, z, :, :, here] = out.astype(BF16).reshape(2, rows, tile)

    def pair(job, z):
        return remote(
            part.at[job, z, 1 - me.t], from_pair.at[job, z], pair_send.at[job, z],
            pair_recv.at[job, z], me.sibling(),
        )

    def pass_on(job, way, k):
        _, target = reach(me, 1 - way, k)
        ahead = me.z + 1 if way == 0 else me.z - 1
        return remote(
            part.at[job, target, me.t], from_line.at[way, k - 1], line_send.at[way, k],
            line_recv.at[way, k - 1], me.at(ahead, me.p),
        )

    def line(job, way, k, behind):
        have, z = reach(me, 1 - way, k)
        before = me.z if way == 0 else LINE - 1 - me.z

        @pl.when(jnp.logical_and(have, before == behind))
        def _():
            pair(job, z).wait_recv()
            terms = (part.at[job, z, me.t], from_pair.at[job, z])
            if behind:
                arrival(from_line.at[way, k], line_recv.at[way, k])
                terms += (from_line.at[way, k],)
            add_rows(part.at[job, z, me.t], terms, rows)
            pass_on(job, way, k).start()

    def total(job):
        pair(job, me.z).wait_recv()
        add_rows(total_ref, (part.at[job, me.z, me.t], from_pair.at[job, me.z]), rows)
        for way in range(2):

            @pl.when(reach(me, way, 1)[0])
            def _():
                arrival(from_line.at[way, 0], line_recv.at[way, 0])
                add_rows(total_ref, (total_ref, from_line.at[way, 0]), rows)

    def grads(z):
        per = plane * block

        @pl.loop(0, per // tile)
        def _(n):
            column = pl.ds(pl.multiple_of(z * per + n * tile, tile), tile)
            h = rows_in[pl.ds(0, tokens), column].T
            dm = rows_in[pl.ds(tokens, tokens), column].T
            there = pl.ds((z * per + n * tile) // block, tile // block)
            for job in range(3):
                left = (h, h, dm)[job]
                start = (tokens, 2 * tokens, 0)[job]
                for c in range(units // 512):
                    grad = jnp.dot(
                        left, inner[pl.ds(start, tokens), c * 512 : (c + 1) * 512],
                        preferred_element_type=F32,
                    )
                    weights[there, :, job * units + c * 512 : job * units + (c + 1) * 512] = (
                        grad.astype(BF16).reshape(tile // block, block, 512)
                    )

        keep_grads(z).start()

    def keep_grads(z):
        return pltpu.make_async_copy(
            weights.at[pl.ds(z * plane, plane)], grad_ref.at[pl.ds(z * plane, plane)], grad_sem.at[z]
        )

    keep.wait()
    for load in loads:
        load.wait()
    load_dm.wait()
    for k in range(LINE):
        for way in range(2 if k else 1):
            have, z = reach(me, way, k)

            @pl.when(have)
            def _():
                if k:
                    chain.wait_block(way, k)
                    chain.start(way, k)
                    share(z).start()
                arrival(slot(z, 1 - me.t), pass_recv.at[z])
                compute(z)
                for job in range(2):
                    pair(job, z).start()

        if k:
            for way in range(2):
                line(0, 1 - way, k, 0)
    order = [(behind, k) for behind in range(1, LINE) for k in range(1, LINE - behind)]
    order.sort(key=lambda e: (2 * e[0] + e[1], e[0]))
    for i in range(max(LINE, len(order))):
        if i < LINE:
            grads(i)
        if i < len(order):
            for way in range(2):
                line(0, way, order[i][1], order[i][0])

    def keep_out(z):
        return pltpu.make_async_copy(part.at[1, z, me.t], out_ref.at[z], out_sem.at[z])

    for z in range(LINE):
        pair(1, z).wait_recv()
        add_rows(part.at[1, z, me.t], (part.at[1, z, me.t], from_pair.at[1, z]), rows)
        keep_out(z).start()
    total(0)

    chain.finish()
    for z in range(LINE):
        share(z).wait_send()
        keep_grads(z).wait()
        keep_out(z).wait()
        for job in range(2):
            pair(job, z).wait_send()
    for k in range(1, LINE):
        for way in range(2):

            @pl.when(reach(me, 1 - way, k)[0])
            def _():
                pass_on(0, way, k).wait_send()


def feed_forward(count, h, dm_all, w_all, w_late):
    rows, model = h.shape
    units = w_all.shape[2] // 3
    grads = (count,) + w_all.shape[1:]
    tokens = LINE * 2 * rows
    vmem = pl.BlockSpec(memory_space=pltpu.VMEM)
    return pl.pallas_call(
        functools.partial(feed_forward_kernel, count // LINE),
        name="feed_forward",
        out_shape=(
            jax.ShapeDtypeStruct((rows, model), F32),
            jax.ShapeDtypeStruct((LINE, rows, model), BF16),
            jax.ShapeDtypeStruct(grads, BF16),
        ),
        in_specs=[vmem, ANY, ANY, ANY],
        out_specs=(vmem, ANY, ANY),
        scratch_shapes=[
            pltpu.VMEM((2 * tokens, model), BF16),
            pltpu.VMEM(grads, BF16),
            pltpu.VMEM((3 * tokens, units), BF16),
            pltpu.VMEM((2, LINE, 2, rows, model), BF16),
            pltpu.VMEM((2, LINE, rows, model), BF16),
            pltpu.VMEM((2, LINE - 1, rows, model), BF16),
            DMA((2, LINE)), DMA((2, LINE)), DMA((LINE,)), DMA((LINE,)), DMA((2, LINE)), DMA((2, LINE)),
            DMA((2, LINE)), DMA((2, LINE)), DMA((3,)), DMA, DMA((LINE,)), DMA((LINE,)),
        ],
        compiler_params=pltpu.CompilerParams(
            collective_id=1, has_side_effects=True, vmem_limit_bytes=60 * MB
        ),
    )(h, dm_all, w_all, w_late)


def add_rows(target, terms, rows, start=0):
    step = 16

    @pl.loop(0, rows // step)
    def _(i):
        at = pl.ds(pl.multiple_of(start + i * step, step), step)
        total = terms[0][at].astype(F32)
        for term in terms[1:]:
            total += term[at].astype(F32)
        target[at] = total.astype(target.dtype)


class PlaneSum:
    def __init__(self, me, grad, own, other, first, second, sems):
        self.me, self.grad, self.own, self.other, self.first, self.second = me, grad, own, other, first, second
        (
            self.first_send, self.first_recv, self.second_send, self.second_recv, self.load_sem, self.other_sem,
        ) = sems
        self.rows = own.shape[1]
        half = self.rows // 2
        self.half = half
        self.halves = (pl.ds(0, half), pl.ds(half, half))
        self.square = me.plane == 4
        if self.square:
            self.near = (me.px, me.py)
            self.far = (me.py, me.px)

    def load(self, z):
        return pltpu.make_async_copy(
            self.grad.at[z * self.me.plane + self.me.p], self.own.at[z], self.load_sem.at[z]
        )

    def load_other(self, z, i):
        return pltpu.make_async_copy(
            self.grad.at[z * self.me.plane + self.far[i], self.halves[i]],
            self.other.at[z, self.halves[i]], self.other_sem.at[z, i],
        )

    def load_all(self):
        for z in range(LINE):
            self.load(z).start()
            if self.square:
                for i in range(2):
                    self.load_other(z, i).start()

    def give(self, z, i, which):
        me = self.me
        if not self.square:
            target = lax.rem(me.p + which + 1, me.plane)
            return remote(
                self.grad.at[z * me.plane + target], self.first.at[z, which],
                self.first_send.at[z, which], self.first_recv.at[z, which], me.at(me.z, target),
            )
        block = (self.near[i], me.pd)[which]
        return remote(
            self.grad.at[z * me.plane + block, self.halves[i]], self.first.at[z, which, self.halves[i]],
            self.first_send.at[z, 2 * i + which], self.first_recv.at[z, 2 * i + which],
            me.at(me.z, self.near[i]),
        )

    def give_both(self, z, i):
        return remote(
            self.other.at[z, self.halves[i]], self.second.at[z, self.halves[i]],
            self.second_send.at[z, i], self.second_recv.at[z, i], self.me.at(self.me.z, self.far[i]),
        )

    def gives(self, z):
        if self.square:
            return [self.give(z, i, which) for which in (1, 0) for i in range(2)]
        return [self.give(z, 0, which) for which in range(self.me.plane - 1)]

    def begin(self, z):
        for copy in self.gives(z):
            copy.start()

    def middle(self, z):
        if not self.square:
            return
        for i in range(2):
            arrival(self.first.at[z, 1, self.halves[i]], self.first_recv.at[z, 2 * i + 1])
            self.load_other(z, i).wait()
            add_rows(
                self.other.at[z], (self.other.at[z], self.first.at[z, 1]), self.half, i * self.half
            )
            self.give_both(z, i).start()

    def end(self, z):
        self.load(z).wait()
        if self.square:
            for i in range(2):
                arrival(self.first.at[z, 0, self.halves[i]], self.first_recv.at[z, 2 * i])
                arrival(self.second.at[z, self.halves[i]], self.second_recv.at[z, i])
            terms = (self.first.at[z, 0], self.second.at[z])
        else:
            for which in range(self.me.plane - 1):
                arrival(self.first.at[z, which], self.first_recv.at[z, which])
            terms = tuple(self.first.at[z, which] for which in range(self.me.plane - 1))
        add_rows(self.own.at[z], (self.own.at[z],) + terms, self.rows)

    def finish(self):
        for z in range(LINE):
            for copy in self.gives(z):
                copy.wait_send()
            if self.square:
                for i in range(2):
                    self.give_both(z, i).wait_send()

    @staticmethod
    def scratch(count, rows, width):
        plane = count // LINE
        square = plane == 4
        slots = 2 if square else plane - 1
        small = (LINE, rows, width) if square else (1, 16, 128)
        return [
            pltpu.VMEM((LINE, rows, width), BF16),
            pltpu.VMEM(small, BF16),
            pltpu.VMEM((LINE, slots, rows, width), BF16),
            pltpu.VMEM(small, BF16),
        ], [
            DMA((LINE, max(4, slots))), DMA((LINE, max(4, slots))), DMA((LINE, 2)), DMA((LINE, 2)),
            DMA((LINE,)), DMA((LINE, 2)),
        ]


FAR_FIRST = [(way, k) for k in range(LINE - 1, 0, -1) for way in range(2)] + [(0, 0)]


def on(me, event, act):
    way, k = event
    have, z = reach(me, 1 - way, k)
    if k == 0:
        act(me.z)
    else:

        @pl.when(have)
        def _():
            act(z)


def greet_plane(me):
    barrier = pltpu.get_barrier_semaphore()
    for step in range(1, me.plane):
        target = lax.rem(me.p + step, me.plane)
        pl.semaphore_signal(barrier, inc=1, device_id=me.at(me.z, target), device_id_type=MESH)
    pl.semaphore_signal(barrier, inc=1, device_id=me.sibling(), device_id_type=MESH)
    pl.semaphore_wait(barrier, me.plane)


def row_loop(rows, step, act):
    @pl.loop(0, rows // step)
    def _(i):
        act(pl.ds(pl.multiple_of(i * step, step), step))


def columns_of(weights, start, width):
    count, rows, _ = weights.shape
    return weights[:, :, pl.ds(start, width)].reshape(count * rows, width)


def rows_of(weights, n, height, start, width):
    _, rows, _ = weights.shape
    per = height // rows
    return weights[pl.ds(n * per, per), :, pl.ds(start, width)].reshape(height, width)


def attention_forward_kernel(
    plane, tok_ref, gain_ref, cos_ref, sin_ref, mask_ref, a_ref, w_last, x1_ref, h2_ref, h1_ref,
    qkv_ref, probs_ref, o_ref, w_late, weights, part, from_pair, plane_send, plane_recv, pair_send,
    pair_recv, load_sem,
):
    me = Place(plane)
    _, rows, model = tok_ref.shape
    wide = 2 * rows
    heads, _, _ = probs_ref.shape
    q_width = heads * HEAD_SIZE
    kv_width = (qkv_ref.shape[1] - q_width) // 2
    kv_heads = kv_width // HEAD_SIZE
    half = HEAD_SIZE // 2
    load = pltpu.make_async_copy(a_ref, weights, load_sem.at[0])
    load.start()
    keep = pltpu.make_async_copy(w_last, w_late.at[me.p], load_sem.at[1])
    keep.start()
    greet_plane(me)
    gather = PlaneGather(me, 0, w_late, w_last.shape[0], plane_send, plane_recv)
    gather.start(0, w_last)

    for t in range(2):

        def norm(at, t=t):
            x = tok_ref[t, at, :].astype(F32)
            factor = lax.rsqrt(jnp.mean(x * x, -1, keepdims=True) + EPS)
            h1_ref[pl.ds(t * rows + at.start, at.size), :] = (x * factor * gain_ref[0:1, :]).astype(BF16)

        row_loop(rows, 32, norm)
    load.wait()

    def project(i):
        start = pl.multiple_of(i * HEAD_SIZE, HEAD_SIZE)
        return start, jnp.dot(
            h1_ref[...], columns_of(weights, start, HEAD_SIZE), preferred_element_type=F32
        )

    @pl.loop(0, heads + kv_heads)
    def _(i):
        start, values = project(i)
        first, second = values[:, :half], values[:, half:]
        cos, sin = cos_ref[...], sin_ref[...]
        qkv_ref[:, pl.ds(start, half)] = (first * cos - second * sin).astype(BF16)
        qkv_ref[:, pl.ds(start + half, half)] = (second * cos + first * sin).astype(BF16)

    @pl.loop(heads + kv_heads, heads + 2 * kv_heads)
    def _(i):
        start, values = project(i)
        qkv_ref[:, pl.ds(start, HEAD_SIZE)] = values.astype(BF16)

    gather.forward(0)
    for i in range(heads):
        m = i * kv_heads // heads
        q = qkv_ref[:, i * HEAD_SIZE : (i + 1) * HEAD_SIZE]
        k = qkv_ref[:, q_width + m * HEAD_SIZE : q_width + (m + 1) * HEAD_SIZE]
        v = qkv_ref[:, q_width + kv_width + m * HEAD_SIZE : q_width + kv_width + (m + 1) * HEAD_SIZE]
        scores = dot_cols(q, k) * HEAD_SIZE ** (-0.5)
        scores = jnp.where(mask_ref[...] > 0, scores, -1e30)
        grown = jnp.exp(scores - jnp.max(scores, -1, keepdims=True))
        probs = grown / jnp.sum(grown, -1, keepdims=True)
        probs_ref[i] = probs
        o_ref[:, i * HEAD_SIZE : (i + 1) * HEAD_SIZE] = jnp.dot(
            probs.astype(BF16), v, preferred_element_type=F32
        ).astype(BF16)

    tile = 512

    @pl.loop(0, model // tile)
    def _(n):
        here = pl.ds(pl.multiple_of(n * tile, tile), tile)
        value = dot_cols(o_ref[...], rows_of(weights, n, tile, q_width + 2 * kv_width, q_width))
        part[:, :, here] = value.reshape(2, rows, tile)

    swap = remote(part.at[1 - me.t], from_pair, pair_send, pair_recv, me.sibling())
    swap.start()
    swap.wait_recv()

    def add(at):
        x1 = tok_ref[me.t, at, :].astype(F32) + (part[me.t, at, :] + from_pair[at, :])
        x1_ref[at, :] = x1
        factor = lax.rsqrt(jnp.mean(x1 * x1, -1, keepdims=True) + EPS)
        h2_ref[at, :] = (x1 * factor * gain_ref[1:2, :]).astype(BF16)

    row_loop(rows, 32, add)
    swap.wait_send()
    gather.finish(range(1))
    keep.wait()


VMEM = pl.BlockSpec(memory_space=pltpu.VMEM)


def attention_forward(count, heads, tokens_all, gains, cos, sin, mask, attn_all, w_last):
    _, rows, model = tokens_all.shape
    wide = 2 * rows
    q_width = heads * HEAD_SIZE
    qkv_width = attn_all.shape[2] - q_width
    plane = count // LINE
    kinds = max(6, plane - 1)
    return pl.pallas_call(
        functools.partial(attention_forward_kernel, plane),
        name="attention_forward",
        out_shape=(
            jax.ShapeDtypeStruct((rows, model), F32),
            jax.ShapeDtypeStruct((rows, model), BF16),
            jax.ShapeDtypeStruct((wide, model), BF16),
            jax.ShapeDtypeStruct((wide, qkv_width), BF16),
            jax.ShapeDtypeStruct((heads, wide, wide), F32),
            jax.ShapeDtypeStruct((wide, q_width), BF16),
            jax.ShapeDtypeStruct((plane,) + w_last.shape, BF16),
        ),
        in_specs=[VMEM] * 5 + [ANY] * 2,
        out_specs=(VMEM,) * 6 + (ANY,),
        scratch_shapes=[
            pltpu.VMEM(attn_all.shape, BF16),
            pltpu.VMEM((2, rows, model), F32),
            pltpu.VMEM((rows, model), F32),
            DMA((1, 1, kinds)), DMA((1, 1, kinds)), DMA, DMA, DMA((2,)),
        ],
        compiler_params=pltpu.CompilerParams(
            collective_id=2, has_side_effects=True, vmem_limit_bytes=48 * MB
        ),
    )(tokens_all, gains, cos, sin, mask, attn_all, w_last)


def attention_backward_kernel(
    plane, total_ref, x1_ref, dm_ref, tok_ref, gain_ref, cos_ref, sin_ref, h1_ref, qkv_ref, probs_ref,
    o_ref, a_ref, gw_ref, ga_ref, w_out, grad_tokens, gain_parts, weights, own, other, first, second,
    dx, da, do, dqkv, dh1, from_pair, first_send, first_recv, second_send, second_recv, load_sem,
    other_sem, part_send, part_recv, pair_send, pair_recv, a_sem, keep_sem, grad_sem,
):
    me = Place(plane)
    _, rows, model = tok_ref.shape
    block = weights.shape[1]
    heads, _, _ = probs_ref.shape
    q_width = heads * HEAD_SIZE
    qkv_width = qkv_ref.shape[1]
    kv_width = (qkv_width - q_width) // 2
    kv_heads = kv_width // HEAD_SIZE
    half = HEAD_SIZE // 2
    scale = HEAD_SIZE ** (-0.5)
    summed = PlaneSum(
        me, gw_ref, own, other, first, second,
        (first_send, first_recv, second_send, second_recv, load_sem, other_sem),
    )
    load = pltpu.make_async_copy(a_ref, weights, a_sem)
    load.start()
    summed.load_all()
    greet_all(me, plane * LINE)

    def part(way, k):
        _, target = reach(me, 1 - way, k)
        return remote(
            own.at[target], w_out.at[me.z], part_send.at[way, k], part_recv.at[way, k],
            me.at(target, me.p),
        )

    give_da = remote(da.at[me.t], da.at[me.t], pair_send.at[0], pair_recv.at[0], me.sibling())
    give_dh1 = remote(dh1.at[1 - me.t], from_pair, pair_send.at[1], pair_recv.at[1], me.sibling())

    def mid_norm():
        gain_parts[...] = jnp.zeros_like(gain_parts)

        def act(at):
            x, up = x1_ref[at, :], total_ref[at, :]
            factor = lax.rsqrt(jnp.mean(x * x, -1, keepdims=True) + EPS)
            scaled = up * gain_ref[1:2, :]
            grad = dm_ref[at, :].astype(F32) + (
                factor * scaled - x * factor**3 * jnp.mean(scaled * x, -1, keepdims=True)
            )
            dx[at, :] = grad
            da[me.t, at, :] = grad.astype(BF16)
            gain_parts[1:2, :] += jnp.sum(up * x * factor, 0, keepdims=True)

        row_loop(rows, 32, act)
        give_da.start()

    def grad_o():
        load.wait()
        give_da.wait_recv()

        @pl.loop(0, q_width // HEAD_SIZE)
        def _(c):
            here = pl.multiple_of(c * HEAD_SIZE, HEAD_SIZE)
            value = jnp.dot(
                da[...].reshape(2 * rows, model),
                columns_of(weights, qkv_width + here, HEAD_SIZE),
                preferred_element_type=F32,
            )
            do[:, pl.ds(here, HEAD_SIZE)] = value.astype(BF16)

    def rotate(values, start):
        first, second = values[:, :half], values[:, half:]
        cos, sin = cos_ref[...], sin_ref[...]
        dqkv[:, start : start + half] = (first * cos + second * sin).astype(BF16)
        dqkv[:, start + half : start + 2 * half] = (second * cos - first * sin).astype(BF16)

    def grad_heads():
        group = heads // kv_heads
        for m in range(kv_heads):
            at_k = q_width + m * HEAD_SIZE
            at_v = at_k + kv_width
            k = qkv_ref[:, at_k : at_k + HEAD_SIZE]
            v = qkv_ref[:, at_v : at_v + HEAD_SIZE]
            grad_k = grad_v = None
            for i in range(m * group, (m + 1) * group):
                at = slice(i * HEAD_SIZE, (i + 1) * HEAD_SIZE)
                probs = probs_ref[i]
                grad_probs = dot_cols(do[:, at], v)
                grad_scores = probs * (
                    grad_probs - jnp.sum(probs * grad_probs, -1, keepdims=True)
                )
                low = grad_scores.astype(BF16)
                rotate(jnp.dot(low, k, preferred_element_type=F32) * scale, i * HEAD_SIZE)
                more_k = dot_tn(low, qkv_ref[:, at])
                more_v = dot_tn(probs.astype(BF16), do[:, at])
                grad_k = more_k if grad_k is None else grad_k + more_k
                grad_v = more_v if grad_v is None else grad_v + more_v
            rotate(grad_k * scale, at_k)
            dqkv[:, at_v : at_v + HEAD_SIZE] = grad_v.astype(BF16)

    tile = 512

    def grad_h1():
        @pl.loop(0, model // tile)
        def _(n):
            here = pl.ds(pl.multiple_of(n * tile, tile), tile)
            value = dot_cols(dqkv[...], rows_of(weights, n, tile, 0, qkv_width))
            dh1[:, :, here] = value.reshape(2, rows, tile)

        give_dh1.start()

    def keep_grads(n):
        per = tile // block
        return pltpu.make_async_copy(
            weights.at[pl.ds(n * per, per)], ga_ref.at[pl.ds(n * per, per)], grad_sem.at[n]
        )

    def grads():
        @pl.loop(0, model // tile)
        def _(n):
            here = pl.ds(pl.multiple_of(n * tile, tile), tile)
            there = pl.ds(n * (tile // block), tile // block)
            left = h1_ref[:, here].T
            for c in range(qkv_width // tile):
                at = slice(c * tile, (c + 1) * tile)
                value = jnp.dot(left, dqkv[:, at], preferred_element_type=F32)
                weights[there, :, at] = value.astype(BF16).reshape(tile // block, block, tile)
            left = da[:, :, here].reshape(2 * rows, tile).T
            for c in range(q_width // tile):
                at = slice(c * tile, (c + 1) * tile)
                value = jnp.dot(left, o_ref[:, at], preferred_element_type=F32)
                at = slice(qkv_width + c * tile, qkv_width + (c + 1) * tile)
                weights[there, :, at] = value.astype(BF16).reshape(tile // block, block, tile)

        for n in range(model // tile):
            keep_grads(n).start()

    def in_norm():
        give_dh1.wait_recv()

        def act(at):
            x = tok_ref[me.t, at, :].astype(F32)
            up = dh1[me.t, at, :] + from_pair[at, :]
            factor = lax.rsqrt(jnp.mean(x * x, -1, keepdims=True) + EPS)
            scaled = up * gain_ref[0:1, :]
            grad_tokens[at, :] = dx[at, :] + (
                factor * scaled - x * factor**3 * jnp.mean(scaled * x, -1, keepdims=True)
            )
            gain_parts[0:1, :] += jnp.sum(up * x * factor, 0, keepdims=True)

        row_loop(rows, 32, act)

    lead, lag = 4, 2
    last = len(FAR_FIRST)
    for i in range(lead):
        on(me, FAR_FIRST[i], summed.begin)
    mid_norm()
    grad_o()
    stages = [grad_heads, grad_h1, grads, in_norm]
    for i in range(last + lag):
        if i + lead < last:
            on(me, FAR_FIRST[i + lead], summed.begin)
        if i < len(stages):
            stages[i]()
        if i < last:
            on(me, FAR_FIRST[i], summed.middle)
        if i >= lag:
            event = FAR_FIRST[i - lag]
            on(me, event, summed.end)
            if event[1]:
                on(me, event, lambda z: part(*event).start())

    keep = pltpu.make_async_copy(own.at[me.z], w_out.at[me.z], keep_sem)
    keep.start()
    for way, k in FAR_FIRST[:-1]:

        @pl.when(reach(me, 1 - way, k)[0])
        def _():
            part(way, k).wait_send()

        @pl.when(reach(me, way, k)[0])
        def _():
            arrival(w_out.at[me.z], part_recv.at[way, k])

    summed.finish()
    give_da.wait_send()
    give_dh1.wait_send()
    for n in range(model // tile):
        keep_grads(n).wait()
    keep.wait()


def attention_backward(
    count, total, x1, dm, tokens_all, gains, cos, sin, h1, qkv, probs, o, attn_all, grad_mlp
):
    _, rows, model = tokens_all.shape
    _, block, width = attn_all.shape
    wide = 2 * rows
    heads = probs.shape[0]
    q_width = heads * HEAD_SIZE
    buffers, sems = PlaneSum.scratch(count, block, width)
    return pl.pallas_call(
        functools.partial(attention_backward_kernel, count // LINE),
        name="attention_backward",
        out_shape=(
            jax.ShapeDtypeStruct(attn_all.shape, BF16),
            jax.ShapeDtypeStruct((LINE, block, width), BF16),
            jax.ShapeDtypeStruct((rows, model), F32),
            jax.ShapeDtypeStruct((2, model), F32),
        ),
        in_specs=[VMEM] * 11 + [ANY] * 2,
        out_specs=(ANY, ANY, VMEM, VMEM),
        scratch_shapes=[
            pltpu.VMEM(attn_all.shape, BF16),
            *buffers,
            pltpu.VMEM((rows, model), F32),
            pltpu.VMEM((2, rows, model), BF16),
            pltpu.VMEM((wide, q_width), BF16),
            pltpu.VMEM(qkv.shape, BF16),
            pltpu.VMEM((2, rows, model), F32),
            pltpu.VMEM((rows, model), F32),
            *sems,
            DMA((2, LINE)), DMA((2, LINE)), DMA((2,)), DMA((2,)), DMA, DMA, DMA((model // 512,)),
        ],
        compiler_params=pltpu.CompilerParams(
            collective_id=3, has_side_effects=True, vmem_limit_bytes=60 * MB
        ),
    )(total, x1, dm, tokens_all, gains, cos, sin, h1, qkv, probs, o, attn_all, grad_mlp)


def grad_sum_kernel(
    count, x1_ref, ga_ref, out_ref, gain_ref, a_out, output, gain_out, own, other, first, second,
    from_line, out_own, out_line, gain_in, gain_pair, first_send, first_recv, second_send, second_recv,
    load_sem, other_sem, line_send, line_recv, out_send, out_recv, out_sem, gain_send, gain_recv,
):
    plane = count // LINE
    me = Place(plane)
    rows = a_out.shape[0]
    summed = PlaneSum(
        me, ga_ref, own, other, first, second,
        (first_send, first_recv, second_send, second_recv, load_sem, other_sem),
    )

    class Line:
        def __init__(self, held, landing, send, recv):
            self.held, self.landing, self.send, self.recv = held, landing, send, recv

        def pass_on(self, way, k):
            _, target = reach(me, 1 - way, k)
            ahead = me.z + 1 if way == 0 else me.z - 1
            return remote(
                self.held.at[target], self.landing.at[way, k - 1], self.send.at[way, k],
                self.recv.at[way, k - 1], me.at(ahead, me.p),
            )

        def step(self, way, k, behind=None):
            have, z = reach(me, 1 - way, k)
            before = me.z if way == 0 else LINE - 1 - me.z

            @pl.when(have if behind is None else jnp.logical_and(have, before == behind))
            def _():
                @pl.when(before > 0)
                def _():
                    arrival(self.landing.at[way, k], self.recv.at[way, k])
                    add_rows(
                        self.held.at[z], (self.held.at[z], self.landing.at[way, k]), self.held.shape[1]
                    )

                self.pass_on(way, k).start()

        def total(self, act):
            for way in range(2):

                @pl.when(reach(me, way, 1)[0])
                def _():
                    arrival(self.landing.at[way, 0], self.recv.at[way, 0])
                    act(self.landing.at[way, 0])

        def finish(self):
            for way, k in FAR_FIRST[:-1]:

                @pl.when(reach(me, 1 - way, k)[0])
                def _():
                    self.pass_on(way, k).wait_send()

    grads = Line(own, from_line, line_send, line_recv)
    outs = Line(out_own, out_line, out_send, out_recv)
    summed.load_all()
    load_out = pltpu.make_async_copy(out_ref, out_own, out_sem)
    load_out.start()
    greet_all(me, count)

    def give_gain(step):
        target = lax.rem(me.d + step, count)
        return remote(
            gain_ref.at[target], gain_in.at[step], gain_send.at[step], gain_recv.at[step], (target, me.t)
        )

    lead, lag, line_lag = 4, 2, 5
    last = len(FAR_FIRST)
    for i in range(lead):
        on(me, FAR_FIRST[i], summed.begin)
    for step in range(1, count):
        give_gain(step).start()
    load_out.wait()
    for k in range(LINE - 1, 0, -1):
        for way in range(2):
            outs.step(way, k, 0)
    order = [(behind, k) for behind in range(1, LINE) for k in range(LINE - 1 - behind, 0, -1)]
    for i in range(last + line_lag):
        if i + lead < last:
            on(me, FAR_FIRST[i + lead], summed.begin)
        if i < last:
            on(me, FAR_FIRST[i], summed.middle)
        if i < len(order):
            for way in range(2):
                outs.step(way, order[i][1], order[i][0])
        if 0 <= i - lag < last:
            on(me, FAR_FIRST[i - lag], summed.end)
        if 0 <= i - line_lag < last - 1:
            grads.step(*FAR_FIRST[i - line_lag])

    def add_out(landed):
        def act(at):
            output[at, :] = output[at, :] + landed[at, :].astype(F32)

        row_loop(output.shape[0], 16, act)

    def out_start(at):
        output[at, :] = x1_ref[at, :] + out_own[me.z, at, :].astype(F32)

    row_loop(output.shape[0], 16, out_start)
    outs.total(add_out)
    add_rows(a_out, (own.at[me.z],), rows)
    grads.total(lambda landed: add_rows(a_out, (a_out, landed), rows))

    total = gain_ref[me.d]
    for step in range(1, count):
        give_gain(step).wait()
        total += gain_in[step]
    gain_pair[0] = total
    swap = remote(gain_pair.at[0], gain_pair.at[1], gain_send.at[0], gain_recv.at[0], me.sibling())
    swap.start()
    swap.wait()
    gain_out[...] = gain_pair[0] + gain_pair[1]
    outs.finish()
    grads.finish()
    summed.finish()


def grad_sum(count, x1, ga, out_parts, gains):
    _, block, width = ga.shape
    _, rows, model = out_parts.shape
    buffers, sems = PlaneSum.scratch(count, block, width)
    return pl.pallas_call(
        functools.partial(grad_sum_kernel, count),
        name="grad_sum",
        out_shape=(
            jax.ShapeDtypeStruct((block, width), F32),
            jax.ShapeDtypeStruct((rows, model), F32),
            jax.ShapeDtypeStruct(gains.shape[1:], F32),
        ),
        in_specs=[VMEM, ANY, ANY, VMEM],
        out_specs=(VMEM,) * 3,
        scratch_shapes=[
            *buffers,
            pltpu.VMEM((2, LINE - 1, block, width), BF16),
            pltpu.VMEM(out_parts.shape, BF16),
            pltpu.VMEM((2, LINE - 1, rows, model), BF16),
            pltpu.VMEM(gains.shape, F32),
            pltpu.VMEM((2,) + gains.shape[1:], F32),
            *sems,
            DMA((2, LINE)), DMA((2, LINE)), DMA((2, LINE)), DMA((2, LINE)), DMA,
            DMA((count,)), DMA((count,)),
        ],
        compiler_params=pltpu.CompilerParams(
            collective_id=4, has_side_effects=True, vmem_limit_bytes=48 * MB
        ),
    )(x1, ga, out_parts, gains)


def shards(
    tokens, w_query, key_weight, value_weight, w_out, gain_attn, w_gate, w_up, w_down, gain_mlp,
    cotangent, lengths, seq_of_group,
):
    count = lax.axis_size("dp")
    local_rows = tokens.shape[0]
    full_rows = local_rows * lax.axis_size("tensor")
    rows = w_query.shape[0]
    model = rows * count
    q_width = w_query.shape[1]
    kv_width = key_weight.shape[1]
    units = w_gate.shape[1] // LINE
    chosen = jnp.sum(
        jnp.where(jnp.arange(lengths.shape[0], dtype=jnp.int32) == seq_of_group[0], lengths, 0)
    )
    positions = lax.axis_index("tensor") * local_rows + jnp.arange(local_rows, dtype=jnp.int32)
    row_ids = jnp.arange(full_rows, dtype=jnp.int32)
    key_allowed = (row_ids[None, :] <= row_ids[:, None]) & (row_ids[None, :] < chosen)
    cos, sin = (table[:, 0, :] for table in rope_tables(full_rows, HEAD_SIZE))
    dm = jnp.where((positions < chosen)[:, None], cotangent, jnp.zeros_like(cotangent))

    attn_pack = jnp.concatenate([w_query, key_weight, value_weight, w_out.T], axis=1)
    down_t = w_down.T
    mlp_pack = jnp.stack(
        [
            jnp.concatenate([m[:, z * units : (z + 1) * units] for m in (w_gate, w_up, down_t)], axis=1)
            for z in range(LINE)
        ]
    )
    lanes = -rows % 128
    gains = jnp.pad(jnp.stack([gain_attn, gain_mlp]), ((0, 14), (0, lanes)))
    attn_all, mlp_all, mlp_last, gains_all, tokens_all, dm_all = gather_all(
        count, attn_pack, mlp_pack, gains, tokens, dm
    )
    gains_full = gains_all[:, :2, :rows].transpose(1, 0, 2).reshape(2, model).astype(F32)
    x1, h2, h1, qkv, probs, attended, mlp_late = attention_forward(
        count, q_width // HEAD_SIZE, tokens_all, gains_full, cos, sin, key_allowed.astype(F32),
        attn_all, mlp_last,
    )
    grad_h2, out_parts, grad_mlp_w = feed_forward(
        count, h2, dm_all.reshape(-1, model), mlp_all, mlp_late
    )
    grad_attn_w, mlp_sum, grad_tokens, gain_parts = attention_backward(
        count, grad_h2, x1, dm, tokens_all, gains_full, cos, sin, h1, qkv, probs, attended, attn_all,
        grad_mlp_w,
    )
    gain_parts = gain_parts.reshape(2, count, rows).transpose(1, 0, 2)
    gain_parts = jnp.pad(gain_parts, ((0, 0), (0, 6), (0, lanes)))
    attn_sum, output, gain_sum = grad_sum(count, x1, grad_attn_w, out_parts, gain_parts)
    mlp_sum = mlp_sum.astype(F32)
    grad_gate_w, grad_up_w, grad_down_t = (
        jnp.concatenate([mlp_sum[z, :, i * units : (i + 1) * units] for z in range(LINE)], axis=1)
        for i in range(3)
    )
    return (
        output.astype(BF16),
        grad_tokens,
        attn_sum[:, :q_width],
        attn_sum[:, q_width : q_width + kv_width],
        attn_sum[:, q_width + kv_width : q_width + 2 * kv_width],
        attn_sum[:, q_width + 2 * kv_width :].T,
        gain_sum[0, :rows],
        grad_gate_w,
        grad_up_w,
        grad_down_t.T,
        gain_sum[1, :rows],
    )


def solution(mesh):
    both = P(("dp", "tensor"), None)
    row = P("dp", "tensor")
    column = P("tensor", "dp")
    in_specs = (
        both, row, row, row, column, P("dp"), row, row, column, P("dp"), both, P(), P("dp"),
    )
    out_specs = (both, both, row, row, row, column, P("dp"), row, row, column, P("dp"))
    return jax.shard_map(shards, mesh=mesh, in_specs=in_specs, out_specs=out_specs, check_vma=False)
```

time: 841 us -> 675 us (0.80)
  matrix products: 101 us -> 0 us
  other arithmetic: 53.7 us -> 16.5 us
  Pallas kernels: 592 us -> 629 us
  waiting for transfers between devices: 27 us -> 0 us
  local copies, waits for them, and re-layouts: 41.9 us -> 19 us
  between operations: 15.6 us -> 2.12 us
    pallas_call x2 -> x3, Pallas kernels: 121 us -> 290 us  [the longest x1 141 us: attention_backward(): pl.pallas_call(functools.partial(attention_backward_kernel, count // LINE...]
    pallas_call x1, Pallas kernels: 248 us -> 140 us  [grad_sum(): pl.pallas_call(functools.partial(grad_sum_kernel, count), name='grad_sum'...]
    dot_general x17 -> x0, matrix products: 99.5 us -> none  [the longest x4 33.7 us: dot_nn(): return jnp.dot(left, right, preferred_element_type=F32)]
    pallas_call x1, Pallas kernels: 224 us -> 199 us  [gather_all(): pl.pallas_call(functools.partial(gather_kernel, count), name='gather_all'...]
    reduce_scatter x2 -> x0, waiting for transfers between devices: 24.9 us -> none  [sum_rows(): return lax.psum_scatter(values, 'tensor', scatter_dimension=0, tiled=True)]
    concatenate x4 -> x0, other arithmetic: 18.6 us -> none  [the longest x1 9.25 us: shards(): jnp.concatenate([dot_tn(normed_all, grad_gate_up), dot_tn(dm_all, hidden)...]
    dot_general x4 -> x0, local copies, waits for them, and re-layouts: 15.1 us -> none  [dot_tn(): lax.dot_general(left, right, (((0,), (0,)), ((), ())), preferred_element_...]
    another operation x5 -> x0, other arithmetic: 9.02 us -> none  [the longest x1 6.16 us: shards(): jnp.stack([dot_nt(grad_gate_up, gate_up), dot_nt(hidden, down_full)])]
  transfers between devices with their start and end apart: 3 -> 0, of which waited for: 2 -> 0; matrix products, arithmetic and copies ran while one was open for 7% -> 0% of each run, Pallas kernels for 0% -> 0%
where the time goes in v2:
time: 675 us; the launch traced here: 666 us
  Pallas kernels  629 us (93%)
  local copies, waits for them, and re-layouts  19 us (3%)
  other arithmetic  16.5 us (2%)
    pallas_call x1, Pallas kernels, gather_all(): pl.pallas_call(functools.partial(gather_kernel, count), name='gather_all'...  199 us
    pallas_call x1, Pallas kernels, attention_backward(): pl.pallas_call(functools.partial(attention_backward_kernel, count // LINE...  141 us
    pallas_call x1, Pallas kernels, grad_sum(): pl.pallas_call(functools.partial(grad_sum_kernel, count), name='grad_sum'...  140 us
    pallas_call x1, Pallas kernels, feed_forward(): pl.pallas_call(functools.partial(feed_forward_kernel, count // LINE), nam...  118 us
    pallas_call x1, Pallas kernels, attention_forward(): pl.pallas_call(functools.partial(attention_forward_kernel, plane), name='...  30.6 us
    unnamed x47, local copies, waits for them, and re-layouts  13.7 us

profile of v2, /device:TPU:8, one launch (start us, length us, event | category | flops | bytes accessed | tf_op | source)
XLA Modules:
  0.0 666.3 jit_solution(5787694452077396790)
XLA Ops:
  0.6 0.0 copy-start.14
  0.7 0.0 copy-start.19
  0.7 0.0 copy-start.20
  0.7 0.0 copy-start.18
  1.4 1.3 fusion.7
  2.7 0.7 add_compare_fusion
  3.4 0.7 iota_compare_fusion.2
  4.1 1.3 fusion.6.gain_ref
  5.4 0.5 fusion.2
  5.9 0.0 copy-start.3
  5.9 0.0 copy-start.4
  5.9 1.2 copy.24
  7.1 1.9 broadcast_select_fusion.dm_ref
  9.0 0.0 copy-done.19
  9.0 0.0 copy-done.20
  9.0 0.0 copy-done.18
  9.0 0.9 pad_maximum_fusion.3.a_ref
  10.0 0.0 copy-done.14
  10.0 0.5 copy.25
  10.5 0.0 copy-start.15
  10.5 0.0 copy-start.16
  10.5 0.1 fusion.11
  10.6 1.1 copy-done.15
  11.7 0.1 fusion.9
  11.8 0.2 copy-done.16
  12.1 0.1 fusion.10
  12.1 0.1 maximum_bitcast_fusion.1
  12.3 0.1 maximum_bitcast_fusion.3
  12.4 1.9 pad_maximum_fusion.w_ref
  14.2 198.7 %gather_all.1 = (bf16[16,128,3072]{2,1,0:T(8,128)(2,1)}, bf16[12,128,3072]{2,1,0:T(8,128)(2,1)}, bf16[128,3072]{1,0:T(8,128)(2,1)}, bf16[16,16,128]{2,1,0:T(8,12...) custom-call(bf16[128,3072]{1,0:T(8,128)(2,1)} %pad_maximum_fusion.3.a_ref, ...), custom_call_target="tpu_custom_call" | custom-call | tf_op jit(solution)/shard_map/gather_all/pallas_call | solution.py:318
  212.9 0.8 convert_bitcast_fusion.gain_ref
  213.7 0.0 copy-done.3
  213.7 0.0 copy-done.4
  213.7 0.0 copy-start.7
  213.7 1.1 copy-done.7
  214.8 30.6 %attention_forward.1 = (f32[128,2048]{1,0:T(8,128)S(1)}, bf16[128,2048]{1,0:T(8,128)(2,1)S(1)}, bf16[256,2048]{1,0:T(8,128)(2,1)S(1)}, bf16[256,2048]{1,0:T(8,12...) custom-call(bf16[2,128,2048]{2,1,0:T(8,128)(2,1)} %get-tuple-element.34.tok_ref, ...), custom_call_target="tpu_custom_call" | custom-call | tf_op jit(solution)/shard_map/attention_forward/pallas_call | solution.py:840
  245.4 0.0 copy-done.10
  245.4 0.0 copy-start
  245.4 1.0 copy-done
  246.4 1.0 copy-done.5
  247.3 1.0 copy-done.6
  248.3 0.8 copy-done.8
  249.1 0.8 copy-done.9
  249.9 118.0 %feed_forward.1 = (f32[128,2048]{1,0:T(8,128)}, bf16[4,128,2048]{2,1,0:T(8,128)(2,1)}, bf16[16,128,3072]{2,1,0:T(8,128)(2,1)}) custom-call(bf16[128,2048]{1,0:T(8,128)(2,1)} %copy-done.9, bf16[1024,2048]{1,0:T(8,128)(2,1)} %bitcast.55, bf16[12,128,3072]{2,1,0:T(8,128)(2,1)} %get-tuple-element.41.w_ref, bf16[4,128,3072]{2,1,0:T(8,128)(2,1)} %get-tuple-element.42.w_late), custom_call_target="tpu_custom_call" | custom-call | tf_op jit(solution)/shard_map/feed_forward/pallas_call | solution.py:550
  367.9 0.0 copy-start.1
  367.9 0.0 copy-start.2
  367.9 141.4 %attention_backward.1 = (bf16[16,128,3072]{2,1,0:T(8,128)(2,1)}, bf16[4,128,3072]{2,1,0:T(8,128)(2,1)}, f32[128,2048]{1,0:T(8,128)}, f32[2,2048]{1,0:T(2,128)}) custom-call(f32[128,2048]{1,0:T(8,128)} %get-tuple-element.43.total_ref, f32[128,2048]{1,0:T(8,128)} %copy-done, bf16[128,2048]{1,0:T(8,128)(2,1)} %broadcast_select_fusion.dm_ref, ...), custom_call_target="tpu_custom_call" | custom-call | tf_op jit(solution)/shard_map/attention_backward/pallas_call | solution.py:1063
  509.3 0.7 pad.9.gain_ref
  510.1 0.0 copy-done.1
  510.1 0.0 copy-done.2
  510.1 140.0 %grad_sum.1 = (f32[128,3072]{1,0:T(8,128)S(1)}, f32[128,2048]{1,0:T(8,128)S(1)}, f32[8,128]{1,0:T(8,128)S(1)}) custom-call(f32[128,2048]{1,0:T(8,128)S(1)} %copy-done.1, bf16[16,128,3072]{2,1,0:T(8,128)(2,1)} %get-tuple-element.49.ga_ref, bf16[4,128,2048]{2,1,0:T(8,128)(2,1)S(1)} %copy-done.2, f32[16,8,128]{2,1,0:T(8,128)S(1)} %pad.9.gain_ref), custom_call_target="tpu_custom_call" | custom-call | tf_op jit(solution)/shard_map/grad_sum/pallas_call | solution.py:1216
  650.1 0.9 convert_element_type.24
  650.9 0.5 slice_bitcast_fusion.13
  651.5 0.8 fusion.8
  652.3 1.1 slice_bitcast_fusion.12
  653.4 2.0 copy.26
  655.4 0.8 convert_element_type.25
  656.2 2.0 slice_bitcast_fusion.3
  658.2 0.1 maximum_bitcast_fusion
  658.3 1.8 copy.27
  660.1 3.1 pad_maximum_fusion.2
  663.3 1.5 pad_maximum_fusion.1
  664.8 0.1 copy-done.17
  664.9 1.0 copy.30
  (14 shorter events, 0.1 us)
Async XLA Ops:
  0.6 9.3 %copy-start.14 = (bf16[4096,128]{1,0:T(8,128)(2,1)S(1)}, bf16[4096,128]{1,0:T(8,128)(2,1)}, u32[]{:S(2)}) copy-start(bf16[4096,128]{1,0:T(8,128)(2,1)} %param.21) | copy-start | bytes 3145732
  0.7 8.4 %copy-start.19 = (bf16[128,512]{1,0:T(8,128)(2,1)S(1)}, bf16[128,512]{1,0:T(8,128)(2,1)}, u32[]{:S(2)}) copy-start(bf16[128,512]{1,0:T(8,128)(2,1)} %param.16) | copy-start | bytes 393220
  0.7 8.4 %copy-start.20 = (bf16[128,512]{1,0:T(8,128)(2,1)S(1)}, bf16[128,512]{1,0:T(8,128)(2,1)}, u32[]{:S(2)}) copy-start(bf16[128,512]{1,0:T(8,128)(2,1)} %param.15) | copy-start | bytes 393220
  0.7 8.4 %copy-start.18 = (bf16[128,1024]{1,0:T(8,128)(2,1)S(1)}, bf16[128,1024]{1,0:T(8,128)(2,1)}, u32[]{:S(2)}) copy-start(bf16[128,1024]{1,0:T(8,128)(2,1)} %param.14) | copy-start | bytes 786436
  5.9 207.8 %copy-start.3 = (f32[256,128]{1,0:T(8,128)}, f32[256,128]{1,0:T(8,128)S(1)}, u32[]{:S(2)}) copy-start(f32[256,128]{1,0:T(8,128)S(1)} %get-tuple-element.98.sin_ref) | copy-start | bytes 393220
  5.9 207.8 %copy-start.4 = (f32[256,128]{1,0:T(8,128)}, f32[256,128]{1,0:T(8,128)S(1)}, u32[]{:S(2)}) copy-start(f32[256,128]{1,0:T(8,128)S(1)} %get-tuple-element.99.cos_ref) | copy-start | bytes 393220
  10.5 1.2 copy-start.15
  10.5 1.5 copy-start.16
  213.7 1.1 copy-start.7
  214.8 30.6 %copy-start.10 = (f32[2,2048]{1,0:T(2,128)}, f32[2,2048]{1,0:T(2,128)S(1)}, u32[]{:S(2)}) copy-start(f32[2,2048]{1,0:T(2,128)S(1)} %convert_bitcast_fusion.gain_ref) | copy-start | bytes 49156
  245.4 1.0 copy-start
  246.4 1.0 copy-start.5
  247.3 1.0 copy-start.6
  248.3 0.8 copy-start.8
  249.1 0.8 copy-start.9
  367.9 142.2 %copy-start.1 = (f32[128,2048]{1,0:T(8,128)S(1)}, f32[128,2048]{1,0:T(8,128)}, u32[]{:S(2)}) copy-start(f32[128,2048]{1,0:T(8,128)} %copy-done) | copy-start | bytes 3145732
  367.9 142.2 %copy-start.2 = (bf16[4,128,2048]{2,1,0:T(8,128)(2,1)S(1)}, bf16[4,128,2048]{2,1,0:T(8,128)(2,1)}, u32[]{:S(2)}) copy-start(bf16[4,128,2048]{2,1,0:T(8,128)(2,1)} %get-tuple-element.50.out_ref) | copy-start | bytes 6291460
  651.5 3.9 copy-start.11
  660.1 3.1 copy-start.12
  660.1 3.1 copy-start.13
  663.3 1.6 copy-start.17

commit v3 on v2

--- a/solution.py
+++ b/solution.py
@@ -232,17 +232,35 @@
         src = dm_all.at[z, me.t] if first is None else first
         return remote(src, dm_all.at[z, me.t], pair_send.at[z], pair_recv.at[z], me.sibling())
 
-    for way in range(2):
-        attn.start(way, 0)
-    planes[0].start(me.z, a_ref)
-    for k in range(1, LINE):
+    def start_parts(k):
         for way in range(2):
-
             for last in range(2):
 
                 @pl.when(jnp.logical_and(reach(me, 1 - way, k)[0], (me.z == late) == bool(last)))
                 def _():
                     part(way, k, last).start()
+
+    def each(k, act):
+        for way in range(2):
+            have, z = reach(me, way, k)
+
+            @pl.when(have)
+            def _():
+                act(way, k, z)
+
+    def attn_step(way, k, z):
+        attn.wait_block(way, k)
+        attn.start(way, k)
+        planes[0].start(z)
+
+    def part_step(way, k, z):
+        arrival(w_last, part_recv.at[way, k])
+        planes[1].start(z)
+
+    def dm_step(way, k, z):
+        dms.wait_block(way, k)
+        dms.start(way, k)
+        pair(z).start()
 
     def give_gain(step):
         target = lax.rem(me.d + step, count)
@@ -250,42 +268,34 @@
             gain_ref, gain_all.at[me.d], gain_send.at[step], gain_recv.at[step], (target, me.t)
         )
 
+    for way in range(2):
+        attn.start(way, 0)
+    planes[0].start(me.z, a_ref)
+    tokens = remote(tok_ref, tok_all.at[me.t], pair_send.at[LINE], pair_recv.at[LINE], me.sibling())
+    tokens.start()
     for step in range(1, count):
         give_gain(step).start()
-    tokens = remote(tok_ref, tok_all.at[me.t], pair_send.at[LINE], pair_recv.at[LINE], me.sibling())
-    tokens.start()
-    planes[1].start(me.z, w_ref.at[me.z])
+    for k in range(1, LINE):
+        each(k, attn_step)
+        start_parts(k)
+        if k == 1:
+            planes[0].forward(me.z)
+            planes[1].start(me.z, w_ref.at[me.z])
+        else:
+            each(k - 1, lambda way, k, z: planes[0].forward(z))
     for way in range(2):
         dms.start(way, 0)
     pair(me.z, dm_ref).start()
-
-    for k in range(1, LINE + 1):
-        if k < LINE:
-            for way in range(2):
-                have, z = reach(me, way, k)
-
-                @pl.when(have)
-                def _():
-                    attn.wait_block(way, k)
-                    attn.start(way, k)
-                    planes[0].start(z)
-                    arrival(w_last, part_recv.at[way, k])
-                    planes[1].start(z)
-                    dms.wait_block(way, k)
-                    dms.start(way, k)
-                    pair(z).start()
-
+    for k in range(1, LINE):
+        each(k, part_step)
         if k == 1:
-            planes[0].forward(me.z)
+            each(LINE - 1, lambda way, k, z: planes[0].forward(z))
             planes[1].forward(me.z)
         else:
-            for way in range(2):
-                have, z = reach(me, way, k - 1)
-
-                @pl.when(have)
-                def _():
-                    planes[0].forward(z)
-                    planes[1].forward(z)
+            each(k - 1, lambda way, k, z: planes[1].forward(z))
+            each(k - 1, dm_step)
+    each(LINE - 1, lambda way, k, z: planes[1].forward(z))
+    each(LINE - 1, dm_step)
 
     attn.finish()
     dms.finish()
@@ -337,13 +347,164 @@
     )(attn, mlp, gains, tokens, dm)
 
 
+RANKS = ((3, 2, 1, 0), (3, 0, 2, 1), (0, 3, 1, 2), (0, 1, 2, 3))
+FAR_FIRST = [(way, k) for k in range(LINE - 1, 0, -1) for way in range(2)]
+
+
+def ranked(me, rank):
+    z = jnp.int32(RANKS[0][rank])
+    for at in range(1, LINE):
+        z = jnp.where(me.z == at, RANKS[at][rank], z)
+    return z
+
+
+def way_to(me, z):
+    down = (z < me.z).astype(jnp.int32)
+    return down, jnp.where(z < me.z, me.z - z, z - me.z)
+
+
+def add_rows(target, terms, rows, start=0):
+    step = 16
+
+    @pl.loop(0, rows // step)
+    def _(i):
+        at = pl.ds(pl.multiple_of(start + i * step, step), step)
+        total = terms[0][at].astype(F32)
+        for term in terms[1:]:
+            total += term[at].astype(F32)
+        target[at] = total.astype(target.dtype)
+
+
+class PlaneSum:
+    def __init__(self, me, grad, own, other, first, second, sems, ranks=range(LINE)):
+        self.me, self.grad, self.own, self.other, self.first, self.second = me, grad, own, other, first, second
+        (
+            self.first_send, self.first_recv, self.second_send, self.second_recv, self.load_sem, self.other_sem,
+        ) = sems
+        self.ranks = ranks
+        self.rows = own.shape[1]
+        half = self.rows // 2
+        self.half = half
+        self.halves = (pl.ds(0, half), pl.ds(half, half))
+        self.square = me.plane == 4
+        if self.square:
+            self.near = (me.px, me.py)
+            self.far = (me.py, me.px)
+
+    def slot(self, rank):
+        return rank - self.ranks[0]
+
+    def block(self, rank, p):
+        return self.grad.at[ranked(self.me, rank) * self.me.plane + p]
+
+    def load(self, rank):
+        s = self.slot(rank)
+        return pltpu.make_async_copy(self.block(rank, self.me.p), self.own.at[s], self.load_sem.at[s])
+
+    def load_other(self, rank, i):
+        s = self.slot(rank)
+        return pltpu.make_async_copy(
+            self.block(rank, self.far[i]).at[self.halves[i]], self.other.at[s, self.halves[i]],
+            self.other_sem.at[s, i],
+        )
+
+    def load_all(self):
+        for rank in self.ranks:
+            self.load(rank).start()
+            if self.square:
+                for i in range(2):
+                    self.load_other(rank, i).start()
+
+    def give(self, rank, i, which):
+        me, s = self.me, self.slot(rank)
+        if not self.square:
+            target = lax.rem(me.p + which + 1, me.plane)
+            return remote(
+                self.block(rank, target), self.first.at[s, which], self.first_send.at[s, which],
+                self.first_recv.at[s, which], me.at(me.z, target),
+            )
+        owner = (self.near[i], me.pd)[which]
+        return remote(
+            self.block(rank, owner).at[self.halves[i]], self.first.at[s, which, self.halves[i]],
+            self.first_send.at[s, 2 * i + which], self.first_recv.at[s, 2 * i + which],
+            me.at(me.z, self.near[i]),
+        )
+
+    def give_both(self, rank, i):
+        s = self.slot(rank)
+        return remote(
+            self.other.at[s, self.halves[i]], self.second.at[s, self.halves[i]],
+            self.second_send.at[s, i], self.second_recv.at[s, i], self.me.at(self.me.z, self.far[i]),
+        )
+
+    def gives(self, rank):
+        if self.square:
+            return [self.give(rank, i, which) for which in (1, 0) for i in range(2)]
+        return [self.give(rank, 0, which) for which in range(self.me.plane - 1)]
+
+    def begin(self, rank):
+        for copy in self.gives(rank):
+            copy.start()
+
+    def middle(self, rank):
+        if not self.square:
+            return
+        s = self.slot(rank)
+        for i in range(2):
+            arrival(self.first.at[s, 1, self.halves[i]], self.first_recv.at[s, 2 * i + 1])
+            self.load_other(rank, i).wait()
+            add_rows(
+                self.other.at[s], (self.other.at[s], self.first.at[s, 1]), self.half, i * self.half
+            )
+            self.give_both(rank, i).start()
+
+    def end(self, rank):
+        s = self.slot(rank)
+        self.load(rank).wait()
+        if self.square:
+            for i in range(2):
+                arrival(self.first.at[s, 0, self.halves[i]], self.first_recv.at[s, 2 * i])
+                arrival(self.second.at[s, self.halves[i]], self.second_recv.at[s, i])
+            terms = (self.first.at[s, 0], self.second.at[s])
+        else:
+            for which in range(self.me.plane - 1):
+                arrival(self.first.at[s, which], self.first_recv.at[s, which])
+            terms = tuple(self.first.at[s, which] for which in range(self.me.plane - 1))
+        add_rows(self.own.at[s], (self.own.at[s],) + terms, self.rows)
+
+    def finish(self):
+        for rank in self.ranks:
+            for copy in self.gives(rank):
+                copy.wait_send()
+            if self.square:
+                for i in range(2):
+                    self.give_both(rank, i).wait_send()
+
+    @staticmethod
+    def scratch(count, rows, width, ranks=LINE):
+        plane = count // LINE
+        square = plane == 4
+        slots = 2 if square else plane - 1
+        small = (ranks, rows, width) if square else (1, 16, 128)
+        return [
+            pltpu.VMEM((ranks, rows, width), BF16),
+            pltpu.VMEM(small, BF16),
+            pltpu.VMEM((ranks, slots, rows, width), BF16),
+            pltpu.VMEM(small, BF16),
+        ], [
+            DMA((ranks, max(4, slots))), DMA((ranks, max(4, slots))), DMA((ranks, 2)), DMA((ranks, 2)),
+            DMA((ranks,)), DMA((ranks, 2)),
+        ]
+
+
 def dot_cols(left, right):
     return lax.dot_general(left, right, (((1,), (1,)), ((), ())), preferred_element_type=F32)
 
 
 def feed_forward_kernel(
-    plane, h_ref, dm_ref, w_ref, w_late, total_ref, out_ref, grad_ref, rows_in, weights, inner, part,
-    from_pair, from_line, chain_send, chain_recv, pass_send, pass_recv, pair_send, pair_recv,
+    plane, h_ref, dm_ref, w_ref, w_late, total_ref, out_ref, grad_ref, sum_ref, rows_in, weights, inner, part,
+    from_pair, from_line, own, other, first, second, first_send, first_recv, second_send, second_recv,
+    own_sem, other_sem, chain_send, chain_recv, pass_send, pass_recv, pair_send, pair_recv,
     line_send, line_recv, load_sem, dm_sem, grad_sem, out_sem,
 ):
     me = Place(plane)
@@ -367,7 +528,11 @@
     load_dm.start()
     keep = pltpu.make_async_copy(h_ref, slot(me.z, me.t), load_sem.at[1])
     keep.start()
-    greet_line(me)
+    greet_all(me, plane * LINE)
+    summed = PlaneSum(
+        me, weights, own, other, first, second,
+        (first_send, first_recv, second_send, second_recv, own_sem, other_sem), range(1),
+    )
     chain = Chain(me, h_ref, lambda z: slot(z, me.t), chain_send, chain_recv)
 
     def share(z, first=None):
@@ -417,8 +582,16 @@
                 inner[pl.ds(pl.multiple_of(2 * tokens + z * wide, wide), wide)], w_rows(n, tile, units)
             )
             part[0, z, :, :, here] = grad.astype(BF16).reshape(2, rows, tile)
+
+        pair(0, z).start()
+
+        @pl.loop(0, model // tile)
+        def _(n):
+            here = pl.ds(pl.multiple_of(n * tile, tile), tile)
             out = dot_cols(inner[at, :], w_rows(n, tile, 2 * units))
             part[1, z, :, :, here] = out.astype(BF16).reshape(2, rows, tile)
+
+        pair(1, z).start()
 
     def pair(job, z):
         return remote(
@@ -426,37 +599,43 @@
             pair_recv.at[job, z], me.sibling(),
         )
 
-    def pass_on(job, way, k):
+    half = rows // 2
+    halves = (pl.ds(0, half), pl.ds(half, half))
+
+    def pass_on(way, k, i):
         _, target = reach(me, 1 - way, k)
         ahead = me.z + 1 if way == 0 else me.z - 1
         return remote(
-            part.at[job, target, me.t], from_line.at[way, k - 1], line_send.at[way, k],
-            line_recv.at[way, k - 1], me.at(ahead, me.p),
-        )
-
-    def line(job, way, k, behind):
+            part.at[0, target, me.t, halves[i]], from_line.at[way, k - 1, halves[i]],
+            line_send.at[way, k, i], line_recv.at[way, k - 1, i], me.at(ahead, me.p),
+        )
+
+    def line(way, k, behind):
         have, z = reach(me, 1 - way, k)
         before = me.z if way == 0 else LINE - 1 - me.z
 
         @pl.when(jnp.logical_and(have, before == behind))
         def _():
-            pair(job, z).wait_recv()
-            terms = (part.at[job, z, me.t], from_pair.at[job, z])
+            pair(0, z).wait_recv()
+            terms = (part.at[0, z, me.t], from_pair.at[0, z])
             if behind:
-                arrival(from_line.at[way, k], line_recv.at[way, k])
                 terms += (from_line.at[way, k],)
-            add_rows(part.at[job, z, me.t], terms, rows)
-            pass_on(job, way, k).start()
-
-    def total(job):
-        pair(job, me.z).wait_recv()
-        add_rows(total_ref, (part.at[job, me.z, me.t], from_pair.at[job, me.z]), rows)
+            for i in range(2):
+                if behind:
+                    arrival(from_line.at[way, k, halves[i]], line_recv.at[way, k, i])
+                add_rows(part.at[0, z, me.t], terms, half, i * half)
+                pass_on(way, k, i).start()
+
+    def total():
+        pair(0, me.z).wait_recv()
+        add_rows(total_ref, (part.at[0, me.z, me.t], from_pair.at[0, me.z]), rows)
         for way in range(2):
 
             @pl.when(reach(me, way, 1)[0])
             def _():
-                arrival(from_line.at[way, 0], line_recv.at[way, 0])
-                add_rows(total_ref, (total_ref, from_line.at[way, 0]), rows)
+                for i in range(2):
+                    arrival(from_line.at[way, 0, halves[i]], line_recv.at[way, 0, i])
+                    add_rows(total_ref, (total_ref, from_line.at[way, 0]), half, i * half)
 
     def grads(z):
         per = plane * block
@@ -502,30 +681,37 @@
                     share(z).start()
                 arrival(slot(z, 1 - me.t), pass_recv.at[z])
                 compute(z)
-                for job in range(2):
-                    pair(job, z).start()
 
         if k:
             for way in range(2):
-                line(0, 1 - way, k, 0)
+                line(1 - way, k, 0)
     order = [(behind, k) for behind in range(1, LINE) for k in range(1, LINE - behind)]
     order.sort(key=lambda e: (2 * e[0] + e[1], e[0]))
-    for i in range(max(LINE, len(order))):
-        if i < LINE:
-            grads(i)
+
+    def keep_out(z):
+        return pltpu.make_async_copy(part.at[1, z, me.t], out_ref.at[z], out_sem.at[z])
+
+    for i in range(LINE):
+        grads(ranked(me, i))
+        if i == 0:
+            summed.load_all()
+            summed.begin(0)
+        if i == 1:
+            summed.middle(0)
         if i < len(order):
             for way in range(2):
-                line(0, way, order[i][1], order[i][0])
-
-    def keep_out(z):
-        return pltpu.make_async_copy(part.at[1, z, me.t], out_ref.at[z], out_sem.at[z])
-
+                line(way, order[i][1], order[i][0])
     for z in range(LINE):
         pair(1, z).wait_recv()
         add_rows(part.at[1, z, me.t], (part.at[1, z, me.t], from_pair.at[1, z]), rows)
         keep_out(z).start()
-    total(0)
-
+    summed.end(0)
+    keep_sum = pltpu.make_async_copy(own.at[0], sum_ref, load_sem.at[0])
+    keep_sum.start()
+    total()
+
+    summed.finish()
+    keep_sum.wait()
     chain.finish()
     for z in range(LINE):
         share(z).wait_send()
@@ -538,13 +724,15 @@
 
             @pl.when(reach(me, 1 - way, k)[0])
             def _():
-                pass_on(0, way, k).wait_send()
+                for i in range(2):
+                    pass_on(way, k, i).wait_send()
 
 
 def feed_forward(count, h, dm_all, w_all, w_late):
     rows, model = h.shape
     units = w_all.shape[2] // 3
     grads = (count,) + w_all.shape[1:]
+    buffers, sems = PlaneSum.scratch(count, *w_late.shape[1:], 1)
     tokens = LINE * 2 * rows
     vmem = pl.BlockSpec(memory_space=pltpu.VMEM)
     return pl.pallas_call(
@@ -554,9 +742,10 @@
             jax.ShapeDtypeStruct((rows, model), F32),
             jax.ShapeDtypeStruct((LINE, rows, model), BF16),
             jax.ShapeDtypeStruct(grads, BF16),
+            jax.ShapeDtypeStruct(w_late.shape[1:], BF16),
         ),
         in_specs=[vmem, ANY, ANY, ANY],
-        out_specs=(vmem, ANY, ANY),
+        out_specs=(vmem, ANY, ANY, ANY),
         scratch_shapes=[
             pltpu.VMEM((2 * tokens, model), BF16),
             pltpu.VMEM(grads, BF16),
@@ -564,152 +753,15 @@
             pltpu.VMEM((2, LINE, 2, rows, model), BF16),
             pltpu.VMEM((2, LINE, rows, model), BF16),
             pltpu.VMEM((2, LINE - 1, rows, model), BF16),
+            *buffers,
+            *sems,
             DMA((2, LINE)), DMA((2, LINE)), DMA((LINE,)), DMA((LINE,)), DMA((2, LINE)), DMA((2, LINE)),
-            DMA((2, LINE)), DMA((2, LINE)), DMA((3,)), DMA, DMA((LINE,)), DMA((LINE,)),
+            DMA((2, LINE, 2)), DMA((2, LINE, 2)), DMA((3,)), DMA, DMA((LINE,)), DMA((LINE,)),
         ],
         compiler_params=pltpu.CompilerParams(
             collective_id=1, has_side_effects=True, vmem_limit_bytes=60 * MB
         ),
     )(h, dm_all, w_all, w_late)
-
-
-def add_rows(target, terms, rows, start=0):
-    step = 16
-
-    @pl.loop(0, rows // step)
-    def _(i):
-        at = pl.ds(pl.multiple_of(start + i * step, step), step)
-        total = terms[0][at].astype(F32)
-        for term in terms[1:]:
-            total += term[at].astype(F32)
-        target[at] = total.astype(target.dtype)
-
-
-class PlaneSum:
-    def __init__(self, me, grad, own, other, first, second, sems):
-        self.me, self.grad, self.own, self.other, self.first, self.second = me, grad, own, other, first, second
-        (
-            self.first_send, self.first_recv, self.second_send, self.second_recv, self.load_sem, self.other_sem,
-        ) = sems
-        self.rows = own.shape[1]
-        half = self.rows // 2
-        self.half = half
-        self.halves = (pl.ds(0, half), pl.ds(half, half))
-        self.square = me.plane == 4
-        if self.square:
-            self.near = (me.px, me.py)
-            self.far = (me.py, me.px)
-
-    def load(self, z):
-        return pltpu.make_async_copy(
-            self.grad.at[z * self.me.plane + self.me.p], self.own.at[z], self.load_sem.at[z]
-        )
-
-    def load_other(self, z, i):
-        return pltpu.make_async_copy(
-            self.grad.at[z * self.me.plane + self.far[i], self.halves[i]],
-            self.other.at[z, self.halves[i]], self.other_sem.at[z, i],
-        )
-
-    def load_all(self):
-        for z in range(LINE):
-            self.load(z).start()
-            if self.square:
-                for i in range(2):
-                    self.load_other(z, i).start()
-
-    def give(self, z, i, which):
-        me = self.me
-        if not self.square:
-            target = lax.rem(me.p + which + 1, me.plane)
-            return remote(
-                self.grad.at[z * me.plane + target], self.first.at[z, which],
-                self.first_send.at[z, which], self.first_recv.at[z, which], me.at(me.z, target),
-            )
-        block = (self.near[i], me.pd)[which]
-        return remote(
-            self.grad.at[z * me.plane + block, self.halves[i]], self.first.at[z, which, self.halves[i]],
-            self.first_send.at[z, 2 * i + which], self.first_recv.at[z, 2 * i + which],
-            me.at(me.z, self.near[i]),
-        )
-
-    def give_both(self, z, i):
-        return remote(
-            self.other.at[z, self.halves[i]], self.second.at[z, self.halves[i]],
-            self.second_send.at[z, i], self.second_recv.at[z, i], self.me.at(self.me.z, self.far[i]),
-        )
-
-    def gives(self, z):
-        if self.square:
-            return [self.give(z, i, which) for which in (1, 0) for i in range(2)]
-        return [self.give(z, 0, which) for which in range(self.me.plane - 1)]
-
-    def begin(self, z):
-        for copy in self.gives(z):
-            copy.start()
-
-    def middle(self, z):
-        if not self.square:
-            return
-        for i in range(2):
-            arrival(self.first.at[z, 1, self.halves[i]], self.first_recv.at[z, 2 * i + 1])
-            self.load_other(z, i).wait()
-            add_rows(
-                self.other.at[z], (self.other.at[z], self.first.at[z, 1]), self.half, i * self.half
-            )
-            self.give_both(z, i).start()
-
-    def end(self, z):
-        self.load(z).wait()
-        if self.square:
-            for i in range(2):
-                arrival(self.first.at[z, 0, self.halves[i]], self.first_recv.at[z, 2 * i])
-                arrival(self.second.at[z, self.halves[i]], self.second_recv.at[z, i])
-            terms = (self.first.at[z, 0], self.second.at[z])
-        else:
-            for which in range(self.me.plane - 1):
-                arrival(self.first.at[z, which], self.first_recv.at[z, which])
-            terms = tuple(self.first.at[z, which] for which in range(self.me.plane - 1))
-        add_rows(self.own.at[z], (self.own.at[z],) + terms, self.rows)
-
-    def finish(self):
-        for z in range(LINE):
-            for copy in self.gives(z):
-                copy.wait_send()
-            if self.square:
-                for i in range(2):
-                    self.give_both(z, i).wait_send()
-
-    @staticmethod
-    def scratch(count, rows, width):
-        plane = count // LINE
-        square = plane == 4
-        slots = 2 if square else plane - 1
-        small = (LINE, rows, width) if square else (1, 16, 128)
-        return [
-            pltpu.VMEM((LINE, rows, width), BF16),
-            pltpu.VMEM(small, BF16),
-            pltpu.VMEM((LINE, slots, rows, width), BF16),
-            pltpu.VMEM(small, BF16),
-        ], [
-            DMA((LINE, max(4, slots))), DMA((LINE, max(4, slots))), DMA((LINE, 2)), DMA((LINE, 2)),
-            DMA((LINE,)), DMA((LINE, 2)),
-        ]
-
-
-FAR_FIRST = [(way, k) for k in range(LINE - 1, 0, -1) for way in range(2)] + [(0, 0)]
-
-
-def on(me, event, act):
-    way, k = event
-    have, z = reach(me, 1 - way, k)
-    if k == 0:
-        act(me.z)
-    else:
-
-        @pl.when(have)
-        def _():
-            act(z)
 
 
 def greet_plane(me):
@@ -865,7 +917,7 @@
 
 def attention_backward_kernel(
     plane, total_ref, x1_ref, dm_ref, tok_ref, gain_ref, cos_ref, sin_ref, h1_ref, qkv_ref, probs_ref,
-    o_ref, a_ref, gw_ref, ga_ref, w_out, grad_tokens, gain_parts, weights, own, other, first, second,
+    o_ref, a_ref, gw_ref, sum_ref, ga_ref, w_out, grad_tokens, gain_parts, weights, own, other, first, second,
     dx, da, do, dqkv, dh1, from_pair, first_send, first_recv, second_send, second_recv, load_sem,
     other_sem, part_send, part_recv, pair_send, pair_recv, a_sem, keep_sem, grad_sem,
 ):
@@ -881,18 +933,19 @@
     scale = HEAD_SIZE ** (-0.5)
     summed = PlaneSum(
         me, gw_ref, own, other, first, second,
-        (first_send, first_recv, second_send, second_recv, load_sem, other_sem),
+        (first_send, first_recv, second_send, second_recv, load_sem, other_sem), range(1, LINE),
     )
     load = pltpu.make_async_copy(a_ref, weights, a_sem)
     load.start()
     summed.load_all()
     greet_all(me, plane * LINE)
 
-    def part(way, k):
-        _, target = reach(me, 1 - way, k)
+    def part(rank):
+        target = ranked(me, rank)
+        way, k = way_to(me, target)
+        src = own.at[summed.slot(rank)] if rank else sum_ref
         return remote(
-            own.at[target], w_out.at[me.z], part_send.at[way, k], part_recv.at[way, k],
-            me.at(target, me.p),
+            src, w_out.at[me.z], part_send.at[way, k], part_recv.at[way, k], me.at(target, me.p)
         )
 
     give_da = remote(da.at[me.t], da.at[me.t], pair_send.at[0], pair_recv.at[0], me.sibling())
@@ -1011,33 +1064,26 @@
 
         row_loop(rows, 32, act)
 
-    lead, lag = 4, 2
-    last = len(FAR_FIRST)
-    for i in range(lead):
-        on(me, FAR_FIRST[i], summed.begin)
+    summed.begin(1)
+    part(0).start()
     mid_norm()
     grad_o()
-    stages = [grad_heads, grad_h1, grads, in_norm]
-    for i in range(last + lag):
-        if i + lead < last:
-            on(me, FAR_FIRST[i + lead], summed.begin)
-        if i < len(stages):
-            stages[i]()
-        if i < last:
-            on(me, FAR_FIRST[i], summed.middle)
-        if i >= lag:
-            event = FAR_FIRST[i - lag]
-            on(me, event, summed.end)
-            if event[1]:
-                on(me, event, lambda z: part(*event).start())
-
-    keep = pltpu.make_async_copy(own.at[me.z], w_out.at[me.z], keep_sem)
+    stages = [[], [grad_heads, grad_h1], [grads], [in_norm]]
+    for rank in range(1, LINE):
+        summed.middle(rank)
+        if rank + 1 < LINE:
+            summed.begin(rank + 1)
+        for stage in stages[rank]:
+            stage()
+        summed.end(rank)
+        if rank < LINE - 1:
+            part(rank).start()
+
+    keep = pltpu.make_async_copy(own.at[LINE - 2], w_out.at[me.z], keep_sem)
     keep.start()
-    for way, k in FAR_FIRST[:-1]:
-
-        @pl.when(reach(me, 1 - way, k)[0])
-        def _():
-            part(way, k).wait_send()
+    for rank in range(LINE - 1):
+        part(rank).wait_send()
+    for way, k in FAR_FIRST:
 
         @pl.when(reach(me, way, k)[0])
         def _():
@@ -1052,14 +1098,14 @@
 
 
 def attention_backward(
-    count, total, x1, dm, tokens_all, gains, cos, sin, h1, qkv, probs, o, attn_all, grad_mlp
+    count, total, x1, dm, tokens_all, gains, cos, sin, h1, qkv, probs, o, attn_all, grad_mlp, first_sum
 ):
     _, rows, model = tokens_all.shape
     _, block, width = attn_all.shape
     wide = 2 * rows
     heads = probs.shape[0]
     q_width = heads * HEAD_SIZE
-    buffers, sems = PlaneSum.scratch(count, block, width)
+    buffers, sems = PlaneSum.scratch(count, block, width, LINE - 1)
     return pl.pallas_call(
         functools.partial(attention_backward_kernel, count // LINE),
         name="attention_backward",
@@ -1069,7 +1115,7 @@
             jax.ShapeDtypeStruct((rows, model), F32),
             jax.ShapeDtypeStruct((2, model), F32),
         ),
-        in_specs=[VMEM] * 11 + [ANY] * 2,
+        in_specs=[VMEM] * 11 + [ANY] * 3,
         out_specs=(ANY, ANY, VMEM, VMEM),
         scratch_shapes=[
             pltpu.VMEM(attn_all.shape, BF16),
@@ -1086,7 +1132,7 @@
         compiler_params=pltpu.CompilerParams(
             collective_id=3, has_side_effects=True, vmem_limit_bytes=60 * MB
         ),
-    )(total, x1, dm, tokens_all, gains, cos, sin, h1, qkv, probs, o, attn_all, grad_mlp)
+    )(total, x1, dm, tokens_all, gains, cos, sin, h1, qkv, probs, o, attn_all, grad_mlp, first_sum)
 
 
 def grad_sum_kernel(
@@ -1106,28 +1152,25 @@
         def __init__(self, held, landing, send, recv):
             self.held, self.landing, self.send, self.recv = held, landing, send, recv
 
-        def pass_on(self, way, k):
-            _, target = reach(me, 1 - way, k)
-            ahead = me.z + 1 if way == 0 else me.z - 1
+        def pass_on(self, rank):
+            way, k = way_to(me, ranked(me, rank))
+            ahead = jnp.where(way == 0, me.z + 1, me.z - 1)
             return remote(
-                self.held.at[target], self.landing.at[way, k - 1], self.send.at[way, k],
+                self.held(rank), self.landing.at[way, k - 1], self.send.at[way, k],
                 self.recv.at[way, k - 1], me.at(ahead, me.p),
             )
 
-        def step(self, way, k, behind=None):
-            have, z = reach(me, 1 - way, k)
-            before = me.z if way == 0 else LINE - 1 - me.z
-
-            @pl.when(have if behind is None else jnp.logical_and(have, before == behind))
+        def step(self, rank):
+            way, k = way_to(me, ranked(me, rank))
+            before = jnp.where(way == 0, me.z, LINE - 1 - me.z)
+            held = self.held(rank)
+
+            @pl.when(before > 0)
             def _():
-                @pl.when(before > 0)
-                def _():
-                    arrival(self.landing.at[way, k], self.recv.at[way, k])
-                    add_rows(
-                        self.held.at[z], (self.held.at[z], self.landing.at[way, k]), self.held.shape[1]
-                    )
-
-                self.pass_on(way, k).start()
+                arrival(self.landing.at[way, k], self.recv.at[way, k])
+                add_rows(held, (held, self.landing.at[way, k]), held.shape[0])
+
+            self.pass_on(rank).start()
 
         def total(self, act):
             for way in range(2):
@@ -1138,14 +1181,11 @@
                     act(self.landing.at[way, 0])
 
         def finish(self):
-            for way, k in FAR_FIRST[:-1]:
-
-                @pl.when(reach(me, 1 - way, k)[0])
-                def _():
-                    self.pass_on(way, k).wait_send()
-
-    grads = Line(own, from_line, line_send, line_recv)
-    outs = Line(out_own, out_line, out_send, out_recv)
+            for rank in range(LINE - 1):
+                self.pass_on(rank).wait_send()
+
+    grads = Line(lambda rank: own.at[rank], from_line, line_send, line_recv)
+    outs = Line(lambda rank: out_own.at[ranked(me, rank)], out_line, out_send, out_recv)
     summed.load_all()
     load_out = pltpu.make_async_copy(out_ref, out_own, out_sem)
     load_out.start()
@@ -1157,29 +1197,29 @@
             gain_ref.at[target], gain_in.at[step], gain_send.at[step], gain_recv.at[step], (target, me.t)
         )
 
-    lead, lag, line_lag = 4, 2, 5
-    last = len(FAR_FIRST)
-    for i in range(lead):
-        on(me, FAR_FIRST[i], summed.begin)
+    summed.begin(0)
     for step in range(1, count):
         give_gain(step).start()
     load_out.wait()
-    for k in range(LINE - 1, 0, -1):
-        for way in range(2):
-            outs.step(way, k, 0)
-    order = [(behind, k) for behind in range(1, LINE) for k in range(LINE - 1 - behind, 0, -1)]
-    for i in range(last + line_lag):
-        if i + lead < last:
-            on(me, FAR_FIRST[i + lead], summed.begin)
-        if i < last:
-            on(me, FAR_FIRST[i], summed.middle)
-        if i < len(order):
-            for way in range(2):
-                outs.step(way, order[i][1], order[i][0])
-        if 0 <= i - lag < last:
-            on(me, FAR_FIRST[i - lag], summed.end)
-        if 0 <= i - line_lag < last - 1:
-            grads.step(*FAR_FIRST[i - line_lag])
+    for rank in range(LINE - 1):
+
+        @pl.when(jnp.logical_or(me.z == 0, me.z == LINE - 1))
+        def _():
+            outs.step(rank)
+
+    for rank in range(LINE):
+        summed.middle(rank)
+        if rank + 1 < LINE:
+            summed.begin(rank + 1)
+        if rank < LINE - 1:
+
+            @pl.when(jnp.logical_and(me.z > 0, me.z < LINE - 1))
+            def _():
+                outs.step(rank)
+
+        summed.end(rank)
+        if rank:
+            grads.step(rank - 1)
 
     def add_out(landed):
         def act(at):
@@ -1192,7 +1232,7 @@
 
     row_loop(output.shape[0], 16, out_start)
     outs.total(add_out)
-    add_rows(a_out, (own.at[me.z],), rows)
+    add_rows(a_out, (own.at[LINE - 1],), rows)
     grads.total(lambda landed: add_rows(a_out, (a_out, landed), rows))
 
     total = gain_ref[me.d]
@@ -1279,12 +1319,12 @@
         count, q_width // HEAD_SIZE, tokens_all, gains_full, cos, sin, key_allowed.astype(F32),
         attn_all, mlp_last,
     )
-    grad_h2, out_parts, grad_mlp_w = feed_forward(
+    grad_h2, out_parts, grad_mlp_w, first_sum = feed_forward(
         count, h2, dm_all.reshape(-1, model), mlp_all, mlp_late
     )
     grad_attn_w, mlp_sum, grad_tokens, gain_parts = attention_backward(
         count, grad_h2, x1, dm, tokens_all, gains_full, cos, sin, h1, qkv, probs, attended, attn_all,
-        grad_mlp_w,
+        grad_mlp_w, first_sum,
     )
     gain_parts = gain_parts.reshape(2, count, rows).transpose(1, 0, 2)
     gain_parts = jnp.pad(gain_parts, ((0, 0), (0, 6), (0, lanes)))

time: 675 us -> 570 us (0.84)
  Pallas kernels: 629 us -> 524 us
    pallas_call x1, Pallas kernels: 141 us -> 89.8 us  [attention_backward(): pl.pallas_call(functools.partial(attention_backward_kernel, count // LINE...]
    pallas_call x1, Pallas kernels: 118 us -> 92.1 us  [feed_forward(): pl.pallas_call(functools.partial(feed_forward_kernel, count // LINE), nam...]
    pallas_call x1, Pallas kernels: 140 us -> 126 us  [grad_sum(): pl.pallas_call(functools.partial(grad_sum_kernel, count), name='grad_sum'...]
    pallas_call x1, Pallas kernels: 199 us -> 186 us  [gather_all(): pl.pallas_call(functools.partial(gather_kernel, count), name='gather_all'...]
where the time goes in v3:
time: 570 us; the launch traced here: 562 us
  Pallas kernels  524 us (92%)
  local copies, waits for them, and re-layouts  19 us (3%)
  other arithmetic  16.5 us (3%)
    pallas_call x1, Pallas kernels, gather_all(): pl.pallas_call(functools.partial(gather_kernel, count), name='gather_all'...  186 us
    pallas_call x1, Pallas kernels, grad_sum(): pl.pallas_call(functools.partial(grad_sum_kernel, count), name='grad_sum'...  126 us
    pallas_call x1, Pallas kernels, feed_forward(): pl.pallas_call(functools.partial(feed_forward_kernel, count // LINE), nam...  92.1 us
    pallas_call x1, Pallas kernels, attention_backward(): pl.pallas_call(functools.partial(attention_backward_kernel, count // LINE...  89.8 us
    pallas_call x1, Pallas kernels, attention_forward(): pl.pallas_call(functools.partial(attention_forward_kernel, plane), name='...  30.6 us
    unnamed x47, local copies, waits for them, and re-layouts  13.7 us

profile of v3, /device:TPU:8, one launch (start us, length us, event | category | flops | bytes accessed | tf_op | source)
XLA Modules:
  0.0 562.0 jit_solution(2611501468919222001)
XLA Ops:
  0.6 0.0 copy-start.14
  0.7 0.0 copy-start.19
  0.7 0.0 copy-start.20
  0.7 0.0 copy-start.18
  1.4 1.3 fusion.7
  2.7 0.7 add_compare_fusion
  3.4 0.7 iota_compare_fusion.2
  4.1 1.3 fusion.6.gain_ref
  5.4 0.5 fusion.2
  5.9 0.0 copy-start.3
  5.9 0.0 copy-start.4
  5.9 1.2 copy.24
  7.1 1.9 broadcast_select_fusion.dm_ref
  9.0 0.0 copy-done.19
  9.0 0.0 copy-done.20
  9.0 0.0 copy-done.18
  9.0 0.9 pad_maximum_fusion.3.a_ref
  10.0 0.0 copy-done.14
  10.0 0.5 copy.25
  10.5 0.0 copy-start.15
  10.5 0.0 copy-start.16
  10.5 0.1 fusion.11
  10.6 1.1 copy-done.15
  11.7 0.1 fusion.9
  11.8 0.2 copy-done.16
  12.1 0.1 fusion.10
  12.1 0.1 maximum_bitcast_fusion.1
  12.3 0.1 maximum_bitcast_fusion.3
  12.4 1.9 pad_maximum_fusion.w_ref
  14.2 186.1 %gather_all.1 = (bf16[16,128,3072]{2,1,0:T(8,128)(2,1)}, bf16[12,128,3072]{2,1,0:T(8,128)(2,1)}, bf16[128,3072]{1,0:T(8,128)(2,1)}, bf16[16,16,128]{2,1,0:T(8,12...) custom-call(bf16[128,3072]{1,0:T(8,128)(2,1)} %pad_maximum_fusion.3.a_ref, ...), custom_call_target="tpu_custom_call" | custom-call | tf_op jit(solution)/shard_map/gather_all/pallas_call | solution.py:328
  200.3 0.8 convert_bitcast_fusion.gain_ref
  201.1 0.0 copy-done.3
  201.1 0.0 copy-done.4
  201.1 0.0 copy-start.7
  201.1 1.1 copy-done.7
  202.2 30.6 %attention_forward.1 = (f32[128,2048]{1,0:T(8,128)S(1)}, bf16[128,2048]{1,0:T(8,128)(2,1)S(1)}, bf16[256,2048]{1,0:T(8,128)(2,1)S(1)}, bf16[256,2048]{1,0:T(8,12...) custom-call(bf16[2,128,2048]{2,1,0:T(8,128)(2,1)} %get-tuple-element.35.tok_ref, ...), custom_call_target="tpu_custom_call" | custom-call | tf_op jit(solution)/shard_map/attention_forward/pallas_call | solution.py:892
  232.8 0.0 copy-done.10
  232.8 0.0 copy-start
  232.8 1.0 copy-done
  233.8 1.0 copy-done.5
  234.7 1.0 copy-done.6
  235.7 0.8 copy-done.8
  236.5 0.8 copy-done.9
  237.3 92.1 %feed_forward.1 = (f32[128,2048]{1,0:T(8,128)}, bf16[4,128,2048]{2,1,0:T(8,128)(2,1)}, bf16[16,128,3072]{2,1,0:T(8,128)(2,1)}, bf16[128,3072]{1,0:T(8,128)(2,1)}) custom-call(bf16[128,2048]{1,0:T(8,128)(2,1)} %copy-done.8, bf16[1024,2048]{1,0:T(8,128)(2,1)} %bitcast.55, bf16[12,128,3072]{2,1,0:T(8,128)(2,1)} %get-tuple-element.42.w_ref, ...), custom_call_target="tpu_custom_call" | custom-call | tf_op jit(solution)/shard_map/feed_forward/pallas_call | solution.py:738
  329.4 0.0 copy-start.1
  329.4 89.8 %attention_backward.1 = (bf16[16,128,3072]{2,1,0:T(8,128)(2,1)}, bf16[4,128,3072]{2,1,0:T(8,128)(2,1)}, f32[128,2048]{1,0:T(8,128)}, f32[2,2048]{1,0:T(2,128)}) custom-call(f32[128,2048]{1,0:T(8,128)} %get-tuple-element.44.total_ref, f32[128,2048]{1,0:T(8,128)} %copy-done, bf16[128,2048]{1,0:T(8,128)(2,1)} %broadcast_select_fusion.dm_ref, ...), custom_call_target="tpu_custom_call" | custom-call | tf_op jit(solution)/shard_map/attention_backward/pallas_call | solution.py:1109
  419.2 0.7 pad.9.gain_ref
  419.9 0.0 copy-done.1
  419.9 125.8 %grad_sum.1 = (f32[128,3072]{1,0:T(8,128)S(1)}, f32[128,2048]{1,0:T(8,128)S(1)}, f32[8,128]{1,0:T(8,128)S(1)}) custom-call(f32[128,2048]{1,0:T(8,128)S(1)} %copy-done.1, bf16[16,128,3072]{2,1,0:T(8,128)(2,1)} %get-tuple-element.51.ga_ref, bf16[4,128,2048]{2,1,0:T(8,128)(2,1)S(1)} %copy-done.2, f32[16,8,128]{2,1,0:T(8,128)S(1)} %pad.9.gain_ref), custom_call_target="tpu_custom_call" | custom-call | tf_op jit(solution)/shard_map/grad_sum/pallas_call | solution.py:1256
  545.8 0.9 convert_element_type.24
  546.6 0.5 slice_bitcast_fusion.13
  547.2 0.8 fusion.8
  548.0 1.1 slice_bitcast_fusion.12
  549.1 2.0 copy.26
  551.1 0.0 copy-done.11
  551.1 0.8 convert_element_type.25
  551.9 2.0 slice_bitcast_fusion.3
  553.9 0.1 maximum_bitcast_fusion
  554.0 1.8 copy.27
  555.9 3.1 pad_maximum_fusion.2
  559.0 0.0 copy-done.12
  559.0 1.5 pad_maximum_fusion.1
  560.5 0.1 copy-done.17
  560.6 1.0 copy.30
  (14 shorter events, 0.1 us)
Async XLA Ops:
  0.6 9.3 %copy-start.14 = (bf16[4096,128]{1,0:T(8,128)(2,1)S(1)}, bf16[4096,128]{1,0:T(8,128)(2,1)}, u32[]{:S(2)}) copy-start(bf16[4096,128]{1,0:T(8,128)(2,1)} %param.21) | copy-start | bytes 3145732
  0.7 8.4 %copy-start.19 = (bf16[128,512]{1,0:T(8,128)(2,1)S(1)}, bf16[128,512]{1,0:T(8,128)(2,1)}, u32[]{:S(2)}) copy-start(bf16[128,512]{1,0:T(8,128)(2,1)} %param.16) | copy-start | bytes 393220
  0.7 8.4 %copy-start.20 = (bf16[128,512]{1,0:T(8,128)(2,1)S(1)}, bf16[128,512]{1,0:T(8,128)(2,1)}, u32[]{:S(2)}) copy-start(bf16[128,512]{1,0:T(8,128)(2,1)} %param.15) | copy-start | bytes 393220
  0.7 8.4 %copy-start.18 = (bf16[128,1024]{1,0:T(8,128)(2,1)S(1)}, bf16[128,1024]{1,0:T(8,128)(2,1)}, u32[]{:S(2)}) copy-start(bf16[128,1024]{1,0:T(8,128)(2,1)} %param.14) | copy-start | bytes 786436
  5.9 195.2 %copy-start.3 = (f32[256,128]{1,0:T(8,128)}, f32[256,128]{1,0:T(8,128)S(1)}, u32[]{:S(2)}) copy-start(f32[256,128]{1,0:T(8,128)S(1)} %get-tuple-element.100.sin_ref) | copy-start | bytes 393220
  5.9 195.2 %copy-start.4 = (f32[256,128]{1,0:T(8,128)}, f32[256,128]{1,0:T(8,128)S(1)}, u32[]{:S(2)}) copy-start(f32[256,128]{1,0:T(8,128)S(1)} %get-tuple-element.101.cos_ref) | copy-start | bytes 393220
  10.5 1.2 copy-start.15
  10.5 1.5 copy-start.16
  201.1 1.1 copy-start.7
  202.2 30.6 %copy-start.10 = (f32[2,2048]{1,0:T(2,128)}, f32[2,2048]{1,0:T(2,128)S(1)}, u32[]{:S(2)}) copy-start(f32[2,2048]{1,0:T(2,128)S(1)} %convert_bitcast_fusion.gain_ref) | copy-start | bytes 49156
  232.8 1.0 copy-start
  233.8 1.0 copy-start.5
  234.7 1.0 copy-start.6
  235.7 0.8 copy-start.8
  236.5 0.8 copy-start.9
  329.4 90.5 %copy-start.1 = (f32[128,2048]{1,0:T(8,128)S(1)}, f32[128,2048]{1,0:T(8,128)}, u32[]{:S(2)}) copy-start(f32[128,2048]{1,0:T(8,128)} %copy-done) | copy-start | bytes 3145732
  329.4 90.5 %copy-start.2 = (bf16[4,128,2048]{2,1,0:T(8,128)(2,1)S(1)}, bf16[4,128,2048]{2,1,0:T(8,128)(2,1)}, u32[]{:S(2)}) copy-start(bf16[4,128,2048]{2,1,0:T(8,128)(2,1)} %get-tuple-element.52.out_ref) | copy-start | bytes 6291460
  547.2 3.9 copy-start.11
  555.9 3.1 copy-start.12
  555.9 3.1 copy-start.13
  559.0 1.6 copy-start.17

commit v4 on v3

--- a/solution.py
+++ b/solution.py
@@ -16,6 +16,8 @@
 BF16 = jnp.bfloat16
 F32 = jnp.float32
 MB = 1024 * 1024
+LATE = 1
+EARLY = 1
 
 
 def rope_tables(count, head_dim):
@@ -23,7 +25,7 @@
     index = jnp.arange(half, dtype=jnp.float32)
     freqs = jnp.exp(index * (-2.0 * math.log(THETA) / head_dim))
     angles = jnp.arange(count, dtype=jnp.float32)[:, None] * freqs[None, :]
-    return (jnp.cos(angles)[:, None, :], jnp.sin(angles)[:, None, :])
+    return jnp.cos(angles), jnp.sin(angles)
 
 
 def dot_tn(left, right):
@@ -124,9 +126,8 @@
 
 
 class PlaneGather:
-    def __init__(self, me, job, held, rows, send, recv, late=None):
+    def __init__(self, me, job, held, rows, send, recv):
         self.me, self.job, self.held, self.send, self.recv = me, job, held, send, recv
-        self.late = late
         self.half = rows // 2
 
     def piece(self, z, p, half):
@@ -148,36 +149,21 @@
             ref, dst, self.send.at[self.job, z, kind], self.recv.at[self.job, z, kind], me.at(me.z, target)
         )
 
-    def unless_late(self, z, act):
-        if self.late is None:
-            act()
-        else:
-            pl.when(z != self.late)(act)
-
     def start(self, z, first=None):
         kinds = (0, 2, 1, 3) if self.me.plane == 4 else range(self.me.plane - 1)
-
-        def act():
-            for kind in kinds:
-                self.copy(z, kind, first).start()
-
-        self.unless_late(z, act)
+        for kind in kinds:
+            self.copy(z, kind, first).start()
 
     def forward(self, z):
-        def act():
+        if self.me.plane == 4:
             self.copy(z, 0).wait_recv()
             self.copy(z, 4).start()
             self.copy(z, 2).wait_recv()
             self.copy(z, 5).start()
 
-        if self.me.plane == 4:
-            self.unless_late(z, act)
-
     def finish(self, zs=range(LINE)):
         kinds = 6 if self.me.plane == 4 else self.me.plane - 1
         for z in zs:
-            if z == self.late:
-                continue
             for kind in range(kinds):
                 copy = self.copy(z, kind)
                 if self.me.plane != 4 or kind not in (0, 2):
@@ -185,60 +171,76 @@
                 copy.wait_send()
 
 
+def copy_in(src, dst, sem):
+    return pltpu.make_async_copy(src, dst, sem)
+
+
+def row_loop(rows, step, act):
+    @pl.loop(0, rows // step)
+    def _(i):
+        act(pl.ds(pl.multiple_of(i * step, step), step))
+
+
 def gather_kernel(
-    count, a_ref, w_ref, gain_ref, tok_ref, dm_ref, a_all, w_all, w_last, gain_all, tok_all, dm_all,
-    chain_send, chain_recv, part_send, part_recv, plane_send, plane_recv, gain_send, gain_recv,
-    pair_send, pair_recv, local_sem,
+    count, len_ref, seq_ref, q_ref, k_ref, v_ref, o_ref, g_ref, u_ref, d_ref, gain_ref, tok_ref, cot_ref,
+    a_all, gu_all, down, gain_all, tok_all, dm_all, o_v, a_v, gu_v, d_v, d_t, dm, chain_send, chain_recv,
+    part_send, part_recv, plane_send, plane_recv, gain_send, gain_recv, pair_send, pair_recv, local_sem,
 ):
     plane = count // LINE
     me = Place(plane)
-    rows = a_ref.shape[0]
-    late = LINE - 1
-    own_w = [
-        pltpu.make_async_copy(w_ref.at[me.z], w_all.at[me.d], local_sem.at[1]),
-        pltpu.make_async_copy(w_ref.at[me.z], w_last, local_sem.at[1]),
+    rows, q_width = q_ref.shape
+    kv_width = k_ref.shape[1]
+    units = g_ref.shape[1] // LINE
+    qkv_width = q_width + 2 * kv_width
+
+    def columns(ref, z):
+        return ref.at[:, pl.ds(pl.multiple_of(z * units, units), units)]
+
+    local = [
+        copy_in(o_ref, o_v, local_sem.at[0]),
+        copy_in(q_ref, a_v.at[:, pl.ds(0, q_width)], local_sem.at[1]),
+        copy_in(k_ref, a_v.at[:, pl.ds(q_width, kv_width)], local_sem.at[2]),
+        copy_in(v_ref, a_v.at[:, pl.ds(q_width + kv_width, kv_width)], local_sem.at[3]),
+        copy_in(d_ref, d_v, local_sem.at[4]),
+        copy_in(cot_ref, dm, local_sem.at[5]),
+        copy_in(columns(g_ref, me.z), gu_v.at[:, pl.ds(0, units)], local_sem.at[6]),
+        copy_in(columns(u_ref, me.z), gu_v.at[:, pl.ds(units, units)], local_sem.at[7]),
+        copy_in(gain_ref, gain_all.at[me.d], local_sem.at[8]),
+        copy_in(tok_ref, tok_all.at[me.t], local_sem.at[9]),
     ]
-    for ref, here in zip(own_w, (me.z != late, me.z == late)):
-
-        @pl.when(here)
-        def _():
-            ref.start()
-
-    local = [
-        pltpu.make_async_copy(a_ref, a_all.at[me.d], local_sem.at[0]),
-        pltpu.make_async_copy(gain_ref, gain_all.at[me.d], local_sem.at[2]),
-        pltpu.make_async_copy(tok_ref, tok_all.at[me.t], local_sem.at[3]),
-        pltpu.make_async_copy(dm_ref, dm_all.at[me.z, me.t], local_sem.at[4]),
-    ]
-    for copy in local:
+    for copy in local[:4]:
         copy.start()
-    greet_all(me, count)
-
-    attn = Chain(me, a_ref, lambda z: a_all.at[z * plane + me.p], chain_send.at[0], chain_recv.at[0])
-    dms = Chain(me, dm_ref, lambda z: dm_all.at[z, me.t], chain_send.at[1], chain_recv.at[1])
+    keep_a = copy_in(a_v, a_all.at[me.d], local_sem.at[10])
+    keep_down = copy_in(d_t.at[me.z], down.at[me.z], local_sem.at[11])
+    keep_dm = copy_in(dm, dm_all.at[me.z, me.t], local_sem.at[12])
+    keep_gu = copy_in(gu_v, gu_all.at[me.d], local_sem.at[13])
+
+    attn = Chain(me, a_v, lambda z: a_all.at[z * plane + me.p], chain_send.at[0], chain_recv.at[0])
+    dms = Chain(me, dm, lambda z: dm_all.at[z, me.t], chain_send.at[1], chain_recv.at[1])
     planes = (
         PlaneGather(me, 0, a_all, rows, plane_send, plane_recv),
-        PlaneGather(me, 1, w_all, rows, plane_send, plane_recv, late),
+        PlaneGather(me, 1, gu_all, rows, plane_send, plane_recv),
     )
 
-    def part(way, k, last):
+    def part(way, k, kind):
         _, target = reach(me, 1 - way, k)
-        dst = w_last if last else w_all.at[me.d]
+        src = d_t.at[target] if kind == 2 else columns((g_ref, u_ref)[kind], target)
+        dst = down.at[me.z] if kind == 2 else gu_all.at[me.d, :, pl.ds(kind * units, units)]
         return remote(
-            w_ref.at[target], dst, part_send.at[way, k], part_recv.at[way, k], me.at(target, me.p)
+            src, dst, part_send.at[way, k, kind], part_recv.at[way, k, kind], me.at(target, me.p)
         )
 
     def pair(z, first=None):
         src = dm_all.at[z, me.t] if first is None else first
         return remote(src, dm_all.at[z, me.t], pair_send.at[z], pair_recv.at[z], me.sibling())
 
-    def start_parts(k):
+    def start_parts(k, kinds):
         for way in range(2):
-            for last in range(2):
-
-                @pl.when(jnp.logical_and(reach(me, 1 - way, k)[0], (me.z == late) == bool(last)))
-                def _():
-                    part(way, k, last).start()
+
+            @pl.when(reach(me, 1 - way, k)[0])
+            def _():
+                for kind in kinds:
+                    part(way, k, kind).start()
 
     def each(k, act):
         for way in range(2):
@@ -254,7 +256,8 @@
         planes[0].start(z)
 
     def part_step(way, k, z):
-        arrival(w_last, part_recv.at[way, k])
+        for kind in range(2):
+            arrival(gu_all.at[z * plane + me.p, :, pl.ds(kind * units, units)], part_recv.at[way, k, kind])
         planes[1].start(z)
 
     def dm_step(way, k, z):
@@ -268,24 +271,53 @@
             gain_ref, gain_all.at[me.d], gain_send.at[step], gain_recv.at[step], (target, me.t)
         )
 
+    local[0].wait()
+    a_v[:, qkv_width:] = o_v[...].T
+    greet_all(me, count)
+    for copy in local[1:4]:
+        copy.wait()
     for way in range(2):
         attn.start(way, 0)
-    planes[0].start(me.z, a_ref)
+    planes[0].start(me.z, a_v)
+    for copy in local[4:]:
+        copy.start()
+    keep_a.start()
     tokens = remote(tok_ref, tok_all.at[me.t], pair_send.at[LINE], pair_recv.at[LINE], me.sibling())
     tokens.start()
     for step in range(1, count):
         give_gain(step).start()
+
+    local[4].wait()
+    for z in range(LINE):
+        d_t[z] = d_v[z * units : (z + 1) * units, :].T
+    keep_down.start()
+    local[5].wait()
+    chosen = len_ref[seq_ref[0]]
+
+    def mask(at):
+        value = dm[at, :].astype(F32)
+        row = lax.broadcasted_iota(jnp.int32, value.shape, 0) + (me.t * dm.shape[0] + at.start)
+        dm[at, :] = jnp.where(row < chosen, value, 0.0).astype(BF16)
+
+    row_loop(dm.shape[0], 32, mask)
+    keep_dm.start()
+
     for k in range(1, LINE):
         each(k, attn_step)
-        start_parts(k)
+        start_parts(k, (0, 1))
         if k == 1:
             planes[0].forward(me.z)
-            planes[1].start(me.z, w_ref.at[me.z])
+            for copy in local[6:8]:
+                copy.wait()
+            keep_gu.start()
+            planes[1].start(me.z, gu_v)
         else:
             each(k - 1, lambda way, k, z: planes[0].forward(z))
+    for k in range(1, LINE):
+        start_parts(k, (2,))
     for way in range(2):
         dms.start(way, 0)
-    pair(me.z, dm_ref).start()
+    pair(me.z, dm).start()
     for k in range(1, LINE):
         each(k, part_step)
         if k == 1:
@@ -304,8 +336,10 @@
 
             @pl.when(reach(me, 1 - way, k)[0])
             def _():
-                part(way, k, 1).wait_send()
-
+                for kind in range(3):
+                    part(way, k, kind).wait_send()
+
+        each(k, lambda way, k, z: arrival(down.at[z], part_recv.at[way, k, 2]))
     for step in range(1, count):
         give_gain(step).wait()
     tokens.wait()
@@ -313,38 +347,50 @@
         pair(z).wait()
     for job in planes:
         job.finish()
-    for copy in local:
+    for copy in local[8:] + [keep_a, keep_down, keep_dm, keep_gu]:
         copy.wait()
-    own_w[1].wait()
 
 
 ANY = pl.BlockSpec(memory_space=pl.ANY)
+VMEM = pl.BlockSpec(memory_space=pltpu.VMEM)
+SMEM = pl.BlockSpec(memory_space=pltpu.SMEM)
 DMA = pltpu.SemaphoreType.DMA
 
 
-def gather_all(count, attn, mlp, gains, tokens, dm):
-    rows, width = attn.shape
+def gather_all(count, lengths, seq, weights, gains, tokens, cotangent):
+    w_query, key_weight, _, w_out, w_gate, _, w_down = weights
+    rows, q_width = w_query.shape
+    width = 2 * (q_width + key_weight.shape[1])
+    units = w_gate.shape[1] // LINE
     kinds = max(6, count // LINE - 1)
     return pl.pallas_call(
         functools.partial(gather_kernel, count),
         name="gather_all",
         out_shape=(
             jax.ShapeDtypeStruct((count, rows, width), BF16),
-            jax.ShapeDtypeStruct((count - count // LINE, rows, width), BF16),
-            jax.ShapeDtypeStruct((rows, width), BF16),
+            jax.ShapeDtypeStruct((count, rows, 2 * units), BF16),
+            jax.ShapeDtypeStruct((LINE, rows, units), BF16),
             jax.ShapeDtypeStruct((count,) + gains.shape, gains.dtype),
             jax.ShapeDtypeStruct((2,) + tokens.shape, BF16),
-            jax.ShapeDtypeStruct((LINE, 2) + dm.shape, BF16),
+            jax.ShapeDtypeStruct((LINE, 2) + cotangent.shape, BF16),
         ),
-        in_specs=[ANY] * 5,
+        in_specs=[SMEM] * 2 + [ANY] * 10,
         out_specs=(ANY,) * 6,
         scratch_shapes=[
-            DMA((2, 2, LINE)), DMA((2, 2, LINE)), DMA((2, LINE)), DMA((2, LINE)),
+            pltpu.VMEM(w_out.shape, BF16),
+            pltpu.VMEM((rows, width), BF16),
+            pltpu.VMEM((rows, 2 * units), BF16),
+            pltpu.VMEM(w_down.shape, BF16),
+            pltpu.VMEM((LINE, rows, units), BF16),
+            pltpu.VMEM(cotangent.shape, BF16),
+            DMA((2, 2, LINE)), DMA((2, 2, LINE)), DMA((2, LINE, 3)), DMA((2, LINE, 3)),
             DMA((2, LINE, kinds)), DMA((2, LINE, kinds)), DMA((count,)), DMA((count,)),
-            DMA((LINE + 1,)), DMA((LINE + 1,)), DMA((5,)),
+            DMA((LINE + 1,)), DMA((LINE + 1,)), DMA((14,)),
         ],
-        compiler_params=pltpu.CompilerParams(collective_id=0, has_side_effects=True),
-    )(attn, mlp, gains, tokens, dm)
+        compiler_params=pltpu.CompilerParams(
+            collective_id=0, has_side_effects=True, vmem_limit_bytes=60 * MB
+        ),
+    )(lengths, seq, *weights, gains, tokens, cotangent)
 
 
 RANKS = ((3, 2, 1, 0), (3, 0, 2, 1), (0, 3, 1, 2), (0, 1, 2, 3))
@@ -408,12 +454,15 @@
             self.other_sem.at[s, i],
         )
 
+    def load_rank(self, rank):
+        self.load(rank).start()
+        if self.square:
+            for i in range(2):
+                self.load_other(rank, i).start()
+
     def load_all(self):
         for rank in self.ranks:
-            self.load(rank).start()
-            if self.square:
-                for i in range(2):
-                    self.load_other(rank, i).start()
+            self.load_rank(rank)
 
     def give(self, rank, i, which):
         me, s = self.me, self.slot(rank)
@@ -502,26 +551,30 @@
 
 
 def feed_forward_kernel(
-    plane, h_ref, dm_ref, w_ref, w_late, total_ref, out_ref, grad_ref, sum_ref, rows_in, weights, inner, part,
+    plane, h_ref, dm_ref, gu_ref, down, down_ref, total_ref, out_ref, grad_ref, sum_ref, rows_in, weights, inner, part,
     from_pair, from_line, own, other, first, second, first_send, first_recv, second_send, second_recv,
     own_sem, other_sem, chain_send, chain_recv, pass_send, pass_recv, pair_send, pair_recv,
-    line_send, line_recv, load_sem, dm_sem, grad_sem, out_sem,
+    line_send, line_recv, plane_send, plane_recv, load_sem, dm_sem, grad_sem, out_sem,
 ):
     me = Place(plane)
     rows, model = h_ref.shape
     units = inner.shape[1]
     wide = 2 * rows
     tokens = LINE * wide
-    most, block, _ = w_ref.shape
+    most, block, _ = down_ref.shape
     tile = 512
 
     def slot(z, t):
         return rows_in.at[pl.ds(pl.multiple_of((z * 2 + t) * rows, rows), rows)]
 
     loads = [
-        pltpu.make_async_copy(w_ref, weights.at[pl.ds(0, most)], load_sem.at[0]),
-        pltpu.make_async_copy(w_late, weights.at[pl.ds(most, plane)], load_sem.at[2]),
+        copy_in(gu_ref, weights.at[:, :, pl.ds(0, 2 * units)], load_sem.at[0]),
+        copy_in(down_ref, weights.at[pl.ds(0, most), :, pl.ds(2 * units, units)], load_sem.at[2]),
     ]
+    late = range(LINE - LATE, LINE)
+    for z in late:
+        own_down = weights.at[z * plane + me.p, :, pl.ds(2 * units, units)]
+        loads.append(copy_in(down.at[z], own_down, load_sem.at[3 + z]))
     for load in loads:
         load.start()
     load_dm = pltpu.make_async_copy(dm_ref, rows_in.at[pl.ds(tokens, tokens)], dm_sem)
@@ -529,9 +582,14 @@
     keep = pltpu.make_async_copy(h_ref, slot(me.z, me.t), load_sem.at[1])
     keep.start()
     greet_all(me, plane * LINE)
+    gather = PlaneGather(
+        me, 0, weights.at[:, :, pl.ds(2 * units, units)], block, plane_send, plane_recv
+    )
+    for z in late:
+        gather.start(z, down.at[z])
     summed = PlaneSum(
         me, weights, own, other, first, second,
-        (first_send, first_recv, second_send, second_recv, own_sem, other_sem), range(1),
+        (first_send, first_recv, second_send, second_recv, own_sem, other_sem), range(EARLY),
     )
     chain = Chain(me, h_ref, lambda z: slot(z, me.t), chain_send, chain_recv)
 
@@ -669,6 +727,9 @@
     for load in loads:
         load.wait()
     load_dm.wait()
+    for z in late:
+        gather.forward(z)
+    gather.finish(late)
     for k in range(LINE):
         for way in range(2 if k else 1):
             have, z = reach(me, way, k)
@@ -693,11 +754,14 @@
 
     for i in range(LINE):
         grads(ranked(me, i))
+        if i < EARLY:
+            summed.load_rank(i)
         if i == 0:
-            summed.load_all()
             summed.begin(0)
         if i == 1:
             summed.middle(0)
+            if EARLY > 1:
+                summed.begin(1)
         if i < len(order):
             for way in range(2):
                 line(way, order[i][1], order[i][0])
@@ -705,13 +769,20 @@
         pair(1, z).wait_recv()
         add_rows(part.at[1, z, me.t], (part.at[1, z, me.t], from_pair.at[1, z]), rows)
         keep_out(z).start()
+    keep_sums = [
+        pltpu.make_async_copy(own.at[rank], sum_ref.at[rank], load_sem.at[rank]) for rank in range(EARLY)
+    ]
     summed.end(0)
-    keep_sum = pltpu.make_async_copy(own.at[0], sum_ref, load_sem.at[0])
-    keep_sum.start()
+    keep_sums[0].start()
+    if EARLY > 1:
+        summed.middle(1)
     total()
-
+    if EARLY > 1:
+        summed.end(1)
+        keep_sums[1].start()
     summed.finish()
-    keep_sum.wait()
+    for copy in keep_sums:
+        copy.wait()
     chain.finish()
     for z in range(LINE):
         share(z).wait_send()
@@ -728,11 +799,12 @@
                     pass_on(way, k, i).wait_send()
 
 
-def feed_forward(count, h, dm_all, w_all, w_late):
+def feed_forward(count, h, dm_all, gu_all, down, down_all):
     rows, model = h.shape
-    units = w_all.shape[2] // 3
-    grads = (count,) + w_all.shape[1:]
-    buffers, sems = PlaneSum.scratch(count, *w_late.shape[1:], 1)
+    _, block, units = down.shape
+    kinds = max(6, count // LINE - 1)
+    grads = (count, block, 3 * units)
+    buffers, sems = PlaneSum.scratch(count, *grads[1:], EARLY)
     tokens = LINE * 2 * rows
     vmem = pl.BlockSpec(memory_space=pltpu.VMEM)
     return pl.pallas_call(
@@ -742,9 +814,9 @@
             jax.ShapeDtypeStruct((rows, model), F32),
             jax.ShapeDtypeStruct((LINE, rows, model), BF16),
             jax.ShapeDtypeStruct(grads, BF16),
-            jax.ShapeDtypeStruct(w_late.shape[1:], BF16),
+            jax.ShapeDtypeStruct((EARLY,) + grads[1:], BF16),
         ),
-        in_specs=[vmem, ANY, ANY, ANY],
+        in_specs=[ANY] * 5,
         out_specs=(vmem, ANY, ANY, ANY),
         scratch_shapes=[
             pltpu.VMEM((2 * tokens, model), BF16),
@@ -756,12 +828,12 @@
             *buffers,
             *sems,
             DMA((2, LINE)), DMA((2, LINE)), DMA((LINE,)), DMA((LINE,)), DMA((2, LINE)), DMA((2, LINE)),
-            DMA((2, LINE, 2)), DMA((2, LINE, 2)), DMA((3,)), DMA, DMA((LINE,)), DMA((LINE,)),
+            DMA((2, LINE, 2)), DMA((2, LINE, 2)), DMA((1, LINE, kinds)), DMA((1, LINE, kinds)), DMA((3 + LINE,)), DMA, DMA((LINE,)), DMA((LINE,)),
         ],
         compiler_params=pltpu.CompilerParams(
             collective_id=1, has_side_effects=True, vmem_limit_bytes=60 * MB
         ),
-    )(h, dm_all, w_all, w_late)
+    )(h, dm_all, gu_all, down, down_all)
 
 
 def greet_plane(me):
@@ -773,12 +845,6 @@
     pl.semaphore_wait(barrier, me.plane)
 
 
-def row_loop(rows, step, act):
-    @pl.loop(0, rows // step)
-    def _(i):
-        act(pl.ds(pl.multiple_of(i * step, step), step))
-
-
 def columns_of(weights, start, width):
     count, rows, _ = weights.shape
     return weights[:, :, pl.ds(start, width)].reshape(count * rows, width)
@@ -791,9 +857,9 @@
 
 
 def attention_forward_kernel(
-    plane, tok_ref, gain_ref, cos_ref, sin_ref, mask_ref, a_ref, w_last, x1_ref, h2_ref, h1_ref,
-    qkv_ref, probs_ref, o_ref, w_late, weights, part, from_pair, plane_send, plane_recv, pair_send,
-    pair_recv, load_sem,
+    plane, len_ref, seq_ref, gain_ref, cos_ref, sin_ref, tok_in, a_ref, down, x1_out, h2_out, h1_out,
+    qkv_out, probs_out, o_out, down_all, weights, tok_ref, x1_ref, h2_ref, h1_ref, qkv_ref, probs_ref,
+    o_ref, part, from_pair, plane_send, plane_recv, pair_send, pair_recv, load_sem, keep_sem,
 ):
     me = Place(plane)
     _, rows, model = tok_ref.shape
@@ -803,13 +869,29 @@
     kv_width = (qkv_ref.shape[1] - q_width) // 2
     kv_heads = kv_width // HEAD_SIZE
     half = HEAD_SIZE // 2
-    load = pltpu.make_async_copy(a_ref, weights, load_sem.at[0])
+    load_tok = copy_in(tok_in, tok_ref, load_sem.at[0])
+    load_tok.start()
+    load = copy_in(a_ref, weights, load_sem.at[1])
     load.start()
-    keep = pltpu.make_async_copy(w_last, w_late.at[me.p], load_sem.at[1])
-    keep.start()
+    keep = [
+        copy_in(down.at[z], down_all.at[z * plane + me.p], load_sem.at[2 + z]) for z in range(LINE - LATE)
+    ]
+    for copy in keep:
+        copy.start()
+    outs = [
+        copy_in(src, dst, keep_sem.at[i])
+        for i, (src, dst) in enumerate(
+            (
+                (h1_ref, h1_out), (qkv_ref, qkv_out), (probs_ref, probs_out), (o_ref, o_out),
+                (x1_ref, x1_out), (h2_ref, h2_out),
+            )
+        )
+    ]
     greet_plane(me)
-    gather = PlaneGather(me, 0, w_late, w_last.shape[0], plane_send, plane_recv)
-    gather.start(0, w_last)
+    gather = PlaneGather(me, 0, down_all, down.shape[1], plane_send, plane_recv)
+    for z in range(LINE - LATE):
+        gather.start(z, down.at[z])
+    load_tok.wait()
 
     for t in range(2):
 
@@ -819,6 +901,7 @@
             h1_ref[pl.ds(t * rows + at.start, at.size), :] = (x * factor * gain_ref[0:1, :]).astype(BF16)
 
         row_loop(rows, 32, norm)
+    outs[0].start()
     load.wait()
 
     def project(i):
@@ -840,14 +923,18 @@
         start, values = project(i)
         qkv_ref[:, pl.ds(start, HEAD_SIZE)] = values.astype(BF16)
 
+    outs[1].start()
     gather.forward(0)
+    row = lax.broadcasted_iota(jnp.int32, (wide, wide), 0)
+    key = lax.broadcasted_iota(jnp.int32, (wide, wide), 1)
+    allowed = jnp.logical_and(key <= row, key < len_ref[seq_ref[0]])
     for i in range(heads):
         m = i * kv_heads // heads
         q = qkv_ref[:, i * HEAD_SIZE : (i + 1) * HEAD_SIZE]
         k = qkv_ref[:, q_width + m * HEAD_SIZE : q_width + (m + 1) * HEAD_SIZE]
         v = qkv_ref[:, q_width + kv_width + m * HEAD_SIZE : q_width + kv_width + (m + 1) * HEAD_SIZE]
         scores = dot_cols(q, k) * HEAD_SIZE ** (-0.5)
-        scores = jnp.where(mask_ref[...] > 0, scores, -1e30)
+        scores = jnp.where(allowed, scores, -1e30)
         grown = jnp.exp(scores - jnp.max(scores, -1, keepdims=True))
         probs = grown / jnp.sum(grown, -1, keepdims=True)
         probs_ref[i] = probs
@@ -855,6 +942,9 @@
             probs.astype(BF16), v, preferred_element_type=F32
         ).astype(BF16)
 
+    outs[2].start()
+    outs[3].start()
+    gather.forward(1)
     tile = 512
 
     @pl.loop(0, model // tile)
@@ -865,6 +955,8 @@
 
     swap = remote(part.at[1 - me.t], from_pair, pair_send, pair_recv, me.sibling())
     swap.start()
+    for z in range(2, LINE - LATE):
+        gather.forward(z)
     swap.wait_recv()
 
     def add(at):
@@ -874,52 +966,54 @@
         h2_ref[at, :] = (x1 * factor * gain_ref[1:2, :]).astype(BF16)
 
     row_loop(rows, 32, add)
+    outs[4].start()
+    outs[5].start()
     swap.wait_send()
-    gather.finish(range(1))
-    keep.wait()
-
-
-VMEM = pl.BlockSpec(memory_space=pltpu.VMEM)
-
-
-def attention_forward(count, heads, tokens_all, gains, cos, sin, mask, attn_all, w_last):
+    gather.finish(range(LINE - LATE))
+    for copy in keep + outs:
+        copy.wait()
+
+
+def attention_forward(count, heads, lengths, seq, gains, cos, sin, tokens_all, attn_all, down):
     _, rows, model = tokens_all.shape
     wide = 2 * rows
     q_width = heads * HEAD_SIZE
     qkv_width = attn_all.shape[2] - q_width
     plane = count // LINE
     kinds = max(6, plane - 1)
+    outs = (
+        jax.ShapeDtypeStruct((rows, model), F32),
+        jax.ShapeDtypeStruct((rows, model), BF16),
+        jax.ShapeDtypeStruct((wide, model), BF16),
+        jax.ShapeDtypeStruct((wide, qkv_width), BF16),
+        jax.ShapeDtypeStruct((heads, wide, wide), F32),
+        jax.ShapeDtypeStruct((wide, q_width), BF16),
+    )
     return pl.pallas_call(
         functools.partial(attention_forward_kernel, plane),
         name="attention_forward",
-        out_shape=(
-            jax.ShapeDtypeStruct((rows, model), F32),
-            jax.ShapeDtypeStruct((rows, model), BF16),
-            jax.ShapeDtypeStruct((wide, model), BF16),
-            jax.ShapeDtypeStruct((wide, qkv_width), BF16),
-            jax.ShapeDtypeStruct((heads, wide, wide), F32),
-            jax.ShapeDtypeStruct((wide, q_width), BF16),
-            jax.ShapeDtypeStruct((plane,) + w_last.shape, BF16),
-        ),
-        in_specs=[VMEM] * 5 + [ANY] * 2,
-        out_specs=(VMEM,) * 6 + (ANY,),
+        out_shape=outs + (jax.ShapeDtypeStruct((count - LATE * plane,) + down.shape[1:], BF16),),
+        in_specs=[SMEM] * 2 + [VMEM] * 3 + [ANY] * 3,
+        out_specs=(ANY,) * 7,
         scratch_shapes=[
             pltpu.VMEM(attn_all.shape, BF16),
+            pltpu.VMEM(tokens_all.shape, BF16),
+            *[pltpu.VMEM(out.shape, out.dtype) for out in outs],
             pltpu.VMEM((2, rows, model), F32),
             pltpu.VMEM((rows, model), F32),
-            DMA((1, 1, kinds)), DMA((1, 1, kinds)), DMA, DMA, DMA((2,)),
+            DMA((1, LINE, kinds)), DMA((1, LINE, kinds)), DMA, DMA, DMA((2 + LINE,)), DMA((6,)),
         ],
         compiler_params=pltpu.CompilerParams(
-            collective_id=2, has_side_effects=True, vmem_limit_bytes=48 * MB
+            collective_id=2, has_side_effects=True, vmem_limit_bytes=60 * MB
         ),
-    )(tokens_all, gains, cos, sin, mask, attn_all, w_last)
+    )(lengths, seq, gains, cos, sin, tokens_all, attn_all, down)
 
 
 def attention_backward_kernel(
-    plane, total_ref, x1_ref, dm_ref, tok_ref, gain_ref, cos_ref, sin_ref, h1_ref, qkv_ref, probs_ref,
-    o_ref, a_ref, gw_ref, sum_ref, ga_ref, w_out, grad_tokens, gain_parts, weights, own, other, first, second,
-    dx, da, do, dqkv, dh1, from_pair, first_send, first_recv, second_send, second_recv, load_sem,
-    other_sem, part_send, part_recv, pair_send, pair_recv, a_sem, keep_sem, grad_sem,
+    plane, gain_ref, cos_ref, sin_ref, total_in, x1_in, dm_in, tok_in, h1_in, qkv_in, probs_in, o_in,
+    a_ref, gw_ref, sum_ref, ga_ref, w_out, grad_tokens, gain_parts, weights, own, other, first, second,
+    total_ref, x1_ref, dm_ref, tok_ref, h1_ref, qkv_ref, probs_ref, o_ref, dx, da, do, dqkv, dh1, from_pair, first_send, first_recv, second_send, second_recv, load_sem,
+    other_sem, part_send, part_recv, pair_send, pair_recv, a_sem, keep_sem, grad_sem, in_sem,
 ):
     me = Place(plane)
     _, rows, model = tok_ref.shape
@@ -933,17 +1027,30 @@
     scale = HEAD_SIZE ** (-0.5)
     summed = PlaneSum(
         me, gw_ref, own, other, first, second,
-        (first_send, first_recv, second_send, second_recv, load_sem, other_sem), range(1, LINE),
+        (first_send, first_recv, second_send, second_recv, load_sem, other_sem), range(EARLY, LINE),
     )
+    ins = [
+        copy_in(src, dst, in_sem.at[i])
+        for i, (src, dst) in enumerate(
+            (
+                (total_in, total_ref), (x1_in, x1_ref), (dm_in.at[me.z, me.t], dm_ref), (tok_in, tok_ref),
+                (h1_in, h1_ref), (qkv_in, qkv_ref), (probs_in, probs_ref), (o_in, o_ref),
+            )
+        )
+    ]
+    for copy in ins[:3]:
+        copy.start()
     load = pltpu.make_async_copy(a_ref, weights, a_sem)
     load.start()
+    for copy in ins[3:]:
+        copy.start()
     summed.load_all()
     greet_all(me, plane * LINE)
 
     def part(rank):
         target = ranked(me, rank)
         way, k = way_to(me, target)
-        src = own.at[summed.slot(rank)] if rank else sum_ref
+        src = own.at[summed.slot(rank)] if rank >= EARLY else sum_ref.at[rank]
         return remote(
             src, w_out.at[me.z], part_send.at[way, k], part_recv.at[way, k], me.at(target, me.p)
         )
@@ -1064,12 +1171,19 @@
 
         row_loop(rows, 32, act)
 
-    summed.begin(1)
-    part(0).start()
+    summed.begin(EARLY)
+    for rank in range(EARLY):
+        part(rank).start()
+    for copy in ins[:3]:
+        copy.wait()
     mid_norm()
     grad_o()
-    stages = [[], [grad_heads, grad_h1], [grads], [in_norm]]
-    for rank in range(1, LINE):
+    for copy in ins[3:]:
+        copy.wait()
+    stages = {LINE - 2: [grad_heads, grad_h1], LINE - 1: [grads, in_norm]}
+    if EARLY < LINE - 2:
+        stages = {1: [grad_heads, grad_h1], 2: [grads], 3: [in_norm]}
+    for rank in range(EARLY, LINE):
         summed.middle(rank)
         if rank + 1 < LINE:
             summed.begin(rank + 1)
@@ -1079,7 +1193,7 @@
         if rank < LINE - 1:
             part(rank).start()
 
-    keep = pltpu.make_async_copy(own.at[LINE - 2], w_out.at[me.z], keep_sem)
+    keep = pltpu.make_async_copy(own.at[LINE - 1 - EARLY], w_out.at[me.z], keep_sem)
     keep.start()
     for rank in range(LINE - 1):
         part(rank).wait_send()
@@ -1098,14 +1212,14 @@
 
 
 def attention_backward(
-    count, total, x1, dm, tokens_all, gains, cos, sin, h1, qkv, probs, o, attn_all, grad_mlp, first_sum
+    count, gains, cos, sin, total, x1, dm_all, tokens_all, h1, qkv, probs, o, attn_all, grad_mlp, first_sum
 ):
     _, rows, model = tokens_all.shape
     _, block, width = attn_all.shape
     wide = 2 * rows
     heads = probs.shape[0]
     q_width = heads * HEAD_SIZE
-    buffers, sems = PlaneSum.scratch(count, block, width, LINE - 1)
+    buffers, sems = PlaneSum.scratch(count, block, width, LINE - EARLY)
     return pl.pallas_call(
         functools.partial(attention_backward_kernel, count // LINE),
         name="attention_backward",
@@ -1115,11 +1229,15 @@
             jax.ShapeDtypeStruct((rows, model), F32),
             jax.ShapeDtypeStruct((2, model), F32),
         ),
-        in_specs=[VMEM] * 11 + [ANY] * 3,
+        in_specs=[VMEM] * 3 + [ANY] * 11,
         out_specs=(ANY, ANY, VMEM, VMEM),
         scratch_shapes=[
             pltpu.VMEM(attn_all.shape, BF16),
             *buffers,
+            *[
+                pltpu.VMEM(ref.shape, ref.dtype)
+                for ref in (total, x1, dm_all[0, 0], tokens_all, h1, qkv, probs, o)
+            ],
             pltpu.VMEM((rows, model), F32),
             pltpu.VMEM((2, rows, model), BF16),
             pltpu.VMEM((wide, q_width), BF16),
@@ -1127,18 +1245,18 @@
             pltpu.VMEM((2, rows, model), F32),
             pltpu.VMEM((rows, model), F32),
             *sems,
-            DMA((2, LINE)), DMA((2, LINE)), DMA((2,)), DMA((2,)), DMA, DMA, DMA((model // 512,)),
+            DMA((2, LINE)), DMA((2, LINE)), DMA((2,)), DMA((2,)), DMA, DMA, DMA((model // 512,)), DMA((8,)),
         ],
         compiler_params=pltpu.CompilerParams(
             collective_id=3, has_side_effects=True, vmem_limit_bytes=60 * MB
         ),
-    )(total, x1, dm, tokens_all, gains, cos, sin, h1, qkv, probs, o, attn_all, grad_mlp, first_sum)
+    )(gains, cos, sin, total, x1, dm_all, tokens_all, h1, qkv, probs, o, attn_all, grad_mlp, first_sum)
 
 
 def grad_sum_kernel(
-    count, x1_ref, ga_ref, out_ref, gain_ref, a_out, output, gain_out, own, other, first, second,
-    from_line, out_own, out_line, gain_in, gain_pair, first_send, first_recv, second_send, second_recv,
-    load_sem, other_sem, line_send, line_recv, out_send, out_recv, out_sem, gain_send, gain_recv,
+    count, gain_ref, x1_in, ga_ref, out_ref, mlp_ref, q_out, k_out, v_out, o_out, gate_out, up_out,
+    down_out, output, gain_out, own, other, first, second, a_out, x1_ref, mlp, from_line, out_own, out_line, gain_in, gain_pair, first_send, first_recv, second_send, second_recv,
+    load_sem, other_sem, line_send, line_recv, out_send, out_recv, load_out_sem, gain_send, gain_recv,
 ):
     plane = count // LINE
     me = Place(plane)
@@ -1187,8 +1305,12 @@
     grads = Line(lambda rank: own.at[rank], from_line, line_send, line_recv)
     outs = Line(lambda rank: out_own.at[ranked(me, rank)], out_line, out_send, out_recv)
     summed.load_all()
-    load_out = pltpu.make_async_copy(out_ref, out_own, out_sem)
+    load_out = copy_in(out_ref, out_own, load_out_sem.at[0])
     load_out.start()
+    load_x1 = copy_in(x1_in, x1_ref, load_out_sem.at[1])
+    load_x1.start()
+    load_mlp = copy_in(mlp_ref, mlp, load_out_sem.at[2])
+    load_mlp.start()
     greet_all(me, count)
 
     def give_gain(step):
@@ -1207,77 +1329,116 @@
         def _():
             outs.step(rank)
 
+    at_end = jnp.logical_or(me.z == 0, me.z == LINE - 1)
+
+    def out_start(at):
+        x1_ref[at, :] = x1_ref[at, :] + out_own[me.z, at, :].astype(F32)
+
+    def add_out(landed):
+        def act(at):
+            x1_ref[at, :] = x1_ref[at, :] + landed[at, :].astype(F32)
+
+        row_loop(output.shape[0], 16, act)
+
+    def out_end(at):
+        output[at, :] = x1_ref[at, :].astype(BF16)
+
+    units = mlp.shape[2] // 3
+
+    def feed_forward_grads(z):
+        here = slice(z * units, (z + 1) * units)
+        gate_out[:, here] = mlp[z, :, :units].astype(F32)
+        up_out[:, here] = mlp[z, :, units : 2 * units].astype(F32)
+        down_out[here, :] = mlp[z, :, 2 * units :].astype(F32).T
+
     for rank in range(LINE):
         summed.middle(rank)
         if rank + 1 < LINE:
             summed.begin(rank + 1)
+            if rank == 0:
+                load_mlp.wait()
+        else:
+            load_x1.wait()
+            row_loop(output.shape[0], 16, out_start)
+            outs.total(add_out)
+            row_loop(output.shape[0], 16, out_end)
+            total = gain_ref[me.d]
+            for step in range(1, count):
+                give_gain(step).wait()
+                total += gain_in[step]
+            gain_pair[0] = total
+            swap = remote(
+                gain_pair.at[0], gain_pair.at[1], gain_send.at[0], gain_recv.at[0], me.sibling()
+            )
+            swap.start()
+            swap.wait()
+            gain_out[...] = gain_pair[0] + gain_pair[1]
+        feed_forward_grads(rank)
+        summed.end(rank)
         if rank < LINE - 1:
 
-            @pl.when(jnp.logical_and(me.z > 0, me.z < LINE - 1))
+            @pl.when(at_end)
             def _():
-                outs.step(rank)
-
-        summed.end(rank)
-        if rank:
-            grads.step(rank - 1)
-
-    def add_out(landed):
-        def act(at):
-            output[at, :] = output[at, :] + landed[at, :].astype(F32)
-
-        row_loop(output.shape[0], 16, act)
-
-    def out_start(at):
-        output[at, :] = x1_ref[at, :] + out_own[me.z, at, :].astype(F32)
-
-    row_loop(output.shape[0], 16, out_start)
-    outs.total(add_out)
+                grads.step(rank)
+
+        if 0 < rank < LINE - 1:
+            @pl.when(jnp.logical_not(at_end))
+            def _():
+                for late in (range(rank - 1, rank) if rank < LINE - 2 else range(rank - 1, LINE - 1)):
+                    outs.step(late)
+                    grads.step(late)
+
     add_rows(a_out, (own.at[LINE - 1],), rows)
     grads.total(lambda landed: add_rows(a_out, (a_out, landed), rows))
-
-    total = gain_ref[me.d]
-    for step in range(1, count):
-        give_gain(step).wait()
-        total += gain_in[step]
-    gain_pair[0] = total
-    swap = remote(gain_pair.at[0], gain_pair.at[1], gain_send.at[0], gain_recv.at[0], me.sibling())
-    swap.start()
-    swap.wait()
-    gain_out[...] = gain_pair[0] + gain_pair[1]
+    start = 0
+    for ref in (q_out, k_out, v_out):
+        ref[...] = a_out[:, start : start + ref.shape[1]]
+        start += ref.shape[1]
+    o_out[...] = a_out[:, start:].T
     outs.finish()
     grads.finish()
     summed.finish()
 
 
-def grad_sum(count, x1, ga, out_parts, gains):
+def grad_sum(count, q_width, kv_width, x1, ga, out_parts, mlp, gains):
     _, block, width = ga.shape
     _, rows, model = out_parts.shape
+    hidden = LINE * (mlp.shape[2] // 3)
     buffers, sems = PlaneSum.scratch(count, block, width)
     return pl.pallas_call(
         functools.partial(grad_sum_kernel, count),
         name="grad_sum",
         out_shape=(
-            jax.ShapeDtypeStruct((block, width), F32),
-            jax.ShapeDtypeStruct((rows, model), F32),
+            jax.ShapeDtypeStruct((block, q_width), F32),
+            jax.ShapeDtypeStruct((block, kv_width), F32),
+            jax.ShapeDtypeStruct((block, kv_width), F32),
+            jax.ShapeDtypeStruct((q_width, block), F32),
+            jax.ShapeDtypeStruct((block, hidden), F32),
+            jax.ShapeDtypeStruct((block, hidden), F32),
+            jax.ShapeDtypeStruct((hidden, block), F32),
+            jax.ShapeDtypeStruct((rows, model), BF16),
             jax.ShapeDtypeStruct(gains.shape[1:], F32),
         ),
-        in_specs=[VMEM, ANY, ANY, VMEM],
-        out_specs=(VMEM,) * 3,
+        in_specs=[VMEM] + [ANY] * 4,
+        out_specs=(VMEM,) * 9,
         scratch_shapes=[
             *buffers,
+            pltpu.VMEM((block, width), F32),
+            pltpu.VMEM((rows, model), F32),
+            pltpu.VMEM(mlp.shape, BF16),
             pltpu.VMEM((2, LINE - 1, block, width), BF16),
             pltpu.VMEM(out_parts.shape, BF16),
             pltpu.VMEM((2, LINE - 1, rows, model), BF16),
             pltpu.VMEM(gains.shape, F32),
             pltpu.VMEM((2,) + gains.shape[1:], F32),
             *sems,
-            DMA((2, LINE)), DMA((2, LINE)), DMA((2, LINE)), DMA((2, LINE)), DMA,
+            DMA((2, LINE)), DMA((2, LINE)), DMA((2, LINE)), DMA((2, LINE)), DMA((3,)),
             DMA((count,)), DMA((count,)),
         ],
         compiler_params=pltpu.CompilerParams(
-            collective_id=4, has_side_effects=True, vmem_limit_bytes=48 * MB
+            collective_id=4, has_side_effects=True, vmem_limit_bytes=60 * MB
         ),
-    )(x1, ga, out_parts, gains)
+    )(gains, x1, ga, out_parts, mlp)
 
 
 def shards(
@@ -1285,67 +1446,36 @@
     cotangent, lengths, seq_of_group,
 ):
     count = lax.axis_size("dp")
-    local_rows = tokens.shape[0]
-    full_rows = local_rows * lax.axis_size("tensor")
-    rows = w_query.shape[0]
+    rows, q_width = w_query.shape
+    kv_width = key_weight.shape[1]
     model = rows * count
-    q_width = w_query.shape[1]
-    kv_width = key_weight.shape[1]
-    units = w_gate.shape[1] // LINE
-    chosen = jnp.sum(
-        jnp.where(jnp.arange(lengths.shape[0], dtype=jnp.int32) == seq_of_group[0], lengths, 0)
-    )
-    positions = lax.axis_index("tensor") * local_rows + jnp.arange(local_rows, dtype=jnp.int32)
-    row_ids = jnp.arange(full_rows, dtype=jnp.int32)
-    key_allowed = (row_ids[None, :] <= row_ids[:, None]) & (row_ids[None, :] < chosen)
-    cos, sin = (table[:, 0, :] for table in rope_tables(full_rows, HEAD_SIZE))
-    dm = jnp.where((positions < chosen)[:, None], cotangent, jnp.zeros_like(cotangent))
-
-    attn_pack = jnp.concatenate([w_query, key_weight, value_weight, w_out.T], axis=1)
-    down_t = w_down.T
-    mlp_pack = jnp.stack(
-        [
-            jnp.concatenate([m[:, z * units : (z + 1) * units] for m in (w_gate, w_up, down_t)], axis=1)
-            for z in range(LINE)
-        ]
-    )
+    cos, sin = rope_tables(tokens.shape[0] * lax.axis_size("tensor"), HEAD_SIZE)
     lanes = -rows % 128
     gains = jnp.pad(jnp.stack([gain_attn, gain_mlp]), ((0, 14), (0, lanes)))
-    attn_all, mlp_all, mlp_last, gains_all, tokens_all, dm_all = gather_all(
-        count, attn_pack, mlp_pack, gains, tokens, dm
+    attn_all, gate_up_all, down, gains_all, tokens_all, dm_all = gather_all(
+        count, lengths, seq_of_group,
+        (w_query, key_weight, value_weight, w_out, w_gate, w_up, w_down), gains, tokens, cotangent,
     )
     gains_full = gains_all[:, :2, :rows].transpose(1, 0, 2).reshape(2, model).astype(F32)
-    x1, h2, h1, qkv, probs, attended, mlp_late = attention_forward(
-        count, q_width // HEAD_SIZE, tokens_all, gains_full, cos, sin, key_allowed.astype(F32),
-        attn_all, mlp_last,
+    x1, h2, h1, qkv, probs, attended, down_all = attention_forward(
+        count, q_width // HEAD_SIZE, lengths, seq_of_group, gains_full, cos, sin, tokens_all, attn_all,
+        down,
     )
     grad_h2, out_parts, grad_mlp_w, first_sum = feed_forward(
-        count, h2, dm_all.reshape(-1, model), mlp_all, mlp_late
+        count, h2, dm_all.reshape(-1, model), gate_up_all, down, down_all
     )
     grad_attn_w, mlp_sum, grad_tokens, gain_parts = attention_backward(
-        count, grad_h2, x1, dm, tokens_all, gains_full, cos, sin, h1, qkv, probs, attended, attn_all,
+        count, gains_full, cos, sin, grad_h2, x1, dm_all, tokens_all, h1, qkv, probs, attended, attn_all,
         grad_mlp_w, first_sum,
     )
     gain_parts = gain_parts.reshape(2, count, rows).transpose(1, 0, 2)
     gain_parts = jnp.pad(gain_parts, ((0, 0), (0, 6), (0, lanes)))
-    attn_sum, output, gain_sum = grad_sum(count, x1, grad_attn_w, out_parts, gain_parts)
-    mlp_sum = mlp_sum.astype(F32)
-    grad_gate_w, grad_up_w, grad_down_t = (
-        jnp.concatenate([mlp_sum[z, :, i * units : (i + 1) * units] for z in range(LINE)], axis=1)
-        for i in range(3)
-    )
+    (
+        grad_query, grad_key, grad_value, grad_out, grad_gate, grad_up, grad_down, output, gain_sum,
+    ) = grad_sum(count, q_width, kv_width, x1, grad_attn_w, out_parts, mlp_sum, gain_parts)
     return (
-        output.astype(BF16),
-        grad_tokens,
-        attn_sum[:, :q_width],
-        attn_sum[:, q_width : q_width + kv_width],
-        attn_sum[:, q_width + kv_width : q_width + 2 * kv_width],
-        attn_sum[:, q_width + 2 * kv_width :].T,
-        gain_sum[0, :rows],
-        grad_gate_w,
-        grad_up_w,
-        grad_down_t.T,
-        gain_sum[1, :rows],
+        output, grad_tokens, grad_query, grad_key, grad_value, grad_out, gain_sum[0, :rows],
+        grad_gate, grad_up, grad_down, gain_sum[1, :rows],
     )
 
 

time: 570 us -> 539 us (0.946)
  other arithmetic: 16.5 us -> 3.86 us
  Pallas kernels: 524 us -> 512 us
    pallas_call x1, Pallas kernels: 126 us -> 117 us  [grad_sum(): pl.pallas_call(functools.partial(grad_sum_kernel, count), name='grad_sum'...]
    pallas_call x1, Pallas kernels: 186 us -> 180 us  [gather_all(): pl.pallas_call(functools.partial(gather_kernel, count), name='gather_all'...]
    unnamed x47 -> x25, local copies, waits for them, and re-layouts: 13.7 us -> 11 us
where the time goes in v4:
time: 539 us; the launch traced here: 531 us
  Pallas kernels  512 us (95%)
  local copies, waits for them, and re-layouts  13.7 us (3%)
    pallas_call x1, Pallas kernels, gather_all(): pl.pallas_call(functools.partial(gather_kernel, count), name='gather_all'...  180 us
    pallas_call x1, Pallas kernels, grad_sum(): pl.pallas_call(functools.partial(grad_sum_kernel, count), name='grad_sum'...  117 us
    pallas_call x1, Pallas kernels, feed_forward(): pl.pallas_call(functools.partial(feed_forward_kernel, count // LINE), nam...  97.6 us
    pallas_call x1, Pallas kernels, attention_backward(): pl.pallas_call(functools.partial(attention_backward_kernel, count // LINE...  87.4 us
    pallas_call x1, Pallas kernels, attention_forward(): pl.pallas_call(functools.partial(attention_forward_kernel, plane), name='...  30 us
    unnamed x25, local copies, waits for them, and re-layouts  11 us

profile of v4, /device:TPU:8, one launch (start us, length us, event | category | flops | bytes accessed | tf_op | source)
XLA Modules:
  0.0 531.3 jit_solution(13817787358693458871)
XLA Ops:
  1.3 1.3 fusion.4.gain_ref
  2.6 1.2 fusion
  3.8 179.5 %gather_all.1 = (bf16[16,128,3072]{2,1,0:T(8,128)(2,1)}, bf16[16,128,2048]{2,1,0:T(8,128)(2,1)}, bf16[4,128,1024]{2,1,0:T(8,128)(2,1)}, bf16[16,16,128]{2,1,0:T(...) custom-call(s32[16]{0:T(128)} %len_ref.3, s32[1]{0:T(128)S(6)} %copy.33.seq_ref, ...), custom_call_target="tpu_custom_call" | custom-call | tf_op jit(solution)/shard_map/gather_all/pallas_call | solution.py:366
  183.3 1.4 convert_bitcast_fusion.gain_ref
  184.7 30.0 %attention_forward.1 = (f32[128,2048]{1,0:T(8,128)}, bf16[128,2048]{1,0:T(8,128)(2,1)}, bf16[256,2048]{1,0:T(8,128)(2,1)}, bf16[256,2048]{1,0:T(8,128)(2,1)}, f3...) custom-call(s32[16]{0:T(128)} %len_ref.3, s32[1]{0:T(128)S(6)} %copy.33.seq_ref, ...), custom_call_target="tpu_custom_call" | custom-call | tf_op jit(solution)/shard_map/attention_forward/pallas_call | solution.py:992
  214.7 97.6 %feed_forward.1 = (f32[128,2048]{1,0:T(8,128)}, bf16[4,128,2048]{2,1,0:T(8,128)(2,1)}, bf16[16,128,3072]{2,1,0:T(8,128)(2,1)}, bf16[1,128,3072]{2,1,0:T(8,128)(2,1)}) custom-call(bf16[128,2048]{1,0:T(8,128)(2,1)} %get-tuple-element.45.h_ref, bf16[1024,2048]{1,0:T(8,128)(2,1)} %bitcast.14, bf16[16,128,2048]{2,1,0:T(8,128)(2,1)} %get-tuple-element.47.gu_ref, ...), custom_call_target="tpu_custom_call" | custom-call | tf_op jit(solution)/shard_map/feed_forward/pallas_call | solution.py:810
  312.3 87.4 %attention_backward.1 = (bf16[16,128,3072]{2,1,0:T(8,128)(2,1)}, bf16[4,128,3072]{2,1,0:T(8,128)(2,1)}, f32[128,2048]{1,0:T(8,128)}, f32[2,2048]{1,0:T(2,128)}) custom-call(f32[2,2048]{1,0:T(2,128)} %convert_bitcast_fusion.gain_ref, f32[256,128]{1,0:T(8,128)} %get-tuple-element.74.cos_ref, f32[256,128]{1,0:T(8,128)} %get-tuple-element.73.sin_ref, ...), custom_call_target="tpu_custom_call" | custom-call | tf_op jit(solution)/shard_map/attention_backward/pallas_call | solution.py:1223
  399.7 1.4 pad.9.gain_ref
  401.1 0.0 copy-start.3
  401.1 117.4 %grad_sum.1 = (f32[128,1024]{1,0:T(8,128)}, f32[128,512]{1,0:T(8,128)}, f32[128,512]{1,0:T(8,128)}, f32[1024,128]{1,0:T(8,128)}, f32[128,4096]{1,0:T(8,128)}, /*...) custom-call(f32[16,8,128]{2,1,0:T(8,128)} %pad.9.gain_ref, ...), custom_call_target="tpu_custom_call" | custom-call | tf_op jit(solution)/shard_map/grad_sum/pallas_call | solution.py:1408
  518.5 0.0 copy-start.5
  518.5 0.0 copy-start.7
  518.5 0.0 copy-start.6
  518.5 0.0 copy-start.4
  518.6 1.3 slice_bitcast_fusion
  519.9 0.0 copy-start.2
  519.9 2.0 copy.34
  521.9 0.0 copy-done.3
  521.9 1.0 copy.35
  522.9 0.0 copy-done.5
  522.9 0.8 copy.36
  523.7 0.0 copy-done.7
  523.7 0.0 copy-start.1
  523.7 0.7 copy.37
  524.4 0.0 copy-done.6
  524.4 0.7 copy.38
  525.1 0.0 copy-done.4
  525.1 0.8 copy.39
  525.9 0.0 copy-done.2
  525.9 1.3 copy.40
  527.2 0.0 copy-done.1
  527.2 0.0 copy-start
  527.2 1.3 copy.41
  528.5 1.0 copy-done
  529.5 1.3 copy.42
  (1 shorter events, 0.0 us)
Async XLA Ops:
  401.1 120.8 %copy-start.3 = (f32[128,2048]{1,0:T(8,128)S(1)}, f32[128,2048]{1,0:T(8,128)}, u32[]{:S(2)}) copy-start(f32[128,2048]{1,0:T(8,128)} %get-tuple-element.87) | copy-start | bytes 3145732
  518.5 4.4 copy-start.5
  518.5 5.1 copy-start.7
  518.5 5.8 %copy-start.6 = (f32[128,512]{1,0:T(8,128)S(1)}, f32[128,512]{1,0:T(8,128)}, u32[]{:S(2)}) copy-start(f32[128,512]{1,0:T(8,128)} %get-tuple-element.90) | copy-start | bytes 786436
  518.5 6.5 %copy-start.4 = (f32[1024,128]{1,0:T(8,128)S(1)}, f32[1024,128]{1,0:T(8,128)}, u32[]{:S(2)}) copy-start(f32[1024,128]{1,0:T(8,128)} %get-tuple-element.91) | copy-start | bytes 1572868
  519.9 6.0 %copy-start.2 = (f32[128,4096]{1,0:T(8,128)S(1)}, f32[128,4096]{1,0:T(8,128)}, u32[]{:S(2)}) copy-start(f32[128,4096]{1,0:T(8,128)} %get-tuple-element.93) | copy-start | bytes 6291460
  523.7 3.5 copy-start.1
  527.2 2.3 copy-start

commit v5 on v4

--- a/solution.py
+++ b/solution.py
@@ -16,8 +16,7 @@
 BF16 = jnp.bfloat16
 F32 = jnp.float32
 MB = 1024 * 1024
-LATE = 1
-EARLY = 1
+SOON = 1
 
 
 def rope_tables(count, head_dim):
@@ -183,7 +182,7 @@
 
 def gather_kernel(
     count, len_ref, seq_ref, q_ref, k_ref, v_ref, o_ref, g_ref, u_ref, d_ref, gain_ref, tok_ref, cot_ref,
-    a_all, gu_all, down, gain_all, tok_all, dm_all, o_v, a_v, gu_v, d_v, d_t, dm, chain_send, chain_recv,
+    a_all, gate_all, up_soon, up, down_t, gain_all, tok_all, dm_all, o_v, a_v, g_v, u_v, d_v, d_t, dm, chain_send, chain_recv,
     part_send, part_recv, plane_send, plane_recv, gain_send, gain_recv, pair_send, pair_recv, local_sem,
 ):
     plane = count // LINE
@@ -203,29 +202,31 @@
         copy_in(v_ref, a_v.at[:, pl.ds(q_width + kv_width, kv_width)], local_sem.at[3]),
         copy_in(d_ref, d_v, local_sem.at[4]),
         copy_in(cot_ref, dm, local_sem.at[5]),
-        copy_in(columns(g_ref, me.z), gu_v.at[:, pl.ds(0, units)], local_sem.at[6]),
-        copy_in(columns(u_ref, me.z), gu_v.at[:, pl.ds(units, units)], local_sem.at[7]),
+        copy_in(columns(g_ref, me.z), g_v, local_sem.at[6]),
+        copy_in(columns(u_ref, me.z), u_v, local_sem.at[7]),
         copy_in(gain_ref, gain_all.at[me.d], local_sem.at[8]),
         copy_in(tok_ref, tok_all.at[me.t], local_sem.at[9]),
     ]
     for copy in local[:4]:
         copy.start()
     keep_a = copy_in(a_v, a_all.at[me.d], local_sem.at[10])
-    keep_down = copy_in(d_t.at[me.z], down.at[me.z], local_sem.at[11])
+    keep_down = copy_in(d_t, down_t, local_sem.at[11])
     keep_dm = copy_in(dm, dm_all.at[me.z, me.t], local_sem.at[12])
-    keep_gu = copy_in(gu_v, gu_all.at[me.d], local_sem.at[13])
+    keep_gate = copy_in(g_v, gate_all.at[me.d], local_sem.at[13])
+    keep_up = copy_in(u_v, up.at[me.z], local_sem.at[14])
 
     attn = Chain(me, a_v, lambda z: a_all.at[z * plane + me.p], chain_send.at[0], chain_recv.at[0])
     dms = Chain(me, dm, lambda z: dm_all.at[z, me.t], chain_send.at[1], chain_recv.at[1])
     planes = (
         PlaneGather(me, 0, a_all, rows, plane_send, plane_recv),
-        PlaneGather(me, 1, gu_all, rows, plane_send, plane_recv),
+        PlaneGather(me, 1, gate_all, rows, plane_send, plane_recv),
+        PlaneGather(me, 2, up_soon, rows, plane_send, plane_recv),
     )
 
     def part(way, k, kind):
         _, target = reach(me, 1 - way, k)
-        src = d_t.at[target] if kind == 2 else columns((g_ref, u_ref)[kind], target)
-        dst = down.at[me.z] if kind == 2 else gu_all.at[me.d, :, pl.ds(kind * units, units)]
+        src = columns((g_ref, u_ref)[kind], target)
+        dst = (gate_all.at[me.d], up.at[me.z])[kind]
         return remote(
             src, dst, part_send.at[way, k, kind], part_recv.at[way, k, kind], me.at(target, me.p)
         )
@@ -233,6 +234,9 @@
     def pair(z, first=None):
         src = dm_all.at[z, me.t] if first is None else first
         return remote(src, dm_all.at[z, me.t], pair_send.at[z], pair_recv.at[z], me.sibling())
+
+    def keep_soon(soon, src):
+        return copy_in(src, up_soon.at[soon * plane + me.p], local_sem.at[15 + soon])
 
     def start_parts(k, kinds):
         for way in range(2):
@@ -256,9 +260,15 @@
         planes[0].start(z)
 
     def part_step(way, k, z):
-        for kind in range(2):
-            arrival(gu_all.at[z * plane + me.p, :, pl.ds(kind * units, units)], part_recv.at[way, k, kind])
+        arrival(gate_all.at[z * plane + me.p], part_recv.at[way, k, 0])
         planes[1].start(z)
+        arrival(up.at[z], part_recv.at[way, k, 1])
+        for soon in range(SOON):
+
+            @pl.when(z == soon)
+            def _():
+                planes[2].start(soon, up.at[soon])
+                keep_soon(soon, up.at[soon]).start()
 
     def dm_step(way, k, z):
         dms.wait_block(way, k)
@@ -309,12 +319,18 @@
             planes[0].forward(me.z)
             for copy in local[6:8]:
                 copy.wait()
-            keep_gu.start()
-            planes[1].start(me.z, gu_v)
+            keep_gate.start()
+            keep_up.start()
+            planes[1].start(me.z, g_v)
+            for soon in range(SOON):
+
+                @pl.when(me.z == soon)
+                def _():
+                    planes[2].start(soon, u_v)
+                    keep_soon(soon, u_v).start()
+
         else:
             each(k - 1, lambda way, k, z: planes[0].forward(z))
-    for k in range(1, LINE):
-        start_parts(k, (2,))
     for way in range(2):
         dms.start(way, 0)
     pair(me.z, dm).start()
@@ -327,6 +343,8 @@
             each(k - 1, lambda way, k, z: planes[1].forward(z))
             each(k - 1, dm_step)
     each(LINE - 1, lambda way, k, z: planes[1].forward(z))
+    for soon in range(SOON):
+        planes[2].forward(soon)
     each(LINE - 1, dm_step)
 
     attn.finish()
@@ -336,18 +354,19 @@
 
             @pl.when(reach(me, 1 - way, k)[0])
             def _():
-                for kind in range(3):
+                for kind in range(2):
                     part(way, k, kind).wait_send()
 
-        each(k, lambda way, k, z: arrival(down.at[z], part_recv.at[way, k, 2]))
     for step in range(1, count):
         give_gain(step).wait()
     tokens.wait()
     for z in range(LINE):
         pair(z).wait()
-    for job in planes:
-        job.finish()
-    for copy in local[8:] + [keep_a, keep_down, keep_dm, keep_gu]:
+    for job, zs in zip(planes, (LINE, LINE, SOON)):
+        job.finish(range(zs))
+    for soon in range(SOON):
+        keep_soon(soon, u_v).wait()
+    for copy in local[8:] + [keep_a, keep_down, keep_dm, keep_gate, keep_up]:
         copy.wait()
 
 
@@ -368,24 +387,27 @@
         name="gather_all",
         out_shape=(
             jax.ShapeDtypeStruct((count, rows, width), BF16),
-            jax.ShapeDtypeStruct((count, rows, 2 * units), BF16),
+            jax.ShapeDtypeStruct((count, rows, units), BF16),
+            jax.ShapeDtypeStruct((count // LINE * SOON, rows, units), BF16),
+            jax.ShapeDtypeStruct((LINE, rows, units), BF16),
             jax.ShapeDtypeStruct((LINE, rows, units), BF16),
             jax.ShapeDtypeStruct((count,) + gains.shape, gains.dtype),
             jax.ShapeDtypeStruct((2,) + tokens.shape, BF16),
             jax.ShapeDtypeStruct((LINE, 2) + cotangent.shape, BF16),
         ),
         in_specs=[SMEM] * 2 + [ANY] * 10,
-        out_specs=(ANY,) * 6,
+        out_specs=(ANY,) * 8,
         scratch_shapes=[
             pltpu.VMEM(w_out.shape, BF16),
             pltpu.VMEM((rows, width), BF16),
-            pltpu.VMEM((rows, 2 * units), BF16),
+            pltpu.VMEM((rows, units), BF16),
+            pltpu.VMEM((rows, units), BF16),
             pltpu.VMEM(w_down.shape, BF16),
             pltpu.VMEM((LINE, rows, units), BF16),
             pltpu.VMEM(cotangent.shape, BF16),
-            DMA((2, 2, LINE)), DMA((2, 2, LINE)), DMA((2, LINE, 3)), DMA((2, LINE, 3)),
-            DMA((2, LINE, kinds)), DMA((2, LINE, kinds)), DMA((count,)), DMA((count,)),
-            DMA((LINE + 1,)), DMA((LINE + 1,)), DMA((14,)),
+            DMA((2, 2, LINE)), DMA((2, 2, LINE)), DMA((2, LINE, 2)), DMA((2, LINE, 2)),
+            DMA((3, LINE, kinds)), DMA((3, LINE, kinds)), DMA((count,)), DMA((count,)),
+            DMA((LINE + 1,)), DMA((LINE + 1,)), DMA((15 + SOON,)),
         ],
         compiler_params=pltpu.CompilerParams(
             collective_id=0, has_side_effects=True, vmem_limit_bytes=60 * MB
@@ -419,6 +441,26 @@
         for term in terms[1:]:
             total += term[at].astype(F32)
         target[at] = total.astype(target.dtype)
+
+
+def grad_rows(at, per, left_ref, right_ref, first, targets, there):
+    tile = 512
+    tokens = left_ref.shape[0]
+
+    @pl.loop(0, per // tile)
+    def _(n):
+        left = left_ref[:, pl.ds(pl.multiple_of(at + n * tile, tile), tile)].T
+        for job, ref, start in targets:
+            block, units = ref.shape[1], right_ref.shape[1]
+            rows = pl.ds(there + n * (tile // block), tile // block)
+            for c in range(units // tile):
+                grad = jnp.dot(
+                    left, right_ref[pl.ds(first + job * tokens, tokens), c * tile : (c + 1) * tile],
+                    preferred_element_type=F32,
+                )
+                ref[rows, :, start + c * tile : start + (c + 1) * tile] = grad.astype(BF16).reshape(
+                    tile // block, block, tile
+                )
 
 
 class PlaneSum:
@@ -441,6 +483,8 @@
         return rank - self.ranks[0]
 
     def block(self, rank, p):
+        if callable(self.grad):
+            return self.grad(rank, p)
         return self.grad.at[ranked(self.me, rank) * self.me.plane + p]
 
     def load(self, rank):
@@ -551,30 +595,37 @@
 
 
 def feed_forward_kernel(
-    plane, h_ref, dm_ref, gu_ref, down, down_ref, total_ref, out_ref, grad_ref, sum_ref, rows_in, weights, inner, part,
+    plane, h_ref, dm_ref, gate_ref, up_soon, up_rest, down, total_ref, out_ref, grad_ref, sum_ref,
+    h_out, inner_out, rows_in, weights, inner, down_grad, part,
     from_pair, from_line, own, other, first, second, first_send, first_recv, second_send, second_recv,
     own_sem, other_sem, chain_send, chain_recv, pass_send, pass_recv, pair_send, pair_recv,
-    line_send, line_recv, plane_send, plane_recv, load_sem, dm_sem, grad_sem, out_sem,
+    line_send, line_recv, plane_send, plane_recv, load_sem, dm_sem, grad_sem, out_sem, sum_sem,
 ):
     me = Place(plane)
     rows, model = h_ref.shape
     units = inner.shape[1]
     wide = 2 * rows
     tokens = LINE * wide
-    most, block, _ = down_ref.shape
+    block = down.shape[1]
+    soon = up_soon.shape[0]
     tile = 512
 
     def slot(z, t):
         return rows_in.at[pl.ds(pl.multiple_of((z * 2 + t) * rows, rows), rows)]
 
     loads = [
-        copy_in(gu_ref, weights.at[:, :, pl.ds(0, 2 * units)], load_sem.at[0]),
-        copy_in(down_ref, weights.at[pl.ds(0, most), :, pl.ds(2 * units, units)], load_sem.at[2]),
+        copy_in(gate_ref, weights.at[:, :, pl.ds(0, units)], load_sem.at[0]),
+        copy_in(up_soon, weights.at[pl.ds(0, soon), :, pl.ds(units, units)], load_sem.at[2]),
+        copy_in(
+            up_rest, weights.at[pl.ds(soon, up_rest.shape[0]), :, pl.ds(units, units)], load_sem.at[3]
+        ),
     ]
-    late = range(LINE - LATE, LINE)
-    for z in late:
-        own_down = weights.at[z * plane + me.p, :, pl.ds(2 * units, units)]
-        loads.append(copy_in(down.at[z], own_down, load_sem.at[3 + z]))
+    own_down = [
+        copy_in(
+            down.at[z], weights.at[z * plane + me.p, :, pl.ds(2 * units, units)], load_sem.at[4 + z]
+        )
+        for z in range(LINE)
+    ]
     for load in loads:
         load.start()
     load_dm = pltpu.make_async_copy(dm_ref, rows_in.at[pl.ds(tokens, tokens)], dm_sem)
@@ -585,11 +636,9 @@
     gather = PlaneGather(
         me, 0, weights.at[:, :, pl.ds(2 * units, units)], block, plane_send, plane_recv
     )
-    for z in late:
-        gather.start(z, down.at[z])
     summed = PlaneSum(
-        me, weights, own, other, first, second,
-        (first_send, first_recv, second_send, second_recv, own_sem, other_sem), range(EARLY),
+        me, down_grad, own, other, first, second,
+        (first_send, first_recv, second_send, second_recv, own_sem, other_sem),
     )
     chain = Chain(me, h_ref, lambda z: slot(z, me.t), chain_send, chain_recv)
 
@@ -600,61 +649,65 @@
     for way in range(2):
         chain.start(way, 0)
     share(me.z, h_ref).start()
+    for z in range(2):
+        gather.start(z, down.at[z])
+    for copy in own_down:
+        copy.start()
 
     def w_rows(n, width, column):
         return weights[pl.ds(n * (width // block), width // block), :, pl.ds(column, units)].reshape(
             width, units
         )
 
-    def compute(z):
-        at = pl.ds(pl.multiple_of(z * wide, wide), wide)
-        dm_at = pl.ds(pl.multiple_of(tokens + z * wide, wide), wide)
-
+    def pair_rows(z, job=0):
+        return pl.ds(pl.multiple_of(job * tokens + z * wide, wide), wide)
+
+    def columns(c, job):
+        return weights[:, :, pl.ds(pl.multiple_of(job * units + c * tile, tile), tile)].reshape(model, tile)
+
+    def project(z):
         @pl.loop(0, units // tile)
         def _(c):
-            def column(job):
-                return weights[:, :, pl.ds(pl.multiple_of(job * units + c * tile, tile), tile)].reshape(
-                    model, tile
-                )
-
-            h = rows_in[at, :]
-            gate = jnp.dot(h, column(0), preferred_element_type=F32)
-            up = jnp.dot(h, column(1), preferred_element_type=F32)
-            grad_hidden = jnp.dot(rows_in[dm_at, :], column(2), preferred_element_type=F32)
+            here = pl.ds(pl.multiple_of(c * tile, tile), tile)
+            h = rows_in[pair_rows(z), :]
+            gate = jnp.dot(h, columns(c, 0), preferred_element_type=F32)
+            up = jnp.dot(h, columns(c, 1), preferred_element_type=F32)
             sigmoid = jax.nn.sigmoid(gate)
             silu = gate * sigmoid
+            inner[pair_rows(z), here] = (silu * up).astype(BF16)
+            inner[pair_rows(z, 1), here] = (up * sigmoid * (1.0 + gate * (1.0 - sigmoid))).astype(BF16)
+            inner[pair_rows(z, 2), here] = silu.astype(BF16)
+
+    def back(z):
+        @pl.loop(0, units // tile)
+        def _(c):
             here = pl.ds(pl.multiple_of(c * tile, tile), tile)
-            inner[at, here] = (silu * up).astype(BF16)
-            inner[pl.ds(pl.multiple_of(tokens + z * wide, wide), wide), here] = (
-                grad_hidden * up * sigmoid * (1.0 + gate * (1.0 - sigmoid))
-            ).astype(BF16)
-            inner[pl.ds(pl.multiple_of(2 * tokens + z * wide, wide), wide), here] = (
-                grad_hidden * silu
-            ).astype(BF16)
+            grad_hidden = jnp.dot(rows_in[pair_rows(z, 1), :], columns(c, 2), preferred_element_type=F32)
+            for job in range(1, 3):
+                at = pair_rows(z, job)
+                inner[at, here] = (grad_hidden * inner[at, here].astype(F32)).astype(BF16)
 
         @pl.loop(0, model // tile)
         def _(n):
             here = pl.ds(pl.multiple_of(n * tile, tile), tile)
-            grad = dot_cols(inner[pl.ds(pl.multiple_of(tokens + z * wide, wide), wide)], w_rows(n, tile, 0))
-            grad += dot_cols(
-                inner[pl.ds(pl.multiple_of(2 * tokens + z * wide, wide), wide)], w_rows(n, tile, units)
-            )
+            grad = dot_cols(inner[pair_rows(z, 1)], w_rows(n, tile, 0))
+            grad += dot_cols(inner[pair_rows(z, 2)], w_rows(n, tile, units))
             part[0, z, :, :, here] = grad.astype(BF16).reshape(2, rows, tile)
 
-        pair(0, z).start()
-
+        pair(z).start()
+
+    def out(z):
         @pl.loop(0, model // tile)
         def _(n):
             here = pl.ds(pl.multiple_of(n * tile, tile), tile)
-            out = dot_cols(inner[at, :], w_rows(n, tile, 2 * units))
-            part[1, z, :, :, here] = out.astype(BF16).reshape(2, rows, tile)
-
-        pair(1, z).start()
-
-    def pair(job, z):
+            value = dot_cols(inner[pair_rows(z), :], w_rows(n, tile, 2 * units))
+            part[1, z, :, :, here] = value.astype(BF16).reshape(2, rows, tile)
+
+        keep_out(z).start()
+
+    def pair(z):
         return remote(
-            part.at[job, z, 1 - me.t], from_pair.at[job, z], pair_send.at[job, z],
-            pair_recv.at[job, z], me.sibling(),
+            part.at[0, z, 1 - me.t], from_pair.at[z], pair_send.at[z], pair_recv.at[z], me.sibling()
         )
 
     half = rows // 2
@@ -674,8 +727,8 @@
 
         @pl.when(jnp.logical_and(have, before == behind))
         def _():
-            pair(0, z).wait_recv()
-            terms = (part.at[0, z, me.t], from_pair.at[0, z])
+            pair(z).wait_recv()
+            terms = (part.at[0, z, me.t], from_pair.at[z])
             if behind:
                 terms += (from_line.at[way, k],)
             for i in range(2):
@@ -685,8 +738,8 @@
                 pass_on(way, k, i).start()
 
     def total():
-        pair(0, me.z).wait_recv()
-        add_rows(total_ref, (part.at[0, me.z, me.t], from_pair.at[0, me.z]), rows)
+        pair(me.z).wait_recv()
+        add_rows(total_ref, (part.at[0, me.z, me.t], from_pair.at[me.z]), rows)
         for way in range(2):
 
             @pl.when(reach(me, way, 1)[0])
@@ -695,41 +748,32 @@
                     arrival(from_line.at[way, 0, halves[i]], line_recv.at[way, 0, i])
                     add_rows(total_ref, (total_ref, from_line.at[way, 0]), half, i * half)
 
-    def grads(z):
-        per = plane * block
-
-        @pl.loop(0, per // tile)
-        def _(n):
-            column = pl.ds(pl.multiple_of(z * per + n * tile, tile), tile)
-            h = rows_in[pl.ds(0, tokens), column].T
-            dm = rows_in[pl.ds(tokens, tokens), column].T
-            there = pl.ds((z * per + n * tile) // block, tile // block)
-            for job in range(3):
-                left = (h, h, dm)[job]
-                start = (tokens, 2 * tokens, 0)[job]
-                for c in range(units // 512):
-                    grad = jnp.dot(
-                        left, inner[pl.ds(start, tokens), c * 512 : (c + 1) * 512],
-                        preferred_element_type=F32,
-                    )
-                    weights[there, :, job * units + c * 512 : job * units + (c + 1) * 512] = (
-                        grad.astype(BF16).reshape(tile // block, block, 512)
-                    )
-
-        keep_grads(z).start()
-
-    def keep_grads(z):
-        return pltpu.make_async_copy(
-            weights.at[pl.ds(z * plane, plane)], grad_ref.at[pl.ds(z * plane, plane)], grad_sem.at[z]
-        )
+    per = plane * block
+
+    def down_grads(rank):
+        z = ranked(me, rank)
+        grad_rows(
+            z * per, per, rows_in.at[pl.ds(tokens, tokens)], inner, 0, [(0, down_grad, 0)], z * plane
+        )
+        summed.load_rank(rank)
+
+    keeps = [
+        copy_in(weights.at[pl.ds(0, plane), :, pl.ds(0, 2 * units)], grad_ref, grad_sem.at[0]),
+        copy_in(rows_in.at[pl.ds(0, tokens)], h_out, grad_sem.at[1]),
+        copy_in(inner.at[pl.ds(tokens, 2 * tokens)], inner_out, grad_sem.at[2]),
+    ]
+
+    def grads():
+        targets = [(0, weights, 0), (1, weights, units)]
+        z = ranked(me, 0)
+        grad_rows(z * per, per, rows_in.at[pl.ds(0, tokens)], inner, tokens, targets, 0)
+
+    def keep_sum(rank):
+        return copy_in(own.at[rank], sum_ref.at[rank], sum_sem.at[rank])
 
     keep.wait()
     for load in loads:
         load.wait()
-    load_dm.wait()
-    for z in late:
-        gather.forward(z)
-    gather.finish(late)
     for k in range(LINE):
         for way in range(2 if k else 1):
             have, z = reach(me, way, k)
@@ -741,55 +785,59 @@
                     chain.start(way, k)
                     share(z).start()
                 arrival(slot(z, 1 - me.t), pass_recv.at[z])
-                compute(z)
-
-        if k:
+                project(z)
+
+        gather.forward(k)
+        if k + 2 < LINE:
+            gather.start(k + 2, down.at[k + 2])
+    def keep_out(z):
+        return copy_in(part.at[1, z], out_ref.at[z], out_sem.at[z])
+
+    load_dm.wait()
+    keeps[1].start()
+    down_grads(0)
+    summed.begin(0)
+    for copy in own_down:
+        copy.wait()
+    gather.finish()
+    passing = {1: (1, 2), 2: (2, 1), 3: (1, 1)}
+    for rank in range(LINE):
+        if rank:
+            down_grads(rank)
+            if rank - 1 in passing:
+                for way in range(2):
+                    line(way, passing[rank - 1][1], passing[rank - 1][0])
+            summed.middle(rank - 1)
+            summed.begin(rank)
+            if rank > 1:
+                summed.end(rank - 2)
+                keep_sum(rank - 2).start()
+        back(ranked(me, rank))
+        if rank < LINE - 1:
+            out(ranked(me, rank))
             for way in range(2):
-                line(1 - way, k, 0)
-    order = [(behind, k) for behind in range(1, LINE) for k in range(1, LINE - behind)]
-    order.sort(key=lambda e: (2 * e[0] + e[1], e[0]))
-
-    def keep_out(z):
-        return pltpu.make_async_copy(part.at[1, z, me.t], out_ref.at[z], out_sem.at[z])
-
-    for i in range(LINE):
-        grads(ranked(me, i))
-        if i < EARLY:
-            summed.load_rank(i)
-        if i == 0:
-            summed.begin(0)
-        if i == 1:
-            summed.middle(0)
-            if EARLY > 1:
-                summed.begin(1)
-        if i < len(order):
-            for way in range(2):
-                line(way, order[i][1], order[i][0])
-    for z in range(LINE):
-        pair(1, z).wait_recv()
-        add_rows(part.at[1, z, me.t], (part.at[1, z, me.t], from_pair.at[1, z]), rows)
-        keep_out(z).start()
-    keep_sums = [
-        pltpu.make_async_copy(own.at[rank], sum_ref.at[rank], load_sem.at[rank]) for rank in range(EARLY)
-    ]
-    summed.end(0)
-    keep_sums[0].start()
-    if EARLY > 1:
-        summed.middle(1)
+                line(way, LINE - 1 - rank, 0)
+    for way in range(2):
+        line(way, passing[LINE - 1][1], passing[LINE - 1][0])
+    keeps[2].start()
+    summed.middle(LINE - 1)
+    summed.end(LINE - 2)
+    keep_sum(LINE - 2).start()
+    grads()
+    keeps[0].start()
+    out(ranked(me, LINE - 1))
+    summed.end(LINE - 1)
+    keep_sum(LINE - 1).start()
     total()
-    if EARLY > 1:
-        summed.end(1)
-        keep_sums[1].start()
     summed.finish()
-    for copy in keep_sums:
-        copy.wait()
     chain.finish()
     for z in range(LINE):
         share(z).wait_send()
-        keep_grads(z).wait()
         keep_out(z).wait()
-        for job in range(2):
-            pair(job, z).wait_send()
+        keep_sum(z).wait()
+        pair(z).wait_send()
+    for copy in keeps:
+        copy.wait()
     for k in range(1, LINE):
         for way in range(2):
 
@@ -799,12 +847,11 @@
                     pass_on(way, k, i).wait_send()
 
 
-def feed_forward(count, h, dm_all, gu_all, down, down_all):
+def feed_forward(count, h, dm_all, gate_all, up_soon, up_rest, down):
     rows, model = h.shape
     _, block, units = down.shape
     kinds = max(6, count // LINE - 1)
-    grads = (count, block, 3 * units)
-    buffers, sems = PlaneSum.scratch(count, *grads[1:], EARLY)
+    buffers, sems = PlaneSum.scratch(count, block, units)
     tokens = LINE * 2 * rows
     vmem = pl.BlockSpec(memory_space=pltpu.VMEM)
     return pl.pallas_call(
@@ -812,28 +859,32 @@
         name="feed_forward",
         out_shape=(
             jax.ShapeDtypeStruct((rows, model), F32),
-            jax.ShapeDtypeStruct((LINE, rows, model), BF16),
-            jax.ShapeDtypeStruct(grads, BF16),
-            jax.ShapeDtypeStruct((EARLY,) + grads[1:], BF16),
+            jax.ShapeDtypeStruct((LINE, 2, rows, model), BF16),
+            jax.ShapeDtypeStruct((count // LINE, block, 2 * units), BF16),
+            jax.ShapeDtypeStruct((LINE, block, units), BF16),
+            jax.ShapeDtypeStruct((tokens, model), BF16),
+            jax.ShapeDtypeStruct((2 * tokens, units), BF16),
         ),
-        in_specs=[ANY] * 5,
-        out_specs=(vmem, ANY, ANY, ANY),
+        in_specs=[ANY] * 6,
+        out_specs=(vmem,) + (ANY,) * 5,
         scratch_shapes=[
             pltpu.VMEM((2 * tokens, model), BF16),
-            pltpu.VMEM(grads, BF16),
+            pltpu.VMEM((count, block, 3 * units), BF16),
             pltpu.VMEM((3 * tokens, units), BF16),
+            pltpu.VMEM((count, block, units), BF16),
             pltpu.VMEM((2, LINE, 2, rows, model), BF16),
-            pltpu.VMEM((2, LINE, rows, model), BF16),
+            pltpu.VMEM((LINE, rows, model), BF16),
             pltpu.VMEM((2, LINE - 1, rows, model), BF16),
             *buffers,
             *sems,
-            DMA((2, LINE)), DMA((2, LINE)), DMA((LINE,)), DMA((LINE,)), DMA((2, LINE)), DMA((2, LINE)),
-            DMA((2, LINE, 2)), DMA((2, LINE, 2)), DMA((1, LINE, kinds)), DMA((1, LINE, kinds)), DMA((3 + LINE,)), DMA, DMA((LINE,)), DMA((LINE,)),
+            DMA((2, LINE)), DMA((2, LINE)), DMA((LINE,)), DMA((LINE,)), DMA((LINE,)), DMA((LINE,)),
+            DMA((2, LINE, 2)), DMA((2, LINE, 2)), DMA((1, LINE, kinds)), DMA((1, LINE, kinds)),
+            DMA((4 + LINE,)), DMA, DMA((LINE,)), DMA((LINE,)), DMA((LINE,)),
         ],
         compiler_params=pltpu.CompilerParams(
             collective_id=1, has_side_effects=True, vmem_limit_bytes=60 * MB
         ),
-    )(h, dm_all, gu_all, down, down_all)
+    )(h, dm_all, gate_all, up_soon, up_rest, down)
 
 
 def greet_plane(me):
@@ -857,9 +908,9 @@
 
 
 def attention_forward_kernel(
-    plane, len_ref, seq_ref, gain_ref, cos_ref, sin_ref, tok_in, a_ref, down, x1_out, h2_out, h1_out,
-    qkv_out, probs_out, o_out, down_all, weights, tok_ref, x1_ref, h2_ref, h1_ref, qkv_ref, probs_ref,
-    o_ref, part, from_pair, plane_send, plane_recv, pair_send, pair_recv, load_sem, keep_sem,
+    plane, len_ref, seq_ref, gain_ref, cos_ref, sin_ref, tok_in, a_ref, up, down_t, x1_out, h2_out, h1_out,
+    qkv_out, probs_out, o_out, up_rest, down, weights, tok_ref, x1_ref, h2_ref, h1_ref, qkv_ref, probs_ref,
+    o_ref, part, from_pair, plane_send, plane_recv, part_send, part_recv, pair_send, pair_recv, load_sem, keep_sem,
 ):
     me = Place(plane)
     _, rows, model = tok_ref.shape
@@ -874,8 +925,10 @@
     load = copy_in(a_ref, weights, load_sem.at[1])
     load.start()
     keep = [
-        copy_in(down.at[z], down_all.at[z * plane + me.p], load_sem.at[2 + z]) for z in range(LINE - LATE)
+        copy_in(up.at[z], up_rest.at[(z - SOON) * plane + me.p], load_sem.at[2 + z])
+        for z in range(SOON, LINE)
     ]
+    keep.append(copy_in(down_t.at[me.z], down.at[me.z], load_sem.at[2 + LINE]))
     for copy in keep:
         copy.start()
     outs = [
@@ -887,10 +940,25 @@
             )
         )
     ]
-    greet_plane(me)
-    gather = PlaneGather(me, 0, down_all, down.shape[1], plane_send, plane_recv)
-    for z in range(LINE - LATE):
-        gather.start(z, down.at[z])
+    greet_all(me, plane * LINE)
+    gather = PlaneGather(me, 0, up_rest, up.shape[1], plane_send, plane_recv)
+    for z in range(LINE - SOON):
+        gather.start(z, up.at[z + SOON])
+
+    def give_down(way, k):
+        _, target = reach(me, 1 - way, k)
+        return remote(
+            down_t.at[target], down.at[me.z], part_send.at[way, k], part_recv.at[way, k],
+            me.at(target, me.p),
+        )
+
+    for k in range(1, LINE):
+        for way in range(2):
+
+            @pl.when(reach(me, 1 - way, k)[0])
+            def _():
+                give_down(way, k).start()
+
     load_tok.wait()
 
     for t in range(2):
@@ -955,7 +1023,7 @@
 
     swap = remote(part.at[1 - me.t], from_pair, pair_send, pair_recv, me.sibling())
     swap.start()
-    for z in range(2, LINE - LATE):
+    for z in range(2, LINE - SOON):
         gather.forward(z)
     swap.wait_recv()
 
@@ -969,12 +1037,23 @@
     outs[4].start()
     outs[5].start()
     swap.wait_send()
-    gather.finish(range(LINE - LATE))
+    gather.finish(range(LINE - SOON))
+    for k in range(1, LINE):
+        for way in range(2):
+
+            @pl.when(reach(me, 1 - way, k)[0])
+            def _():
+                give_down(way, k).wait_send()
+
+            @pl.when(reach(me, way, k)[0])
+            def _():
+                arrival(down.at[me.z], part_recv.at[way, k])
+
     for copy in keep + outs:
         copy.wait()
 
 
-def attention_forward(count, heads, lengths, seq, gains, cos, sin, tokens_all, attn_all, down):
+def attention_forward(count, heads, lengths, seq, gains, cos, sin, tokens_all, attn_all, up, down_t):
     _, rows, model = tokens_all.shape
     wide = 2 * rows
     q_width = heads * HEAD_SIZE
@@ -992,27 +1071,32 @@
     return pl.pallas_call(
         functools.partial(attention_forward_kernel, plane),
         name="attention_forward",
-        out_shape=outs + (jax.ShapeDtypeStruct((count - LATE * plane,) + down.shape[1:], BF16),),
-        in_specs=[SMEM] * 2 + [VMEM] * 3 + [ANY] * 3,
-        out_specs=(ANY,) * 7,
+        out_shape=outs
+        + (
+            jax.ShapeDtypeStruct((count - SOON * plane,) + up.shape[1:], BF16),
+            jax.ShapeDtypeStruct(down_t.shape, BF16),
+        ),
+        in_specs=[SMEM] * 2 + [VMEM] * 3 + [ANY] * 4,
+        out_specs=(ANY,) * 8,
         scratch_shapes=[
             pltpu.VMEM(attn_all.shape, BF16),
             pltpu.VMEM(tokens_all.shape, BF16),
             *[pltpu.VMEM(out.shape, out.dtype) for out in outs],
             pltpu.VMEM((2, rows, model), F32),
             pltpu.VMEM((rows, model), F32),
-            DMA((1, LINE, kinds)), DMA((1, LINE, kinds)), DMA, DMA, DMA((2 + LINE,)), DMA((6,)),
+            DMA((1, LINE, kinds)), DMA((1, LINE, kinds)), DMA((2, LINE)), DMA((2, LINE)), DMA, DMA,
+            DMA((3 + LINE,)), DMA((6,)),
         ],
         compiler_params=pltpu.CompilerParams(
             collective_id=2, has_side_effects=True, vmem_limit_bytes=60 * MB
         ),
-    )(lengths, seq, gains, cos, sin, tokens_all, attn_all, down)
+    )(lengths, seq, gains, cos, sin, tokens_all, attn_all, up, down_t)
 
 
 def attention_backward_kernel(
     plane, gain_ref, cos_ref, sin_ref, total_in, x1_in, dm_in, tok_in, h1_in, qkv_in, probs_in, o_in,
-    a_ref, gw_ref, sum_ref, ga_ref, w_out, grad_tokens, gain_parts, weights, own, other, first, second,
-    total_ref, x1_ref, dm_ref, tok_ref, h1_ref, qkv_ref, probs_ref, o_ref, dx, da, do, dqkv, dh1, from_pair, first_send, first_recv, second_send, second_recv, load_sem,
+    a_ref, gw_ref, sum_ref, h_in, inner_in, ga_ref, w_out, grad_tokens, gain_parts, weights, own, other, first, second,
+    total_ref, x1_ref, dm_ref, tok_ref, h1_ref, qkv_ref, probs_ref, o_ref, rows_in, inner, gw, dx, da, do, dqkv, dh1, from_pair, first_send, first_recv, second_send, second_recv, load_sem,
     other_sem, part_send, part_recv, pair_send, pair_recv, a_sem, keep_sem, grad_sem, in_sem,
 ):
     me = Place(plane)
@@ -1026,8 +1110,9 @@
     half = HEAD_SIZE // 2
     scale = HEAD_SIZE ** (-0.5)
     summed = PlaneSum(
-        me, gw_ref, own, other, first, second,
-        (first_send, first_recv, second_send, second_recv, load_sem, other_sem), range(EARLY, LINE),
+        me, lambda rank, p: gw.at[(rank - 1) * plane + p] if rank else gw_ref.at[p],
+        own, other, first, second,
+        (first_send, first_recv, second_send, second_recv, load_sem, other_sem),
     )
     ins = [
         copy_in(src, dst, in_sem.at[i])
@@ -1035,26 +1120,34 @@
             (
                 (total_in, total_ref), (x1_in, x1_ref), (dm_in.at[me.z, me.t], dm_ref), (tok_in, tok_ref),
                 (h1_in, h1_ref), (qkv_in, qkv_ref), (probs_in, probs_ref), (o_in, o_ref),
+                (h_in, rows_in), (inner_in, inner),
             )
         )
     ]
-    for copy in ins[:3]:
+    for copy in ins[:3] + ins[8:]:
         copy.start()
     load = pltpu.make_async_copy(a_ref, weights, a_sem)
     load.start()
-    for copy in ins[3:]:
+    for copy in ins[3:8]:
         copy.start()
-    summed.load_all()
+    summed.load_rank(0)
     greet_all(me, plane * LINE)
 
-    def part(rank):
+    wide = own.shape[2]
+    spans = (pl.ds(0, wide), pl.ds(wide, sum_ref.shape[2]))
+
+    def part(rank, kind):
         target = ranked(me, rank)
         way, k = way_to(me, target)
-        src = own.at[summed.slot(rank)] if rank >= EARLY else sum_ref.at[rank]
         return remote(
-            src, w_out.at[me.z], part_send.at[way, k], part_recv.at[way, k], me.at(target, me.p)
-        )
-
+            (own, sum_ref)[kind].at[rank], w_out.at[me.z, :, spans[kind]], part_send.at[way, k, kind],
+            part_recv.at[way, k, kind], me.at(target, me.p),
+        )
+
+    keeps = [
+        copy_in((own, sum_ref)[kind].at[LINE - 1], w_out.at[me.z, :, spans[kind]], keep_sem.at[kind])
+        for kind in range(2)
+    ]
     give_da = remote(da.at[me.t], da.at[me.t], pair_send.at[0], pair_recv.at[0], me.sibling())
     give_dh1 = remote(dh1.at[1 - me.t], from_pair, pair_send.at[1], pair_recv.at[1], me.sibling())
 
@@ -1171,19 +1264,30 @@
 
         row_loop(rows, 32, act)
 
-    summed.begin(EARLY)
-    for rank in range(EARLY):
-        part(rank).start()
+    summed.begin(0)
+    for rank in range(LINE - 1):
+        part(rank, 1).start()
+    keeps[1].start()
+    def mlp_grads(rank):
+        per = plane * block
+        targets = [(0, gw, 0), (1, gw, inner.shape[1])]
+        z = ranked(me, rank)
+        grad_rows(z * per, per, rows_in, inner, 0, targets, (rank - 1) * plane)
+        summed.load_rank(rank)
+
     for copy in ins[:3]:
         copy.wait()
     mid_norm()
+    for copy in ins[8:]:
+        copy.wait()
+    mlp_grads(1)
     grad_o()
-    for copy in ins[3:]:
+    for copy in ins[3:8]:
         copy.wait()
-    stages = {LINE - 2: [grad_heads, grad_h1], LINE - 1: [grads, in_norm]}
-    if EARLY < LINE - 2:
-        stages = {1: [grad_heads, grad_h1], 2: [grads], 3: [in_norm]}
-    for rank in range(EARLY, LINE):
+    stages = (
+        [grad_heads, lambda: mlp_grads(2)], [grad_h1, lambda: mlp_grads(3)], [grads], [in_norm],
+    )
+    for rank in range(LINE):
         summed.middle(rank)
         if rank + 1 < LINE:
             summed.begin(rank + 1)
@@ -1191,35 +1295,37 @@
             stage()
         summed.end(rank)
         if rank < LINE - 1:
-            part(rank).start()
-
-    keep = pltpu.make_async_copy(own.at[LINE - 1 - EARLY], w_out.at[me.z], keep_sem)
-    keep.start()
-    for rank in range(LINE - 1):
-        part(rank).wait_send()
-    for way, k in FAR_FIRST:
-
-        @pl.when(reach(me, way, k)[0])
-        def _():
-            arrival(w_out.at[me.z], part_recv.at[way, k])
+            part(rank, 0).start()
+
+    keeps[0].start()
+    for kind in range(2):
+        for rank in range(LINE - 1):
+            part(rank, kind).wait_send()
+        for way, k in FAR_FIRST:
+
+            @pl.when(reach(me, way, k)[0])
+            def _():
+                arrival(w_out.at[me.z, :, spans[kind]], part_recv.at[way, k, kind])
 
     summed.finish()
     give_da.wait_send()
     give_dh1.wait_send()
     for n in range(model // tile):
         keep_grads(n).wait()
-    keep.wait()
+    for copy in keeps:
+        copy.wait()
 
 
 def attention_backward(
-    count, gains, cos, sin, total, x1, dm_all, tokens_all, h1, qkv, probs, o, attn_all, grad_mlp, first_sum
+    count, gains, cos, sin, total, x1, dm_all, tokens_all, h1, qkv, probs, o, attn_all, grad_mlp, first_sum, rows_in,
+    inner,
 ):
     _, rows, model = tokens_all.shape
     _, block, width = attn_all.shape
     wide = 2 * rows
     heads = probs.shape[0]
     q_width = heads * HEAD_SIZE
-    buffers, sems = PlaneSum.scratch(count, block, width, LINE - EARLY)
+    buffers, sems = PlaneSum.scratch(count, block, grad_mlp.shape[2])
     return pl.pallas_call(
         functools.partial(attention_backward_kernel, count // LINE),
         name="attention_backward",
@@ -1229,15 +1335,16 @@
             jax.ShapeDtypeStruct((rows, model), F32),
             jax.ShapeDtypeStruct((2, model), F32),
         ),
-        in_specs=[VMEM] * 3 + [ANY] * 11,
+        in_specs=[VMEM] * 3 + [ANY] * 13,
         out_specs=(ANY, ANY, VMEM, VMEM),
         scratch_shapes=[
             pltpu.VMEM(attn_all.shape, BF16),
             *buffers,
             *[
                 pltpu.VMEM(ref.shape, ref.dtype)
-                for ref in (total, x1, dm_all[0, 0], tokens_all, h1, qkv, probs, o)
+                for ref in (total, x1, dm_all[0, 0], tokens_all, h1, qkv, probs, o, rows_in, inner)
             ],
+            pltpu.VMEM(((LINE - 1) * grad_mlp.shape[0],) + grad_mlp.shape[1:], BF16),
             pltpu.VMEM((rows, model), F32),
             pltpu.VMEM((2, rows, model), BF16),
             pltpu.VMEM((wide, q_width), BF16),
@@ -1245,18 +1352,19 @@
             pltpu.VMEM((2, rows, model), F32),
             pltpu.VMEM((rows, model), F32),
             *sems,
-            DMA((2, LINE)), DMA((2, LINE)), DMA((2,)), DMA((2,)), DMA, DMA, DMA((model // 512,)), DMA((8,)),
+            DMA((2, LINE, 2)), DMA((2, LINE, 2)), DMA((2,)), DMA((2,)), DMA, DMA((2,)),
+            DMA((model // 512,)), DMA((10,)),
         ],
         compiler_params=pltpu.CompilerParams(
             collective_id=3, has_side_effects=True, vmem_limit_bytes=60 * MB
         ),
-    )(gains, cos, sin, total, x1, dm_all, tokens_all, h1, qkv, probs, o, attn_all, grad_mlp, first_sum)
+    )(gains, cos, sin, total, x1, dm_all, tokens_all, h1, qkv, probs, o, attn_all, grad_mlp, first_sum, rows_in, inner)
 
 
 def grad_sum_kernel(
-    count, gain_ref, x1_in, ga_ref, out_ref, mlp_ref, q_out, k_out, v_out, o_out, gate_out, up_out,
-    down_out, output, gain_out, own, other, first, second, a_out, x1_ref, mlp, from_line, out_own, out_line, gain_in, gain_pair, first_send, first_recv, second_send, second_recv,
-    load_sem, other_sem, line_send, line_recv, out_send, out_recv, load_out_sem, gain_send, gain_recv,
+    count, gain_ref, x1_in, ga_ref, out_ref, a_out, output, gain_out, own, other, first, second, x1_ref,
+    from_line, out_own, out_pair, out_line, gain_in, gain_pair, first_send, first_recv, second_send, second_recv,
+    load_sem, other_sem, line_send, line_recv, out_send, out_recv, load_out_sem, pair_send, pair_recv, gain_send, gain_recv,
 ):
     plane = count // LINE
     me = Place(plane)
@@ -1305,12 +1413,10 @@
     grads = Line(lambda rank: own.at[rank], from_line, line_send, line_recv)
     outs = Line(lambda rank: out_own.at[ranked(me, rank)], out_line, out_send, out_recv)
     summed.load_all()
-    load_out = copy_in(out_ref, out_own, load_out_sem.at[0])
+    load_out = copy_in(out_ref.at[:, me.t], out_own, load_out_sem.at[0])
     load_out.start()
     load_x1 = copy_in(x1_in, x1_ref, load_out_sem.at[1])
     load_x1.start()
-    load_mlp = copy_in(mlp_ref, mlp, load_out_sem.at[2])
-    load_mlp.start()
     greet_all(me, count)
 
     def give_gain(step):
@@ -1322,7 +1428,16 @@
     summed.begin(0)
     for step in range(1, count):
         give_gain(step).start()
+    pairs = [
+        remote(out_ref.at[z, 1 - me.t], out_pair.at[z], pair_send.at[z], pair_recv.at[z], me.sibling())
+        for z in range(LINE)
+    ]
+    for copy in pairs:
+        copy.start()
     load_out.wait()
+    for z in range(LINE):
+        pairs[z].wait_recv()
+        add_rows(out_own.at[z], (out_own.at[z], out_pair.at[z]), out_own.shape[1])
     for rank in range(LINE - 1):
 
         @pl.when(jnp.logical_or(me.z == 0, me.z == LINE - 1))
@@ -1342,21 +1457,11 @@
 
     def out_end(at):
         output[at, :] = x1_ref[at, :].astype(BF16)
-
-    units = mlp.shape[2] // 3
-
-    def feed_forward_grads(z):
-        here = slice(z * units, (z + 1) * units)
-        gate_out[:, here] = mlp[z, :, :units].astype(F32)
-        up_out[:, here] = mlp[z, :, units : 2 * units].astype(F32)
-        down_out[here, :] = mlp[z, :, 2 * units :].astype(F32).T
 
     for rank in range(LINE):
         summed.middle(rank)
         if rank + 1 < LINE:
             summed.begin(rank + 1)
-            if rank == 0:
-                load_mlp.wait()
         else:
             load_x1.wait()
             row_loop(output.shape[0], 16, out_start)
@@ -1373,7 +1478,6 @@
             swap.start()
             swap.wait()
             gain_out[...] = gain_pair[0] + gain_pair[1]
-        feed_forward_grads(rank)
         summed.end(rank)
         if rank < LINE - 1:
 
@@ -1390,55 +1494,115 @@
 
     add_rows(a_out, (own.at[LINE - 1],), rows)
     grads.total(lambda landed: add_rows(a_out, (a_out, landed), rows))
-    start = 0
-    for ref in (q_out, k_out, v_out):
-        ref[...] = a_out[:, start : start + ref.shape[1]]
-        start += ref.shape[1]
-    o_out[...] = a_out[:, start:].T
+    for copy in pairs:
+        copy.wait_send()
     outs.finish()
     grads.finish()
     summed.finish()
 
 
-def grad_sum(count, q_width, kv_width, x1, ga, out_parts, mlp, gains):
+def grad_sum(count, x1, ga, out_parts, gains):
     _, block, width = ga.shape
-    _, rows, model = out_parts.shape
-    hidden = LINE * (mlp.shape[2] // 3)
+    _, _, rows, model = out_parts.shape
     buffers, sems = PlaneSum.scratch(count, block, width)
     return pl.pallas_call(
         functools.partial(grad_sum_kernel, count),
         name="grad_sum",
         out_shape=(
-            jax.ShapeDtypeStruct((block, q_width), F32),
-            jax.ShapeDtypeStruct((block, kv_width), F32),
-            jax.ShapeDtypeStruct((block, kv_width), F32),
-            jax.ShapeDtypeStruct((q_width, block), F32),
-            jax.ShapeDtypeStruct((block, hidden), F32),
-            jax.ShapeDtypeStruct((block, hidden), F32),
-            jax.ShapeDtypeStruct((hidden, block), F32),
+            jax.ShapeDtypeStruct((block, width), F32),
             jax.ShapeDtypeStruct((rows, model), BF16),
             jax.ShapeDtypeStruct(gains.shape[1:], F32),
         ),
-        in_specs=[VMEM] + [ANY] * 4,
-        out_specs=(VMEM,) * 9,
+        in_specs=[VMEM] + [ANY] * 3,
+        out_specs=(VMEM,) * 3,
         scratch_shapes=[
             *buffers,
-            pltpu.VMEM((block, width), F32),
             pltpu.VMEM((rows, model), F32),
-            pltpu.VMEM(mlp.shape, BF16),
             pltpu.VMEM((2, LINE - 1, block, width), BF16),
-            pltpu.VMEM(out_parts.shape, BF16),
+            pltpu.VMEM((LINE, rows, model), BF16),
+            pltpu.VMEM((LINE, rows, model), BF16),
             pltpu.VMEM((2, LINE - 1, rows, model), BF16),
             pltpu.VMEM(gains.shape, F32),
             pltpu.VMEM((2,) + gains.shape[1:], F32),
             *sems,
-            DMA((2, LINE)), DMA((2, LINE)), DMA((2, LINE)), DMA((2, LINE)), DMA((3,)),
-            DMA((count,)), DMA((count,)),
+            DMA((2, LINE)), DMA((2, LINE)), DMA((2, LINE)), DMA((2, LINE)), DMA((2,)), DMA((LINE,)),
+            DMA((LINE,)), DMA((count,)), DMA((count,)),
         ],
         compiler_params=pltpu.CompilerParams(
             collective_id=4, has_side_effects=True, vmem_limit_bytes=60 * MB
         ),
-    )(gains, x1, ga, out_parts, mlp)
+    )(gains, x1, ga, out_parts)
+
+
+def layouts_kernel(
+    a_ref, mlp_ref, output_ref, tokens_ref, q_out, k_out, v_out, o_out, gate_out, up_out, down_out,
+    output_out, tokens_out, a_v, mlp_v, output_v, tokens_v, q_v, k_v, v_v, o_v, gate_v, up_v, down_v,
+    in_sem, out_sem,
+):
+    ins = [
+        copy_in(src, dst, in_sem.at[i])
+        for i, (src, dst) in enumerate(
+            ((mlp_ref, mlp_v), (a_ref, a_v), (tokens_ref, tokens_v), (output_ref, output_v))
+        )
+    ]
+    for copy in ins:
+        copy.start()
+    sent = []
+
+    def give(src, dst):
+        sent.append(copy_in(src, dst, out_sem.at[len(sent)]))
+        sent[-1].start()
+
+    units = mlp_v.shape[2] // 3
+    ins[0].wait()
+    for z in range(LINE):
+        here = pl.ds(z * units, units)
+        gate_v[:, here] = mlp_v[z, :, :units].astype(F32)
+        give(gate_v.at[:, here], gate_out.at[:, here])
+        up_v[:, here] = mlp_v[z, :, units : 2 * units].astype(F32)
+        give(up_v.at[:, here], up_out.at[:, here])
+        down_v[here, :] = mlp_v[z, :, 2 * units :].astype(F32).T
+        give(down_v.at[here], down_out.at[here])
+    for copy in ins[1:]:
+        copy.wait()
+    give(tokens_v, tokens_out)
+    give(output_v, output_out)
+    start = 0
+    for src, dst in ((q_v, q_out), (k_v, k_out), (v_v, v_out)):
+        src[...] = a_v[:, start : start + src.shape[1]]
+        start += src.shape[1]
+        give(src, dst)
+    o_v[...] = a_v[:, start:].T
+    give(o_v, o_out)
+    for copy in sent:
+        copy.wait()
+
+
+def layouts(q_width, kv_width, a, mlp, output, grad_tokens):
+    block = a.shape[0]
+    hidden = LINE * (mlp.shape[2] // 3)
+    outs = (
+        jax.ShapeDtypeStruct((block, q_width), F32),
+        jax.ShapeDtypeStruct((block, kv_width), F32),
+        jax.ShapeDtypeStruct((block, kv_width), F32),
+        jax.ShapeDtypeStruct((q_width, block), F32),
+        jax.ShapeDtypeStruct((block, hidden), F32),
+        jax.ShapeDtypeStruct((block, hidden), F32),
+        jax.ShapeDtypeStruct((hidden, block), F32),
+    )
+    ins = (a, mlp, output, grad_tokens)
+    return pl.pallas_call(
+        layouts_kernel,
+        name="layouts",
+        out_shape=outs + tuple(jax.ShapeDtypeStruct(ref.shape, ref.dtype) for ref in ins[2:]),
+        in_specs=[ANY] * 4,
+        out_specs=(ANY,) * 9,
+        scratch_shapes=[
+            *[pltpu.VMEM(ref.shape, ref.dtype) for ref in ins + outs],
+            DMA((4,)), DMA((3 * LINE + 6,)),
+        ],
+        compiler_params=pltpu.CompilerParams(vmem_limit_bytes=60 * MB),
+    )(*ins)
 
 
 def shards(
@@ -1452,27 +1616,28 @@
     cos, sin = rope_tables(tokens.shape[0] * lax.axis_size("tensor"), HEAD_SIZE)
     lanes = -rows % 128
     gains = jnp.pad(jnp.stack([gain_attn, gain_mlp]), ((0, 14), (0, lanes)))
-    attn_all, gate_up_all, down, gains_all, tokens_all, dm_all = gather_all(
+    attn_all, gate_all, up_soon, up, down_t, gains_all, tokens_all, dm_all = gather_all(
         count, lengths, seq_of_group,
         (w_query, key_weight, value_weight, w_out, w_gate, w_up, w_down), gains, tokens, cotangent,
     )
     gains_full = gains_all[:, :2, :rows].transpose(1, 0, 2).reshape(2, model).astype(F32)
-    x1, h2, h1, qkv, probs, attended, down_all = attention_forward(
+    x1, h2, h1, qkv, probs, attended, up_rest, down = attention_forward(
         count, q_width // HEAD_SIZE, lengths, seq_of_group, gains_full, cos, sin, tokens_all, attn_all,
-        down,
+        up, down_t,
     )
-    grad_h2, out_parts, grad_mlp_w, first_sum = feed_forward(
-        count, h2, dm_all.reshape(-1, model), gate_up_all, down, down_all
+    grad_h2, out_parts, grad_mlp_w, down_sum, rows_in, inner = feed_forward(
+        count, h2, dm_all.reshape(-1, model), gate_all, up_soon, up_rest, down
     )
     grad_attn_w, mlp_sum, grad_tokens, gain_parts = attention_backward(
         count, gains_full, cos, sin, grad_h2, x1, dm_all, tokens_all, h1, qkv, probs, attended, attn_all,
-        grad_mlp_w, first_sum,
+        grad_mlp_w, down_sum, rows_in, inner,
     )
     gain_parts = gain_parts.reshape(2, count, rows).transpose(1, 0, 2)
     gain_parts = jnp.pad(gain_parts, ((0, 0), (0, 6), (0, lanes)))
+    attn_sum, output, gain_sum = grad_sum(count, x1, grad_attn_w, out_parts, gain_parts)
     (
-        grad_query, grad_key, grad_value, grad_out, grad_gate, grad_up, grad_down, output, gain_sum,
-    ) = grad_sum(count, q_width, kv_width, x1, grad_attn_w, out_parts, mlp_sum, gain_parts)
+        grad_query, grad_key, grad_value, grad_out, grad_gate, grad_up, grad_down, output, grad_tokens,
+    ) = layouts(q_width, kv_width, attn_sum, mlp_sum, output, grad_tokens)
     return (
         output, grad_tokens, grad_query, grad_key, grad_value, grad_out, gain_sum[0, :rows],
         grad_gate, grad_up, grad_down, gain_sum[1, :rows],

time: 539 us -> 512 us (0.950)
  Pallas kernels: 512 us -> 499 us
  local copies, waits for them, and re-layouts: 13.7 us -> 2.63 us
    pallas_call x1, Pallas kernels: 180 us -> 155 us  [gather_all(): pl.pallas_call(functools.partial(gather_kernel, count), name='gather_all'...]
    pallas_call x1, Pallas kernels: 97.6 us -> 113 us  [feed_forward(): pl.pallas_call(functools.partial(feed_forward_kernel, count // LINE), nam...]
    pallas_call x1, Pallas kernels: 87.4 us -> 76.2 us  [attention_backward(): pl.pallas_call(functools.partial(attention_backward_kernel, count // LINE...]
    unnamed x25 -> x0, local copies, waits for them, and re-layouts: 11 us -> none
    pallas_call x0 -> x1, Pallas kernels: none -> 5.79 us  [layouts(): pl.pallas_call(layouts_kernel, name='layouts', out_shape=outs + tuple((ja...]
where the time goes in v5:
time: 512 us; the launch traced here: 507 us
  Pallas kernels  499 us (97%)
    pallas_call x1, Pallas kernels, gather_all(): pl.pallas_call(functools.partial(gather_kernel, count), name='gather_all'...  155 us
    pallas_call x1, Pallas kernels, grad_sum(): pl.pallas_call(functools.partial(grad_sum_kernel, count), name='grad_sum'...  114 us
    pallas_call x1, Pallas kernels, feed_forward(): pl.pallas_call(functools.partial(feed_forward_kernel, count // LINE), nam...  113 us
    pallas_call x1, Pallas kernels, attention_backward(): pl.pallas_call(functools.partial(attention_backward_kernel, count // LINE...  76.2 us
    pallas_call x1, Pallas kernels, attention_forward(): pl.pallas_call(functools.partial(attention_forward_kernel, plane), name='...  34.6 us

profile of v5, /device:TPU:8, one launch (start us, length us, event | category | flops | bytes accessed | tf_op | source)
XLA Modules:
  0.0 507.0 jit_solution(18006290303898171949)
XLA Ops:
  1.3 1.3 fusion.4.gain_ref
  2.6 1.2 fusion
  3.8 154.6 %gather_all.1 = (bf16[16,128,3072]{2,1,0:T(8,128)(2,1)}, bf16[16,128,1024]{2,1,0:T(8,128)(2,1)}, bf16[4,128,1024]{2,1,0:T(8,128)(2,1)}, bf16[4,128,1024]{2,1,0:T...) custom-call(s32[16]{0:T(128)} %len_ref.3, ...), custom_call_target="tpu_custom_call" | custom-call | tf_op jit(solution)/shard_map/gather_all/pallas_call | solution.py:385
  158.3 1.4 convert_bitcast_fusion.gain_ref
  159.7 34.6 %attention_forward.1 = (f32[128,2048]{1,0:T(8,128)}, bf16[128,2048]{1,0:T(8,128)(2,1)}, bf16[256,2048]{1,0:T(8,128)(2,1)}, bf16[256,2048]{1,0:T(8,128)(2,1)}, f3...) custom-call(s32[16]{0:T(128)} %len_ref.3, ...), custom_call_target="tpu_custom_call" | custom-call | tf_op jit(solution)/shard_map/attention_forward/pallas_call | solution.py:1071
  194.3 113.4 %feed_forward.1 = (f32[128,2048]{1,0:T(8,128)}, bf16[4,2,128,2048]{3,2,1,0:T(8,128)(2,1)}, bf16[4,128,2048]{2,1,0:T(8,128)(2,1)}, bf16[4,128,1024]{2,1,0:T(8,128...) custom-call(bf16[128,2048]{1,0:T(8,128)(2,1)} %get-tuple-element.54.h_ref, bf16[1024,2048]{1,0:T(8,128)(2,1)} %bitcast.14, ...), custom_call_target="tpu_custom_call" | custom-call | tf_op jit(solution)/shard_map/feed_forward/pallas_call | solution.py:857
  307.7 76.2 %attention_backward.1 = (bf16[16,128,3072]{2,1,0:T(8,128)(2,1)}, bf16[4,128,3072]{2,1,0:T(8,128)(2,1)}, f32[128,2048]{1,0:T(8,128)}, f32[2,2048]{1,0:T(2,128)}) custom-call(f32[2,2048]{1,0:T(2,128)} %convert_bitcast_fusion.gain_ref, f32[256,128]{1,0:T(8,128)} %get-tuple-element.90.cos_ref, f32[256,128]{1,0:T(8,128)} %get-tuple-element.89.sin_ref, ...), custom_call_target="tpu_custom_call" | custom-call | tf_op jit(solution)/shard_map/attention_backward/pallas_call | solution.py:1329
  383.9 1.4 pad.9.gain_ref
  385.3 114.5 %grad_sum.1 = (f32[128,3072]{1,0:T(8,128)}, bf16[128,2048]{1,0:T(8,128)(2,1)}, f32[8,128]{1,0:T(8,128)}) custom-call(f32[16,8,128]{2,1,0:T(8,128)} %pad.9.gain_ref, f32[128,2048]{1,0:T(8,128)} %get-tuple-element.61.x1_in, bf16[16,128,3072]{2,1,0:T(8,128)(2,1)} %get-tuple-element.71.ga_ref, bf16[4,2,128,2048]{3,2,1,0:T(8,128)(2,1)} %get-tuple-element.72.out_ref), custom_call_target="tpu_custom_call" | custom-call | tf_op jit(solution)/shard_map/grad_sum/pallas_call | solution.py:1508
  499.8 1.3 slice_bitcast_fusion
  501.0 5.8 %layouts.1 = (f32[128,1024]{1,0:T(8,128)}, f32[128,512]{1,0:T(8,128)}, f32[128,512]{1,0:T(8,128)}, f32[1024,128]{1,0:T(8,128)}, f32[128,4096]{1,0:T(8,128)}, /*i...) custom-call(f32[128,3072]{1,0:T(8,128)} %get-tuple-element.73.a_ref, ...), custom_call_target="tpu_custom_call" | custom-call | tf_op jit(solution)/shard_map/layouts/pallas_call | solution.py:1594
  (1 shorter events, 0.0 us)

commit v6 on v5

--- a/solution.py
+++ b/solution.py
@@ -16,7 +16,7 @@
 BF16 = jnp.bfloat16
 F32 = jnp.float32
 MB = 1024 * 1024
-SOON = 1
+SOON = 2
 
 
 def rope_tables(count, head_dim):
@@ -38,6 +38,7 @@
         self.plane = plane
         self.z = lax.div(self.d, plane)
         self.p = lax.rem(self.d, plane)
+        self.h = lax.rem(self.z, 2)
         if plane == 4:
             x = lax.rem(self.p, 2)
             y = lax.div(self.p, 2)
@@ -50,6 +51,9 @@
 
     def sibling(self):
         return (self.d, 1 - self.t)
+
+    def mate(self):
+        return self.at(self.z + 1 - 2 * self.h, self.p)
 
 
 def remote(src, dst, send, recv, device):
@@ -170,6 +174,67 @@
                 copy.wait_send()
 
 
+class Quad:
+    def __init__(self, me, blocks, send, recv):
+        self.me, self.blocks, self.send, self.recv = me, blocks, send, recv
+
+    def copy(self, i, first=None):
+        me = self.me
+        dst = self.blocks.at[me.h if i < 2 else 1 - me.h, me.t]
+        device = me.mate() if i == 1 else me.sibling()
+        return remote(dst if first is None else first, dst, self.send.at[i], self.recv.at[i], device)
+
+    def start(self, first=None):
+        for i in (1, 0):
+            self.copy(i, first).start()
+
+    def forward(self):
+        arrival(self.blocks.at[1 - self.me.h, self.me.t], self.recv.at[1])
+        self.copy(2).start()
+
+    def finish(self):
+        me = self.me
+        arrival(self.blocks.at[me.h, 1 - me.t], self.recv.at[0])
+        arrival(self.blocks.at[1 - me.h, 1 - me.t], self.recv.at[2])
+
+    def finish_sends(self):
+        for i in range(3):
+            self.copy(i).wait_send()
+
+
+class QuadSum:
+    def __init__(self, me, part, from_pair, low, from_mate, send, recv):
+        self.me, self.part, self.from_pair, self.low, self.from_mate = me, part, from_pair, low, from_mate
+        self.pair = remote(part.at[:, 1 - me.t], from_pair, send.at[0], recv.at[0], me.sibling())
+        self.mate = remote(low, from_mate, send.at[1], recv.at[1], me.mate())
+
+    def start(self):
+        self.pair.start()
+
+    def to_mate(self):
+        me = self.me
+        self.pair.wait_recv()
+
+        def act(at):
+            total = self.part[1 - me.h, me.t, at, :] + self.from_pair[1 - me.h, at, :]
+            self.low[at, :] = total.astype(BF16)
+
+        row_loop(self.low.shape[0], 32, act)
+        self.mate.start()
+
+    def wait(self):
+        self.mate.wait_recv()
+
+    def rows(self, at):
+        me = self.me
+        total = self.part[me.h, me.t, at, :] + self.from_pair[me.h, at, :]
+        return total + self.from_mate[at, :].astype(F32)
+
+    def finish_sends(self):
+        self.pair.wait_send()
+        self.mate.wait_send()
+
+
 def copy_in(src, dst, sem):
     return pltpu.make_async_copy(src, dst, sem)
 
@@ -181,42 +246,44 @@
 
 
 def gather_kernel(
-    count, len_ref, seq_ref, q_ref, k_ref, v_ref, o_ref, g_ref, u_ref, d_ref, gain_ref, tok_ref, cot_ref,
-    a_all, gate_all, up_soon, up, down_t, gain_all, tok_all, dm_all, o_v, a_v, g_v, u_v, d_v, d_t, dm, chain_send, chain_recv,
-    part_send, part_recv, plane_send, plane_recv, gain_send, gain_recv, pair_send, pair_recv, local_sem,
+    count, len_ref, seq_ref, gain_ref, q_ref, k_ref, v_ref, o_ref, g_ref, u_ref, d_ref, tok_ref, cot_ref,
+    a_all, gate_all, up_soon, up, down_t, gain_all, tok_all, dm_all, o_v, a_v, g_v, u_v, d_v, d_t, dm,
+    gain_v, chain_send, chain_recv, part_send, part_recv, plane_send, plane_recv, gain_send, gain_recv,
+    pair_send, pair_recv, tok_send, tok_recv, local_sem,
 ):
     plane = count // LINE
     me = Place(plane)
-    rows, q_width = q_ref.shape
-    kv_width = k_ref.shape[1]
+    rows = q_ref.shape[0]
     units = g_ref.shape[1] // LINE
-    qkv_width = q_width + 2 * kv_width
+    q_half, kv_half = q_ref.shape[1] // 2, k_ref.shape[1] // 2
+    qkv_half = q_half + 2 * kv_half
 
     def columns(ref, z):
         return ref.at[:, pl.ds(pl.multiple_of(z * units, units), units)]
 
-    local = [
-        copy_in(o_ref, o_v, local_sem.at[0]),
-        copy_in(q_ref, a_v.at[:, pl.ds(0, q_width)], local_sem.at[1]),
-        copy_in(k_ref, a_v.at[:, pl.ds(q_width, kv_width)], local_sem.at[2]),
-        copy_in(v_ref, a_v.at[:, pl.ds(q_width + kv_width, kv_width)], local_sem.at[3]),
-        copy_in(d_ref, d_v, local_sem.at[4]),
-        copy_in(cot_ref, dm, local_sem.at[5]),
-        copy_in(columns(g_ref, me.z), g_v, local_sem.at[6]),
-        copy_in(columns(u_ref, me.z), u_v, local_sem.at[7]),
-        copy_in(gain_ref, gain_all.at[me.d], local_sem.at[8]),
-        copy_in(tok_ref, tok_all.at[me.t], local_sem.at[9]),
-    ]
-    for copy in local[:4]:
+    local = [copy_in(o_ref, o_v, local_sem.at[0])]
+    for h in range(2):
+        start = 0
+        for ref, width in ((q_ref, q_half), (k_ref, kv_half), (v_ref, kv_half)):
+            src = ref.at[:, pl.ds(h * width, width)]
+            local.append(copy_in(src, a_v.at[h, :, pl.ds(start, width)], local_sem.at[len(local)]))
+            start += width
+    early = len(local)
+    for src, dst in (
+        (d_ref, d_v), (cot_ref, dm), (columns(g_ref, me.z), g_v), (columns(u_ref, me.z), u_v),
+        (tok_ref, tok_all.at[me.h, me.t]),
+    ):
+        local.append(copy_in(src, dst, local_sem.at[len(local)]))
+    for copy in local[:early]:
         copy.start()
-    keep_a = copy_in(a_v, a_all.at[me.d], local_sem.at[10])
-    keep_down = copy_in(d_t, down_t, local_sem.at[11])
-    keep_dm = copy_in(dm, dm_all.at[me.z, me.t], local_sem.at[12])
-    keep_gate = copy_in(g_v, gate_all.at[me.d], local_sem.at[13])
-    keep_up = copy_in(u_v, up.at[me.z], local_sem.at[14])
-
-    attn = Chain(me, a_v, lambda z: a_all.at[z * plane + me.p], chain_send.at[0], chain_recv.at[0])
-    dms = Chain(me, dm, lambda z: dm_all.at[z, me.t], chain_send.at[1], chain_recv.at[1])
+    keep_a = copy_in(a_v.at[me.h], a_all.at[me.d], local_sem.at[12])
+    keep_down = copy_in(d_t, down_t, local_sem.at[13])
+    keep_dm = copy_in(dm, dm_all.at[me.z, me.t], local_sem.at[14])
+    keep_gate = copy_in(g_v, gate_all.at[me.d], local_sem.at[15])
+    keep_up = copy_in(u_v, up.at[me.z], local_sem.at[16])
+    keep_gain = copy_in(gain_v, gain_all.at[me.d], local_sem.at[17])
+
+    dms = Chain(me, dm, lambda z: dm_all.at[z, me.t], chain_send, chain_recv)
     planes = (
         PlaneGather(me, 0, a_all, rows, plane_send, plane_recv),
         PlaneGather(me, 1, gate_all, rows, plane_send, plane_recv),
@@ -225,8 +292,8 @@
 
     def part(way, k, kind):
         _, target = reach(me, 1 - way, k)
-        src = columns((g_ref, u_ref)[kind], target)
-        dst = (gate_all.at[me.d], up.at[me.z])[kind]
+        src = columns((g_ref, u_ref)[kind - 1], target) if kind else a_v.at[lax.rem(target, 2)]
+        dst = (a_all.at[me.d], gate_all.at[me.d], up.at[me.z])[kind]
         return remote(
             src, dst, part_send.at[way, k, kind], part_recv.at[way, k, kind], me.at(target, me.p)
         )
@@ -236,7 +303,7 @@
         return remote(src, dm_all.at[z, me.t], pair_send.at[z], pair_recv.at[z], me.sibling())
 
     def keep_soon(soon, src):
-        return copy_in(src, up_soon.at[soon * plane + me.p], local_sem.at[15 + soon])
+        return copy_in(src, up_soon.at[soon * plane + me.p], local_sem.at[18 + soon])
 
     def start_parts(k, kinds):
         for way in range(2):
@@ -255,14 +322,13 @@
                 act(way, k, z)
 
     def attn_step(way, k, z):
-        attn.wait_block(way, k)
-        attn.start(way, k)
+        arrival(a_all.at[z * plane + me.p], part_recv.at[way, k, 0])
         planes[0].start(z)
 
     def part_step(way, k, z):
-        arrival(gate_all.at[z * plane + me.p], part_recv.at[way, k, 0])
+        arrival(gate_all.at[z * plane + me.p], part_recv.at[way, k, 1])
         planes[1].start(z)
-        arrival(up.at[z], part_recv.at[way, k, 1])
+        arrival(up.at[z], part_recv.at[way, k, 2])
         for soon in range(SOON):
 
             @pl.when(z == soon)
@@ -278,31 +344,35 @@
     def give_gain(step):
         target = lax.rem(me.d + step, count)
         return remote(
-            gain_ref, gain_all.at[me.d], gain_send.at[step], gain_recv.at[step], (target, me.t)
-        )
-
+            gain_v, gain_all.at[me.d], gain_send.at[step], gain_recv.at[step], (target, me.t)
+        )
+
+    chosen = len_ref[seq_ref[0]]
+    kind_of = lax.broadcasted_iota(jnp.int32, gain_ref.shape, 0)
+    gain_v[...] = jnp.where(kind_of == 2, chosen.astype(F32), gain_ref[...].astype(F32)).astype(BF16)
     local[0].wait()
-    a_v[:, qkv_width:] = o_v[...].T
+    for h in range(2):
+        a_v[h, :, qkv_half:] = o_v[h * q_half : (h + 1) * q_half, :].T
     greet_all(me, count)
-    for copy in local[1:4]:
+    for copy in local[1:early]:
         copy.wait()
-    for way in range(2):
-        attn.start(way, 0)
-    planes[0].start(me.z, a_v)
-    for copy in local[4:]:
+    toks = Quad(me, tok_all, tok_send, tok_recv)
+    for k in range(1, LINE):
+        start_parts(k, (0,))
+    planes[0].start(me.z, a_v.at[me.h])
+    toks.start(tok_ref)
+    for step in range(1, count):
+        give_gain(step).start()
+    for copy in local[early:]:
         copy.start()
     keep_a.start()
-    tokens = remote(tok_ref, tok_all.at[me.t], pair_send.at[LINE], pair_recv.at[LINE], me.sibling())
-    tokens.start()
-    for step in range(1, count):
-        give_gain(step).start()
-
-    local[4].wait()
+    keep_gain.start()
+
+    local[early].wait()
     for z in range(LINE):
         d_t[z] = d_v[z * units : (z + 1) * units, :].T
     keep_down.start()
-    local[5].wait()
-    chosen = len_ref[seq_ref[0]]
+    local[early + 1].wait()
 
     def mask(at):
         value = dm[at, :].astype(F32)
@@ -314,10 +384,11 @@
 
     for k in range(1, LINE):
         each(k, attn_step)
-        start_parts(k, (0, 1))
+        start_parts(k, (1,))
         if k == 1:
+            toks.forward()
             planes[0].forward(me.z)
-            for copy in local[6:8]:
+            for copy in local[early + 2 : early + 4]:
                 copy.wait()
             keep_gate.start()
             keep_up.start()
@@ -331,6 +402,8 @@
 
         else:
             each(k - 1, lambda way, k, z: planes[0].forward(z))
+    for k in range(1, LINE):
+        start_parts(k, (2,))
     for way in range(2):
         dms.start(way, 0)
     pair(me.z, dm).start()
@@ -347,26 +420,26 @@
         planes[2].forward(soon)
     each(LINE - 1, dm_step)
 
-    attn.finish()
     dms.finish()
     for k in range(1, LINE):
         for way in range(2):
 
             @pl.when(reach(me, 1 - way, k)[0])
             def _():
-                for kind in range(2):
+                for kind in range(3):
                     part(way, k, kind).wait_send()
 
     for step in range(1, count):
         give_gain(step).wait()
-    tokens.wait()
+    toks.finish()
+    toks.finish_sends()
     for z in range(LINE):
         pair(z).wait()
     for job, zs in zip(planes, (LINE, LINE, SOON)):
         job.finish(range(zs))
     for soon in range(SOON):
         keep_soon(soon, u_v).wait()
-    for copy in local[8:] + [keep_a, keep_down, keep_dm, keep_gate, keep_up]:
+    for copy in local[early + 4 :] + [keep_a, keep_down, keep_dm, keep_gate, keep_up, keep_gain]:
         copy.wait()
 
 
@@ -376,43 +449,45 @@
 DMA = pltpu.SemaphoreType.DMA
 
 
-def gather_all(count, lengths, seq, weights, gains, tokens, cotangent):
+def gather_all(count, lengths, seq, gains, weights, tokens, cotangent):
     w_query, key_weight, _, w_out, w_gate, _, w_down = weights
     rows, q_width = w_query.shape
-    width = 2 * (q_width + key_weight.shape[1])
+    width = q_width + key_weight.shape[1]
     units = w_gate.shape[1] // LINE
-    kinds = max(6, count // LINE - 1)
+    plane = count // LINE
+    kinds = max(6, plane - 1)
     return pl.pallas_call(
         functools.partial(gather_kernel, count),
         name="gather_all",
         out_shape=(
             jax.ShapeDtypeStruct((count, rows, width), BF16),
             jax.ShapeDtypeStruct((count, rows, units), BF16),
-            jax.ShapeDtypeStruct((count // LINE * SOON, rows, units), BF16),
+            jax.ShapeDtypeStruct((plane * SOON, rows, units), BF16),
             jax.ShapeDtypeStruct((LINE, rows, units), BF16),
             jax.ShapeDtypeStruct((LINE, rows, units), BF16),
             jax.ShapeDtypeStruct((count,) + gains.shape, gains.dtype),
-            jax.ShapeDtypeStruct((2,) + tokens.shape, BF16),
+            jax.ShapeDtypeStruct((2, 2) + tokens.shape, BF16),
             jax.ShapeDtypeStruct((LINE, 2) + cotangent.shape, BF16),
         ),
-        in_specs=[SMEM] * 2 + [ANY] * 10,
+        in_specs=[SMEM] * 2 + [VMEM] + [ANY] * 9,
         out_specs=(ANY,) * 8,
         scratch_shapes=[
             pltpu.VMEM(w_out.shape, BF16),
-            pltpu.VMEM((rows, width), BF16),
+            pltpu.VMEM((2, rows, width), BF16),
             pltpu.VMEM((rows, units), BF16),
             pltpu.VMEM((rows, units), BF16),
             pltpu.VMEM(w_down.shape, BF16),
             pltpu.VMEM((LINE, rows, units), BF16),
             pltpu.VMEM(cotangent.shape, BF16),
-            DMA((2, 2, LINE)), DMA((2, 2, LINE)), DMA((2, LINE, 2)), DMA((2, LINE, 2)),
+            pltpu.VMEM(gains.shape, BF16),
+            DMA((2, LINE)), DMA((2, LINE)), DMA((2, LINE, 3)), DMA((2, LINE, 3)),
             DMA((3, LINE, kinds)), DMA((3, LINE, kinds)), DMA((count,)), DMA((count,)),
-            DMA((LINE + 1,)), DMA((LINE + 1,)), DMA((15 + SOON,)),
+            DMA((LINE,)), DMA((LINE,)), DMA((3,)), DMA((3,)), DMA((18 + SOON,)),
         ],
         compiler_params=pltpu.CompilerParams(
             collective_id=0, has_side_effects=True, vmem_limit_bytes=60 * MB
         ),
-    )(lengths, seq, *weights, gains, tokens, cotangent)
+    )(lengths, seq, gains, *weights, tokens, cotangent)
 
 
 RANKS = ((3, 2, 1, 0), (3, 0, 2, 1), (0, 3, 1, 2), (0, 1, 2, 3))
@@ -908,15 +983,16 @@
 
 
 def attention_forward_kernel(
-    plane, len_ref, seq_ref, gain_ref, cos_ref, sin_ref, tok_in, a_ref, up, down_t, x1_out, h2_out, h1_out,
+    plane, gain_ref, lens_ref, cos_ref, sin_ref, tok_in, a_ref, up, down_t, x1_out, h2_out, h1_out,
     qkv_out, probs_out, o_out, up_rest, down, weights, tok_ref, x1_ref, h2_ref, h1_ref, qkv_ref, probs_ref,
-    o_ref, part, from_pair, plane_send, plane_recv, part_send, part_recv, pair_send, pair_recv, load_sem, keep_sem,
+    o_ref, part, from_pair, low, from_mate, plane_send, plane_recv, part_send, part_recv, sum_send,
+    sum_recv, load_sem, keep_sem,
 ):
     me = Place(plane)
-    _, rows, model = tok_ref.shape
+    _, _, rows, model = tok_ref.shape
     wide = 2 * rows
-    heads, _, _ = probs_ref.shape
-    q_width = heads * HEAD_SIZE
+    q_width = o_ref.shape[1]
+    heads = q_width // HEAD_SIZE
     kv_width = (qkv_ref.shape[1] - q_width) // 2
     kv_heads = kv_width // HEAD_SIZE
     half = HEAD_SIZE // 2
@@ -961,12 +1037,12 @@
 
     load_tok.wait()
 
-    for t in range(2):
-
-        def norm(at, t=t):
-            x = tok_ref[t, at, :].astype(F32)
+    for n in range(4):
+
+        def norm(at, n=n):
+            x = tok_ref[n // 2, n % 2, at, :].astype(F32)
             factor = lax.rsqrt(jnp.mean(x * x, -1, keepdims=True) + EPS)
-            h1_ref[pl.ds(t * rows + at.start, at.size), :] = (x * factor * gain_ref[0:1, :]).astype(BF16)
+            h1_ref[pl.ds(n * rows + at.start, at.size), :] = (x * factor * gain_ref[0:1, :]).astype(BF16)
 
         row_loop(rows, 32, norm)
     outs[0].start()
@@ -981,10 +1057,12 @@
     @pl.loop(0, heads + kv_heads)
     def _(i):
         start, values = project(i)
-        first, second = values[:, :half], values[:, half:]
         cos, sin = cos_ref[...], sin_ref[...]
-        qkv_ref[:, pl.ds(start, half)] = (first * cos - second * sin).astype(BF16)
-        qkv_ref[:, pl.ds(start + half, half)] = (second * cos + first * sin).astype(BF16)
+        for n in range(2):
+            at = slice(n * wide, (n + 1) * wide)
+            first, second = values[at, :half], values[at, half:]
+            qkv_ref[at, pl.ds(start, half)] = (first * cos - second * sin).astype(BF16)
+            qkv_ref[at, pl.ds(start + half, half)] = (second * cos + first * sin).astype(BF16)
 
     @pl.loop(heads + kv_heads, heads + 2 * kv_heads)
     def _(i):
@@ -995,40 +1073,44 @@
     gather.forward(0)
     row = lax.broadcasted_iota(jnp.int32, (wide, wide), 0)
     key = lax.broadcasted_iota(jnp.int32, (wide, wide), 1)
-    allowed = jnp.logical_and(key <= row, key < len_ref[seq_ref[0]])
-    for i in range(heads):
-        m = i * kv_heads // heads
-        q = qkv_ref[:, i * HEAD_SIZE : (i + 1) * HEAD_SIZE]
-        k = qkv_ref[:, q_width + m * HEAD_SIZE : q_width + (m + 1) * HEAD_SIZE]
-        v = qkv_ref[:, q_width + kv_width + m * HEAD_SIZE : q_width + kv_width + (m + 1) * HEAD_SIZE]
-        scores = dot_cols(q, k) * HEAD_SIZE ** (-0.5)
-        scores = jnp.where(allowed, scores, -1e30)
-        grown = jnp.exp(scores - jnp.max(scores, -1, keepdims=True))
-        probs = grown / jnp.sum(grown, -1, keepdims=True)
-        probs_ref[i] = probs
-        o_ref[:, i * HEAD_SIZE : (i + 1) * HEAD_SIZE] = jnp.dot(
-            probs.astype(BF16), v, preferred_element_type=F32
-        ).astype(BF16)
+    for n in range(2):
+        length = lens_ref[me.d - me.h * plane + n * plane, 2:3, 0:1].astype(F32)
+        allowed = jnp.logical_and(key <= row, key.astype(F32) < length)
+        at = slice(n * wide, (n + 1) * wide)
+        for i in range(heads):
+            m = i * kv_heads // heads
+            q = qkv_ref[at, i * HEAD_SIZE : (i + 1) * HEAD_SIZE]
+            k = qkv_ref[at, q_width + m * HEAD_SIZE : q_width + (m + 1) * HEAD_SIZE]
+            v_start = q_width + kv_width + m * HEAD_SIZE
+            v = qkv_ref[at, v_start : v_start + HEAD_SIZE]
+            scores = dot_cols(q, k) * HEAD_SIZE ** (-0.5)
+            scores = jnp.where(allowed, scores, -1e30)
+            grown = jnp.exp(scores - jnp.max(scores, -1, keepdims=True))
+            probs = grown / jnp.sum(grown, -1, keepdims=True)
+            probs_ref[n * heads + i] = probs
+            o_ref[at, i * HEAD_SIZE : (i + 1) * HEAD_SIZE] = jnp.dot(
+                probs.astype(BF16), v, preferred_element_type=F32
+            ).astype(BF16)
 
     outs[2].start()
     outs[3].start()
-    gather.forward(1)
     tile = 512
 
     @pl.loop(0, model // tile)
     def _(n):
         here = pl.ds(pl.multiple_of(n * tile, tile), tile)
         value = dot_cols(o_ref[...], rows_of(weights, n, tile, q_width + 2 * kv_width, q_width))
-        part[:, :, here] = value.reshape(2, rows, tile)
-
-    swap = remote(part.at[1 - me.t], from_pair, pair_send, pair_recv, me.sibling())
-    swap.start()
-    for z in range(2, LINE - SOON):
+        part[:, :, :, here] = value.reshape(2, 2, rows, tile)
+
+    total = QuadSum(me, part, from_pair, low, from_mate, sum_send, sum_recv)
+    total.start()
+    for z in range(1, LINE - SOON):
         gather.forward(z)
-    swap.wait_recv()
+    total.to_mate()
+    total.wait()
 
     def add(at):
-        x1 = tok_ref[me.t, at, :].astype(F32) + (part[me.t, at, :] + from_pair[at, :])
+        x1 = tok_ref[me.h, me.t, at, :].astype(F32) + total.rows(at)
         x1_ref[at, :] = x1
         factor = lax.rsqrt(jnp.mean(x1 * x1, -1, keepdims=True) + EPS)
         h2_ref[at, :] = (x1 * factor * gain_ref[1:2, :]).astype(BF16)
@@ -1036,7 +1118,7 @@
     row_loop(rows, 32, add)
     outs[4].start()
     outs[5].start()
-    swap.wait_send()
+    total.finish_sends()
     gather.finish(range(LINE - SOON))
     for k in range(1, LINE):
         for way in range(2):
@@ -1053,20 +1135,18 @@
         copy.wait()
 
 
-def attention_forward(count, heads, lengths, seq, gains, cos, sin, tokens_all, attn_all, up, down_t):
-    _, rows, model = tokens_all.shape
+def attention_forward(count, q_width, kv_width, gains, lens, cos, sin, tokens_all, attn_all, up, down_t):
+    _, _, rows, model = tokens_all.shape
     wide = 2 * rows
-    q_width = heads * HEAD_SIZE
-    qkv_width = attn_all.shape[2] - q_width
     plane = count // LINE
     kinds = max(6, plane - 1)
     outs = (
         jax.ShapeDtypeStruct((rows, model), F32),
         jax.ShapeDtypeStruct((rows, model), BF16),
-        jax.ShapeDtypeStruct((wide, model), BF16),
-        jax.ShapeDtypeStruct((wide, qkv_width), BF16),
-        jax.ShapeDtypeStruct((heads, wide, wide), F32),
-        jax.ShapeDtypeStruct((wide, q_width), BF16),
+        jax.ShapeDtypeStruct((2 * wide, model), BF16),
+        jax.ShapeDtypeStruct((2 * wide, q_width + 2 * kv_width), BF16),
+        jax.ShapeDtypeStruct((2 * q_width // HEAD_SIZE, wide, wide), F32),
+        jax.ShapeDtypeStruct((2 * wide, q_width), BF16),
     )
     return pl.pallas_call(
         functools.partial(attention_forward_kernel, plane),
@@ -1076,34 +1156,38 @@
             jax.ShapeDtypeStruct((count - SOON * plane,) + up.shape[1:], BF16),
             jax.ShapeDtypeStruct(down_t.shape, BF16),
         ),
-        in_specs=[SMEM] * 2 + [VMEM] * 3 + [ANY] * 4,
+        in_specs=[VMEM] * 4 + [ANY] * 4,
         out_specs=(ANY,) * 8,
         scratch_shapes=[
             pltpu.VMEM(attn_all.shape, BF16),
             pltpu.VMEM(tokens_all.shape, BF16),
             *[pltpu.VMEM(out.shape, out.dtype) for out in outs],
+            pltpu.VMEM((2, 2, rows, model), F32),
             pltpu.VMEM((2, rows, model), F32),
-            pltpu.VMEM((rows, model), F32),
-            DMA((1, LINE, kinds)), DMA((1, LINE, kinds)), DMA((2, LINE)), DMA((2, LINE)), DMA, DMA,
-            DMA((3 + LINE,)), DMA((6,)),
+            pltpu.VMEM((rows, model), BF16),
+            pltpu.VMEM((rows, model), BF16),
+            DMA((1, LINE, kinds)), DMA((1, LINE, kinds)), DMA((2, LINE)), DMA((2, LINE)), DMA((2,)),
+            DMA((2,)), DMA((3 + LINE,)), DMA((6,)),
         ],
         compiler_params=pltpu.CompilerParams(
             collective_id=2, has_side_effects=True, vmem_limit_bytes=60 * MB
         ),
-    )(lengths, seq, gains, cos, sin, tokens_all, attn_all, up, down_t)
+    )(gains, lens, cos, sin, tokens_all, attn_all, up, down_t)
 
 
 def attention_backward_kernel(
     plane, gain_ref, cos_ref, sin_ref, total_in, x1_in, dm_in, tok_in, h1_in, qkv_in, probs_in, o_in,
     a_ref, gw_ref, sum_ref, h_in, inner_in, ga_ref, w_out, grad_tokens, gain_parts, weights, own, other, first, second,
-    total_ref, x1_ref, dm_ref, tok_ref, h1_ref, qkv_ref, probs_ref, o_ref, rows_in, inner, gw, dx, da, do, dqkv, dh1, from_pair, first_send, first_recv, second_send, second_recv, load_sem,
-    other_sem, part_send, part_recv, pair_send, pair_recv, a_sem, keep_sem, grad_sem, in_sem,
+    total_ref, x1_ref, dm_ref, tok_ref, h1_ref, qkv_ref, probs_ref, o_ref, rows_in, inner, gw, dx, da, do,
+    dqkv, dh1, from_pair, low, from_mate, first_send, first_recv, second_send, second_recv, load_sem,
+    other_sem, part_send, part_recv, da_send, da_recv, sum_send, sum_recv, a_sem, keep_sem, grad_sem, in_sem,
 ):
     me = Place(plane)
-    _, rows, model = tok_ref.shape
+    rows, model = tok_ref.shape
     block = weights.shape[1]
-    heads, _, _ = probs_ref.shape
-    q_width = heads * HEAD_SIZE
+    q_width = o_ref.shape[1]
+    heads = q_width // HEAD_SIZE
+    seq = 2 * rows
     qkv_width = qkv_ref.shape[1]
     kv_width = (qkv_width - q_width) // 2
     kv_heads = kv_width // HEAD_SIZE
@@ -1118,7 +1202,8 @@
         copy_in(src, dst, in_sem.at[i])
         for i, (src, dst) in enumerate(
             (
-                (total_in, total_ref), (x1_in, x1_ref), (dm_in.at[me.z, me.t], dm_ref), (tok_in, tok_ref),
+                (total_in, total_ref), (x1_in, x1_ref), (dm_in.at[me.z, me.t], dm_ref),
+                (tok_in.at[me.h, me.t], tok_ref),
                 (h1_in, h1_ref), (qkv_in, qkv_ref), (probs_in, probs_ref), (o_in, o_ref),
                 (h_in, rows_in), (inner_in, inner),
             )
@@ -1148,8 +1233,8 @@
         copy_in((own, sum_ref)[kind].at[LINE - 1], w_out.at[me.z, :, spans[kind]], keep_sem.at[kind])
         for kind in range(2)
     ]
-    give_da = remote(da.at[me.t], da.at[me.t], pair_send.at[0], pair_recv.at[0], me.sibling())
-    give_dh1 = remote(dh1.at[1 - me.t], from_pair, pair_send.at[1], pair_recv.at[1], me.sibling())
+    das = Quad(me, da, da_send, da_recv)
+    dh1_sum = QuadSum(me, dh1, from_pair, low, from_mate, sum_send, sum_recv)
 
     def mid_norm():
         gain_parts[...] = jnp.zeros_like(gain_parts)
@@ -1162,55 +1247,58 @@
                 factor * scaled - x * factor**3 * jnp.mean(scaled * x, -1, keepdims=True)
             )
             dx[at, :] = grad
-            da[me.t, at, :] = grad.astype(BF16)
+            da[me.h, me.t, at, :] = grad.astype(BF16)
             gain_parts[1:2, :] += jnp.sum(up * x * factor, 0, keepdims=True)
 
         row_loop(rows, 32, act)
-        give_da.start()
+        das.start()
 
     def grad_o():
         load.wait()
-        give_da.wait_recv()
+        das.finish()
 
         @pl.loop(0, q_width // HEAD_SIZE)
         def _(c):
             here = pl.multiple_of(c * HEAD_SIZE, HEAD_SIZE)
             value = jnp.dot(
-                da[...].reshape(2 * rows, model),
+                da[...].reshape(2 * seq, model),
                 columns_of(weights, qkv_width + here, HEAD_SIZE),
                 preferred_element_type=F32,
             )
             do[:, pl.ds(here, HEAD_SIZE)] = value.astype(BF16)
 
-    def rotate(values, start):
+    def rotate(values, rows_at, start):
         first, second = values[:, :half], values[:, half:]
         cos, sin = cos_ref[...], sin_ref[...]
-        dqkv[:, start : start + half] = (first * cos + second * sin).astype(BF16)
-        dqkv[:, start + half : start + 2 * half] = (second * cos - first * sin).astype(BF16)
-
-    def grad_heads():
+        dqkv[rows_at, start : start + half] = (first * cos + second * sin).astype(BF16)
+        dqkv[rows_at, start + half : start + 2 * half] = (second * cos - first * sin).astype(BF16)
+
+    def grad_heads(n):
         group = heads // kv_heads
+        here = slice(n * seq, (n + 1) * seq)
         for m in range(kv_heads):
             at_k = q_width + m * HEAD_SIZE
             at_v = at_k + kv_width
-            k = qkv_ref[:, at_k : at_k + HEAD_SIZE]
-            v = qkv_ref[:, at_v : at_v + HEAD_SIZE]
+            k = qkv_ref[here, at_k : at_k + HEAD_SIZE]
+            v = qkv_ref[here, at_v : at_v + HEAD_SIZE]
             grad_k = grad_v = None
             for i in range(m * group, (m + 1) * group):
                 at = slice(i * HEAD_SIZE, (i + 1) * HEAD_SIZE)
-                probs = probs_ref[i]
-                grad_probs = dot_cols(do[:, at], v)
+                probs = probs_ref[n * heads + i]
+                grad_probs = dot_cols(do[here, at], v)
                 grad_scores = probs * (
                     grad_probs - jnp.sum(probs * grad_probs, -1, keepdims=True)
                 )
-                low = grad_scores.astype(BF16)
-                rotate(jnp.dot(low, k, preferred_element_type=F32) * scale, i * HEAD_SIZE)
-                more_k = dot_tn(low, qkv_ref[:, at])
-                more_v = dot_tn(probs.astype(BF16), do[:, at])
+                low_scores = grad_scores.astype(BF16)
+                rotate(
+                    jnp.dot(low_scores, k, preferred_element_type=F32) * scale, here, i * HEAD_SIZE
+                )
+                more_k = dot_tn(low_scores, qkv_ref[here, at])
+                more_v = dot_tn(probs.astype(BF16), do[here, at])
                 grad_k = more_k if grad_k is None else grad_k + more_k
                 grad_v = more_v if grad_v is None else grad_v + more_v
-            rotate(grad_k * scale, at_k)
-            dqkv[:, at_v : at_v + HEAD_SIZE] = grad_v.astype(BF16)
+            rotate(grad_k * scale, here, at_k)
+            dqkv[here, at_v : at_v + HEAD_SIZE] = grad_v.astype(BF16)
 
     tile = 512
 
@@ -1219,9 +1307,9 @@
         def _(n):
             here = pl.ds(pl.multiple_of(n * tile, tile), tile)
             value = dot_cols(dqkv[...], rows_of(weights, n, tile, 0, qkv_width))
-            dh1[:, :, here] = value.reshape(2, rows, tile)
-
-        give_dh1.start()
+            dh1[:, :, :, here] = value.reshape(2, 2, rows, tile)
+
+        dh1_sum.start()
 
     def keep_grads(n):
         per = tile // block
@@ -1239,7 +1327,7 @@
                 at = slice(c * tile, (c + 1) * tile)
                 value = jnp.dot(left, dqkv[:, at], preferred_element_type=F32)
                 weights[there, :, at] = value.astype(BF16).reshape(tile // block, block, tile)
-            left = da[:, :, here].reshape(2 * rows, tile).T
+            left = da[:, :, :, here].reshape(2 * seq, tile).T
             for c in range(q_width // tile):
                 at = slice(c * tile, (c + 1) * tile)
                 value = jnp.dot(left, o_ref[:, at], preferred_element_type=F32)
@@ -1250,11 +1338,11 @@
             keep_grads(n).start()
 
     def in_norm():
-        give_dh1.wait_recv()
+        dh1_sum.wait()
 
         def act(at):
-            x = tok_ref[me.t, at, :].astype(F32)
-            up = dh1[me.t, at, :] + from_pair[at, :]
+            x = tok_ref[at, :].astype(F32)
+            up = dh1_sum.rows(at)
             factor = lax.rsqrt(jnp.mean(x * x, -1, keepdims=True) + EPS)
             scaled = up * gain_ref[0:1, :]
             grad_tokens[at, :] = dx[at, :] + (
@@ -1281,21 +1369,32 @@
     for copy in ins[8:]:
         copy.wait()
     mlp_grads(1)
-    grad_o()
+    summed.middle(0)
+    summed.begin(1)
+    das.forward()
+    mlp_grads(2)
     for copy in ins[3:8]:
         copy.wait()
-    stages = (
-        [grad_heads, lambda: mlp_grads(2)], [grad_h1, lambda: mlp_grads(3)], [grads], [in_norm],
-    )
-    for rank in range(LINE):
-        summed.middle(rank)
-        if rank + 1 < LINE:
-            summed.begin(rank + 1)
-        for stage in stages[rank]:
-            stage()
-        summed.end(rank)
-        if rank < LINE - 1:
-            part(rank, 0).start()
+    grad_o()
+    grad_heads(0)
+    grad_heads(1)
+    summed.end(0)
+    part(0, 0).start()
+    grad_h1()
+    summed.middle(1)
+    summed.begin(2)
+    dh1_sum.to_mate()
+    mlp_grads(3)
+    summed.end(1)
+    part(1, 0).start()
+    grads()
+    summed.middle(2)
+    summed.begin(3)
+    in_norm()
+    summed.end(2)
+    part(2, 0).start()
+    summed.middle(3)
+    summed.end(3)
 
     keeps[0].start()
     for kind in range(2):
@@ -1308,8 +1407,8 @@
                 arrival(w_out.at[me.z, :, spans[kind]], part_recv.at[way, k, kind])
 
     summed.finish()
-    give_da.wait_send()
-    give_dh1.wait_send()
+    das.finish_sends()
+    dh1_sum.finish_sends()
     for n in range(model // tile):
         keep_grads(n).wait()
     for copy in keeps:
@@ -1320,18 +1419,15 @@
     count, gains, cos, sin, total, x1, dm_all, tokens_all, h1, qkv, probs, o, attn_all, grad_mlp, first_sum, rows_in,
     inner,
 ):
-    _, rows, model = tokens_all.shape
-    _, block, width = attn_all.shape
-    wide = 2 * rows
-    heads = probs.shape[0]
-    q_width = heads * HEAD_SIZE
+    _, _, rows, model = tokens_all.shape
+    _, block, _ = attn_all.shape
     buffers, sems = PlaneSum.scratch(count, block, grad_mlp.shape[2])
     return pl.pallas_call(
         functools.partial(attention_backward_kernel, count // LINE),
         name="attention_backward",
         out_shape=(
             jax.ShapeDtypeStruct(attn_all.shape, BF16),
-            jax.ShapeDtypeStruct((LINE, block, width), BF16),
+            jax.ShapeDtypeStruct((LINE, block, grad_mlp.shape[2] + first_sum.shape[2]), BF16),
             jax.ShapeDtypeStruct((rows, model), F32),
             jax.ShapeDtypeStruct((2, model), F32),
         ),
@@ -1342,17 +1438,19 @@
             *buffers,
             *[
                 pltpu.VMEM(ref.shape, ref.dtype)
-                for ref in (total, x1, dm_all[0, 0], tokens_all, h1, qkv, probs, o, rows_in, inner)
+                for ref in (total, x1, dm_all[0, 0], dm_all[0, 0], h1, qkv, probs, o, rows_in, inner)
             ],
             pltpu.VMEM(((LINE - 1) * grad_mlp.shape[0],) + grad_mlp.shape[1:], BF16),
             pltpu.VMEM((rows, model), F32),
-            pltpu.VMEM((2, rows, model), BF16),
-            pltpu.VMEM((wide, q_width), BF16),
+            pltpu.VMEM((2, 2, rows, model), BF16),
+            pltpu.VMEM(o.shape, BF16),
             pltpu.VMEM(qkv.shape, BF16),
+            pltpu.VMEM((2, 2, rows, model), F32),
             pltpu.VMEM((2, rows, model), F32),
-            pltpu.VMEM((rows, model), F32),
+            pltpu.VMEM((rows, model), BF16),
+            pltpu.VMEM((rows, model), BF16),
             *sems,
-            DMA((2, LINE, 2)), DMA((2, LINE, 2)), DMA((2,)), DMA((2,)), DMA, DMA((2,)),
+            DMA((2, LINE, 2)), DMA((2, LINE, 2)), DMA((3,)), DMA((3,)), DMA((2,)), DMA((2,)), DMA, DMA((2,)),
             DMA((model // 512,)), DMA((10,)),
         ],
         compiler_params=pltpu.CompilerParams(
@@ -1363,12 +1461,12 @@
 
 def grad_sum_kernel(
     count, gain_ref, x1_in, ga_ref, out_ref, a_out, output, gain_out, own, other, first, second, x1_ref,
-    from_line, out_own, out_pair, out_line, gain_in, gain_pair, first_send, first_recv, second_send, second_recv,
-    load_sem, other_sem, line_send, line_recv, out_send, out_recv, load_out_sem, pair_send, pair_recv, gain_send, gain_recv,
+    landed, out_own, out_pair, out_line, gain_in, gain_pair, first_send, first_recv, second_send, second_recv,
+    load_sem, other_sem, part_send, part_recv, out_send, out_recv, load_out_sem, pair_send, pair_recv, gain_send, gain_recv,
 ):
     plane = count // LINE
     me = Place(plane)
-    rows = a_out.shape[0]
+    rows = a_out.shape[1]
     summed = PlaneSum(
         me, ga_ref, own, other, first, second,
         (first_send, first_recv, second_send, second_recv, load_sem, other_sem),
@@ -1410,7 +1508,14 @@
             for rank in range(LINE - 1):
                 self.pass_on(rank).wait_send()
 
-    grads = Line(lambda rank: own.at[rank], from_line, line_send, line_recv)
+    def part(rank):
+        target = ranked(me, rank)
+        way, k = way_to(me, target)
+        return remote(
+            own.at[rank], landed.at[me.z], part_send.at[way, k], part_recv.at[way, k],
+            me.at(target, me.p),
+        )
+
     outs = Line(lambda rank: out_own.at[ranked(me, rank)], out_line, out_send, out_recv)
     summed.load_all()
     load_out = copy_in(out_ref.at[:, me.t], out_own, load_out_sem.at[0])
@@ -1480,24 +1585,30 @@
             gain_out[...] = gain_pair[0] + gain_pair[1]
         summed.end(rank)
         if rank < LINE - 1:
-
-            @pl.when(at_end)
-            def _():
-                grads.step(rank)
-
+            part(rank).start()
         if 0 < rank < LINE - 1:
             @pl.when(jnp.logical_not(at_end))
             def _():
                 for late in (range(rank - 1, rank) if rank < LINE - 2 else range(rank - 1, LINE - 1)):
                     outs.step(late)
-                    grads.step(late)
-
-    add_rows(a_out, (own.at[LINE - 1],), rows)
-    grads.total(lambda landed: add_rows(a_out, (a_out, landed), rows))
+
+    keep = copy_in(own.at[LINE - 1], landed.at[me.z], load_out_sem.at[2])
+    keep.start()
+    for way, k in FAR_FIRST:
+        have, z = reach(me, way, k)
+
+        @pl.when(have)
+        def _():
+            arrival(landed.at[z], part_recv.at[way, k])
+
+    keep.wait()
+    for h in range(2):
+        add_rows(a_out.at[h], tuple(landed.at[z] for z in range(h, LINE, 2)), rows)
+    for rank in range(LINE - 1):
+        part(rank).wait_send()
     for copy in pairs:
         copy.wait_send()
     outs.finish()
-    grads.finish()
     summed.finish()
 
 
@@ -1509,7 +1620,7 @@
         functools.partial(grad_sum_kernel, count),
         name="grad_sum",
         out_shape=(
-            jax.ShapeDtypeStruct((block, width), F32),
+            jax.ShapeDtypeStruct((2, block, width), F32),
             jax.ShapeDtypeStruct((rows, model), BF16),
             jax.ShapeDtypeStruct(gains.shape[1:], F32),
         ),
@@ -1518,14 +1629,14 @@
         scratch_shapes=[
             *buffers,
             pltpu.VMEM((rows, model), F32),
-            pltpu.VMEM((2, LINE - 1, block, width), BF16),
+            pltpu.VMEM((LINE, block, width), BF16),
             pltpu.VMEM((LINE, rows, model), BF16),
             pltpu.VMEM((LINE, rows, model), BF16),
             pltpu.VMEM((2, LINE - 1, rows, model), BF16),
             pltpu.VMEM(gains.shape, F32),
             pltpu.VMEM((2,) + gains.shape[1:], F32),
             *sems,
-            DMA((2, LINE)), DMA((2, LINE)), DMA((2, LINE)), DMA((2, LINE)), DMA((2,)), DMA((LINE,)),
+            DMA((2, LINE)), DMA((2, LINE)), DMA((2, LINE)), DMA((2, LINE)), DMA((3,)), DMA((LINE,)),
             DMA((LINE,)), DMA((count,)), DMA((count,)),
         ],
         compiler_params=pltpu.CompilerParams(
@@ -1569,17 +1680,21 @@
     give(output_v, output_out)
     start = 0
     for src, dst in ((q_v, q_out), (k_v, k_out), (v_v, v_out)):
-        src[...] = a_v[:, start : start + src.shape[1]]
-        start += src.shape[1]
+        half = src.shape[1] // 2
+        for h in range(2):
+            src[:, h * half : (h + 1) * half] = a_v[h, :, start : start + half]
+        start += half
         give(src, dst)
-    o_v[...] = a_v[:, start:].T
+    half = o_v.shape[0] // 2
+    for h in range(2):
+        o_v[h * half : (h + 1) * half, :] = a_v[h, :, start:].T
     give(o_v, o_out)
     for copy in sent:
         copy.wait()
 
 
 def layouts(q_width, kv_width, a, mlp, output, grad_tokens):
-    block = a.shape[0]
+    block = a.shape[1]
     hidden = LINE * (mlp.shape[2] // 3)
     outs = (
         jax.ShapeDtypeStruct((block, q_width), F32),
@@ -1617,13 +1732,13 @@
     lanes = -rows % 128
     gains = jnp.pad(jnp.stack([gain_attn, gain_mlp]), ((0, 14), (0, lanes)))
     attn_all, gate_all, up_soon, up, down_t, gains_all, tokens_all, dm_all = gather_all(
-        count, lengths, seq_of_group,
-        (w_query, key_weight, value_weight, w_out, w_gate, w_up, w_down), gains, tokens, cotangent,
+        count, lengths, seq_of_group, gains,
+        (w_query, key_weight, value_weight, w_out, w_gate, w_up, w_down), tokens, cotangent,
     )
     gains_full = gains_all[:, :2, :rows].transpose(1, 0, 2).reshape(2, model).astype(F32)
     x1, h2, h1, qkv, probs, attended, up_rest, down = attention_forward(
-        count, q_width // HEAD_SIZE, lengths, seq_of_group, gains_full, cos, sin, tokens_all, attn_all,
-        up, down_t,
+        count, q_width // 2, kv_width // 2, gains_full, gains_all, cos, sin, tokens_all, attn_all, up,
+        down_t,
     )
     grad_h2, out_parts, grad_mlp_w, down_sum, rows_in, inner = feed_forward(
         count, h2, dm_all.reshape(-1, model), gate_all, up_soon, up_rest, down

time: 512 us -> 477 us (0.932)
  Pallas kernels: 499 us -> 463 us
    pallas_call x1, Pallas kernels: 155 us -> 124 us  [gather_all(): pl.pallas_call(functools.partial(gather_kernel, count), name='gather_all'...]
    pallas_call x1, Pallas kernels: 114 us -> 84.3 us  [grad_sum(): pl.pallas_call(functools.partial(grad_sum_kernel, count), name='grad_sum'...]
    pallas_call x1, Pallas kernels: 76.2 us -> 91.7 us  [attention_backward(): pl.pallas_call(functools.partial(attention_backward_kernel, count // LINE...]
    pallas_call x1, Pallas kernels: 34.6 us -> 42.6 us  [attention_forward(): pl.pallas_call(functools.partial(attention_forward_kernel, plane), name='...]
where the time goes in v6:
time: 477 us; the launch traced here: 471 us
  Pallas kernels  463 us (97%)
    pallas_call x1, Pallas kernels, gather_all(): pl.pallas_call(functools.partial(gather_kernel, count), name='gather_all'...  124 us
    pallas_call x1, Pallas kernels, feed_forward(): pl.pallas_call(functools.partial(feed_forward_kernel, count // LINE), nam...  114 us
    pallas_call x1, Pallas kernels, attention_backward(): pl.pallas_call(functools.partial(attention_backward_kernel, count // LINE...  91.7 us
    pallas_call x1, Pallas kernels, grad_sum(): pl.pallas_call(functools.partial(grad_sum_kernel, count), name='grad_sum'...  84.3 us
    pallas_call x1, Pallas kernels, attention_forward(): pl.pallas_call(functools.partial(attention_forward_kernel, plane), name='...  42.6 us

profile of v6, /device:TPU:8, one launch (start us, length us, event | category | flops | bytes accessed | tf_op | source)
XLA Modules:
  0.0 471.0 jit_solution(609498793598657871)
XLA Ops:
  1.3 1.3 fusion.4.gain_ref
  2.6 1.2 fusion
  3.8 124.0 %gather_all.1 = (bf16[16,128,1536]{2,1,0:T(8,128)(2,1)}, bf16[16,128,1024]{2,1,0:T(8,128)(2,1)}, bf16[8,128,1024]{2,1,0:T(8,128)(2,1)}, bf16[4,128,1024]{2,1,0:T...) custom-call(s32[16]{0:T(128)} %len_ref.1, ...), custom_call_target="tpu_custom_call" | custom-call | tf_op jit(solution)/shard_map/gather_all/pallas_call | solution.py:459
  127.8 1.4 convert_bitcast_fusion.gain_ref
  129.2 42.6 %attention_forward.1 = (f32[128,2048]{1,0:T(8,128)}, bf16[128,2048]{1,0:T(8,128)(2,1)}, bf16[512,2048]{1,0:T(8,128)(2,1)}, bf16[512,1024]{1,0:T(8,128)(2,1)}, f3...) custom-call(f32[2,2048]{1,0:T(2,128)} %convert_bitcast_fusion.gain_r, ...), custom_call_target="tpu_custom_call" | custom-call | tf_op jit(solution)/shard_map/attention_forward/pallas_call | solution.py:1151
  171.8 114.5 %feed_forward.1 = (f32[128,2048]{1,0:T(8,128)}, bf16[4,2,128,2048]{3,2,1,0:T(8,128)(2,1)}, bf16[4,128,2048]{2,1,0:T(8,128)(2,1)}, bf16[4,128,1024]{2,1,0:T(8,128...) custom-call(bf16[128,2048]{1,0:T(8,128)(2,1)} %get-tuple-element.54.h_ref, bf16[1024,2048]{1,0:T(8,128)(2,1)} %bitcast.14, ...), custom_call_target="tpu_custom_call" | custom-call | tf_op jit(solution)/shard_map/feed_forward/pallas_call | solution.py:932
  286.3 91.7 %attention_backward.1 = (bf16[16,128,1536]{2,1,0:T(8,128)(2,1)}, bf16[4,128,3072]{2,1,0:T(8,128)(2,1)}, f32[128,2048]{1,0:T(8,128)}, f32[2,2048]{1,0:T(2,128)}) custom-call(f32[2,2048]{1,0:T(2,128)} %convert_bitcast_fusion.gain_ref, f32[256,128]{1,0:T(8,128)} %get-tuple-element.90.cos_ref, f32[256,128]{1,0:T(8,128)} %get-tuple-element.89.sin_ref, ...), custom_call_target="tpu_custom_call" | custom-call | tf_op jit(solution)/shard_map/attention_backward/pallas_call | solution.py:1425
  378.0 1.4 pad.9.gain_ref
  379.4 84.3 %grad_sum.1 = (f32[2,128,1536]{2,1,0:T(8,128)}, bf16[128,2048]{1,0:T(8,128)(2,1)}, f32[8,128]{1,0:T(8,128)}) custom-call(f32[16,8,128]{2,1,0:T(8,128)} %pad.9.gain_ref, f32[128,2048]{1,0:T(8,128)} %get-tuple-element.61.x1_in, bf16[16,128,1536]{2,1,0:T(8,128)(2,1)} %get-tuple-element.71.ga_ref, bf16[4,2,128,2048]{3,2,1,0:T(8,128)(2,1)} %get-tuple-element.72.out_ref), custom_call_target="tpu_custom_call" | custom-call | tf_op jit(solution)/shard_map/grad_sum/pallas_call | solution.py:1619
  463.7 1.3 slice_bitcast_fusion
  465.0 5.8 %layouts.1 = (f32[128,1024]{1,0:T(8,128)}, f32[128,512]{1,0:T(8,128)}, f32[128,512]{1,0:T(8,128)}, f32[1024,128]{1,0:T(8,128)}, f32[128,4096]{1,0:T(8,128)}, /*i...) custom-call(f32[2,128,1536]{2,1,0:T(8,128)} %get-tuple-element.73.a_ref, ...), custom_call_target="tpu_custom_call" | custom-call | tf_op jit(solution)/shard_map/layouts/pallas_call | solution.py:1709
  (1 shorter events, 0.0 us)

commit v7 on v6

--- a/solution.py
+++ b/solution.py
@@ -3,6 +3,7 @@
 
 import jax
 import jax.numpy as jnp
+import numpy as np
 from jax import lax
 from jax.experimental import pallas as pl
 from jax.experimental.pallas import tpu as pltpu
@@ -16,15 +17,16 @@
 BF16 = jnp.bfloat16
 F32 = jnp.float32
 MB = 1024 * 1024
+AHEAD = 4
 SOON = 2
 
 
 def rope_tables(count, head_dim):
     half = head_dim // 2
-    index = jnp.arange(half, dtype=jnp.float32)
-    freqs = jnp.exp(index * (-2.0 * math.log(THETA) / head_dim))
-    angles = jnp.arange(count, dtype=jnp.float32)[:, None] * freqs[None, :]
-    return jnp.cos(angles), jnp.sin(angles)
+    index = np.arange(half, dtype=np.float32)
+    freqs = np.exp(index * np.float32(-2.0 * math.log(THETA) / head_dim))
+    angles = np.arange(count, dtype=np.float32)[:, None] * freqs[None, :]
+    return np.cos(angles), np.sin(angles)
 
 
 def dot_tn(left, right):
@@ -205,15 +207,21 @@
 class QuadSum:
     def __init__(self, me, part, from_pair, low, from_mate, send, recv):
         self.me, self.part, self.from_pair, self.low, self.from_mate = me, part, from_pair, low, from_mate
-        self.pair = remote(part.at[:, 1 - me.t], from_pair, send.at[0], recv.at[0], me.sibling())
-        self.mate = remote(low, from_mate, send.at[1], recv.at[1], me.mate())
-
-    def start(self):
-        self.pair.start()
+        self.send, self.recv = send, recv
+        self.mate = remote(low, from_mate, send.at[2], recv.at[2], me.mate())
+
+    def pair(self, h):
+        me = self.me
+        return remote(
+            self.part.at[h, 1 - me.t], self.from_pair.at[h], self.send.at[h], self.recv.at[h], me.sibling()
+        )
+
+    def start(self, h):
+        self.pair(h).start()
 
     def to_mate(self):
         me = self.me
-        self.pair.wait_recv()
+        self.pair(1 - me.h).wait_recv()
 
         def act(at):
             total = self.part[1 - me.h, me.t, at, :] + self.from_pair[1 - me.h, at, :]
@@ -223,6 +231,7 @@
         self.mate.start()
 
     def wait(self):
+        self.pair(self.me.h).wait_recv()
         self.mate.wait_recv()
 
     def rows(self, at):
@@ -231,7 +240,8 @@
         return total + self.from_mate[at, :].astype(F32)
 
     def finish_sends(self):
-        self.pair.wait_send()
+        for h in range(2):
+            self.pair(h).wait_send()
         self.mate.wait_send()
 
 
@@ -325,20 +335,20 @@
         arrival(a_all.at[z * plane + me.p], part_recv.at[way, k, 0])
         planes[0].start(z)
 
-    def part_step(way, k, z):
+    def gate_step(way, k, z):
         arrival(gate_all.at[z * plane + me.p], part_recv.at[way, k, 1])
         planes[1].start(z)
+
+    def up_step(way, k, z):
         arrival(up.at[z], part_recv.at[way, k, 2])
-        for soon in range(SOON):
-
-            @pl.when(z == soon)
-            def _():
-                planes[2].start(soon, up.at[soon])
-                keep_soon(soon, up.at[soon]).start()
+
+        @pl.when(z == me.z + 1 - 2 * me.h)
+        def _():
+            planes[2].start(1 - me.h, up.at[z])
+            keep_soon(1 - me.h, up.at[z]).start()
 
     def dm_step(way, k, z):
         dms.wait_block(way, k)
-        dms.start(way, k)
         pair(z).start()
 
     def give_gain(step):
@@ -357,8 +367,27 @@
     for copy in local[1:early]:
         copy.wait()
     toks = Quad(me, tok_all, tok_send, tok_recv)
-    for k in range(1, LINE):
-        start_parts(k, (0,))
+    levels = [(0, 1), (0, 2), (0, 3), (3, 1), (1, 1), (1, 2), (1, 3), (3, 2), (2, 1), (2, 2), (2, 3), (3, 3)]
+
+    def start_level(kind, k):
+        if kind < 3:
+            start_parts(k, (kind,))
+        elif k == 1:
+            for way in range(2):
+                dms.start(way, 0)
+            pair(me.z, dm).start()
+        else:
+            each(k - 1, lambda way, k, z: dms.start(way, k))
+
+    def finish_level(kind, k):
+        each(k, (attn_step, gate_step, up_step, dm_step)[kind])
+
+    def forward_level(kind, k):
+        if kind < 2:
+            each(k, lambda way, k, z: planes[kind].forward(z))
+
+    for level in levels[:2]:
+        start_level(*level)
     planes[0].start(me.z, a_v.at[me.h])
     toks.start(tok_ref)
     for step in range(1, count):
@@ -382,10 +411,14 @@
     row_loop(dm.shape[0], 32, mask)
     keep_dm.start()
 
-    for k in range(1, LINE):
-        each(k, attn_step)
-        start_parts(k, (1,))
-        if k == 1:
+    for i, level in enumerate(levels):
+        if i == 0:
+            for more in levels[2:AHEAD]:
+                start_level(*more)
+        finish_level(*level)
+        if i + AHEAD < len(levels):
+            start_level(*levels[i + AHEAD])
+        if level == (0, 1):
             toks.forward()
             planes[0].forward(me.z)
             for copy in local[early + 2 : early + 4]:
@@ -393,32 +426,16 @@
             keep_gate.start()
             keep_up.start()
             planes[1].start(me.z, g_v)
-            for soon in range(SOON):
-
-                @pl.when(me.z == soon)
-                def _():
-                    planes[2].start(soon, u_v)
-                    keep_soon(soon, u_v).start()
-
-        else:
-            each(k - 1, lambda way, k, z: planes[0].forward(z))
-    for k in range(1, LINE):
-        start_parts(k, (2,))
-    for way in range(2):
-        dms.start(way, 0)
-    pair(me.z, dm).start()
-    for k in range(1, LINE):
-        each(k, part_step)
-        if k == 1:
-            each(LINE - 1, lambda way, k, z: planes[0].forward(z))
+        if level == (0, 3):
             planes[1].forward(me.z)
-        else:
-            each(k - 1, lambda way, k, z: planes[1].forward(z))
-            each(k - 1, dm_step)
-    each(LINE - 1, lambda way, k, z: planes[1].forward(z))
-    for soon in range(SOON):
-        planes[2].forward(soon)
-    each(LINE - 1, dm_step)
+        if level == (1, 3):
+            planes[2].start(me.h, u_v)
+            keep_soon(me.h, u_v).start()
+        if level == (3, 3):
+            planes[2].forward(me.h)
+        if i:
+            forward_level(*levels[i - 1])
+    planes[2].forward(1 - me.h)
 
     dms.finish()
     for k in range(1, LINE):
@@ -690,9 +707,12 @@
 
     loads = [
         copy_in(gate_ref, weights.at[:, :, pl.ds(0, units)], load_sem.at[0]),
-        copy_in(up_soon, weights.at[pl.ds(0, soon), :, pl.ds(units, units)], load_sem.at[2]),
         copy_in(
-            up_rest, weights.at[pl.ds(soon, up_rest.shape[0]), :, pl.ds(units, units)], load_sem.at[3]
+            up_soon, weights.at[pl.ds((me.z - me.h) * plane, soon), :, pl.ds(units, units)], load_sem.at[2]
+        ),
+        copy_in(
+            up_rest, weights.at[pl.ds((SOON - me.z + me.h) * plane, soon), :, pl.ds(units, units)],
+            load_sem.at[3],
         ),
     ]
     own_down = [
@@ -983,7 +1003,7 @@
 
 
 def attention_forward_kernel(
-    plane, gain_ref, lens_ref, cos_ref, sin_ref, tok_in, a_ref, up, down_t, x1_out, h2_out, h1_out,
+    plane, lens_ref, cos_ref, sin_ref, tok_in, a_ref, up, down_t, gain_ref, x1_out, h2_out, h1_out,
     qkv_out, probs_out, o_out, up_rest, down, weights, tok_ref, x1_ref, h2_ref, h1_ref, qkv_ref, probs_ref,
     o_ref, part, from_pair, low, from_mate, plane_send, plane_recv, part_send, part_recv, sum_send,
     sum_recv, load_sem, keep_sem,
@@ -1000,9 +1020,10 @@
     load_tok.start()
     load = copy_in(a_ref, weights, load_sem.at[1])
     load.start()
+    far = SOON - (me.z - me.h)
     keep = [
-        copy_in(up.at[z], up_rest.at[(z - SOON) * plane + me.p], load_sem.at[2 + z])
-        for z in range(SOON, LINE)
+        copy_in(up.at[far + z], up_rest.at[z * plane + me.p], load_sem.at[2 + z])
+        for z in range(LINE - SOON)
     ]
     keep.append(copy_in(down_t.at[me.z], down.at[me.z], load_sem.at[2 + LINE]))
     for copy in keep:
@@ -1019,7 +1040,7 @@
     greet_all(me, plane * LINE)
     gather = PlaneGather(me, 0, up_rest, up.shape[1], plane_send, plane_recv)
     for z in range(LINE - SOON):
-        gather.start(z, up.at[z + SOON])
+        gather.start(z, up.at[far + z])
 
     def give_down(way, k):
         _, target = reach(me, 1 - way, k)
@@ -1035,6 +1056,9 @@
             def _():
                 give_down(way, k).start()
 
+    span = model // (plane * LINE)
+    for d in range(plane * LINE):
+        gain_ref[:, d * span : (d + 1) * span] = lens_ref[d, 0:2, :span].astype(F32)
     load_tok.wait()
 
     for n in range(4):
@@ -1073,10 +1097,13 @@
     gather.forward(0)
     row = lax.broadcasted_iota(jnp.int32, (wide, wide), 0)
     key = lax.broadcasted_iota(jnp.int32, (wide, wide), 1)
-    for n in range(2):
-        length = lens_ref[me.d - me.h * plane + n * plane, 2:3, 0:1].astype(F32)
+    tile = 512
+    total = QuadSum(me, part, from_pair, low, from_mate, sum_send, sum_recv)
+
+    def attend(n):
+        length = lens_ref[me.d + (n - me.h) * plane, 2:3, 0:1].astype(F32)
         allowed = jnp.logical_and(key <= row, key.astype(F32) < length)
-        at = slice(n * wide, (n + 1) * wide)
+        at = pl.ds(pl.multiple_of(n * wide, wide), wide)
         for i in range(heads):
             m = i * kv_heads // heads
             q = qkv_ref[at, i * HEAD_SIZE : (i + 1) * HEAD_SIZE]
@@ -1092,21 +1119,21 @@
                 probs.astype(BF16), v, preferred_element_type=F32
             ).astype(BF16)
 
+        @pl.loop(0, model // tile)
+        def _(c):
+            here = pl.ds(pl.multiple_of(c * tile, tile), tile)
+            value = dot_cols(o_ref[at, :], rows_of(weights, c, tile, q_width + 2 * kv_width, q_width))
+            part[n, :, :, here] = value.reshape(2, rows, tile)
+
+        total.start(n)
+
+    attend(1 - me.h)
+    total.to_mate()
+    attend(me.h)
     outs[2].start()
     outs[3].start()
-    tile = 512
-
-    @pl.loop(0, model // tile)
-    def _(n):
-        here = pl.ds(pl.multiple_of(n * tile, tile), tile)
-        value = dot_cols(o_ref[...], rows_of(weights, n, tile, q_width + 2 * kv_width, q_width))
-        part[:, :, :, here] = value.reshape(2, 2, rows, tile)
-
-    total = QuadSum(me, part, from_pair, low, from_mate, sum_send, sum_recv)
-    total.start()
     for z in range(1, LINE - SOON):
         gather.forward(z)
-    total.to_mate()
     total.wait()
 
     def add(at):
@@ -1135,7 +1162,7 @@
         copy.wait()
 
 
-def attention_forward(count, q_width, kv_width, gains, lens, cos, sin, tokens_all, attn_all, up, down_t):
+def attention_forward(count, q_width, kv_width, lens, cos, sin, tokens_all, attn_all, up, down_t):
     _, _, rows, model = tokens_all.shape
     wide = 2 * rows
     plane = count // LINE
@@ -1151,13 +1178,14 @@
     return pl.pallas_call(
         functools.partial(attention_forward_kernel, plane),
         name="attention_forward",
-        out_shape=outs
+        out_shape=(jax.ShapeDtypeStruct((2, model), F32),)
+        + outs
         + (
             jax.ShapeDtypeStruct((count - SOON * plane,) + up.shape[1:], BF16),
             jax.ShapeDtypeStruct(down_t.shape, BF16),
         ),
-        in_specs=[VMEM] * 4 + [ANY] * 4,
-        out_specs=(ANY,) * 8,
+        in_specs=[VMEM] * 3 + [ANY] * 4,
+        out_specs=(VMEM,) + (ANY,) * 8,
         scratch_shapes=[
             pltpu.VMEM(attn_all.shape, BF16),
             pltpu.VMEM(tokens_all.shape, BF16),
@@ -1166,18 +1194,18 @@
             pltpu.VMEM((2, rows, model), F32),
             pltpu.VMEM((rows, model), BF16),
             pltpu.VMEM((rows, model), BF16),
-            DMA((1, LINE, kinds)), DMA((1, LINE, kinds)), DMA((2, LINE)), DMA((2, LINE)), DMA((2,)),
-            DMA((2,)), DMA((3 + LINE,)), DMA((6,)),
+            DMA((1, LINE, kinds)), DMA((1, LINE, kinds)), DMA((2, LINE)), DMA((2, LINE)), DMA((3,)),
+            DMA((3,)), DMA((3 + LINE,)), DMA((6,)),
         ],
         compiler_params=pltpu.CompilerParams(
             collective_id=2, has_side_effects=True, vmem_limit_bytes=60 * MB
         ),
-    )(gains, lens, cos, sin, tokens_all, attn_all, up, down_t)
+    )(lens, cos, sin, tokens_all, attn_all, up, down_t)
 
 
 def attention_backward_kernel(
     plane, gain_ref, cos_ref, sin_ref, total_in, x1_in, dm_in, tok_in, h1_in, qkv_in, probs_in, o_in,
-    a_ref, gw_ref, sum_ref, h_in, inner_in, ga_ref, w_out, grad_tokens, gain_parts, weights, own, other, first, second,
+    a_ref, gw_ref, sum_ref, h_in, inner_in, ga_ref, w_out, grad_tokens, gain_blocks, gain_parts, weights, own, other, first, second,
     total_ref, x1_ref, dm_ref, tok_ref, h1_ref, qkv_ref, probs_ref, o_ref, rows_in, inner, gw, dx, da, do,
     dqkv, dh1, from_pair, low, from_mate, first_send, first_recv, second_send, second_recv, load_sem,
     other_sem, part_send, part_recv, da_send, da_recv, sum_send, sum_recv, a_sem, keep_sem, grad_sem, in_sem,
@@ -1309,7 +1337,8 @@
             value = dot_cols(dqkv[...], rows_of(weights, n, tile, 0, qkv_width))
             dh1[:, :, :, here] = value.reshape(2, 2, rows, tile)
 
-        dh1_sum.start()
+        for h in range(2):
+            dh1_sum.start(h)
 
     def keep_grads(n):
         per = tile // block
@@ -1371,31 +1400,35 @@
     mlp_grads(1)
     summed.middle(0)
     summed.begin(1)
+    mlp_grads(2)
     das.forward()
-    mlp_grads(2)
     for copy in ins[3:8]:
         copy.wait()
+    summed.end(0)
+    part(0, 0).start()
     grad_o()
+    summed.middle(1)
+    summed.begin(2)
     grad_heads(0)
     grad_heads(1)
-    summed.end(0)
-    part(0, 0).start()
-    grad_h1()
-    summed.middle(1)
-    summed.begin(2)
-    dh1_sum.to_mate()
     mlp_grads(3)
     summed.end(1)
     part(1, 0).start()
-    grads()
+    grad_h1()
     summed.middle(2)
     summed.begin(3)
-    in_norm()
+    dh1_sum.to_mate()
+    grads()
     summed.end(2)
     part(2, 0).start()
     summed.middle(3)
+    in_norm()
     summed.end(3)
 
+    span = model // gain_blocks.shape[0]
+    gain_blocks[...] = jnp.zeros_like(gain_blocks)
+    for d in range(gain_blocks.shape[0]):
+        gain_blocks[d, 0:2, :span] = gain_parts[:, d * span : (d + 1) * span]
     keeps[0].start()
     for kind in range(2):
         for rank in range(LINE - 1):
@@ -1429,11 +1462,12 @@
             jax.ShapeDtypeStruct(attn_all.shape, BF16),
             jax.ShapeDtypeStruct((LINE, block, grad_mlp.shape[2] + first_sum.shape[2]), BF16),
             jax.ShapeDtypeStruct((rows, model), F32),
-            jax.ShapeDtypeStruct((2, model), F32),
+            jax.ShapeDtypeStruct((count, 8, max(128, model // count)), F32),
         ),
         in_specs=[VMEM] * 3 + [ANY] * 13,
         out_specs=(ANY, ANY, VMEM, VMEM),
         scratch_shapes=[
+            pltpu.VMEM((2, model), F32),
             pltpu.VMEM(attn_all.shape, BF16),
             *buffers,
             *[
@@ -1450,7 +1484,7 @@
             pltpu.VMEM((rows, model), BF16),
             pltpu.VMEM((rows, model), BF16),
             *sems,
-            DMA((2, LINE, 2)), DMA((2, LINE, 2)), DMA((3,)), DMA((3,)), DMA((2,)), DMA((2,)), DMA, DMA((2,)),
+            DMA((2, LINE, 2)), DMA((2, LINE, 2)), DMA((3,)), DMA((3,)), DMA((3,)), DMA((3,)), DMA, DMA((2,)),
             DMA((model // 512,)), DMA((10,)),
         ],
         compiler_params=pltpu.CompilerParams(
@@ -1534,21 +1568,26 @@
     for step in range(1, count):
         give_gain(step).start()
     pairs = [
-        remote(out_ref.at[z, 1 - me.t], out_pair.at[z], pair_send.at[z], pair_recv.at[z], me.sibling())
-        for z in range(LINE)
+        remote(
+            out_ref.at[ranked(me, rank), 1 - me.t], out_pair.at[ranked(me, rank)], pair_send.at[rank],
+            pair_recv.at[rank], me.sibling(),
+        )
+        for rank in range(LINE)
     ]
     for copy in pairs:
         copy.start()
     load_out.wait()
-    for z in range(LINE):
-        pairs[z].wait_recv()
+    def out_step(rank):
+        z = ranked(me, rank)
+        pairs[rank].wait_recv()
         add_rows(out_own.at[z], (out_own.at[z], out_pair.at[z]), out_own.shape[1])
-    for rank in range(LINE - 1):
-
-        @pl.when(jnp.logical_or(me.z == 0, me.z == LINE - 1))
-        def _():
-            outs.step(rank)
-
+        if rank < LINE - 1:
+
+            @pl.when(jnp.logical_or(me.z == 0, me.z == LINE - 1))
+            def _():
+                outs.step(rank)
+
+    out_step(0)
     at_end = jnp.logical_or(me.z == 0, me.z == LINE - 1)
 
     def out_start(at):
@@ -1567,11 +1606,9 @@
         summed.middle(rank)
         if rank + 1 < LINE:
             summed.begin(rank + 1)
+            out_step(rank + 1)
         else:
             load_x1.wait()
-            row_loop(output.shape[0], 16, out_start)
-            outs.total(add_out)
-            row_loop(output.shape[0], 16, out_end)
             total = gain_ref[me.d]
             for step in range(1, count):
                 give_gain(step).wait()
@@ -1592,6 +1629,9 @@
                 for late in (range(rank - 1, rank) if rank < LINE - 2 else range(rank - 1, LINE - 1)):
                     outs.step(late)
 
+    row_loop(output.shape[0], 16, out_start)
+    outs.total(add_out)
+    row_loop(output.shape[0], 16, out_end)
     keep = copy_in(own.at[LINE - 1], landed.at[me.z], load_out_sem.at[2])
     keep.start()
     for way, k in FAR_FIRST:
@@ -1646,7 +1686,7 @@
 
 
 def layouts_kernel(
-    a_ref, mlp_ref, output_ref, tokens_ref, q_out, k_out, v_out, o_out, gate_out, up_out, down_out,
+    gain_ref, a_ref, mlp_ref, output_ref, tokens_ref, gain_attn, gain_mlp, q_out, k_out, v_out, o_out, gate_out, up_out, down_out,
     output_out, tokens_out, a_v, mlp_v, output_v, tokens_v, q_v, k_v, v_v, o_v, gate_v, up_v, down_v,
     in_sem, out_sem,
 ):
@@ -1664,6 +1704,9 @@
         sent.append(copy_in(src, dst, out_sem.at[len(sent)]))
         sent[-1].start()
 
+    span = gain_attn.shape[1]
+    gain_attn[...] = gain_ref[0:1, :span]
+    gain_mlp[...] = gain_ref[1:2, :span]
     units = mlp_v.shape[2] // 3
     ins[0].wait()
     for z in range(LINE):
@@ -1693,7 +1736,7 @@
         copy.wait()
 
 
-def layouts(q_width, kv_width, a, mlp, output, grad_tokens):
+def layouts(q_width, kv_width, gain_sum, a, mlp, output, grad_tokens):
     block = a.shape[1]
     hidden = LINE * (mlp.shape[2] // 3)
     outs = (
@@ -1709,15 +1752,17 @@
     return pl.pallas_call(
         layouts_kernel,
         name="layouts",
-        out_shape=outs + tuple(jax.ShapeDtypeStruct(ref.shape, ref.dtype) for ref in ins[2:]),
-        in_specs=[ANY] * 4,
-        out_specs=(ANY,) * 9,
+        out_shape=(jax.ShapeDtypeStruct((1, block), F32),) * 2
+        + outs
+        + tuple(jax.ShapeDtypeStruct(ref.shape, ref.dtype) for ref in ins[2:]),
+        in_specs=[VMEM] + [ANY] * 4,
+        out_specs=(VMEM,) * 2 + (ANY,) * 9,
         scratch_shapes=[
             *[pltpu.VMEM(ref.shape, ref.dtype) for ref in ins + outs],
             DMA((4,)), DMA((3 * LINE + 6,)),
         ],
         compiler_params=pltpu.CompilerParams(vmem_limit_bytes=60 * MB),
-    )(*ins)
+    )(gain_sum, *ins)
 
 
 def shards(
@@ -1735,10 +1780,8 @@
         count, lengths, seq_of_group, gains,
         (w_query, key_weight, value_weight, w_out, w_gate, w_up, w_down), tokens, cotangent,
     )
-    gains_full = gains_all[:, :2, :rows].transpose(1, 0, 2).reshape(2, model).astype(F32)
-    x1, h2, h1, qkv, probs, attended, up_rest, down = attention_forward(
-        count, q_width // 2, kv_width // 2, gains_full, gains_all, cos, sin, tokens_all, attn_all, up,
-        down_t,
+    gains_full, x1, h2, h1, qkv, probs, attended, up_rest, down = attention_forward(
+        count, q_width // 2, kv_width // 2, gains_all, cos, sin, tokens_all, attn_all, up, down_t
     )
     grad_h2, out_parts, grad_mlp_w, down_sum, rows_in, inner = feed_forward(
         count, h2, dm_all.reshape(-1, model), gate_all, up_soon, up_rest, down
@@ -1747,15 +1790,14 @@
         count, gains_full, cos, sin, grad_h2, x1, dm_all, tokens_all, h1, qkv, probs, attended, attn_all,
         grad_mlp_w, down_sum, rows_in, inner,
     )
-    gain_parts = gain_parts.reshape(2, count, rows).transpose(1, 0, 2)
-    gain_parts = jnp.pad(gain_parts, ((0, 0), (0, 6), (0, lanes)))
     attn_sum, output, gain_sum = grad_sum(count, x1, grad_attn_w, out_parts, gain_parts)
     (
-        grad_query, grad_key, grad_value, grad_out, grad_gate, grad_up, grad_down, output, grad_tokens,
-    ) = layouts(q_width, kv_width, attn_sum, mlp_sum, output, grad_tokens)
+        grad_gain_attn, grad_gain_mlp, grad_query, grad_key, grad_value, grad_out, grad_gate, grad_up,
+        grad_down, output, grad_tokens,
+    ) = layouts(q_width, kv_width, gain_sum, attn_sum, mlp_sum, output, grad_tokens)
     return (
-        output, grad_tokens, grad_query, grad_key, grad_value, grad_out, gain_sum[0, :rows],
-        grad_gate, grad_up, grad_down, gain_sum[1, :rows],
+        output, grad_tokens, grad_query, grad_key, grad_value, grad_out, grad_gain_attn.reshape(rows),
+        grad_gate, grad_up, grad_down, grad_gain_mlp.reshape(rows),
     )
 
 

time: 477 us -> 452 us (0.948)
  Pallas kernels: 463 us -> 445 us
    pallas_call x1, Pallas kernels: 91.7 us -> 83.3 us  [attention_backward(): pl.pallas_call(functools.partial(attention_backward_kernel, count // LINE...]
    pallas_call x1, Pallas kernels: 124 us -> 118 us  [gather_all(): pl.pallas_call(functools.partial(gather_kernel, count), name='gather_all'...]
where the time goes in v7:
time: 452 us; the launch traced here: 448 us
  Pallas kernels  445 us (98%)
    pallas_call x1, Pallas kernels, gather_all(): pl.pallas_call(functools.partial(gather_kernel, count), name='gather_all'...  118 us
    pallas_call x1, Pallas kernels, feed_forward(): pl.pallas_call(functools.partial(feed_forward_kernel, count // LINE), nam...  113 us
    pallas_call x1, Pallas kernels, attention_backward(): pl.pallas_call(functools.partial(attention_backward_kernel, count // LINE...  83.3 us
    pallas_call x1, Pallas kernels, grad_sum(): pl.pallas_call(functools.partial(grad_sum_kernel, count), name='grad_sum'...  82 us
    pallas_call x1, Pallas kernels, attention_forward(): pl.pallas_call(functools.partial(attention_forward_kernel, plane), name='...  41.2 us

profile of v7, /device:TPU:8, one launch (start us, length us, event | category | flops | bytes accessed | tf_op | source)
XLA Modules:
  0.0 447.6 jit_solution(8076792702837616268)
XLA Ops:
  1.3 1.3 fusion.2.gain_ref
  2.6 118.0 %gather_all.1 = (bf16[16,128,1536]{2,1,0:T(8,128)(2,1)}, bf16[16,128,1024]{2,1,0:T(8,128)(2,1)}, bf16[8,128,1024]{2,1,0:T(8,128)(2,1)}, bf16[4,128,1024]{2,1,0:T...) custom-call(s32[16]{0:T(128)} %len_ref.1, ...), custom_call_target="tpu_custom_call" | custom-call | tf_op jit(solution)/shard_map/gather_all/pallas_call | solution.py:476
  120.6 41.2 %attention_forward.1 = (f32[2,2048]{1,0:T(2,128)}, f32[128,2048]{1,0:T(8,128)}, bf16[128,2048]{1,0:T(8,128)(2,1)}, bf16[512,2048]{1,0:T(8,128)(2,1)}, bf16[512,1...) custom-call(bf16[16,16,128]{2,1,0:T(8,128)(2,1)} %get-tuple-element., ...), custom_call_target="tpu_custom_call" | custom-call | tf_op jit(solution)/shard_map/attention_forward/pallas_call | solution.py:1178
  161.8 113.3 %feed_forward.1 = (f32[128,2048]{1,0:T(8,128)}, bf16[4,2,128,2048]{3,2,1,0:T(8,128)(2,1)}, bf16[4,128,2048]{2,1,0:T(8,128)(2,1)}, bf16[4,128,1024]{2,1,0:T(8,128...) custom-call(bf16[128,2048]{1,0:T(8,128)(2,1)} %get-tuple-element.58.h_ref, bf16[1024,2048]{1,0:T(8,128)(2,1)} %bitcast.5, ...), custom_call_target="tpu_custom_call" | custom-call | tf_op jit(solution)/shard_map/feed_forward/pallas_call | solution.py:952
  275.1 83.3 %attention_backward.1 = (bf16[16,128,1536]{2,1,0:T(8,128)(2,1)}, bf16[4,128,3072]{2,1,0:T(8,128)(2,1)}, f32[128,2048]{1,0:T(8,128)}, f32[16,8,128]{2,1,0:T(8,128)}) custom-call(f32[2,2048]{1,0:T(2,128)} %get-tuple-element.57.gain_ref, f32[256,128]{1,0:T(8,128)} %constant.7.clone.cos_ref, f32[256,128]{1,0:T(8,128)} %constant.8.clone.sin_ref, ...), custom_call_target="tpu_custom_call" | custom-call | tf_op jit(solution)/shard_map/attention_backward/pallas_call | solution.py:1458
  358.4 82.0 %grad_sum.1 = (f32[2,128,1536]{2,1,0:T(8,128)}, bf16[128,2048]{1,0:T(8,128)(2,1)}, f32[8,128]{1,0:T(8,128)}) custom-call(f32[16,8,128]{2,1,0:T(8,128)} %get-tuple-element.74.gain_ref, f32[128,2048]{1,0:T(8,128)} %get-tuple-element.65.x1_in, bf16[16,128,1536]{2,1,0:T(8,128)(2,1)} %get-tuple-element.75.ga_ref, bf16[4,2,128,2048]{3,2,1,0:T(8,128)(2,1)} %get-tuple-element.76.out_ref), custom_call_target="tpu_custom_call" | custom-call | tf_op jit(solution)/shard_map/grad_sum/pallas_call | solution.py:1659
  440.5 7.0 %layouts.1 = (f32[1,128]{1,0:T(1,128)}, f32[1,128]{1,0:T(1,128)}, f32[128,1024]{1,0:T(8,128)}, f32[128,512]{1,0:T(8,128)}, f32[128,512]{1,0:T(8,128)}, /*index=5...) custom-call(f32[8,128]{1,0:T(8,128)} %get-tuple-element.77.gain_ref,, ...), custom_call_target="tpu_custom_call" | custom-call | tf_op jit(solution)/shard_map/layouts/pallas_call | solution.py:1752

commit v8 on v7

--- a/solution.py
+++ b/solution.py
@@ -1058,7 +1058,7 @@
 
     span = model // (plane * LINE)
     for d in range(plane * LINE):
-        gain_ref[:, d * span : (d + 1) * span] = lens_ref[d, 0:2, :span].astype(F32)
+        gain_ref[:, d * span : (d + 1) * span] = lens_ref[d].astype(F32)[0:2, :span]
     load_tok.wait()
 
     for n in range(4):
@@ -1101,7 +1101,7 @@
     total = QuadSum(me, part, from_pair, low, from_mate, sum_send, sum_recv)
 
     def attend(n):
-        length = lens_ref[me.d + (n - me.h) * plane, 2:3, 0:1].astype(F32)
+        length = lens_ref[me.d + (n - me.h) * plane].astype(F32)[2:3, 0:1]
         allowed = jnp.logical_and(key <= row, key.astype(F32) < length)
         at = pl.ds(pl.multiple_of(n * wide, wide), wide)
         for i in range(heads):
@@ -1623,11 +1623,11 @@
         summed.end(rank)
         if rank < LINE - 1:
             part(rank).start()
-        if 0 < rank < LINE - 1:
+        for late in {0: (0,), 1: (2, 1)}.get(rank, ()):
             @pl.when(jnp.logical_not(at_end))
             def _():
-                for late in (range(rank - 1, rank) if rank < LINE - 2 else range(rank - 1, LINE - 1)):
-                    outs.step(late)
+                outs.step(late)
+
 
     row_loop(output.shape[0], 16, out_start)
     outs.total(add_out)

time: 452 us -> 449 us (level)
  no operation moved by 1% of the time
where the time goes in v8:
time: 449 us; the launch traced here: 445 us
  Pallas kernels  442 us (98%)
    pallas_call x1, Pallas kernels, gather_all(): pl.pallas_call(functools.partial(gather_kernel, count), name='gather_all'...  118 us
    pallas_call x1, Pallas kernels, feed_forward(): pl.pallas_call(functools.partial(feed_forward_kernel, count // LINE), nam...  113 us
    pallas_call x1, Pallas kernels, attention_backward(): pl.pallas_call(functools.partial(attention_backward_kernel, count // LINE...  83.3 us
    pallas_call x1, Pallas kernels, grad_sum(): pl.pallas_call(functools.partial(grad_sum_kernel, count), name='grad_sum'...  79.5 us
    pallas_call x1, Pallas kernels, attention_forward(): pl.pallas_call(functools.partial(attention_forward_kernel, plane), name='...  41.2 us

profile of v8, /device:TPU:8, one launch (start us, length us, event | category | flops | bytes accessed | tf_op | source)
XLA Modules:
  0.0 445.1 jit_solution(8074374802729571102)
XLA Ops:
  1.3 1.3 fusion.2.gain_ref
  2.6 118.0 %gather_all.1 = (bf16[16,128,1536]{2,1,0:T(8,128)(2,1)}, bf16[16,128,1024]{2,1,0:T(8,128)(2,1)}, bf16[8,128,1024]{2,1,0:T(8,128)(2,1)}, bf16[4,128,1024]{2,1,0:T...) custom-call(s32[16]{0:T(128)} %len_ref.1, ...), custom_call_target="tpu_custom_call" | custom-call | tf_op jit(solution)/shard_map/gather_all/pallas_call | solution.py:476
  120.6 41.2 %attention_forward.1 = (f32[2,2048]{1,0:T(2,128)}, f32[128,2048]{1,0:T(8,128)}, bf16[128,2048]{1,0:T(8,128)(2,1)}, bf16[512,2048]{1,0:T(8,128)(2,1)}, bf16[512,1...) custom-call(bf16[16,16,128]{2,1,0:T(8,128)(2,1)} %get-tuple-element., ...), custom_call_target="tpu_custom_call" | custom-call | tf_op jit(solution)/shard_map/attention_forward/pallas_call | solution.py:1178
  161.8 113.3 %feed_forward.1 = (f32[128,2048]{1,0:T(8,128)}, bf16[4,2,128,2048]{3,2,1,0:T(8,128)(2,1)}, bf16[4,128,2048]{2,1,0:T(8,128)(2,1)}, bf16[4,128,1024]{2,1,0:T(8,128...) custom-call(bf16[128,2048]{1,0:T(8,128)(2,1)} %get-tuple-element.58.h_ref, bf16[1024,2048]{1,0:T(8,128)(2,1)} %bitcast.5, ...), custom_call_target="tpu_custom_call" | custom-call | tf_op jit(solution)/shard_map/feed_forward/pallas_call | solution.py:952
  275.1 83.3 %attention_backward.1 = (bf16[16,128,1536]{2,1,0:T(8,128)(2,1)}, bf16[4,128,3072]{2,1,0:T(8,128)(2,1)}, f32[128,2048]{1,0:T(8,128)}, f32[16,8,128]{2,1,0:T(8,128)}) custom-call(f32[2,2048]{1,0:T(2,128)} %get-tuple-element.57.gain_ref, f32[256,128]{1,0:T(8,128)} %constant.7.clone.cos_ref, f32[256,128]{1,0:T(8,128)} %constant.8.clone.sin_ref, ...), custom_call_target="tpu_custom_call" | custom-call | tf_op jit(solution)/shard_map/attention_backward/pallas_call | solution.py:1458
  358.4 79.5 %grad_sum.1 = (f32[2,128,1536]{2,1,0:T(8,128)}, bf16[128,2048]{1,0:T(8,128)(2,1)}, f32[8,128]{1,0:T(8,128)}) custom-call(f32[16,8,128]{2,1,0:T(8,128)} %get-tuple-element.74.gain_ref, f32[128,2048]{1,0:T(8,128)} %get-tuple-element.65.x1_in, bf16[16,128,1536]{2,1,0:T(8,128)(2,1)} %get-tuple-element.75.ga_ref, bf16[4,2,128,2048]{3,2,1,0:T(8,128)(2,1)} %get-tuple-element.76.out_ref), custom_call_target="tpu_custom_call" | custom-call | tf_op jit(solution)/shard_map/grad_sum/pallas_call | solution.py:1659
  437.9 7.0 %layouts.1 = (f32[1,128]{1,0:T(1,128)}, f32[1,128]{1,0:T(1,128)}, f32[128,1024]{1,0:T(8,128)}, f32[128,512]{1,0:T(8,128)}, f32[128,512]{1,0:T(8,128)}, /*index=5...) custom-call(f32[8,128]{1,0:T(8,128)} %get-tuple-element.77.gain_ref,, ...), custom_call_target="tpu_custom_call" | custom-call | tf_op jit(solution)/shard_map/layouts/pallas_call | solution.py:1752

commit v9 on v8

--- a/solution.py
+++ b/solution.py
@@ -78,14 +78,16 @@
     pl.semaphore_wait(barrier, count)
 
 
-def greet_line(me):
+def greet_near(me):
     barrier = pltpu.get_barrier_semaphore()
+    for step in range(1, me.plane):
+        target = lax.rem(me.p + step, me.plane)
+        pl.semaphore_signal(barrier, inc=1, device_id=me.at(me.z, target), device_id_type=MESH)
     for step in range(1, LINE):
-        pl.semaphore_signal(
-            barrier, inc=1, device_id=me.at(lax.rem(me.z + step, LINE), me.p), device_id_type=MESH
-        )
+        target = lax.rem(me.z + step, LINE)
+        pl.semaphore_signal(barrier, inc=1, device_id=me.at(target, me.p), device_id_type=MESH)
     pl.semaphore_signal(barrier, inc=1, device_id=me.sibling(), device_id_type=MESH)
-    pl.semaphore_wait(barrier, LINE)
+    pl.semaphore_wait(barrier, me.plane + LINE - 1)
 
 
 def reach(me, way, k):
@@ -727,7 +729,7 @@
     load_dm.start()
     keep = pltpu.make_async_copy(h_ref, slot(me.z, me.t), load_sem.at[1])
     keep.start()
-    greet_all(me, plane * LINE)
+    greet_near(me)
     gather = PlaneGather(
         me, 0, weights.at[:, :, pl.ds(2 * units, units)], block, plane_send, plane_recv
     )
@@ -982,15 +984,6 @@
     )(h, dm_all, gate_all, up_soon, up_rest, down)
 
 
-def greet_plane(me):
-    barrier = pltpu.get_barrier_semaphore()
-    for step in range(1, me.plane):
-        target = lax.rem(me.p + step, me.plane)
-        pl.semaphore_signal(barrier, inc=1, device_id=me.at(me.z, target), device_id_type=MESH)
-    pl.semaphore_signal(barrier, inc=1, device_id=me.sibling(), device_id_type=MESH)
-    pl.semaphore_wait(barrier, me.plane)
-
-
 def columns_of(weights, start, width):
     count, rows, _ = weights.shape
     return weights[:, :, pl.ds(start, width)].reshape(count * rows, width)
@@ -1037,7 +1030,7 @@
             )
         )
     ]
-    greet_all(me, plane * LINE)
+    greet_near(me)
     gather = PlaneGather(me, 0, up_rest, up.shape[1], plane_send, plane_recv)
     for z in range(LINE - SOON):
         gather.start(z, up.at[far + z])
@@ -1244,7 +1237,7 @@
     for copy in ins[3:8]:
         copy.start()
     summed.load_rank(0)
-    greet_all(me, plane * LINE)
+    greet_near(me)
 
     wide = own.shape[2]
     spans = (pl.ds(0, wide), pl.ds(wide, sum_ref.shape[2]))

time: 449 us -> 447 us (level)
  no operation moved by 1% of the time
where the time goes in v9:
time: 447 us; the launch traced here: 443 us
  Pallas kernels  440 us (98%)
    pallas_call x1, Pallas kernels, gather_all(): pl.pallas_call(functools.partial(gather_kernel, count), name='gather_all'...  118 us
    pallas_call x1, Pallas kernels, feed_forward(): pl.pallas_call(functools.partial(feed_forward_kernel, count // LINE), nam...  111 us
    pallas_call x1, Pallas kernels, grad_sum(): pl.pallas_call(functools.partial(grad_sum_kernel, count), name='grad_sum'...  81.4 us
    pallas_call x1, Pallas kernels, attention_backward(): pl.pallas_call(functools.partial(attention_backward_kernel, count // LINE...  81.3 us
    pallas_call x1, Pallas kernels, attention_forward(): pl.pallas_call(functools.partial(attention_forward_kernel, plane), name='...  41.2 us

profile of v9, /device:TPU:8, one launch (start us, length us, event | category | flops | bytes accessed | tf_op | source)
XLA Modules:
  0.0 442.8 jit_solution(15651414282181048106)
XLA Ops:
  1.3 1.3 fusion.2.gain_ref
  2.6 118.0 %gather_all.1 = (bf16[16,128,1536]{2,1,0:T(8,128)(2,1)}, bf16[16,128,1024]{2,1,0:T(8,128)(2,1)}, bf16[8,128,1024]{2,1,0:T(8,128)(2,1)}, bf16[4,128,1024]{2,1,0:T...) custom-call(s32[16]{0:T(128)} %len_ref.1, ...), custom_call_target="tpu_custom_call" | custom-call | tf_op jit(solution)/shard_map/gather_all/pallas_call | solution.py:478
  120.6 41.2 %attention_forward.1 = (f32[2,2048]{1,0:T(2,128)}, f32[128,2048]{1,0:T(8,128)}, bf16[128,2048]{1,0:T(8,128)(2,1)}, bf16[512,2048]{1,0:T(8,128)(2,1)}, bf16[512,1...) custom-call(bf16[16,16,128]{2,1,0:T(8,128)(2,1)} %get-tuple-element., ...), custom_call_target="tpu_custom_call" | custom-call | tf_op jit(solution)/shard_map/attention_forward/pallas_call | solution.py:1171
  161.8 111.0 %feed_forward.1 = (f32[128,2048]{1,0:T(8,128)}, bf16[4,2,128,2048]{3,2,1,0:T(8,128)(2,1)}, bf16[4,128,2048]{2,1,0:T(8,128)(2,1)}, bf16[4,128,1024]{2,1,0:T(8,128...) custom-call(bf16[128,2048]{1,0:T(8,128)(2,1)} %get-tuple-element.58.h_ref, bf16[1024,2048]{1,0:T(8,128)(2,1)} %bitcast.5, ...), custom_call_target="tpu_custom_call" | custom-call | tf_op jit(solution)/shard_map/feed_forward/pallas_call | solution.py:954
  272.8 81.3 %attention_backward.1 = (bf16[16,128,1536]{2,1,0:T(8,128)(2,1)}, bf16[4,128,3072]{2,1,0:T(8,128)(2,1)}, f32[128,2048]{1,0:T(8,128)}, f32[16,8,128]{2,1,0:T(8,128)}) custom-call(f32[2,2048]{1,0:T(2,128)} %get-tuple-element.57.gain_ref, f32[256,128]{1,0:T(8,128)} %constant.7.clone.cos_ref, f32[256,128]{1,0:T(8,128)} %constant.8.clone.sin_ref, ...), custom_call_target="tpu_custom_call" | custom-call | tf_op jit(solution)/shard_map/attention_backward/pallas_call | solution.py:1451
  354.1 81.4 %grad_sum.1 = (f32[2,128,1536]{2,1,0:T(8,128)}, bf16[128,2048]{1,0:T(8,128)(2,1)}, f32[8,128]{1,0:T(8,128)}) custom-call(f32[16,8,128]{2,1,0:T(8,128)} %get-tuple-element.74.gain_ref, f32[128,2048]{1,0:T(8,128)} %get-tuple-element.65.x1_in, bf16[16,128,1536]{2,1,0:T(8,128)(2,1)} %get-tuple-element.75.ga_ref, bf16[4,2,128,2048]{3,2,1,0:T(8,128)(2,1)} %get-tuple-element.76.out_ref), custom_call_target="tpu_custom_call" | custom-call | tf_op jit(solution)/shard_map/grad_sum/pallas_call | solution.py:1652
  435.6 7.0 %layouts.1 = (f32[1,128]{1,0:T(1,128)}, f32[1,128]{1,0:T(1,128)}, f32[128,1024]{1,0:T(8,128)}, f32[128,512]{1,0:T(8,128)}, f32[128,512]{1,0:T(8,128)}, /*index=5...) custom-call(f32[8,128]{1,0:T(8,128)} %get-tuple-element.77.gain_ref,, ...), custom_call_target="tpu_custom_call" | custom-call | tf_op jit(solution)/shard_map/layouts/pallas_call | solution.py:1745

commit v10 on v9

--- a/solution.py
+++ b/solution.py
@@ -95,16 +95,22 @@
 
 
 class Chain:
-    def __init__(self, me, first, held, send, recv):
+    def __init__(self, me, first, held, send, recv, pieces=1):
         self.me, self.first, self.held, self.send, self.recv = me, first, held, send, recv
-
-    def copy(self, way, k):
+        self.pieces = pieces
+        self.rows = first.shape[0] // pieces
+
+    def piece(self, ref, i):
+        return ref.at[pl.ds(i * self.rows, self.rows)]
+
+    def copy(self, way, k, i):
         me = self.me
         _, origin = reach(me, way, k)
         target = me.z + 1 if way == 0 else me.z - 1
         src = self.first if k == 0 else self.held(origin)
         return remote(
-            src, self.held(origin), self.send.at[way, k], self.recv.at[way, k + 1], me.at(target, me.p)
+            self.piece(src, i), self.piece(self.held(origin), i), self.send.at[way, k, i],
+            self.recv.at[way, k + 1, i], me.at(target, me.p),
         )
 
     def goes(self, way, k):
@@ -112,16 +118,16 @@
         ahead, _ = reach(self.me, 1 - way, 1)
         return jnp.logical_and(have, ahead)
 
-    def start(self, way, k):
+    def start(self, way, k, i=0):
         if k < LINE - 1:
 
             @pl.when(self.goes(way, k))
             def _():
-                self.copy(way, k).start()
-
-    def wait_block(self, way, k):
+                self.copy(way, k, i).start()
+
+    def wait_block(self, way, k, i=0):
         _, origin = reach(self.me, way, k)
-        arrival(self.held(origin), self.recv.at[way, k])
+        arrival(self.piece(self.held(origin), i), self.recv.at[way, k, i])
 
     def finish(self):
         for way in range(2):
@@ -129,7 +135,8 @@
 
                 @pl.when(self.goes(way, k))
                 def _():
-                    self.copy(way, k).wait_send()
+                    for i in range(self.pieces):
+                        self.copy(way, k, i).wait_send()
 
 
 class PlaneGather:
@@ -499,7 +506,7 @@
             pltpu.VMEM((LINE, rows, units), BF16),
             pltpu.VMEM(cotangent.shape, BF16),
             pltpu.VMEM(gains.shape, BF16),
-            DMA((2, LINE)), DMA((2, LINE)), DMA((2, LINE, 3)), DMA((2, LINE, 3)),
+            DMA((2, LINE, 1)), DMA((2, LINE, 1)), DMA((2, LINE, 3)), DMA((2, LINE, 3)),
             DMA((3, LINE, kinds)), DMA((3, LINE, kinds)), DMA((count,)), DMA((count,)),
             DMA((LINE,)), DMA((LINE,)), DMA((3,)), DMA((3,)), DMA((18 + SOON,)),
         ],
@@ -737,15 +744,20 @@
         me, down_grad, own, other, first, second,
         (first_send, first_recv, second_send, second_recv, own_sem, other_sem),
     )
-    chain = Chain(me, h_ref, lambda z: slot(z, me.t), chain_send, chain_recv)
-
-    def share(z, first=None):
+    chain = Chain(me, h_ref, lambda z: slot(z, me.t), chain_send, chain_recv, 2)
+
+    def share(z, i, first=None):
         src = slot(z, me.t) if first is None else first
-        return remote(src, slot(z, me.t), pass_send.at[z], pass_recv.at[z], me.sibling())
-
-    for way in range(2):
-        chain.start(way, 0)
-    share(me.z, h_ref).start()
+        return remote(
+            chain.piece(src, i), chain.piece(slot(z, me.t), i), pass_send.at[z, i], pass_recv.at[z, i],
+            me.sibling(),
+        )
+
+    for i in range(2):
+        for way in range(2):
+            chain.start(way, 0, i)
+    for i in range(2):
+        share(me.z, i, h_ref).start()
     for z in range(2):
         gather.start(z, down.at[z])
     for copy in own_down:
@@ -877,11 +889,13 @@
 
             @pl.when(have)
             def _():
-                if k:
-                    chain.wait_block(way, k)
-                    chain.start(way, k)
-                    share(z).start()
-                arrival(slot(z, 1 - me.t), pass_recv.at[z])
+                for i in range(2):
+                    if k:
+                        chain.wait_block(way, k, i)
+                        chain.start(way, k, i)
+                        share(z, i).start()
+                for i in range(2):
+                    arrival(chain.piece(slot(z, 1 - me.t), i), pass_recv.at[z, i])
                 project(z)
 
         gather.forward(k)
@@ -929,7 +943,8 @@
     summed.finish()
     chain.finish()
     for z in range(LINE):
-        share(z).wait_send()
+        for i in range(2):
+            share(z, i).wait_send()
         keep_out(z).wait()
         keep_sum(z).wait()
         pair(z).wait_send()
@@ -974,7 +989,7 @@
             pltpu.VMEM((2, LINE - 1, rows, model), BF16),
             *buffers,
             *sems,
-            DMA((2, LINE)), DMA((2, LINE)), DMA((LINE,)), DMA((LINE,)), DMA((LINE,)), DMA((LINE,)),
+            DMA((2, LINE, 2)), DMA((2, LINE, 2)), DMA((LINE, 2)), DMA((LINE, 2)), DMA((LINE,)), DMA((LINE,)),
             DMA((2, LINE, 2)), DMA((2, LINE, 2)), DMA((1, LINE, kinds)), DMA((1, LINE, kinds)),
             DMA((4 + LINE,)), DMA, DMA((LINE,)), DMA((LINE,)), DMA((LINE,)),
         ],

time: 447 us -> 445 us (level)
  no operation moved by 1% of the time
where the time goes in v10:
time: 445 us; the launch traced here: 439 us
  Pallas kernels  436 us (98%)
    pallas_call x1, Pallas kernels, gather_all(): pl.pallas_call(functools.partial(gather_kernel, count), name='gather_all'...  118 us
    pallas_call x1, Pallas kernels, feed_forward(): pl.pallas_call(functools.partial(feed_forward_kernel, count // LINE), nam...  108 us
    pallas_call x1, Pallas kernels, attention_backward(): pl.pallas_call(functools.partial(attention_backward_kernel, count // LINE...  80.7 us
    pallas_call x1, Pallas kernels, grad_sum(): pl.pallas_call(functools.partial(grad_sum_kernel, count), name='grad_sum'...  80.5 us
    pallas_call x1, Pallas kernels, attention_forward(): pl.pallas_call(functools.partial(attention_forward_kernel, plane), name='...  41.2 us

profile of v10, /device:TPU:8, one launch (start us, length us, event | category | flops | bytes accessed | tf_op | source)
XLA Modules:
  0.0 438.7 jit_solution(17331954126247653034)
XLA Ops:
  1.3 1.3 fusion.2.gain_ref
  2.6 118.0 %gather_all.1 = (bf16[16,128,1536]{2,1,0:T(8,128)(2,1)}, bf16[16,128,1024]{2,1,0:T(8,128)(2,1)}, bf16[8,128,1024]{2,1,0:T(8,128)(2,1)}, bf16[4,128,1024]{2,1,0:T...) custom-call(s32[16]{0:T(128)} %len_ref.1, ...), custom_call_target="tpu_custom_call" | custom-call | tf_op jit(solution)/shard_map/gather_all/pallas_call | solution.py:485
  120.6 41.2 %attention_forward.1 = (f32[2,2048]{1,0:T(2,128)}, f32[128,2048]{1,0:T(8,128)}, bf16[128,2048]{1,0:T(8,128)(2,1)}, bf16[512,2048]{1,0:T(8,128)(2,1)}, bf16[512,1...) custom-call(bf16[16,16,128]{2,1,0:T(8,128)(2,1)} %get-tuple-element., ...), custom_call_target="tpu_custom_call" | custom-call | tf_op jit(solution)/shard_map/attention_forward/pallas_call | solution.py:1186
  161.8 108.4 %feed_forward.1 = (f32[128,2048]{1,0:T(8,128)}, bf16[4,2,128,2048]{3,2,1,0:T(8,128)(2,1)}, bf16[4,128,2048]{2,1,0:T(8,128)(2,1)}, bf16[4,128,1024]{2,1,0:T(8,128...) custom-call(bf16[128,2048]{1,0:T(8,128)(2,1)} %get-tuple-element.58.h_ref, bf16[1024,2048]{1,0:T(8,128)(2,1)} %bitcast.5, ...), custom_call_target="tpu_custom_call" | custom-call | tf_op jit(solution)/shard_map/feed_forward/pallas_call | solution.py:969
  270.2 80.7 %attention_backward.1 = (bf16[16,128,1536]{2,1,0:T(8,128)(2,1)}, bf16[4,128,3072]{2,1,0:T(8,128)(2,1)}, f32[128,2048]{1,0:T(8,128)}, f32[16,8,128]{2,1,0:T(8,128)}) custom-call(f32[2,2048]{1,0:T(2,128)} %get-tuple-element.57.gain_ref, f32[256,128]{1,0:T(8,128)} %constant.7.clone.cos_ref, f32[256,128]{1,0:T(8,128)} %constant.8.clone.sin_ref, ...), custom_call_target="tpu_custom_call" | custom-call | tf_op jit(solution)/shard_map/attention_backward/pallas_call | solution.py:1466
  350.9 80.5 %grad_sum.1 = (f32[2,128,1536]{2,1,0:T(8,128)}, bf16[128,2048]{1,0:T(8,128)(2,1)}, f32[8,128]{1,0:T(8,128)}) custom-call(f32[16,8,128]{2,1,0:T(8,128)} %get-tuple-element.74.gain_ref, f32[128,2048]{1,0:T(8,128)} %get-tuple-element.65.x1_in, bf16[16,128,1536]{2,1,0:T(8,128)(2,1)} %get-tuple-element.75.ga_ref, bf16[4,2,128,2048]{3,2,1,0:T(8,128)(2,1)} %get-tuple-element.76.out_ref), custom_call_target="tpu_custom_call" | custom-call | tf_op jit(solution)/shard_map/grad_sum/pallas_call | solution.py:1667
  431.5 7.0 %layouts.1 = (f32[1,128]{1,0:T(1,128)}, f32[1,128]{1,0:T(1,128)}, f32[128,1024]{1,0:T(8,128)}, f32[128,512]{1,0:T(8,128)}, f32[128,512]{1,0:T(8,128)}, /*index=5...) custom-call(f32[8,128]{1,0:T(8,128)} %get-tuple-element.77.gain_ref,, ...), custom_call_target="tpu_custom_call" | custom-call | tf_op jit(solution)/shard_map/layouts/pallas_call | solution.py:1760
